TPU v7x, 32 devices: a whole 2x2x4 slice. The times are simulated.
32 devices in a mesh: dp: 4 (over y, x), tensor: 8 (over z, core).
Axes of the slice: x: 2, y: 2, z: 4, core: 2. Of those that a mesh axis runs over, the one named last changes fastest.
Arguments:
- layer_input: bfloat16 [8192, 2048], P('dp', 'tensor'), may hold values from -6 to 6
- cotangent: bfloat16 [8192, 2048], P('dp', 'tensor'), may hold values from -6 to 6
- first_gain: bfloat16 [2048], P('dp'), may hold values from 0.099609375 to 1.8984375
- query_weight: bfloat16 [2048, 3072], P('dp', 'tensor'), may hold values from -0.125 to 0.125
- latent_down: bfloat16 [2048, 576], P('dp'), may hold values from -0.125 to 0.125
- latent_gain: bfloat16 [512], P('dp'), may hold values from 0.099609375 to 1.8984375
- latent_up: bfloat16 [512, 4096], P('dp', 'tensor'), may hold values from -0.25 to 0.25
- output_weight: bfloat16 [2048, 2048], P('tensor', 'dp'), may hold values from -1 to 1
- second_gain: bfloat16 [2048], P('dp'), may hold values from 0.099609375 to 1.8984375
- router_weight: bfloat16 [2048, 16], P('dp'), may hold values from -0.03125 to 0.03125
- expert_gate: bfloat16 [16, 2048, 1408], P(None, 'dp', 'tensor'), may hold values from -0.125 to 0.125
- expert_up: bfloat16 [16, 2048, 1408], P(None, 'dp', 'tensor'), may hold values from -0.125 to 0.125
- expert_down: bfloat16 [16, 1408, 2048], P(None, 'tensor', 'dp'), may hold values from -0.15625 to 0.15625
- shared_gate: bfloat16 [2048, 2816], P('dp', 'tensor'), may hold values from -0.125 to 0.125
- shared_up: bfloat16 [2048, 2816], P('dp', 'tensor'), may hold values from -0.125 to 0.125
- shared_down: bfloat16 [2816, 2048], P('tensor', 'dp'), may hold values from -0.109375 to 0.109375
- routes: int32 [8192, 6], P('dp'), may hold values from 0 to 15, all different within a row
Outputs:
- layer_output: bfloat16 [8192, 2048], P('dp', 'tensor')
- input_delta: float32 [8192, 2048], P('dp', 'tensor')
- first_gain_delta: float32 [2048], P('dp')
- query_weight_delta: float32 [2048, 3072], P('dp', 'tensor')
- latent_down_delta: float32 [2048, 576], P('dp')
- latent_gain_delta: float32 [512], P('dp')
- latent_up_delta: float32 [512, 4096], P('dp', 'tensor')
- output_weight_delta: float32 [2048, 2048], P('tensor', 'dp')
- second_gain_delta: float32 [2048], P('dp')
- router_weight_delta: float32 [2048, 16], P('dp')
- expert_gate_delta: float32 [16, 2048, 1408], P(None, 'dp', 'tensor')
- expert_up_delta: float32 [16, 2048, 1408], P(None, 'dp', 'tensor')
- expert_down_delta: float32 [16, 1408, 2048], P(None, 'tensor', 'dp')
- shared_gate_delta: float32 [2048, 2816], P('dp', 'tensor')
- shared_up_delta: float32 [2048, 2816], P('dp', 'tensor')
- shared_down_delta: float32 [2816, 2048], P('tensor', 'dp')
Inputs may be any that keep to these rules, and one draw needn't show every extreme that they name: `routes`: each token names 6 different experts, in the order in which its pairs take slots; every expert is named by some token.
All inputs are finite; a program needn't handle non-finite values.
Results may differ from a plain program's by a relative error of at most 0.022.
Values may be sent and summed in bfloat16 or wider, within the bound.
No kernel may reach another device: no remote copies, remote signals or barrier semaphores. Data moves between devices by JAX's collectives and lax.ppermute only.
A program may use at most 1 GiB of HBM per device.

v0:
```python
import jax
import jax.numpy as jnp
from jax import lax
from jax.sharding import PartitionSpec as P

D = 2048
DN = 128
DR = 64
DV = 128
R = 512
TOP = 6
E = 16
LEN = 1024
CAP = 864


EPSILON = 1e-06


def normed(values, factor):
    return values * lax.rsqrt(jnp.mean(values * values, axis=-1, keepdims=True) + EPSILON) * factor


def angles(number, halfway):
    position = (jnp.arange(number, dtype=jnp.int32) % LEN).astype(jnp.float32)
    spread = 10000.0 ** (-jnp.arange(halfway, dtype=jnp.float32) / halfway)
    phases = position[:, None] * spread[None, :]
    return (jnp.cos(phases), jnp.sin(phases))


def rotate(values, cosine, sine_term):
    halfway = values.shape[-1] // 2
    leading = values[..., :halfway]
    trailing = values[..., halfway:]
    return jnp.concatenate(
        [leading * cosine - trailing * sine_term, trailing * cosine + leading * sine_term], axis=-1
    )


def slot_plan(routes):
    number = routes.shape[0]
    flattened = routes.reshape(-1)
    matches = (flattened[:, None] == jnp.arange(E, dtype=jnp.int32)[None, :]).astype(jnp.int32)
    earlier = jnp.cumsum(matches, axis=0) - matches
    position = jnp.sum(earlier * matches, axis=1)
    retained = position < CAP
    slot_index = jnp.where(retained, flattened * CAP + position, E * CAP)
    pair_owner = jnp.arange(number * TOP, dtype=jnp.int32) // TOP
    slot_owner = (
        jnp.full((E * CAP + 1,), number, jnp.int32).at[slot_index].set(pair_owner)[: E * CAP]
    )
    return (slot_index.reshape(number, TOP), retained.reshape(number, TOP), slot_owner)


def product(former, latter):
    return jnp.dot(former, latter, preferred_element_type=jnp.float32)


def outer_sum(former, latter):
    return lax.dot_general(
        former, latter, (((0,), (0,)), ((), ())), preferred_element_type=jnp.float32
    )


def product_back(former, latter):
    return lax.dot_general(
        former, latter, (((1,), (1,)), ((), ())), preferred_element_type=jnp.float32
    )


def gated(gate_part, up_part):
    return jax.nn.silu(gate_part) * up_part


def per_device(
    layer_input,
    cotangent,
    first_gain,
    query_weight,
    latent_down,
    latent_gain,
    latent_up,
    output_weight,
    second_gain,
    router_weight,
    expert_gate,
    expert_up,
    expert_down,
    shared_gate,
    shared_up,
    shared_down,
    routes,
):
    fetched = (
        lax.all_gather(first_gain, "dp", axis=0, tiled=True),
        lax.all_gather(query_weight, "dp", axis=0, tiled=True),
        lax.all_gather(latent_down, "dp", axis=0, tiled=True),
        lax.all_gather(latent_gain, "dp", axis=0, tiled=True),
        lax.all_gather(latent_up, "dp", axis=0, tiled=True),
        lax.all_gather(output_weight, "dp", axis=1, tiled=True),
        lax.all_gather(second_gain, "dp", axis=0, tiled=True),
        lax.all_gather(router_weight, "dp", axis=0, tiled=True),
        lax.all_gather(expert_gate, "dp", axis=1, tiled=True),
        lax.all_gather(expert_up, "dp", axis=1, tiled=True),
        lax.all_gather(expert_down, "dp", axis=2, tiled=True),
        lax.all_gather(shared_gate, "dp", axis=0, tiled=True),
        lax.all_gather(shared_up, "dp", axis=0, tiled=True),
        lax.all_gather(shared_down, "dp", axis=1, tiled=True),
    )
    (
        first_gain,
        query_weight,
        latent_down,
        latent_gain,
        latent_up,
        output_weight,
        second_gain,
        router_weight,
        expert_gate,
        expert_up,
        expert_down,
        shared_gate,
        shared_up,
        shared_down,
    ) = fetched
    share_width = D // lax.axis_size("tensor")
    share_start = lax.axis_index("tensor") * share_width
    rows_full = lax.all_gather(layer_input, "tensor", axis=1, tiled=True).astype(jnp.float32)
    number = rows_full.shape[0]
    sequences = number // LEN
    heads_here = output_weight.shape[0] // DV
    cosine, sine_term = angles(number, DR // 2)
    first_exact, first_pull = jax.vjp(normed, rows_full, first_gain.astype(jnp.float32))
    first_round = first_exact.astype(jnp.bfloat16)

    def rotate_queries(raw_queries):
        return jnp.concatenate(
            [
                raw_queries[..., :DN],
                rotate(raw_queries[..., DN:], cosine[:, None], sine_term[:, None]),
            ],
            axis=-1,
        )

    def rotate_keys(raw_keys):
        return rotate(raw_keys, cosine, sine_term)

    raw_queries = product(first_round, query_weight).reshape(number, heads_here, DN + DR)
    queries_exact, queries_pull = jax.vjp(rotate_queries, raw_queries)
    queries = queries_exact.astype(jnp.bfloat16)
    compressed = product(first_round, latent_down)
    latent_exact, latent_pull = jax.vjp(normed, compressed[:, :R], latent_gain.astype(jnp.float32))
    latent = latent_exact.astype(jnp.bfloat16)
    rope_exact, rope_pull = jax.vjp(rotate_keys, compressed[:, R:])
    rope_keys = rope_exact.astype(jnp.bfloat16)
    keys_values = (
        product(latent, latent_up).astype(jnp.bfloat16).reshape(number, heads_here, DN + DV)
    )
    query_seq = queries.reshape(sequences, LEN, heads_here, DN + DR)
    nope_seq = keys_values[..., :DN].reshape(sequences, LEN, heads_here, DN)
    value_seq = keys_values[..., DN:].reshape(sequences, LEN, heads_here, DV)
    rope_seq = rope_keys.reshape(sequences, LEN, DR)
    scaling = (DN + DR) ** (-0.5)
    causal = jnp.arange(LEN)[:, None] >= jnp.arange(LEN)[None, :]

    def scores_of():
        content = jnp.einsum(
            "sihc,sjhc->shij", query_seq[..., :DN], nope_seq, preferred_element_type=jnp.float32
        )
        content = content + jnp.einsum(
            "sihc,sjc->shij", query_seq[..., DN:], rope_seq, preferred_element_type=jnp.float32
        )
        return jnp.where(causal, content * scaling, -1e30)

    scores = scores_of()
    highest = jnp.max(scores, axis=-1, keepdims=True)
    expanded = jnp.exp(scores - highest)
    totals = jnp.sum(expanded, axis=-1, keepdims=True)
    attend_weight = expanded / totals
    log_total = highest + jnp.log(totals)
    mixed_rows = jnp.einsum(
        "shij,sjhc->sihc",
        attend_weight.astype(jnp.bfloat16),
        value_seq,
        preferred_element_type=jnp.float32,
    )
    mixed_rows = mixed_rows.reshape(number, heads_here * DV).astype(jnp.bfloat16)
    attend_rows = lax.psum(product(mixed_rows, output_weight), "tensor")
    hidden_rows = rows_full + attend_rows
    second_exact, second_pull = jax.vjp(normed, hidden_rows, second_gain.astype(jnp.float32))
    second_round = second_exact.astype(jnp.bfloat16)
    gating = jax.nn.softmax(product(second_round, router_weight), axis=-1)
    slot_index, retained, slot_owner = slot_plan(routes)
    retained_float = retained.astype(jnp.float32)
    padded_rows = jnp.concatenate([second_round, jnp.zeros((1, D), jnp.bfloat16)], axis=0)
    buffer = padded_rows[slot_owner].reshape(E, CAP, D)
    gate_hidden = jnp.einsum(
        "ecd,edf->ecf", buffer, expert_gate, preferred_element_type=jnp.float32
    )
    up_hidden = jnp.einsum("ecd,edf->ecf", buffer, expert_up, preferred_element_type=jnp.float32)
    expert_exact, expert_pull = jax.vjp(gated, gate_hidden, up_hidden)
    expert_act = expert_exact.astype(jnp.bfloat16)
    pair_weight = jnp.take_along_axis(gating, routes, axis=1) * retained_float
    slot_weight = (
        jnp.zeros((E * CAP + 1,), jnp.float32)
        .at[slot_index.reshape(-1)]
        .set(pair_weight.reshape(-1))[: E * CAP]
    )
    grad_rows = lax.all_gather(cotangent, "tensor", axis=1, tiled=True)
    grad_round = grad_rows
    grad_rows = grad_rows.astype(jnp.float32)
    padded_grad = jnp.concatenate([grad_rows, jnp.zeros((1, D), jnp.float32)], axis=0)
    expert_result = jnp.einsum(
        "ecf,efd->ecd", expert_act, expert_down, preferred_element_type=jnp.float32
    ).reshape(E * CAP, D)
    result_padded = jnp.concatenate([expert_result, jnp.zeros((1, D), jnp.float32)], axis=0)
    routed_rows = jnp.zeros((number, D), jnp.float32)
    pair_columns = []
    for column in range(TOP):
        picked = result_padded[slot_index[:, column]]
        routed_rows = routed_rows + pair_weight[:, column : column + 1] * picked
        pair_columns.append(jnp.sum(grad_rows * picked, axis=-1))
    pair_delta = jnp.stack(pair_columns, axis=1)
    shared_pre = product(second_round, shared_gate)
    shared_lift = product(second_round, shared_up)
    shared_exact, shared_pull = jax.vjp(gated, shared_pre, shared_lift)
    shared_act = shared_exact.astype(jnp.bfloat16)
    branch = product(shared_act, shared_down) + routed_rows
    branch_share = lax.psum_scatter(
        branch.astype(jnp.bfloat16), "tensor", scatter_dimension=1, tiled=True
    ).astype(jnp.float32)
    layer_output = (
        lax.dynamic_slice_in_dim(hidden_rows, share_start, share_width, 1) + branch_share
    ).astype(jnp.bfloat16)
    delta_shared_down = outer_sum(shared_act, grad_round)
    delta_pre, delta_lift = shared_pull(product_back(grad_round, shared_down))
    delta_pre = delta_pre.astype(jnp.bfloat16)
    delta_lift = delta_lift.astype(jnp.bfloat16)
    delta_shared_gate = outer_sum(second_round, delta_pre)
    delta_shared_up = outer_sum(second_round, delta_lift)
    delta_second = product_back(delta_pre, shared_gate) + product_back(delta_lift, shared_up)
    slot_delta = (
        (slot_weight[:, None] * padded_grad[slot_owner]).astype(jnp.bfloat16).reshape(E, CAP, D)
    )
    delta_expert_down = jnp.einsum(
        "ecf,ecd->efd", expert_act, slot_delta, preferred_element_type=jnp.float32
    )
    delta_act = jnp.einsum(
        "ecd,efd->ecf", slot_delta, expert_down, preferred_element_type=jnp.float32
    )
    delta_gate, delta_up = expert_pull(delta_act)
    delta_gate = delta_gate.astype(jnp.bfloat16)
    delta_up = delta_up.astype(jnp.bfloat16)
    delta_expert_gate = jnp.einsum(
        "ecd,ecf->edf", buffer, delta_gate, preferred_element_type=jnp.float32
    )
    delta_expert_up = jnp.einsum(
        "ecd,ecf->edf", buffer, delta_up, preferred_element_type=jnp.float32
    )
    slot_back = jnp.einsum(
        "ecf,edf->ecd", delta_gate, expert_gate, preferred_element_type=jnp.float32
    ) + jnp.einsum("ecf,edf->ecd", delta_up, expert_up, preferred_element_type=jnp.float32)
    slot_back = jnp.concatenate(
        [slot_back.reshape(E * CAP, D), jnp.zeros((1, D), jnp.float32)], axis=0
    )
    for column in range(TOP):
        delta_second = delta_second + slot_back[slot_index[:, column]]
    delta_second, pair_delta = lax.psum((delta_second, pair_delta), "tensor")
    matches = (routes[:, :, None] == jnp.arange(E, dtype=jnp.int32)[None, None, :]).astype(
        jnp.float32
    )
    delta_gating = jnp.sum((pair_delta * retained_float)[:, :, None] * matches, axis=1)
    delta_logits = gating * (delta_gating - jnp.sum(gating * delta_gating, axis=-1, keepdims=True))
    second_wide = second_round.astype(jnp.float32)
    delta_router = lax.dot_general(
        second_wide, delta_logits, (((0,), (0,)), ((), ())), precision=lax.Precision.HIGHEST
    )
    delta_second = delta_second + lax.dot_general(
        delta_logits,
        router_weight.astype(jnp.float32),
        (((1,), (1,)), ((), ())),
        precision=lax.Precision.HIGHEST,
    )
    delta_hidden, delta_second_gain = second_pull(delta_second)
    delta_hidden = delta_hidden + grad_rows
    delta_attend = delta_hidden.astype(jnp.bfloat16)
    delta_output_weight = outer_sum(mixed_rows, delta_attend)
    delta_mixed = (
        product_back(delta_attend, output_weight)
        .astype(jnp.bfloat16)
        .reshape(sequences, LEN, heads_here, DV)
    )
    again_scores = scores_of()
    again_weight = jnp.exp(again_scores - log_total)
    delta_values = jnp.einsum(
        "shij,sihc->sjhc",
        again_weight.astype(jnp.bfloat16),
        delta_mixed,
        preferred_element_type=jnp.float32,
    )
    delta_weight = jnp.einsum(
        "sihc,sjhc->shij", delta_mixed, value_seq, preferred_element_type=jnp.float32
    )
    row_dot = jnp.sum(again_weight * delta_weight, axis=-1, keepdims=True)
    delta_scores = (again_weight * (delta_weight - row_dot)).astype(jnp.bfloat16)
    delta_nope_query = (
        jnp.einsum("shij,sjhc->sihc", delta_scores, nope_seq, preferred_element_type=jnp.float32)
        * scaling
    )
    delta_rope_query = (
        jnp.einsum("shij,sjc->sihc", delta_scores, rope_seq, preferred_element_type=jnp.float32)
        * scaling
    )
    delta_nope_key = (
        jnp.einsum(
            "shij,sihc->sjhc", delta_scores, query_seq[..., :DN], preferred_element_type=jnp.float32
        )
        * scaling
    )
    delta_rope_key = (
        jnp.einsum(
            "shij,sihc->sjc", delta_scores, query_seq[..., DN:], preferred_element_type=jnp.float32
        )
        * scaling
    )
    delta_rotated = jnp.concatenate([delta_nope_query, delta_rope_query], axis=-1).reshape(
        number, heads_here, DN + DR
    )
    (delta_raw,) = queries_pull(delta_rotated)
    delta_queries = delta_raw.reshape(number, heads_here * (DN + DR)).astype(jnp.bfloat16)
    delta_query_weight = outer_sum(first_round, delta_queries)
    delta_first = product_back(delta_queries, query_weight)
    delta_pairs = (
        jnp.concatenate([delta_nope_key, delta_values], axis=-1)
        .reshape(number, heads_here * (DN + DV))
        .astype(jnp.bfloat16)
    )
    delta_latent_up = outer_sum(latent, delta_pairs)
    delta_latent = product_back(delta_pairs, latent_up)
    delta_first, delta_latent, delta_rope = (
        lax.psum(delta_first.astype(jnp.bfloat16), "tensor").astype(jnp.float32),
        lax.psum(delta_latent.astype(jnp.bfloat16), "tensor").astype(jnp.float32),
        lax.psum(delta_rope_key.reshape(number, DR).astype(jnp.bfloat16), "tensor").astype(
            jnp.float32
        ),
    )
    delta_head, delta_latent_gain = latent_pull(delta_latent)
    (delta_tail,) = rope_pull(delta_rope)
    delta_compressed = jnp.concatenate([delta_head, delta_tail], axis=-1).astype(jnp.bfloat16)
    delta_latent_down = outer_sum(first_round, delta_compressed)
    delta_first = delta_first + product_back(delta_compressed, latent_down)
    delta_rows, delta_first_gain = first_pull(delta_first)
    delta_rows = delta_rows + delta_hidden
    input_delta = lax.dynamic_slice_in_dim(delta_rows, share_start, share_width, 1)
    summed_all = (
        lax.psum_scatter(
            delta_first_gain.astype(jnp.bfloat16), "dp", scatter_dimension=0, tiled=True
        ).astype(jnp.float32),
        lax.psum_scatter(
            delta_query_weight.astype(jnp.bfloat16), "dp", scatter_dimension=0, tiled=True
        ).astype(jnp.float32),
        lax.psum_scatter(
            delta_latent_down.astype(jnp.bfloat16), "dp", scatter_dimension=0, tiled=True
        ).astype(jnp.float32),
        lax.psum_scatter(
            delta_latent_gain.astype(jnp.bfloat16), "dp", scatter_dimension=0, tiled=True
        ).astype(jnp.float32),
        lax.psum_scatter(
            delta_latent_up.astype(jnp.bfloat16), "dp", scatter_dimension=0, tiled=True
        ).astype(jnp.float32),
        lax.psum_scatter(
            delta_output_weight.astype(jnp.bfloat16), "dp", scatter_dimension=1, tiled=True
        ).astype(jnp.float32),
        lax.psum_scatter(
            delta_second_gain.astype(jnp.bfloat16), "dp", scatter_dimension=0, tiled=True
        ).astype(jnp.float32),
        lax.psum_scatter(
            delta_router.astype(jnp.bfloat16), "dp", scatter_dimension=0, tiled=True
        ).astype(jnp.float32),
        lax.psum_scatter(
            delta_expert_gate.astype(jnp.bfloat16), "dp", scatter_dimension=1, tiled=True
        ).astype(jnp.float32),
        lax.psum_scatter(
            delta_expert_up.astype(jnp.bfloat16), "dp", scatter_dimension=1, tiled=True
        ).astype(jnp.float32),
        lax.psum_scatter(
            delta_expert_down.astype(jnp.bfloat16), "dp", scatter_dimension=2, tiled=True
        ).astype(jnp.float32),
        lax.psum_scatter(
            delta_shared_gate.astype(jnp.bfloat16), "dp", scatter_dimension=0, tiled=True
        ).astype(jnp.float32),
        lax.psum_scatter(
            delta_shared_up.astype(jnp.bfloat16), "dp", scatter_dimension=0, tiled=True
        ).astype(jnp.float32),
        lax.psum_scatter(
            delta_shared_down.astype(jnp.bfloat16), "dp", scatter_dimension=1, tiled=True
        ).astype(jnp.float32),
    )
    layer_summed = summed_all[:8]
    expert_summed = summed_all[8:]
    return (layer_output, input_delta) + tuple(layer_summed) + tuple(expert_summed)


def solution(mesh):
    in_specs = (
        P("dp", "tensor"),
        P("dp", "tensor"),
        P("dp"),
        P("dp", "tensor"),
        P("dp", None),
        P("dp"),
        P("dp", "tensor"),
        P("tensor", "dp"),
        P("dp"),
        P("dp", None),
        P(None, "dp", "tensor"),
        P(None, "dp", "tensor"),
        P(None, "tensor", "dp"),
        P("dp", "tensor"),
        P("dp", "tensor"),
        P("tensor", "dp"),
        P("dp", None),
    )
    out_specs = (
        P("dp", "tensor"),
        P("dp", "tensor"),
        P("dp"),
        P("dp", "tensor"),
        P("dp", None),
        P("dp"),
        P("dp", "tensor"),
        P("tensor", "dp"),
        P("dp"),
        P("dp", None),
        P(None, "dp", "tensor"),
        P(None, "dp", "tensor"),
        P(None, "tensor", "dp"),
        P("dp", "tensor"),
        P("dp", "tensor"),
        P("tensor", "dp"),
    )
    return jax.shard_map(
        per_device, mesh=mesh, in_specs=in_specs, out_specs=out_specs, check_vma=False
    )
```

profile of v0, /device:TPU:0, one launch (start us, length us, event | category | flops | bytes accessed | tf_op | source)
XLA Modules:
  0.0 3623.8 jit_solution(14584368151789473191)
XLA Ops:
  38.5 56.3 %all-gather.15.cloned.1.call-done = bf16[2048,2048]{1,0:T(8,128)(2,1)} async-done(((bf16[2048,256]{1,0:T(8,128)(2,1)}), bf16[2048,2048]{1,0:T(8,128)(2,1)}) %all-gather.15.cloned.1.call-update) | async-done | bytes 8388624 | tf_op jit(solution)/shard_map/all_gather | solution.py:128
  325.7 104.2 %gather_fusion.7 = f32[13824,2048]{1,0:T(8,128)} fusion(f32[2049,2048]{1,0:T(8,128)} %concatenate.53, s32[14336]{0:T(1024)S(1)} %pad_clamp_fusion), kind=kCustom, calls=%fused_computation.7 | custom fusion | bytes 226547712 | tf_op jit(solution)/shard_map/gather | solution.py:243
  429.9 180.8 %all-reduce.18.cloned.1.call-done = f32[2048,2048]{1,0:T(8,128)} async-done(((f32[2048,2048]{1,0:T(8,128)}), f32[2048,2048]{1,0:T(8,128)}) %all-reduce.18.cloned.1.call-update) | async-done | bytes 16777232 | tf_op jit(solution)/shard_map/psum | solution.py:188
  639.8 106.7 %gather_fusion = bf16[13824,2048]{1,0:T(8,128)(2,1)} fusion(bf16[2049,2048]{1,0:T(8,128)(2,1)} %concatenate.51, s32[14336]{0:T(1024)S(1)} %pad_clamp_fusion), kind=kCustom, calls=%fused_computation | custom fusion | bytes 113301504 | tf_op jit(solution)/shard_map/gather | solution.py:196
  778.3 63.5 %all-gather.31.cloned.1.call-done = bf16[16,2048,176]{1,2,0:T(8,128)(2,1)} async-done(((bf16[16,512,176]{1,2,0:T(8,128)(2,1)}), bf16[16,2048,176]{1,2,0:T(8,128)(2,1)}) %all-gather.31.cloned.1.call-update) | async-done | bytes 11534352 | tf_op jit(solution)/shard_map/all_gather | solution.py:104
  877.9 79.4 %all-gather.33.cloned.1.call-done = bf16[16,176,2048]{2,1,0:T(8,128)(2,1)} async-done(((bf16[16,176,512]{2,1,0:T(8,128)(2,1)}), bf16[16,176,2048]{2,1,0:T(8,128)(2,1)}) %all-gather.33.cloned.1.call-update) | async-done | bytes 11534352 | tf_op jit(solution)/shard_map/all_gather | solution.py:105
  1001.1 74.8 %concatenate.52 = f32[13825,2048]{1,0:T(8,128)} pad(f32[13824,2048]{1,0:T(8,128)} %bitcast.19, f32[]{:T(128)} %constant.39.clone.1), padding=0_1x0_0 | pad | bytes 226500608 | tf_op jit(solution)/shard_map/concatenate | solution.py:216
  1126.8 51.0 %gather_fusion.5 = f32[2048,2048]{1,0:T(8,128)} fusion(f32[13825,2048]{1,0:T(8,128)} %concatenate.52, s32[2048]{0:T(1024)S(1)} %copy-done.65), kind=kCustom, calls=%fused_computation.5 | custom fusion | bytes 33562624 | tf_op jit(solution)/shard_map/gather | solution.py:220
  1228.7 51.2 %gather_fusion.3 = f32[2048,2048]{1,0:T(8,128)} fusion(f32[13825,2048]{1,0:T(8,128)} %concatenate.52, s32[2048]{0:T(1024)S(1)} %copy-done.69), kind=kCustom, calls=%fused_computation.3 | custom fusion | bytes 33562624 | tf_op jit(solution)/shard_map/gather | solution.py:220
  1279.9 52.8 %gather_fusion.2 = f32[2048,2048]{1,0:T(8,128)} fusion(f32[13825,2048]{1,0:T(8,128)} %concatenate.52, s32[2048]{0:T(1024)S(1)} %copy-done.71), kind=kCustom, calls=%fused_computation.2 | custom fusion | bytes 33562624 | tf_op jit(solution)/shard_map/gather | solution.py:220
  1332.7 65.0 %gather_fusion.1 = f32[2048,2048]{1,0:T(8,128)} fusion(f32[13825,2048]{1,0:T(8,128)} %concatenate.52, s32[2048]{0:T(1024)S(1)} %copy-done.73), kind=kCustom, calls=%fused_computation.1 | custom fusion | bytes 33562624 | tf_op jit(solution)/shard_map/gather | solution.py:220
  1468.2 98.0 %gather_fusion.14 = f32[12288]{0:T(1024)S(1)} fusion(f32[2048,16]{0,1:T(8,128)S(1)} %get-tuple-element.36, s32[12288]{0:T(1024)S(1)} %copy-done.2), kind=kCustom, calls=%fused_computation.14 | custom fusion | bytes 196608 | tf_op jit(solution)/shard_map/jit(take_along_axis)/gather | solution.py:203
  1707.6 79.6 %convolution_add_fusion = f32[16,864,2048]{2,1,0:T(8,128)} fusion(f32[16,864,2048]{2,1,0:T(8,128)} %fusion.120, bf16[16,864,176]{1,2,0:T(8,128)(2,1)} %get-tuple-element.41, bf16[16,2048,176]{1,2,0:T(8,128)(2,1)} %all-gather.31.cloned.1.call-done), kind=kOutput, calls=%fused_computation.18 | convolution fusion | flops 9993977856 | bytes 242892800 | tf_op jit(solution)/shard_map/ecf,edf->ecd/dot_general | solution.py:262
  1787.2 74.3 %concatenate.54 = f32[13825,2048]{1,0:T(8,128)} pad(f32[13824,2048]{1,0:T(8,128)} %bitcast.32, f32[]{:T(128)} %constant.39.clone.1), padding=0_1x0_0 | pad | bytes 226500608 | tf_op jit(solution)/shard_map/concatenate | solution.py:263
  1963.2 51.0 %gather_fusion.11 = f32[2048,2048]{1,0:T(8,128)} fusion(f32[13825,2048]{1,0:T(8,128)} %concatenate.54, s32[2048]{0:T(1024)S(1)} %copy-done.68), kind=kCustom, calls=%fused_computation.11 | custom fusion | bytes 33562624 | tf_op jit(solution)/shard_map/gather | solution.py:267
  2014.2 51.3 %gather_fusion.10 = f32[2048,2048]{1,0:T(8,128)} fusion(f32[13825,2048]{1,0:T(8,128)} %concatenate.54, s32[2048]{0:T(1024)S(1)} %copy-done.70), kind=kCustom, calls=%fused_computation.10 | custom fusion | bytes 33562624 | tf_op jit(solution)/shard_map/gather | solution.py:267
  2065.6 52.6 %gather_fusion.9 = f32[2048,2048]{1,0:T(8,128)} fusion(f32[13825,2048]{1,0:T(8,128)} %concatenate.54, s32[2048]{0:T(1024)S(1)} %copy-done.72), kind=kCustom, calls=%fused_computation.9 | custom fusion | bytes 33562624 | tf_op jit(solution)/shard_map/gather | solution.py:267
  2118.2 64.9 %gather_fusion.8 = f32[2048,2048]{1,0:T(8,128)} fusion(f32[13825,2048]{1,0:T(8,128)} %concatenate.54, s32[2048]{0:T(1024)S(1)} %copy-done.74), kind=kCustom, calls=%fused_computation.8 | custom fusion | bytes 33562624 | tf_op jit(solution)/shard_map/gather | solution.py:267
  2254.9 330.6 %all-reduce.20.cloned.1.call-done = f32[2048,2048]{1,0:T(8,128)} async-done(((f32[2048,2048]{1,0:T(8,128)}), f32[2048,2048]{1,0:T(8,128)}) %all-reduce.20.cloned.1.call-update) | async-done | bytes 16777232 | tf_op jit(solution)/shard_map/psum | solution.py:268
  2786.5 129.3 %all-reduce.22.cloned.1.call-done = (bf16[2048,64]{0,1:T(8,128)(2,1)}, bf16[2048,512]{0,1:T(8,128)(2,1)}, bf16[2048,2048]{1,0:T(8,128)(2,1)}) async-done(((bf16[2048,64]{0,1:T(8,128)(2,1)}, bf16[2048,512]{0,1:T(8,128)(2,1)}, bf16[2048,2048]{1,0:T(8,128)(2,1)}), (bf16[2048,64]{0,1:T(8,128)(2,1)}, bf16[2048,512]{0,1:T(8,128)(2,1)}, bf16[2048,2048]{1,0:T(8,128)(2,1)})) %all-reduce.22.cloned.1.call-update) | async-done | bytes 10747920 | tf_op jit(solution)/shard_map/psum | solution.py:343
  3170.9 56.7 %reduce-scatter.13.cloned.1.call-done = bf16[2048,256]{1,0:T(8,128)(2,1)} async-done(((bf16[2048,2048]{1,0:T(8,128)(2,1)}), bf16[2048,256]{1,0:T(8,128)(2,1)}) %reduce-scatter.13.cloned.1.call-update) | async-done | bytes 1048592 | tf_op jit(solution)/shard_map/reduce_scatter | solution.py:229
  3268.6 112.9 %reduce-scatter.25.cloned.1.call-done = bf16[16,512,176]{1,2,0:T(8,128)(2,1)} async-done(((bf16[16,2048,176]{1,2,0:T(8,128)(2,1)}), bf16[16,512,176]{1,2,0:T(8,128)(2,1)}) %reduce-scatter.25.cloned.1.call-update) | async-done | bytes 2883600 | tf_op jit(solution)/shard_map/reduce_scatter | solution.py:380
  3386.7 110.1 %reduce-scatter.27.cloned.1.call-done = bf16[16,512,176]{1,2,0:T(8,128)(2,1)} async-done(((bf16[16,2048,176]{1,2,0:T(8,128)(2,1)}), bf16[16,512,176]{1,2,0:T(8,128)(2,1)}) %reduce-scatter.27.cloned.1.call-update) | async-done | bytes 2883600 | tf_op jit(solution)/shard_map/reduce_scatter | solution.py:383
  3501.9 109.9 %reduce-scatter.29.cloned.1.call-done = bf16[16,176,512]{2,1,0:T(8,128)(2,1)} async-done(((bf16[16,176,2048]{2,1,0:T(8,128)(2,1)}), bf16[16,176,512]{2,1,0:T(8,128)(2,1)}) %reduce-scatter.29.cloned.1.call-update) | async-done | bytes 2883600 | tf_op jit(solution)/shard_map/reduce_scatter | solution.py:386
  (441 shorter events, 1399.6 us)
Async XLA Ops:
  8.7 156.4 %all-gather.19.cloned.1.call-start = ((), (), s32[]{:S(2)}) async-start(), calls=%async_computation.14 | async-start | bytes 1966080 | tf_op jit(solution)/shard_map/all_gather | solution.py:96
  9.4 211.0 %all-gather.21.cloned.1.call-start = ((), (), s32[]{:S(2)}) async-start(), calls=%async_computation.15 | async-start | bytes 1310720 | tf_op jit(solution)/shard_map/all_gather | solution.py:100
  10.0 304.3 %all-gather.35.cloned.1.call-start = ((), (), s32[]{:S(2)}) async-start(), calls=%async_computation.24 | async-start | bytes 9437184 | tf_op jit(solution)/shard_map/all_gather | solution.py:209
  10.6 600.1 %all-reduce.18.cloned.1.call-start = ((), (), s32[]{:S(2)}) async-start(), calls=%async_computation.16 | async-start | bytes 33554432 | tf_op jit(solution)/shard_map/psum | solution.py:188
  230.3 516.3 %all-gather.29.cloned.1.call-start = ((), (), s32[]{:S(2)}) async-start(), calls=%async_computation.20 | async-start | bytes 14417920 | tf_op jit(solution)/shard_map/all_gather | solution.py:103
  231.0 610.8 %all-gather.31.cloned.1.call-start = ((), (), s32[]{:S(2)}) async-start(), calls=%async_computation.21 | async-start | bytes 14417920 | tf_op jit(solution)/shard_map/all_gather | solution.py:104
  231.8 725.6 %all-gather.33.cloned.1.call-start = ((), (), s32[]{:S(2)}) async-start(), calls=%async_computation.22 | async-start | bytes 14417920 | tf_op jit(solution)/shard_map/all_gather | solution.py:105
  232.5 1950.6 %all-gather.23.cloned.1.call-start = ((), (), s32[]{:S(2)}) async-start(), calls=%async_computation.17 | async-start | bytes 1802240 | tf_op jit(solution)/shard_map/all_gather | solution.py:106
  233.1 1958.5 %all-gather.25.cloned.1.call-start = ((), (), s32[]{:S(2)}) async-start(), calls=%async_computation.18 | async-start | bytes 1802240 | tf_op jit(solution)/shard_map/all_gather | solution.py:107
  233.8 1966.3 %all-gather.27.cloned.1.call-start = ((), (), s32[]{:S(2)}) async-start(), calls=%async_computation.19 | async-start | bytes 1802240 | tf_op jit(solution)/shard_map/all_gather | solution.py:108
  234.4 2351.2 %all-reduce.20.cloned.1.call-start = ((), (), s32[]{:S(2)}) async-start(), calls=%async_computation.25 | async-start | bytes 33554432 | tf_op jit(solution)/shard_map/psum | solution.py:268
  2254.3 661.5 %all-reduce.22.cloned.1.call-start = ((), (), s32[]{:S(2)}) async-start(), calls=%async_computation.37 | async-start | bytes 21495808 | tf_op jit(solution)/shard_map/psum | solution.py:343
  2694.8 346.9 %reduce-scatter.23.cloned.1.call-start = ((), (), s32[]{:S(2)}) async-start(), calls=%async_computation.30 | async-start | bytes 81920 | tf_op jit(solution)/shard_map/reduce_scatter | solution.py:377
  2701.2 341.8 %reduce-scatter.31.cloned.1.call-start = ((), (), s32[]{:S(2)}) async-start(), calls=%async_computation.34 | async-start | bytes 1802240 | tf_op jit(solution)/shard_map/reduce_scatter | solution.py:389
  2709.1 335.9 %reduce-scatter.33.cloned.1.call-start = ((), (), s32[]{:S(2)}) async-start(), calls=%async_computation.35 | async-start | bytes 1802240 | tf_op jit(solution)/shard_map/reduce_scatter | solution.py:392
  2717.0 329.9 %reduce-scatter.35.cloned.1.call-start = ((), (), s32[]{:S(2)}) async-start(), calls=%async_computation.36 | async-start | bytes 1802240 | tf_op jit(solution)/shard_map/reduce_scatter | solution.py:395
  2724.8 345.6 %reduce-scatter.19.cloned.1.call-start = ((), (), s32[]{:S(2)}) async-start(), calls=%async_computation.28 | async-start | bytes 655360 | tf_op jit(solution)/shard_map/reduce_scatter | solution.py:368
  2730.2 371.5 %reduce-scatter.21.cloned.1.call-start = ((), (), s32[]{:S(2)}) async-start(), calls=%async_computation.29 | async-start | bytes 1310720 | tf_op jit(solution)/shard_map/reduce_scatter | solution.py:371
  2739.5 396.1 %reduce-scatter.15.cloned.1.call-start = ((), (), s32[]{:S(2)}) async-start(), calls=%async_computation.26 | async-start | bytes 1966080 | tf_op jit(solution)/shard_map/reduce_scatter | solution.py:359
  2750.0 477.5 %reduce-scatter.13.cloned.1.call-start = ((), (), s32[]{:S(2)}) async-start(), calls=%async_computation.23 | async-start | bytes 9437184 | tf_op jit(solution)/shard_map/reduce_scatter | solution.py:229
  2786.2 480.2 %reduce-scatter.17.cloned.1.call-start = ((), (), s32[]{:S(2)}) async-start(), calls=%async_computation.27 | async-start | bytes 2949120 | tf_op jit(solution)/shard_map/reduce_scatter | solution.py:362
  2931.7 449.8 %reduce-scatter.25.cloned.1.call-start = ((), (), s32[]{:S(2)}) async-start(), calls=%async_computation.31 | async-start | bytes 14417920 | tf_op jit(solution)/shard_map/reduce_scatter | solution.py:380
  2957.8 538.9 %reduce-scatter.27.cloned.1.call-start = ((), (), s32[]{:S(2)}) async-start(), calls=%async_computation.32 | async-start | bytes 14417920 | tf_op jit(solution)/shard_map/reduce_scatter | solution.py:383
  2984.3 627.6 %reduce-scatter.29.cloned.1.call-start = ((), (), s32[]{:S(2)}) async-start(), calls=%async_computation.33 | async-start | bytes 14417920 | tf_op jit(solution)/shard_map/reduce_scatter | solution.py:386
  (105 other events, 5689.6 us)
Sparse Core Ops, SparseCore 0:
  9.6 85.1 all-gather.14
  96.7 35.5 all-gather.16
  134.1 30.9 all-gather.18
  166.8 26.4 all-gather.20
  194.7 82.4 all-gather.34
  279.6 331.0 all-reduce.17
  612.5 113.7 all-gather.28
  728.1 113.6 all-gather.30
  843.6 113.6 all-gather.32
  959.0 29.7 all-gather.22
  990.6 29.7 all-gather.24
  1022.1 29.7 all-gather.26
  2254.4 331.1 all-reduce.19
  2694.9 220.8 all-reduce.21
  2945.8 30.1 reduce-scatter.30
  2978.8 30.0 reduce-scatter.32
  3012.0 30.1 reduce-scatter.34
  3073.9 27.6 reduce-scatter.20
  3104.7 30.9 reduce-scatter.14
  3137.9 89.5 reduce-scatter.12
  3230.6 35.7 reduce-scatter.16
  3269.4 112.1 reduce-scatter.24
  3384.6 112.0 reduce-scatter.26
  3499.7 112.0 reduce-scatter.28
  (2 shorter events, 48.5 us)
where the time goes:
time: 3640 us; the launch traced here: 3620 us
  waiting for transfers between devices  1410 us (39%)
  local copies, waits for them, and re-layouts  1260 us (35%)
  matrix products  686 us (19%)
  other arithmetic  167 us (5%)
  blocking collectives  80.8 us (2%)
    psum x1, waiting for transfers between devices, per_device(): delta_second, pair_delta = lax.psum((delta_second, pair_delta), 'tensor')  331 us
    gather x6, local copies, waits for them, and re-layouts, per_device(): picked = result_padded[slot_index[:, column]]  322 us
    gather x6, local copies, waits for them, and re-layouts, per_device(): delta_second = delta_second + slot_back[slot_index[:, column]]  322 us
    psum x1, waiting for transfers between devices, per_device(): attend_rows = lax.psum(product(mixed_rows, output_weight), 'tensor')  181 us
    psum x1, waiting for transfers between devices, per_device(): lax.psum(delta_rope_key.reshape(number, DR).astype(jnp.bfloat16), 'tensor')  129 us
    reduce_scatter x1, waiting for transfers between devices, per_device(): lax.psum_scatter(delta_expert_gate.astype(jnp.bfloat16), 'dp', scatter_di...  113 us
    reduce_scatter x1, waiting for transfers between devices, per_device(): lax.psum_scatter(delta_expert_up.astype(jnp.bfloat16), 'dp', scatter_dime...  110 us
    reduce_scatter x1, waiting for transfers between devices, per_device(): lax.psum_scatter(delta_expert_down.astype(jnp.bfloat16), 'dp', scatter_di...  110 us
  transfers between devices with their start and end apart: 26, of which 16 were waited for; matrix products, arithmetic and copies ran while one was open for 53% of the time, Pallas kernels for 0%

commit v1 on v0

v1 whole, which is shorter than its diff:
```python
import jax
import jax.numpy as jnp
from jax import lax
from jax.sharding import PartitionSpec as P

D = 2048
DN = 128
DR = 64
DV = 128
R = 512
E = 16
LEN = 1024
CAP = 864
EPSILON = 1e-06
BF = jnp.bfloat16
F32 = jnp.float32


def dot(a, b, ca, cb, out=F32):
    return lax.dot_general(
        a, b, (((ca,), (cb,)), ((), ())), preferred_element_type=F32
    ).astype(out)


def angles(number, halfway):
    position = (jnp.arange(number, dtype=jnp.int32) % LEN).astype(F32)
    spread = 10000.0 ** (-jnp.arange(halfway, dtype=F32) / halfway)
    phases = position[:, None] * spread[None, :]
    return jnp.cos(phases), jnp.sin(phases)


def rotate(values, cosine, sine_term):
    halfway = values.shape[-1] // 2
    u, w = values[..., :halfway], values[..., halfway:]
    return jnp.concatenate([u * cosine - w * sine_term, w * cosine + u * sine_term], axis=-1)


class Line:
    def __init__(self):
        self.n = lax.axis_size("tensor")
        self.chips = self.n // 2
        index = lax.axis_index("tensor")
        self.index = index
        self.z = index // 2
        self.c = index % 2

    def swap(self, a):
        return lax.ppermute(a, "tensor", [(i, i ^ 1) for i in range(self.n)])

    def shift(self, a, step, sources):
        pairs = [
            (2 * s + c, 2 * (s + step) + c)
            for s in sources
            if 0 <= s + step < self.chips
            for c in (0, 1)
        ]
        return lax.ppermute(a, "tensor", pairs)

    def chip_gather(self, s):
        n = self.chips
        left, right = [s], [s]
        for k in range(1, n):
            left.append(self.shift(left[-1], 1, range(k - 1, n)))
            right.append(self.shift(right[-1], -1, range(0, n - k + 1)))
        return [s] + [jnp.where(self.z >= k, left[k], right[n - k]) for k in range(1, n)]

    def gather(self, s, order):
        n = self.chips
        own = self.chip_gather(s)
        out = jnp.zeros((self.n,) + s.shape, s.dtype)
        for k, piece in enumerate(own):
            other = self.swap(piece)
            chip = (self.z - k + n) % n
            start = (0,) * s.ndim
            out = lax.dynamic_update_slice(out, piece[None], (order(chip, self.c),) + start)
            out = lax.dynamic_update_slice(out, other[None], (order(chip, 1 - self.c),) + start)
        return out

    def chip_scatter(self, block):
        n = self.chips
        left = right = None
        for s in range(1, n):
            up = block(jnp.clip(n - s + self.z, 0, n - 1))
            down = block(jnp.clip(self.z - (n - s), 0, n - 1))
            if left is not None:
                up = (up.astype(F32) + left.astype(F32)).astype(BF)
                down = (down.astype(F32) + right.astype(F32)).astype(BF)
            left = self.shift(up, 1, range(0, s))
            right = self.shift(down, -1, range(n - s, n))
        return block(self.z).astype(F32) + left.astype(F32) + right.astype(F32)

    def row_scatter(self, p):
        half = p.shape[0] // 2
        ch = half // self.chips
        mine = lax.dynamic_slice_in_dim(p, self.c * half, half, 0)
        theirs = lax.dynamic_slice_in_dim(p, (1 - self.c) * half, half, 0)
        both = (mine.astype(F32) + self.swap(theirs).astype(F32)).astype(BF)
        return self.chip_scatter(lambda j: lax.dynamic_slice_in_dim(both, j * ch, ch, 0))

    def row_gather(self, s):
        out = self.gather(s, lambda chip, core: core * self.chips + chip)
        return out.reshape(self.n * s.shape[0], s.shape[1])

    def row_start(self, rows):
        ch = rows // self.n
        return (self.c * self.chips + self.z) * ch, ch

    def column_gather(self, s):
        out = self.gather(s, lambda chip, core: chip * 2 + core)
        return out.transpose(1, 0, 2).reshape(s.shape[0], self.n * s.shape[1])

    def column_scatter(self, p):
        rows, wide = p.shape
        ch = wide // self.n
        blocks = p.reshape(rows, self.chips, 2, ch).transpose(2, 1, 0, 3)
        mine = lax.dynamic_index_in_dim(blocks, self.c, 0, False)
        theirs = lax.dynamic_index_in_dim(blocks, 1 - self.c, 0, False)
        both = (mine.astype(F32) + self.swap(theirs).astype(F32)).astype(BF)
        return self.chip_scatter(lambda j: lax.dynamic_index_in_dim(both, j, 0, False))


def gather_rows(parts):
    packed = lax.all_gather(jnp.concatenate(parts, axis=0), "dp", axis=1, tiled=True)
    out, at = [], 0
    for part in parts:
        out.append(packed[at : at + part.shape[0]])
        at += part.shape[0]
    return out


def scatter_rows(parts):
    packed = jnp.concatenate([p.astype(BF) for p in parts], axis=0)
    summed = lax.psum_scatter(packed, "dp", scatter_dimension=1, tiled=True).astype(F32)
    out, at = [], 0
    for part in parts:
        out.append(summed[at : at + part.shape[0]])
        at += part.shape[0]
    return out


def ranks(mask):
    number = mask.shape[0]
    block = 128
    pieces = mask.reshape(number // block, block, E).astype(BF)
    lower = jnp.tril(jnp.ones((block, block), BF), -1)
    inside = jnp.einsum("ij,bje->bie", lower, pieces, preferred_element_type=F32)
    totals = jnp.sum(pieces.astype(F32), axis=1).astype(BF)
    ahead = jnp.tril(jnp.ones((number // block, number // block), BF), -1)
    before = dot(ahead, totals, 1, 0)
    return (inside + before[:, None, :]).reshape(number, E)


def per_device(
    layer_input, cotangent, first_gain, query_weight, latent_down, latent_gain, latent_up,
    output_weight, second_gain, router_weight, expert_gate, expert_up, expert_down,
    shared_gate, shared_up, shared_down, routes,
):
    line = Line()
    n_dp = lax.axis_size("dp")
    wide = D // n_dp
    number = layer_input.shape[0]
    sequences = number // LEN
    heads_here = output_weight.shape[0] // DV
    fe = expert_down.shape[1]
    my_columns = layer_input.shape[1]
    column_start = line.index * my_columns
    row_start, row_count = line.row_start(number)

    up_rows = latent_up.size // wide
    gains = jnp.zeros((16, wide), BF)
    gains = gains.at[0].set(first_gain).at[1].set(second_gain)
    gains = gains.at[2, : latent_gain.shape[0]].set(latent_gain)
    wq, wld, wup, gains, wr, wo = gather_rows(
        [query_weight.T, latent_down.T, latent_up.reshape(up_rows, wide), gains,
         router_weight.T, output_weight]
    )
    wup = wup.reshape(up_rows, n_dp, wide).transpose(1, 0, 2).reshape(R, -1)
    first_g = gains[0].astype(F32)
    second_g = gains[1].astype(F32)
    latent_g = gains[2].reshape(n_dp, wide)[:, : R // n_dp].reshape(R).astype(F32)

    eg = expert_gate.transpose(0, 2, 1)
    eu = expert_up.transpose(0, 2, 1)
    cut = E // 2
    packs = []
    for a, b in ((0, cut), (cut, E)):
        packs.append([m[a:b].reshape((b - a) * fe, wide) for m in (eg, eu, expert_down)])
    packs[-1] += [shared_gate.T, shared_up.T, shared_down]
    packs = [gather_rows(p) for p in packs]

    rows = line.column_gather(layer_input)
    v1 = rows.astype(F32)
    r1 = lax.rsqrt(jnp.mean(v1 * v1, axis=-1, keepdims=True) + EPSILON)
    first_round = (v1 * r1 * first_g).astype(BF)
    cosine, sine_term = angles(number, DR // 2)
    raw = dot(first_round, wq, 1, 1).reshape(number, heads_here, DN + DR)
    queries = jnp.concatenate(
        [raw[..., :DN], rotate(raw[..., DN:], cosine[:, None], sine_term[:, None])], axis=-1
    ).astype(BF)
    compressed = dot(first_round, wld, 1, 1)
    vl = compressed[:, :R]
    rl = lax.rsqrt(jnp.mean(vl * vl, axis=-1, keepdims=True) + EPSILON)
    latent = (vl * rl * latent_g).astype(BF)
    rope_keys = rotate(compressed[:, R:], cosine, sine_term).astype(BF)
    keys_values = dot(latent, wup, 1, 0, BF).reshape(number, heads_here, DN + DV)
    query_seq = queries.reshape(sequences, LEN, heads_here, DN + DR)
    nope_seq = keys_values[..., :DN].reshape(sequences, LEN, heads_here, DN)
    value_seq = keys_values[..., DN:].reshape(sequences, LEN, heads_here, DV)
    rope_seq = rope_keys.reshape(sequences, LEN, DR)
    scaling = (DN + DR) ** (-0.5)
    causal = jnp.arange(LEN)[:, None] >= jnp.arange(LEN)[None, :]

    def scores_of():
        content = jnp.einsum("sihc,sjhc->shij", query_seq[..., :DN], nope_seq, preferred_element_type=F32)
        content = content + jnp.einsum("sihc,sjc->shij", query_seq[..., DN:], rope_seq, preferred_element_type=F32)
        return jnp.where(causal, content * scaling, -1e30)

    scores = scores_of()
    highest = jnp.max(scores, axis=-1, keepdims=True)
    expanded = jnp.exp(scores - highest)
    totals = jnp.sum(expanded, axis=-1, keepdims=True)
    attend_weight = (expanded / totals).astype(BF)
    log_total = highest + jnp.log(totals)
    mixed = jnp.einsum("shij,sjhc->sihc", attend_weight, value_seq, preferred_element_type=F32)
    mixed = mixed.reshape(number, heads_here * DV).astype(BF)
    attend_rows = line.row_scatter(dot(mixed, wo, 1, 0, BF))
    hidden_chunk = lax.dynamic_slice_in_dim(rows, row_start, row_count, 0).astype(F32) + attend_rows
    hidden = line.row_gather(hidden_chunk.astype(BF))

    v2 = hidden.astype(F32)
    r2 = lax.rsqrt(jnp.mean(v2 * v2, axis=-1, keepdims=True) + EPSILON)
    second_round = (v2 * r2 * second_g).astype(BF)
    gating = jax.nn.softmax(dot(second_round, wr, 1, 1), axis=-1)
    named = jnp.any(routes[:, :, None] == jnp.arange(E, dtype=jnp.int32)[None, None, :], axis=1)
    kept = jnp.where(named & (ranks(named) < CAP), 1.0, 0.0)
    pair_weight = gating * kept
    grad = line.column_gather(cotangent)

    def hidden_units(second_round, grad, gate, up, down, weight):
        pre = dot(second_round, gate, 1, 1)
        lift = dot(second_round, up, 1, 1)
        back = dot(grad, down, 1, 1)
        s = jax.nn.sigmoid(pre)
        silu = pre * s
        act = silu * lift
        pair = None
        if weight is not None:
            count = weight.shape[1]
            pair = jnp.sum((act * back).reshape(number, count, fe), axis=-1)
            spread = jnp.broadcast_to(weight[:, :, None], (number, count, fe)).reshape(number, count * fe)
            act = act * spread
            back = back * spread
        act = act.astype(BF)
        pre_delta = (back * lift * (s * (1.0 + pre * (1.0 - s)))).astype(BF)
        lift_delta = (back * silu).astype(BF)
        out = dot(act, down, 1, 0)
        second = dot(pre_delta, gate, 1, 0) + dot(lift_delta, up, 1, 0)
        deltas = [dot(pre_delta, second_round, 0, 0, BF), dot(lift_delta, second_round, 0, 0, BF), dot(act, grad, 0, 0, BF)]
        return out, second, pair, deltas

    first_half = hidden_units(second_round, grad, *packs[0], pair_weight[:, :cut])
    first_deltas, (again_round, again_grad) = lax.optimization_barrier(
        (first_half[3], (second_round, grad))
    )
    half_deltas = [scatter_rows(first_deltas)]
    second_half = hidden_units(again_round, again_grad, *packs[1][:3], pair_weight[:, cut:])
    shared = hidden_units(again_round, again_grad, *packs[1][3:], None)
    branch = (first_half[0] + second_half[0] + shared[0]).astype(BF)
    second_terms = (first_half[1] + second_half[1] + shared[1]).astype(BF)
    pair_terms = jnp.concatenate([first_half[2], second_half[2]], axis=1)

    pad = jnp.zeros((number, 128 - E), BF)
    summed = line.row_scatter(jnp.concatenate([second_terms, pair_terms.astype(BF), pad], axis=1))

    def own_rows(a):
        return lax.dynamic_slice_in_dim(a, row_start, row_count, 0)

    gating_rows, kept_rows, x2 = own_rows(gating), own_rows(kept), own_rows(second_round)
    u = summed[:, D : D + E] * kept_rows
    logits_delta = gating_rows * (u - jnp.sum(gating_rows * u, axis=-1, keepdims=True))
    router_delta = dot(logits_delta.astype(BF), x2, 0, 0)
    d2 = summed[:, :D] + dot(logits_delta.astype(BF), wr, 1, 0)
    v2_rows, r2_rows = own_rows(hidden).astype(F32), own_rows(r2)
    vgd = jnp.mean(v2_rows * second_g * d2, axis=-1, keepdims=True)
    second_gain_delta = jnp.sum(d2 * v2_rows * r2_rows, axis=0)
    hidden_delta_rows = own_rows(grad).astype(F32) + r2_rows * second_g * d2 - v2_rows * (r2_rows**3) * vgd
    hidden_delta = line.row_gather(hidden_delta_rows.astype(BF))
    hidden_delta, late_deltas, half_deltas[0] = lax.optimization_barrier(
        (hidden_delta, second_half[3] + shared[3], half_deltas[0])
    )
    half_deltas.append(scatter_rows(late_deltas))

    branch_share = line.column_scatter(branch)
    layer_output = (
        lax.dynamic_slice_in_dim(hidden, column_start, my_columns, 1).astype(F32) + branch_share
    ).astype(BF)

    delta_wo = dot(mixed, hidden_delta, 0, 0)
    delta_mixed = dot(hidden_delta, wo, 1, 1, BF).reshape(sequences, LEN, heads_here, DV)
    again = jnp.exp(scores_of() - log_total)
    delta_values = jnp.einsum("shij,sihc->sjhc", again.astype(BF), delta_mixed, preferred_element_type=F32)
    delta_weight = jnp.einsum("sihc,sjhc->shij", delta_mixed, value_seq, preferred_element_type=F32)
    row_dot = jnp.sum(again * delta_weight, axis=-1, keepdims=True)
    delta_scores = (again * (delta_weight - row_dot)).astype(BF)
    dq_content = jnp.einsum("shij,sjhc->sihc", delta_scores, nope_seq, preferred_element_type=F32) * scaling
    dq_rope = jnp.einsum("shij,sjc->sihc", delta_scores, rope_seq, preferred_element_type=F32) * scaling
    dk_content = jnp.einsum("shij,sihc->sjhc", delta_scores, query_seq[..., :DN], preferred_element_type=F32) * scaling
    dk_rope = jnp.einsum("shij,sihc->sjc", delta_scores, query_seq[..., DN:], preferred_element_type=F32) * scaling
    dq_content = dq_content.reshape(number, heads_here, DN)
    dq_rope = rotate(dq_rope.reshape(number, heads_here, DR), cosine[:, None], -sine_term[:, None])
    delta_queries = jnp.concatenate([dq_content, dq_rope], axis=-1)
    query_dot = jnp.sum(delta_queries * raw, axis=(1, 2))[:, None]
    delta_queries = delta_queries.reshape(number, heads_here * (DN + DR)).astype(BF)
    delta_pairs = (
        jnp.concatenate([dk_content, delta_values], axis=-1).reshape(number, heads_here * (DN + DV)).astype(BF)
    )
    delta_wq = dot(delta_queries, first_round, 0, 0)
    first_terms = dot(delta_queries, wq, 1, 0, BF)
    delta_wup = dot(latent, delta_pairs, 0, 0)
    latent_terms = dot(delta_pairs, wup, 1, 1, BF)
    small = jnp.concatenate(
        [latent_terms, dk_rope.reshape(number, DR).astype(BF), query_dot.astype(BF), jnp.zeros((number, 63), BF)], axis=1
    )
    small, first_terms, layer_output = lax.optimization_barrier((small, first_terms, layer_output))
    small = line.row_scatter(small)
    dl = small[:, :R]
    vl_rows, rl_rows = own_rows(vl), own_rows(rl)
    latent_gain_delta = jnp.sum(dl * vl_rows * rl_rows, axis=0)
    head = rl_rows * latent_g * dl - vl_rows * (rl_rows**3) * jnp.mean(vl_rows * latent_g * dl, axis=-1, keepdims=True)
    tail = rotate(small[:, R : R + DR], own_rows(cosine), -own_rows(sine_term))
    dots = small[:, R + DR : R + DR + 1] + jnp.sum(jnp.concatenate([head, tail], axis=1) * own_rows(compressed), axis=-1, keepdims=True)
    small = jnp.concatenate([head, tail, dots, jnp.zeros((row_count, 63), F32)], axis=1).astype(BF)
    small = line.row_gather(small)
    delta_compressed = small[:, : R + DR]
    dots = small[:, R + DR : R + DR + 1].astype(F32)
    delta_wld = dot(delta_compressed, first_round, 0, 0)
    first_share = line.column_scatter(first_terms)
    first_share = first_share + dot(delta_compressed, lax.dynamic_slice_in_dim(wld, column_start, my_columns, 1), 1, 0)
    vc = layer_input.astype(F32)
    gc = lax.dynamic_slice_in_dim(first_g, column_start, my_columns, 0)
    input_delta = (
        lax.dynamic_slice_in_dim(hidden_delta, column_start, my_columns, 1).astype(F32)
        + r1 * gc * first_share
        - vc * (r1 * r1) * (dots / D)
    )
    first_gain_delta = lax.dynamic_update_slice(
        jnp.zeros((D,), F32), jnp.sum(first_share * vc * r1, axis=0), (column_start,)
    )
    vectors = jnp.concatenate(
        [router_delta, second_gain_delta[None], first_gain_delta[None],
         jnp.zeros((1, D), F32).at[0, :R].set(latent_gain_delta)], axis=0
    )
    vectors = lax.psum(vectors, ("dp", "tensor"))
    dp_index = lax.axis_index("dp")
    mine = lax.dynamic_slice_in_dim(vectors, dp_index * wide, wide, 1)
    my_latent = R // n_dp
    latent_gain_out = lax.dynamic_slice_in_dim(vectors[E + 2], dp_index * my_latent, my_latent, 0)

    wup_pack = delta_wup.reshape(n_dp, up_rows, wide).transpose(1, 0, 2).reshape(up_rows, D)
    attend_deltas, half_deltas[1] = lax.optimization_barrier(
        ([delta_wo.astype(BF), delta_wq.astype(BF), wup_pack.astype(BF), delta_wld.astype(BF)], half_deltas[1])
    )
    dwo, dwq, dwup, dwld = scatter_rows(attend_deltas)

    def expert_delta(i):
        return jnp.concatenate([half_deltas[0][i], half_deltas[1][i]], axis=0).reshape(E, fe, wide)

    return (
        layer_output, input_delta, mine[E + 1], dwq.T, dwld.T, latent_gain_out,
        dwup.reshape(latent_up.shape), dwo, mine[E], mine[:E].T,
        expert_delta(0).transpose(0, 2, 1), expert_delta(1).transpose(0, 2, 1), expert_delta(2),
        half_deltas[1][3].T, half_deltas[1][4].T, half_deltas[1][5],
    )


def solution(mesh):
    in_specs = (
        P("dp", "tensor"), P("dp", "tensor"), P("dp"), P("dp", "tensor"), P("dp", None), P("dp"),
        P("dp", "tensor"), P("tensor", "dp"), P("dp"), P("dp", None), P(None, "dp", "tensor"),
        P(None, "dp", "tensor"), P(None, "tensor", "dp"), P("dp", "tensor"), P("dp", "tensor"),
        P("tensor", "dp"), P("dp", None),
    )
    out_specs = (
        P("dp", "tensor"), P("dp", "tensor"), P("dp"), P("dp", "tensor"), P("dp", None), P("dp"),
        P("dp", "tensor"), P("tensor", "dp"), P("dp"), P("dp", None), P(None, "dp", "tensor"),
        P(None, "dp", "tensor"), P(None, "tensor", "dp"), P("dp", "tensor"), P("dp", "tensor"),
        P("tensor", "dp"),
    )
    return jax.shard_map(
        per_device, mesh=mesh, in_specs=in_specs, out_specs=out_specs, check_vma=False
    )
```

time: 3640 us -> 2760 us (0.76)
  waiting for transfers between devices: 1410 us -> 680 us
  local copies, waits for them, and re-layouts: 1260 us -> 1080 us
  starting transfers between devices: 1.68 us -> 150 us
  matrix products: 686 us -> 592 us
  blocking collectives: 80.8 us -> 0 us
  other arithmetic: 167 us -> 212 us
    gather x19 -> x0, local copies, waits for them, and re-layouts: 955 us -> none  [the longest x6 322 us: per_device(): picked = result_padded[slot_index[:, column]]]
    dynamic_update_slice x0 -> x33, local copies, waits for them, and re-layouts: none -> 731 us  [the longest x20 372 us: gather(): lax.dynamic_update_slice(out, other[None], (order(chip, 1 - self.c),) + s...]
    psum x3 -> x1, waiting for transfers between devices: 641 us -> 108 us  [per_device(): vectors = lax.psum(vectors, ('dp', 'tensor'))]
    ppermute x0 -> x85, waiting for transfers between devices: none -> 522 us  [the longest x60 506 us: shift(): return lax.ppermute(a, 'tensor', pairs)]
    reduce_scatter x12 -> x3, waiting for transfers between devices: 509 us -> 50 us  [scatter_rows(): lax.psum_scatter(packed, 'dp', scatter_dimension=1, tiled=True).astype(F32)]
    all_gather x11 -> x3, waiting for transfers between devices: 252 us -> 0.01 us  [gather_rows(): lax.all_gather(jnp.concatenate(parts, axis=0), 'dp', axis=1, tiled=True)]
    ppermute x0 -> x85, starting transfers between devices: none -> 149 us  [the longest x60 144 us: shift(): return lax.ppermute(a, 'tensor', pairs)]
    concatenate x7 -> x11, local copies, waits for them, and re-layouts: 175 us -> 30 us  [the longest x1 13.8 us: per_device(): jnp.concatenate([second_terms, pair_terms.astype(BF), pad], axis=1)]
  transfers between devices with their start and end apart: 26 -> 92, of which waited for: 16 -> 36; matrix products, arithmetic and copies ran while one was open for 53% -> 67% of each run, Pallas kernels for 0% -> 0%
where the time goes in v1:
time: 2760 us; the launch traced here: 2730 us
  local copies, waits for them, and re-layouts  1080 us (39%)
  waiting for transfers between devices  680 us (25%)
  matrix products  592 us (21%)
  other arithmetic  212 us (8%)
  starting transfers between devices  150 us (5%)
    dot_general x43, matrix products, dot(): lax.dot_general(a, b, (((ca,), (cb,)), ((), ())), preferred_element_type=...  522 us
    ppermute x60, waiting for transfers between devices, shift(): return lax.ppermute(a, 'tensor', pairs)  506 us
    dynamic_update_slice x20, local copies, waits for them, and re-layouts, gather(): lax.dynamic_update_slice(out, other[None], (order(chip, 1 - self.c),) + s...  372 us
    dynamic_update_slice x12, local copies, waits for them, and re-layouts, gather(): lax.dynamic_update_slice(out, piece[None], (order(chip, self.c),) + start)  359 us
    ppermute x60, starting transfers between devices, shift(): return lax.ppermute(a, 'tensor', pairs)  144 us
    psum x1, waiting for transfers between devices, per_device(): vectors = lax.psum(vectors, ('dp', 'tensor'))  108 us
    unnamed x272, local copies, waits for them, and re-layouts  94.7 us
  transfers between devices with their start and end apart: 92, of which 36 were waited for; matrix products, arithmetic and copies ran while one was open for 67% of the time, Pallas kernels for 0%

profile of v1, /device:TPU:0, one launch (start us, length us, event | category | flops | bytes accessed | tf_op | source)
XLA Modules:
  0.0 2728.1 jit_solution(17104404583623609540)
XLA Ops:
  116.6 44.4 %dynamic_update_slice.124 = bf16[8,2048,256]{2,0,1:T(8,128)(2,1)} dynamic-update-slice(bf16[8,2048,256]{2,0,1:T(8,128)(2,1)} %broadcast.329.clone, bf16[1,2048,256]{2,0,1:T(2,128)(2,1)S(1)} %copy.457, s32[]{:T(128)S(6)} %select_n.369, s32[]{:T(128)} %constant.312.clone.1, s32[]{:T(128)} %constant.312.clone.1) | dynamic-update-slice | bytes 2097156 | tf_op jit(solution)/shard_map/dynamic_update_slice | solution.py:75
  165.5 44.5 %dynamic_update_slice.125 = bf16[8,2048,256]{2,0,1:T(8,128)(2,1)} dynamic-update-slice(bf16[8,2048,256]{2,0,1:T(8,128)(2,1)} %dynamic_update_slice.124, bf16[1,2048,256]{2,0,1:T(2,128)(2,1)S(1)} %copy.458, s32[]{:T(128)S(6)} %select_n.370, s32[]{:T(128)} %constant.312.clone.1, s32[]{:T(128)} %constant.312.clone.1) | dynamic-update-slice | bytes 2097156 | tf_op jit(solution)/shard_map/dynamic_update_slice | solution.py:76
  234.7 44.6 %dynamic_update_slice.126 = bf16[8,2048,256]{2,0,1:T(8,128)(2,1)} dynamic-update-slice(bf16[8,2048,256]{2,0,1:T(8,128)(2,1)} %dynamic_update_slice.125, bf16[1,2048,256]{2,0,1:T(2,128)(2,1)} %copy.459, s32[]{:T(128)S(6)} %select_n.374, s32[]{:T(128)} %constant.312.clone.1, s32[]{:T(128)} %constant.312.clone.1) | dynamic-update-slice | bytes 2097156 | tf_op jit(solution)/shard_map/dynamic_update_slice | solution.py:75
  287.9 44.6 %dynamic_update_slice.127 = bf16[8,2048,256]{2,0,1:T(8,128)(2,1)} dynamic-update-slice(bf16[8,2048,256]{2,0,1:T(8,128)(2,1)} %dynamic_update_slice.126, bf16[1,2048,256]{2,0,1:T(2,128)(2,1)} %copy.460, s32[]{:T(128)S(6)} %select_n.375, s32[]{:T(128)} %constant.312.clone.1, s32[]{:T(128)} %constant.312.clone.1) | dynamic-update-slice | bytes 2097156 | tf_op jit(solution)/shard_map/dynamic_update_slice | solution.py:76
  332.5 44.4 %dynamic_update_slice.128 = bf16[8,2048,256]{2,0,1:T(8,128)(2,1)} dynamic-update-slice(bf16[8,2048,256]{2,0,1:T(8,128)(2,1)} %dynamic_update_slice.127, bf16[1,2048,256]{2,0,1:T(2,128)(2,1)S(1)} %copy.461, s32[]{:T(128)S(6)} %select_n.379, s32[]{:T(128)} %constant.312.clone.1, s32[]{:T(128)} %constant.312.clone.1) | dynamic-update-slice | bytes 2097156 | tf_op jit(solution)/shard_map/dynamic_update_slice | solution.py:75
  376.9 44.7 %dynamic_update_slice.129 = bf16[8,2048,256]{2,0,1:T(8,128)(2,1)} dynamic-update-slice(bf16[8,2048,256]{2,0,1:T(8,128)(2,1)} %dynamic_update_slice.128, bf16[1,2048,256]{2,0,1:T(2,128)(2,1)} %copy.462, s32[]{:T(128)S(6)} %select_n.380, s32[]{:T(128)} %constant.312.clone.1, s32[]{:T(128)} %constant.312.clone.1) | dynamic-update-slice | bytes 2097156 | tf_op jit(solution)/shard_map/dynamic_update_slice | solution.py:76
  421.6 44.6 %dynamic_update_slice.130 = bf16[8,2048,256]{2,0,1:T(8,128)(2,1)} dynamic-update-slice(bf16[8,2048,256]{2,0,1:T(8,128)(2,1)} %dynamic_update_slice.129, bf16[1,2048,256]{2,0,1:T(2,128)(2,1)} %copy.463, s32[]{:T(128)S(6)} %select_n.384, s32[]{:T(128)} %constant.312.clone.1, s32[]{:T(128)} %constant.312.clone.1) | dynamic-update-slice | bytes 2097156 | tf_op jit(solution)/shard_map/dynamic_update_slice | solution.py:75
  466.1 44.6 %dynamic_update_slice.131 = bf16[8,2048,256]{2,0,1:T(8,128)(2,1)} dynamic-update-slice(bf16[8,2048,256]{2,0,1:T(8,128)(2,1)} %dynamic_update_slice.130, bf16[1,2048,256]{2,0,1:T(2,128)(2,1)S(1)} %copy-done.22, s32[]{:T(128)S(6)} %select_n.385, s32[]{:T(128)} %constant.312.clone.1, s32[]{:T(128)} %constant.312.clone.1) | dynamic-update-slice | bytes 2097156 | tf_op jit(solution)/shard_map/dynamic_update_slice | solution.py:76
  748.3 26.0 collective-permute-done.26
  937.4 44.4 %dynamic_update_slice.132 = bf16[8,2048,256]{2,0,1:T(8,128)(2,1)} dynamic-update-slice(bf16[8,2048,256]{2,0,1:T(8,128)(2,1)} %broadcast.329.clone.1, bf16[1,2048,256]{2,0,1:T(2,128)(2,1)S(1)} %copy.479, s32[]{:T(128)S(6)} %select_n.369, s32[]{:T(128)} %constant.312.clone.1, s32[]{:T(128)} %constant.312.clone.1) | dynamic-update-slice | bytes 2097156 | tf_op jit(solution)/shard_map/dynamic_update_slice | solution.py:75
  984.9 44.4 %dynamic_update_slice.133 = bf16[8,2048,256]{2,0,1:T(8,128)(2,1)} dynamic-update-slice(bf16[8,2048,256]{2,0,1:T(8,128)(2,1)} %dynamic_update_slice.132, bf16[1,2048,256]{2,0,1:T(2,128)(2,1)S(1)} %copy.480, s32[]{:T(128)S(6)} %select_n.370, s32[]{:T(128)} %constant.312.clone.1, s32[]{:T(128)} %constant.312.clone.1) | dynamic-update-slice | bytes 2097156 | tf_op jit(solution)/shard_map/dynamic_update_slice | solution.py:76
  1054.0 44.5 %dynamic_update_slice.134 = bf16[8,2048,256]{2,0,1:T(8,128)(2,1)} dynamic-update-slice(bf16[8,2048,256]{2,0,1:T(8,128)(2,1)} %dynamic_update_slice.133, bf16[1,2048,256]{2,0,1:T(2,128)(2,1)} %copy.481, s32[]{:T(128)S(6)} %select_n.374, s32[]{:T(128)} %constant.312.clone.1, s32[]{:T(128)} %constant.312.clone.1) | dynamic-update-slice | bytes 2097156 | tf_op jit(solution)/shard_map/dynamic_update_slice | solution.py:75
  1107.2 44.5 %dynamic_update_slice.135 = bf16[8,2048,256]{2,0,1:T(8,128)(2,1)} dynamic-update-slice(bf16[8,2048,256]{2,0,1:T(8,128)(2,1)} %dynamic_update_slice.134, bf16[1,2048,256]{2,0,1:T(2,128)(2,1)} %copy.482, s32[]{:T(128)S(6)} %select_n.375, s32[]{:T(128)} %constant.312.clone.1, s32[]{:T(128)} %constant.312.clone.1) | dynamic-update-slice | bytes 2097156 | tf_op jit(solution)/shard_map/dynamic_update_slice | solution.py:76
  1151.7 44.5 %dynamic_update_slice.136 = bf16[8,2048,256]{2,0,1:T(8,128)(2,1)} dynamic-update-slice(bf16[8,2048,256]{2,0,1:T(8,128)(2,1)} %dynamic_update_slice.135, bf16[1,2048,256]{2,0,1:T(2,128)(2,1)} %copy.483, s32[]{:T(128)S(6)} %select_n.379, s32[]{:T(128)} %constant.312.clone.1, s32[]{:T(128)} %constant.312.clone.1) | dynamic-update-slice | bytes 2097156 | tf_op jit(solution)/shard_map/dynamic_update_slice | solution.py:75
  1196.3 44.5 %dynamic_update_slice.137 = bf16[8,2048,256]{2,0,1:T(8,128)(2,1)} dynamic-update-slice(bf16[8,2048,256]{2,0,1:T(8,128)(2,1)} %dynamic_update_slice.136, bf16[1,2048,256]{2,0,1:T(2,128)(2,1)} %copy.484, s32[]{:T(128)S(6)} %select_n.380, s32[]{:T(128)} %constant.312.clone.1, s32[]{:T(128)} %constant.312.clone.1) | dynamic-update-slice | bytes 2097156 | tf_op jit(solution)/shard_map/dynamic_update_slice | solution.py:76
  1240.8 44.4 %dynamic_update_slice.138 = bf16[8,2048,256]{2,0,1:T(8,128)(2,1)} dynamic-update-slice(bf16[8,2048,256]{2,0,1:T(8,128)(2,1)} %dynamic_update_slice.137, bf16[1,2048,256]{2,0,1:T(2,128)(2,1)S(1)} %copy.485, s32[]{:T(128)S(6)} %select_n.384, s32[]{:T(128)} %constant.312.clone.1, s32[]{:T(128)} %constant.312.clone.1) | dynamic-update-slice | bytes 2097156 | tf_op jit(solution)/shard_map/dynamic_update_slice | solution.py:75
  1285.2 44.7 %dynamic_update_slice.139 = bf16[8,2048,256]{2,0,1:T(8,128)(2,1)} dynamic-update-slice(bf16[8,2048,256]{2,0,1:T(8,128)(2,1)} %dynamic_update_slice.138, bf16[1,2048,256]{2,0,1:T(2,128)(2,1)} %copy.486, s32[]{:T(128)S(6)} %select_n.385, s32[]{:T(128)} %constant.312.clone.1, s32[]{:T(128)} %constant.312.clone.1) | dynamic-update-slice | bytes 2097156 | tf_op jit(solution)/shard_map/dynamic_update_slice | solution.py:76
  1404.8 29.5 %multiply_multiply_fusion.1 = (f32[2048,1408]{0,1:T(8,128)}, bf16[2048,1408]{0,1:T(8,128)(2,1)}, bf16[2048,1408]{0,1:T(8,128)(2,1)}, bf16[2048,1408]{0,1:T(8,128)(2,1)}) fusion(f32[2048,1408]{0,1:T(8,128)} %fusion.39, f32[2048,1408]{0,1:T(8,128)} %fusion.31, f32[2048,8]{0,1:T(8,128)S(1)} %copy.495, bf16[2048,2048]{1,0:T(8,128)(2,1)} %multiply_convert_fusion.1, ...), kind=kOutput, calls=%fused_computation.81 | convolution fusion | flops 11863064576 | bytes 66125824 | tf_op jit(solution)/shard_map/dot_general | solution.py:20
  1571.9 30.5 %multiply_multiply_fusion = (f32[2048,1408]{0,1:T(8,128)}, bf16[2048,1408]{0,1:T(8,128)(2,1)}, bf16[2048,1408]{0,1:T(8,128)(2,1)}, bf16[2048,1408]{0,1:T(8,128)(2,1)}) fusion(f32[2048,1408]{0,1:T(8,128)} %fusion.23, f32[2048,1408]{0,1:T(8,128)} %fusion.19, f32[2048,8]{0,1:T(8,128)S(1)} %copy-done.68, bf16[2048,2048]{1,0:T(8,128)(2,1)} %bitcast.387, ...), kind=kOutput, calls=%fused_computation.80 | convolution fusion | flops 11863064576 | bytes 66125824 | tf_op jit(solution)/shard_map/dot_general | solution.py:20
  1680.0 32.1 %add_convert_fusion.1 = bf16[2048,2048]{1,0:T(8,128)(2,1)} fusion(f32[2048,2048]{1,0:T(8,128)} %fusion.81, f32[2048,2048]{1,0:T(8,128)} %fusion.17, f32[2048,2048]{1,0:T(8,128)} %fusion.21, f32[2048,2048]{1,0:T(8,128)} %fusion.29, f32[2048,2048]{1,0:T(8,128)} %fusion.33, bf16[2048,352]{0,1:T(8,128)(2,1)} %get-tuple-element.280, ...), kind=kOutput, calls=%fused_computation.16 | convolution fusion | flops 2977955840 | bytes 95158272 | tf_op jit(solution)/shard_map/dot_general | solution.py:20
  1822.3 25.3 collective-permute-done.43
  2178.7 24.5 collective-permute-done.60
  2539.4 108.3 %all-reduce.4.cloned.1.call-done = f32[19,2048]{1,0:T(8,128)} async-done(((f32[19,2048]{1,0:T(8,128)}), f32[19,2048]{1,0:T(8,128)}) %all-reduce.4.cloned.1.call-update) | async-done | bytes 155664 | tf_op jit(solution)/shard_map/psum | solution.py:353
  2665.3 49.9 %reduce-scatter.8.cloned.1.call-done = bf16[1344,512]{1,0:T(8,128)(2,1)} async-done(((bf16[1344,2048]{1,0:T(8,128)(2,1)}), bf16[1344,512]{1,0:T(8,128)(2,1)}) %reduce-scatter.8.cloned.1.call-update) | async-done | bytes 1376272 | tf_op jit(solution)/shard_map/reduce_scatter | solution.py:133
  (742 shorter events, 1672.6 us)
Async XLA Ops:
  7.2 531.5 %all-gather.4.cloned.1.call-start = ((), (), s32[]{:S(2)}) async-start(), calls=%async_computation.3 | async-start | bytes 7208960 | tf_op jit(solution)/shard_map/all_gather | solution.py:123
  20.4 1346.6 %all-gather.6.cloned.1.call-start = ((), (), s32[]{:S(2)}) async-start(), calls=%async_computation.4 | async-start | bytes 21626880 | tf_op jit(solution)/shard_map/all_gather | solution.py:123
  59.3 1474.3 %all-gather.8.cloned.1.call-start = ((), (), s32[]{:S(2)}) async-start(), calls=%async_computation.5 | async-start | bytes 27033600 | tf_op jit(solution)/shard_map/all_gather | solution.py:123
  59.3 103.0 %collective-permute-start = (bf16[2048,256]{1,0:T(8,128)(2,1)}, bf16[2048,256]{1,0:T(8,128)(2,1)}, u32[]{:S(2)}, u32[]{:S(2)}) collective-permute-start(bf16[2048,256]{1,0:T(8,128)(2,1)} %param.25), channel_id=1, source_target_pairs={{0,1},{1,0},{2,3},{3,2},{4,5},{5,4},{6,7},{7,6},{8,9},{9,8},{10,11... | collective-permute-start | bytes 3145736 | tf_op jit(solution)/shard_map/ppermute | solution.py:48
  86.0 127.2 %collective-permute-start.7 = (bf16[2048,256]{1,0:T(8,128)(2,1)}, bf16[2048,256]{1,0:T(8,128)(2,1)}, u32[]{:S(2)}, u32[]{:S(2)}) collective-permute-start(bf16[2048,256]{1,0:T(8,128)(2,1)} %broadcast_select_fusion.9), channel_id=1, source_target_pairs={{0,1},{1,0},{2,3},{3,2},{4,5},{5,4},{6,7},{7,6},{8,9},{9,8},{10,11... | collective-permute-start | bytes 3145736 | tf_op jit(solution)/shard_map/ppermute | solution.py:48
  87.4 191.9 %collective-permute-start.9 = (bf16[2048,256]{1,0:T(8,128)(2,1)S(1)}, bf16[2048,256]{1,0:T(8,128)(2,1)}, u32[]{:S(2)}, u32[]{:S(2)}) collective-permute-start(bf16[2048,256]{1,0:T(8,128)(2,1)S(1)} %broadcast_select_fusion.7), channel_id=1, source_target_pairs={{0,1},{1,0},{2,3},{3,2},{4,5},{5,4},{6,7},{7,6},{8,9},{9,8},{10,11... | collective-permute-start | bytes 3145736 | tf_op jit(solution)/shard_map/ppermute | solution.py:48
  109.7 173.9 %collective-permute-start.5 = (bf16[2048,256]{1,0:T(8,128)(2,1)}, bf16[2048,256]{1,0:T(8,128)(2,1)}, u32[]{:S(2)}, u32[]{:S(2)}) collective-permute-start(bf16[2048,256]{1,0:T(8,128)(2,1)} %broadcast_select_fusion.11), channel_id=1, source_target_pairs={{0,1},{1,0},{2,3},{3,2},{4,5},{5,4},{6,7},{7,6},{8,9},{9,8},{10,11... | collective-permute-start | bytes 3145736 | tf_op jit(solution)/shard_map/ppermute | solution.py:48
  701.3 1283.2 %reduce-scatter.4.cloned.1.call-start = ((), (), s32[]{:S(2)}) async-start(), calls=%async_computation.6 | async-start | bytes 21626880 | tf_op jit(solution)/shard_map/reduce_scatter | solution.py:133
  729.6 44.7 %collective-permute-start.26 = (bf16[256,2048]{1,0:T(8,128)(2,1)S(1)}, bf16[256,2048]{1,0:T(8,128)(2,1)S(1)}, u32[]{:S(2)}, u32[]{:S(2)}) collective-permute-start(bf16[256,2048]{1,0:T(8,128)(2,1)S(1)} %add_convert_fusion.10), channel_id=1, source_target_pairs={{2,0},{3,1},{4,2},{5,3},{6,4},{7,5},{10,8},{11,9},{12,10},{13,11},... | collective-permute-start | bytes 3145736 | tf_op jit(solution)/shard_map/ppermute | solution.py:57
  808.5 49.3 %collective-permute-start.12 = (bf16[2048,256]{1,0:T(8,128)(2,1)}, bf16[2048,256]{1,0:T(8,128)(2,1)}, u32[]{:S(2)}, u32[]{:S(2)}) collective-permute-start(bf16[2048,256]{1,0:T(8,128)(2,1)} %param.26), channel_id=1, source_target_pairs={{2,0},{3,1},{4,2},{5,3},{6,4},{7,5},{10,8},{11,9},{12,10},{13,11},... | collective-permute-start | bytes 3145736 | tf_op jit(solution)/shard_map/ppermute | solution.py:57
  809.8 49.3 %collective-permute-start.11 = (bf16[2048,256]{1,0:T(8,128)(2,1)}, bf16[2048,256]{1,0:T(8,128)(2,1)}, u32[]{:S(2)}, u32[]{:S(2)}) collective-permute-start(bf16[2048,256]{1,0:T(8,128)(2,1)} %param.26), channel_id=1, source_target_pairs={{0,2},{1,3},{2,4},{3,5},{4,6},{5,7},{8,10},{9,11},{10,12},{11,13},... | collective-permute-start | bytes 3145736 | tf_op jit(solution)/shard_map/ppermute | solution.py:57
  816.0 44.8 %collective-permute-start.28 = (bf16[256,2048]{1,0:T(8,128)(2,1)}, bf16[256,2048]{1,0:T(8,128)(2,1)}, u32[]{:S(2)}, u32[]{:S(2)}) collective-permute-start(bf16[256,2048]{1,0:T(8,128)(2,1)} %get-tuple-element.263), channel_id=1, source_target_pairs={{0,2},{1,3},{2,4},{3,5},{4,6},{5,7},{8,10},{9,11},{10,12},{11,13},... | collective-permute-start | bytes 3145736 | tf_op jit(solution)/shard_map/ppermute | solution.py:57
  835.2 44.9 %collective-permute-start.31 = (bf16[256,2048]{1,0:T(8,128)(2,1)S(1)}, bf16[256,2048]{1,0:T(8,128)(2,1)S(1)}, u32[]{:S(2)}, u32[]{:S(2)}) collective-permute-start(bf16[256,2048]{1,0:T(8,128)(2,1)S(1)} %collective-permute-done.30), channel_id=1, source_target_pairs={{2,0},{3,1},{10,8},{11,9},{18,16},{19,17},{26,24},{27,25}} | collective-permute-start | bytes 3145736 | tf_op jit(solution)/shard_map/ppermute | solution.py:57
  882.1 99.7 %collective-permute-start.10 = (bf16[2048,256]{1,0:T(8,128)(2,1)}, bf16[2048,256]{1,0:T(8,128)(2,1)}, u32[]{:S(2)}, u32[]{:S(2)}) collective-permute-start(bf16[2048,256]{1,0:T(8,128)(2,1)} %param.26), channel_id=1, source_target_pairs={{0,1},{1,0},{2,3},{3,2},{4,5},{5,4},{6,7},{7,6},{8,9},{9,8},{10,11... | collective-permute-start | bytes 3145736 | tf_op jit(solution)/shard_map/ppermute | solution.py:48
  900.9 141.3 %collective-permute-start.17 = (bf16[2048,256]{1,0:T(8,128)(2,1)S(1)}, bf16[2048,256]{1,0:T(8,128)(2,1)}, u32[]{:S(2)}, u32[]{:S(2)}) collective-permute-start(bf16[2048,256]{1,0:T(8,128)(2,1)S(1)} %broadcast_select_fusion.8), channel_id=1, source_target_pairs={{0,1},{1,0},{2,3},{3,2},{4,5},{5,4},{6,7},{7,6},{8,9},{9,8},{10,11... | collective-permute-start | bytes 3145736 | tf_op jit(solution)/shard_map/ppermute | solution.py:48
  922.1 176.5 %collective-permute-start.15 = (bf16[2048,256]{1,0:T(8,128)(2,1)}, bf16[2048,256]{1,0:T(8,128)(2,1)}, u32[]{:S(2)}, u32[]{:S(2)}) collective-permute-start(bf16[2048,256]{1,0:T(8,128)(2,1)} %broadcast_select_fusion.10), channel_id=1, source_target_pairs={{0,1},{1,0},{2,3},{3,2},{4,5},{5,4},{6,7},{7,6},{8,9},{9,8},{10,11... | collective-permute-start | bytes 3145736 | tf_op jit(solution)/shard_map/ppermute | solution.py:48
  924.9 178.0 %collective-permute-start.19 = (bf16[2048,256]{1,0:T(8,128)(2,1)}, bf16[2048,256]{1,0:T(8,128)(2,1)}, u32[]{:S(2)}, u32[]{:S(2)}) collective-permute-start(bf16[2048,256]{1,0:T(8,128)(2,1)} %broadcast_select_fusion.6), channel_id=1, source_target_pairs={{0,1},{1,0},{2,3},{3,2},{4,5},{5,4},{6,7},{7,6},{8,9},{9,8},{10,11... | collective-permute-start | bytes 3145736 | tf_op jit(solution)/shard_map/ppermute | solution.py:48
  927.8 412.5 %collective-permute-start.36 = (bf16[256,2048]{1,0:T(8,128)(2,1)}, bf16[256,2048]{1,0:T(8,128)(2,1)}, u32[]{:S(2)}, u32[]{:S(2)}) collective-permute-start(bf16[256,2048]{1,0:T(8,128)(2,1)} %get-tuple-element.257), channel_id=1, source_target_pairs={{0,1},{1,0},{2,3},{3,2},{4,5},{5,4},{6,7},{7,6},{8,9},{9,8},{10,11... | collective-permute-start | bytes 3145736 | tf_op jit(solution)/shard_map/ppermute | solution.py:48
  1492.5 1031.4 %reduce-scatter.6.cloned.1.call-start = ((), (), s32[]{:S(2)}) async-start(), calls=%async_computation.8 | async-start | bytes 27033600 | tf_op jit(solution)/shard_map/reduce_scatter | solution.py:133
  1800.3 47.3 %collective-permute-start.43 = (bf16[256,2176]{1,0:T(8,128)(2,1)S(1)}, bf16[256,2176]{1,0:T(8,128)(2,1)S(1)}, u32[]{:S(2)}, u32[]{:S(2)}) collective-permute-start(bf16[256,2176]{1,0:T(8,128)(2,1)S(1)} %add_convert_fusion.5), channel_id=1, source_target_pairs={{2,0},{3,1},{4,2},{5,3},{6,4},{7,5},{10,8},{11,9},{12,10},{13,11},... | collective-permute-start | bytes 3342344 | tf_op jit(solution)/shard_map/ppermute | solution.py:57
  2009.8 637.9 %all-reduce.4.cloned.1.call-start = ((), (), s32[]{:S(2)}) async-start(), calls=%async_computation.7 | async-start | bytes 393216 | tf_op jit(solution)/shard_map/psum | solution.py:353
  2158.0 45.2 %collective-permute-start.60 = (bf16[2048,256]{1,0:T(8,128)(2,1)S(1)}, bf16[2048,256]{1,0:T(8,128)(2,1)}, u32[]{:S(2)}, u32[]{:S(2)}) collective-permute-start(bf16[2048,256]{1,0:T(8,128)(2,1)S(1)} %fusion.65), channel_id=1, source_target_pairs={{2,0},{3,1},{4,2},{5,3},{6,4},{7,5},{10,8},{11,9},{12,10},{13,11},... | collective-permute-start | bytes 3145736 | tf_op jit(solution)/shard_map/ppermute | solution.py:57
  2334.6 57.7 %collective-permute-start.61 = (bf16[4,2048,256]{2,1,0:T(8,128)(2,1)}, bf16[4,2048,256]{2,1,0:T(8,128)(2,1)}, u32[]{:S(2)}, u32[]{:S(2)}) collective-permute-start(bf16[4,2048,256]{2,1,0:T(8,128)(2,1)} %bitcast.371), channel_id=1, source_target_pairs={{0,1},{1,0},{2,3},{3,2},{4,5},{5,4},{6,7},{7,6},{8,9},{9,8},{10,11... | collective-permute-start | bytes 12582920 | tf_op jit(solution)/shard_map/ppermute | solution.py:48
  2523.6 191.7 %reduce-scatter.8.cloned.1.call-start = ((), (), s32[]{:S(2)}) async-start(), calls=%async_computation.9 | async-start | bytes 6881280 | tf_op jit(solution)/shard_map/reduce_scatter | solution.py:133
  (192 other events, 4582.4 us)
Sparse Core Ops, SparseCore 0:
  20.5 68.4 all-gather.3
  91.5 162.8 all-gather.5
  701.4 196.6 all-gather.7
  1492.7 181.1 reduce-scatter.3
  2009.9 208.7 reduce-scatter.5
  2523.7 123.9 all-reduce.3
  2650.7 64.5 reduce-scatter.7

commit v2 on v1

v2 whole, which is shorter than its diff:
```python
import functools

import jax
import jax.numpy as jnp
import numpy as np
from jax import lax
from jax.experimental import pallas as pl
from jax.experimental.pallas import tpu as pltpu
from jax.sharding import PartitionSpec as P

D = 2048
DN = 128
DR = 64
DV = 128
R = 512
E = 16
LEN = 1024
CAP = 864
EPSILON = 1e-06
SCALE = (DN + DR) ** -0.5
BLOCK = 256
BF = jnp.bfloat16
F32 = jnp.float32


def dot(a, b, ca, cb, out=F32):
    return lax.dot_general(
        a, b, (((ca,), (cb,)), ((), ())), preferred_element_type=F32
    ).astype(out)


VMEM_LIMIT = 58 * 2**20
NT=(((1,),(1,)),((),()))
NN=(((1,),(0,)),((),()))
TN=(((0,),(0,)),((),()))

def mm(a,b,dims):
    return lax.dot_general(a,b,dims,preferred_element_type=F32)

def params(n):
    return pltpu.CompilerParams(dimension_semantics=("arbitrary",)*n, vmem_limit_bytes=VMEM_LIMIT)

def once(shape, index):
    return pl.BlockSpec(shape, index, pipeline_mode=pl.Buffered(1))

def place_matrix(fe, first, count, n):
    col=lax.broadcasted_iota(jnp.int32,(E,n),1); row=(lax.broadcasted_iota(jnp.int32,(E,n),0)-first)*fe
    return jnp.where((col>=row)&(col<row+fe)&(row<count*fe),1.0,0.0).astype(BF)

def units_kernel(fe, first, count, x_ref, wg_ref, wu_ref, b_ref, w_ref, out_ref, pair_ref):
    x=x_ref[...]; n=wg_ref.shape[0]
    pre=mm(x,wg_ref[...],NT); lift=mm(x,wu_ref[...],NT); back=b_ref[...].astype(F32)
    w=w_ref[...]; hi=w.astype(BF); lo=(w-hi.astype(F32)).astype(BF)
    place=place_matrix(fe,first,count,n)
    spread=mm(jnp.concatenate([hi,lo],axis=1),jnp.concatenate([place,place],axis=0),NN)
    if count*fe<n:
        spread=jnp.where(lax.broadcasted_iota(jnp.int32,spread.shape,1)>=count*fe,1.0,spread)
    s=0.5+0.5*jnp.tanh(0.5*pre)
    silu=pre*s
    act=silu*lift
    pair_ref[...]=mm((act*back).astype(BF),place,NT)
    back=back*spread
    out_ref[0]=(back*lift*(s+silu*(1.0-s))).astype(BF)
    out_ref[1]=(back*silu).astype(BF)
    out_ref[2]=(act*spread).astype(BF)

def units(x,packed,back,weight,fe,first,count,bt):
    T,D=x.shape; n=back.shape[1]; r=weight.shape[1]
    ins=[pl.BlockSpec((bt,D),lambda i:(i,0))]+[once((n,D),lambda i,k=k:(k,0)) for k in range(2)]
    ins+=[pl.BlockSpec((bt,n),lambda i:(i,0)),pl.BlockSpec((bt,r),lambda i:(i,0))]
    outs=[jax.ShapeDtypeStruct((3,T,n),BF),jax.ShapeDtypeStruct((T,r),F32)]
    return pl.pallas_call(functools.partial(units_kernel,fe,first,count),grid=(T//bt,),in_specs=ins,
        out_specs=[pl.BlockSpec((3,bt,n),lambda i:(0,i,0)),pl.BlockSpec((bt,r),lambda i:(i,0))],out_shape=outs,
        compiler_params=params(1),
        cost_estimate=pl.CostEstimate(flops=4*T*D*n,bytes_accessed=2*(T*D+2*n*D+4*T*n),transcendentals=T*n))(x,packed,packed,back,weight)

def lift_kernel(g_ref,w_ref,o_ref):
    o_ref[...]=mm(g_ref[...],w_ref[...],NT).astype(BF)

def lift_back(g,packed,at,n,bt):
    T,D=g.shape
    return pl.pallas_call(lift_kernel,grid=(T//bt,),
        in_specs=[pl.BlockSpec((bt,D),lambda i:(i,0)),once((n,D),lambda i:(at,0))],
        out_specs=pl.BlockSpec((bt,n),lambda i:(i,0)),out_shape=jax.ShapeDtypeStruct((T,n),BF),compiler_params=params(1),
        cost_estimate=pl.CostEstimate(flops=2*T*D*n,bytes_accessed=2*(T*D+n*D+T*n),transcendentals=0))(g,packed)

def back_kernel(pairs, added, beside, *refs):
    out=refs[-1]
    acc=None
    if added: acc=refs[0][...].astype(F32)
    rs=refs[added:]
    for k in range(pairs):
        a=rs[2*k]; b=rs[2*k+1]
        a=a[0] if len(a.shape)==3 else a[...]
        p=mm(a,b[...],NN)
        acc=p if acc is None else acc+p
    if beside:
        wide=acc.shape[1]
        out[:,:wide]=acc.astype(out.dtype)
        more=sum(r[...] for r in refs[-1-beside:-1])
        gap=jnp.zeros((acc.shape[0],out.shape[1]-wide-more.shape[1]),F32)
        out[:,wide:]=jnp.concatenate([more,gap],axis=1).astype(out.dtype)
    else:
        out[...]=acc.astype(out.dtype)

def core_kernel(pairs, core_ref, *refs):
    out=refs[-1]
    chips,_,w=out.shape
    for z in range(chips):
        at=pl.ds(pl.multiple_of((2*z+core_ref[0])*w,w),w)
        acc=None
        for k in range(pairs):
            a=refs[2*k]; b=refs[2*k+1]
            p=mm(a[0] if len(a.shape)==3 else a[...],b[:,at],NN)
            acc=p if acc is None else acc+p
        out[z]=acc.astype(BF)

def back(terms, added, out_dtype, bt, beside=(), core=None, chips=0):
    T=terms[0][0].shape[-2]; D=terms[0][2].shape[1]
    ins=[];args=[];fl=0;by=0
    if core is not None:
        ins.append(pl.BlockSpec(memory_space=pltpu.SMEM)); args.append(core)
    if added is not None:
        ins.append(pl.BlockSpec((bt,D),lambda i:(i,0))); args.append(added)
    for st,k,packed,n,at in terms:
        if st.ndim==3: ins.append(pl.BlockSpec((1,bt,n),lambda i,k=k:(k,i,0)))
        else: ins.append(pl.BlockSpec((bt,n),lambda i:(i,0)))
        ins.append(once((n,D),lambda i,at=at:(at,0)))
        args+= [st,packed]; fl+=2*T*D*n; by+=2*(T*n+n*D)
    for more in beside:
        ins.append(pl.BlockSpec((bt,more.shape[1]),lambda i:(i,0))); args.append(more)
    body=functools.partial(back_kernel,len(terms),0 if added is None else 1,len(beside))
    if beside:
        shape=(T,D+128); ospec=pl.BlockSpec((bt,D+128),lambda i:(i,0))
    elif core is not None:
        w=D//(2*chips); fl//=2
        shape=(chips,T,w); ospec=pl.BlockSpec((chips,bt,w),lambda i:(0,i,0))
        body=functools.partial(core_kernel,len(terms))
    else:
        shape=(T,D); ospec=pl.BlockSpec((bt,D),lambda i:(i,0))
    return pl.pallas_call(body,grid=(T//bt,),in_specs=ins,out_specs=ospec,out_shape=jax.ShapeDtypeStruct(shape,out_dtype),
        compiler_params=params(1),cost_estimate=pl.CostEstimate(flops=fl,bytes_accessed=by+4*T*D,transcendentals=0))(*args)

def outer_kernel(s_ref,x_ref,*refs):
    refs[-1][...]=mm(s_ref[0],x_ref[...],TN).astype(BF)

def outer(stack,first,count,x,total,at,into=None,bc=512):
    T,D=x.shape; n=stack.shape[2]
    ins=[pl.BlockSpec((1,T,n),lambda k,j:(first+k,0,0)),pl.BlockSpec((T,bc),lambda k,j:(0,j))]
    args=[stack,x]; al={}
    if into is not None:
        ins.append(pl.BlockSpec(memory_space=pl.ANY)); args.append(into); al={2:0}
    return pl.pallas_call(outer_kernel,grid=(count,D//bc),in_specs=ins,
        out_specs=pl.BlockSpec((n,bc),lambda k,j:(at+k,j)),out_shape=jax.ShapeDtypeStruct((total,D),BF),
        input_output_aliases=al,compiler_params=params(2),
        cost_estimate=pl.CostEstimate(flops=2*count*T*D*n,bytes_accessed=2*count*(T*n+n*D+T*D),transcendentals=0))(*args)


def place_columns_kernel(chips, norm, at_ref, *refs):
    pieces=refs[:2*chips]
    refs=refs[2*chips:]
    if norm:
        gain_ref, out_ref, round_ref, r_ref = refs
    else:
        (out_ref,) = refs
    w=pieces[0].shape[1]
    for k in range(2*chips):
        out_ref[:,pl.ds(pl.multiple_of(at_ref[k]*w,w),w)]=pieces[k][...]
    if norm:
        v=out_ref[...].astype(F32)
        r=lax.rsqrt(jnp.mean(v*v,axis=-1,keepdims=True)+EPSILON)
        round_ref[...]=(v*r*gain_ref[...]).astype(BF)
        r_ref[...]=r

def place_columns(pieces, at, gain=None, bt=256):
    T,w=pieces[0].shape; n=len(pieces)
    ins=[pl.BlockSpec(memory_space=pltpu.SMEM)]+[pl.BlockSpec((bt,w),lambda i:(i,0))]*n
    args=[at]+list(pieces)
    outs=[jax.ShapeDtypeStruct((T,n*w),BF)]; specs=[pl.BlockSpec((bt,n*w),lambda i:(i,0))]
    if gain is not None:
        ins.append(pl.BlockSpec((1,n*w),lambda i:(0,0))); args.append(gain[None])
        outs+=[jax.ShapeDtypeStruct((T,n*w),BF),jax.ShapeDtypeStruct((T,1),F32)]
        specs+=[pl.BlockSpec((bt,n*w),lambda i:(i,0)),pl.BlockSpec((bt,1),lambda i:(i,0))]
    return pl.pallas_call(functools.partial(place_columns_kernel,n//2,gain is not None),grid=(T//bt,),
        in_specs=ins,out_specs=specs,out_shape=outs,compiler_params=params(1),
        cost_estimate=pl.CostEstimate(flops=6*T*n*w,bytes_accessed=6*T*n*w,transcendentals=T))(*args)

def place_rows_kernel(n, at_ref, *refs):
    pieces=refs[:n]; out_ref=refs[n]; sem=refs[n+1]
    rows=pieces[0].shape[0]
    copies=[pltpu.make_async_copy(pieces[k],out_ref.at[pl.ds(pl.multiple_of(at_ref[k]*rows,rows),rows)],sem.at[k]) for k in range(n)]
    for c in copies: c.start()
    for c in copies: c.wait()

def place_rows(pieces, at):
    rows,w=pieces[0].shape; n=len(pieces)
    return pl.pallas_call(functools.partial(place_rows_kernel,n),
        in_specs=[pl.BlockSpec(memory_space=pltpu.SMEM)]+[pl.BlockSpec(memory_space=pltpu.VMEM)]*n,
        out_specs=pl.BlockSpec(memory_space=pl.ANY),out_shape=jax.ShapeDtypeStruct((n*rows,w),BF),
        scratch_shapes=[pltpu.SemaphoreType.DMA((n,))],compiler_params=pltpu.CompilerParams(vmem_limit_bytes=VMEM_LIMIT),
        cost_estimate=pl.CostEstimate(flops=0,bytes_accessed=4*n*rows*w,transcendentals=0))(at,*pieces)

def norm_rows_kernel(n, at_ref, col_ref, gain_ref, wr_ref, kept_ref, *refs):
    pieces=refs[:n]; round_ref,cols_ref,gating_ref,weight_ref,made,cut,sem,sem2=refs[n:]
    rows=pieces[0].shape[0]; w=cut.shape[2]
    copies=[]
    for k in range(n):
        v=pieces[k][...].astype(F32)
        r=lax.rsqrt(jnp.mean(v*v,axis=-1,keepdims=True)+EPSILON)
        made[k]=(v*r*gain_ref[...]).astype(BF)
        cut[k]=pieces[k][:,pl.ds(pl.multiple_of(col_ref[0]*w,w),w)]
        to=pl.ds(pl.multiple_of(at_ref[k]*rows,rows),rows)
        copies.append(pltpu.make_async_copy(made.at[k],round_ref.at[to],sem.at[k]))
        copies.append(pltpu.make_async_copy(cut.at[k],cols_ref.at[to],sem2.at[k]))
        copies[-2].start(); copies[-1].start()
        logits=mm(made[k],wr_ref[...],NT)
        e=jnp.exp(logits-jnp.max(logits,axis=-1,keepdims=True))
        gating=e/jnp.sum(e,axis=-1,keepdims=True)
        gating_ref[to]=gating
        weight_ref[to]=gating*kept_ref[to]
    for c in copies: c.wait()

def norm_rows(pieces, at, column, w, gain, router, kept):
    rows,wide=pieces[0].shape; n=len(pieces)
    vmem=pl.BlockSpec(memory_space=pltpu.VMEM)
    return pl.pallas_call(functools.partial(norm_rows_kernel,n),
        in_specs=[pl.BlockSpec(memory_space=pltpu.SMEM)]*2+[vmem]*(n+3),
        out_specs=[pl.BlockSpec(memory_space=pl.ANY)]*2+[vmem]*2,
        out_shape=[jax.ShapeDtypeStruct((n*rows,wide),BF),jax.ShapeDtypeStruct((n*rows,w),BF)]+[jax.ShapeDtypeStruct((n*rows,E),F32)]*2,
        scratch_shapes=[pltpu.VMEM((n,rows,wide),BF),pltpu.VMEM((n,rows,w),BF),pltpu.SemaphoreType.DMA((n,)),pltpu.SemaphoreType.DMA((n,))],
        compiler_params=pltpu.CompilerParams(vmem_limit_bytes=VMEM_LIMIT),
        cost_estimate=pl.CostEstimate(flops=6*n*rows*wide,bytes_accessed=4*n*rows*wide,transcendentals=n*rows))(at,column,gain[None],router,kept,*pieces)

def latent_back_kernel(small_ref, proj_ref, gain_ref, cos_ref, sin_ref, delta_ref, dots_ref, gain_delta_ref):
    i=pl.program_id(0)
    at=proj_ref.shape[1]-R-DN
    dl=small_ref[:,:R].astype(F32)
    vl=proj_ref[:,at:at+R]
    rl=lax.rsqrt(jnp.mean(vl*vl,axis=-1,keepdims=True)+EPSILON)
    gain=gain_ref[...]
    part=jnp.sum(dl*vl*rl,axis=0,keepdims=True)
    @pl.when(i==0)
    def _(): gain_delta_ref[...]=part
    @pl.when(i>0)
    def _(): gain_delta_ref[...]+=part
    gd=gain*dl
    head=rl*gd-vl*(rl*rl*rl)*jnp.mean(vl*gd,axis=-1,keepdims=True)
    beyond=small_ref[:,R:]
    row=lax.broadcasted_iota(jnp.int32,(DN,DN),0); col=lax.broadcasted_iota(jnp.int32,(DN,DN),1)
    h=DR//2
    put=jnp.where(((row<h)&(col==row))|((row>=h)&(row<DR)&(col==row+h)),1.0,0.0).astype(BF)
    spread=mm(beyond,put,NN)
    tail=spread*cos_ref[...]-pltpu.roll(spread,DR,1)*sin_ref[...]
    delta_ref[:,:R]=head.astype(BF)
    delta_ref[:,R:]=tail.astype(BF)
    own=jnp.sum(head*vl,axis=-1,keepdims=True)+jnp.sum(tail*proj_ref[:,at+R:],axis=-1,keepdims=True)
    lane=lax.broadcasted_iota(jnp.int32,beyond.shape,1)
    dots_ref[...]=own+jnp.sum(jnp.where(lane==DR,beyond.astype(F32),0.0),axis=-1,keepdims=True)

def latent_back(small, proj, gain, cosine, sine, bt=512):
    T,wide=small.shape; turns=LEN//bt
    return pl.pallas_call(latent_back_kernel,grid=(T//bt,),
        in_specs=[pl.BlockSpec((bt,wide),lambda i:(i,0)),pl.BlockSpec((bt,proj.shape[1]),lambda i:(i,0)),
                  pl.BlockSpec((1,R),lambda i:(0,0)),pl.BlockSpec((bt,DN),lambda i:(i%turns,0)),pl.BlockSpec((bt,DN),lambda i:(i%turns,0))],
        out_specs=[pl.BlockSpec((bt,R+DN),lambda i:(i,0)),pl.BlockSpec((bt,1),lambda i:(i,0)),pl.BlockSpec((1,R),lambda i:(0,0))],
        out_shape=[jax.ShapeDtypeStruct((T,R+DN),BF),jax.ShapeDtypeStruct((T,1),F32),jax.ShapeDtypeStruct((1,R),F32)],
        compiler_params=params(1),
        cost_estimate=pl.CostEstimate(flops=30*T*wide,bytes_accessed=8*T*wide,transcendentals=T))(small,proj,gain,cosine,sine)

def last_pack_kernel(delta_ref, x_ref, w_ref, small_ref, g_ref, latent_ref, out_ref):
    n=delta_ref.shape[1]
    d=mm(delta_ref[...],x_ref[...],TN)
    out_ref[:n]=d.astype(BF)
    sums=jnp.sum(w_ref[...].astype(F32)*d,axis=0,keepdims=True)
    row=lax.broadcasted_iota(jnp.int32,(32,DN),0); col=lax.broadcasted_iota(jnp.int32,(32,DN),1)
    at=DR+1
    pick=((row<E)&(col==row+at+2))|((row==E)&(col==at))|((row==E+1)&(col==at+1))
    v=mm(jnp.where(pick,1.0,0.0).astype(BF),small_ref[...],NT)
    line=lax.broadcasted_iota(jnp.int32,v.shape,0)
    v=jnp.where(line==E+1,(v+sums)/g_ref[...],v)
    out_ref[n:]=jnp.where(line==E+2,latent_ref[...],v).astype(BF)

def last_pack(delta, x, w, small, gain, latent_row, bc=512):
    T,D=x.shape; n=delta.shape[1]
    def cols(a): return pl.BlockSpec((a.shape[0],bc),lambda j:(0,j))
    return pl.pallas_call(last_pack_kernel,grid=(D//bc,),
        in_specs=[pl.BlockSpec((T,n),lambda j:(0,0)),cols(x),cols(w),pl.BlockSpec((bc,DN),lambda j:(j,R//DN)),cols(gain),cols(latent_row)],
        out_specs=pl.BlockSpec((n+32,bc),lambda j:(0,j)),out_shape=jax.ShapeDtypeStruct((n+32,D),BF),
        compiler_params=params(1),
        cost_estimate=pl.CostEstimate(flops=2*T*D*n,bytes_accessed=2*(T*D+2*n*D+T*n),transcendentals=0))(delta,x,w,small,gain,latent_row)


def turn(x, cosine, sine):
    return x*cosine+pltpu.roll(x,64,1)*sine

def slot_mask(shape, head):
    lane=lax.broadcasted_iota(jnp.int32,shape,1)
    low=head*(DR//2)
    inside=((lane>=low)&(lane<low+DR//2))|((lane>=low+DR)&(lane<low+DR+DR//2))
    return inside

def causal_scores(q, k, first):
    s=mm(q,k,NT)*SCALE
    row=lax.broadcasted_iota(jnp.int32,s.shape,0)+first
    col=lax.broadcasted_iota(jnp.int32,s.shape,1)
    return jnp.where(col<=row,s,-1e30)

def attend_kernel(heads, proj_ref, up_ref, gain_ref, cos_ref, sin_ref, q_ref, kr_ref, kv_ref, latent_ref, mixed_ref, lse_ref):
    content=heads*DN
    at=content+DN
    q_ref[:,:content]=proj_ref[:,:content].astype(BF)
    cosine,sine=cos_ref[...],sin_ref[...]
    q_ref[:,content:]=turn(proj_ref[:,content:at],cosine,sine).astype(BF)
    vl=proj_ref[:,at:at+R]
    latent_ref[...]=(vl*lax.rsqrt(jnp.mean(vl*vl,axis=-1,keepdims=True)+EPSILON)*gain_ref[...]).astype(BF)
    kr_ref[...]=turn(proj_ref[:,at+R:],cosine,sine).astype(BF)
    kv_ref[...]=mm(latent_ref[...],up_ref[...],NN).astype(BF)
    kr=kr_ref[...]
    for h in range(heads):
        kc=kv_ref[:,h*(DN+DV):h*(DN+DV)+DN]
        v=kv_ref[:,h*(DN+DV)+DN:(h+1)*(DN+DV)]
        k=jnp.concatenate([kc,jnp.where(slot_mask(kr.shape,h),kr,jnp.zeros_like(kr))],axis=1)
        for i in range(LEN//BLOCK):
            a,b=i*BLOCK,(i+1)*BLOCK
            q=jnp.concatenate([q_ref[a:b,h*DN:(h+1)*DN],q_ref[a:b,content:]],axis=1)
            s=causal_scores(q,k[:b],a)
            m=jnp.max(s,axis=-1,keepdims=True)
            e=jnp.exp(s-m)
            t=jnp.sum(e,axis=-1,keepdims=True)
            p=(e*(1.0/t)).astype(BF)
            mixed_ref[a:b,h*DV:(h+1)*DV]=mm(p,v[:b],NN).astype(BF)
            lse_ref[a:b,h:h+1]=m+jnp.log(t)

def attend(proj, up, gain, cosine, sine, heads):
    T=proj.shape[0]; wide=proj.shape[1]
    def rows(n): return pl.BlockSpec((LEN,n),lambda i:(i,0))
    def whole(a): return pl.BlockSpec(a.shape,lambda i:(0,0))
    qn=heads*DN+DN
    outs=[(qn,BF),(DN,BF),(heads*(DN+DV),BF),(R,BF),(heads*DV,BF),(heads,F32)]
    return pl.pallas_call(functools.partial(attend_kernel,heads),grid=(T//LEN,),
        in_specs=[rows(wide),whole(up),whole(gain),whole(cosine),whole(sine)],
        out_specs=[rows(n) for n,_ in outs],out_shape=[jax.ShapeDtypeStruct((T,n),d) for n,d in outs],
        compiler_params=params(1),
        cost_estimate=pl.CostEstimate(flops=T*LEN*heads*512,bytes_accessed=T*8000,transcendentals=T*LEN*heads//2))(proj,up,gain,cosine,sine)

def attend_back_kernel(heads, q_ref, kr_ref, kv_ref, mixed_ref, lse_ref, do_ref, cos_ref, sin_ref, dq_ref, dkv_ref, dkr_ref, dot_ref, dk_acc, dv_acc):
    content=heads*DN
    kr=kr_ref[...]
    for h in range(heads):
        kc=kv_ref[:,h*(DN+DV):h*(DN+DV)+DN]
        v=kv_ref[:,h*(DN+DV)+DN:(h+1)*(DN+DV)]
        mask=slot_mask(kr.shape,h)
        k=jnp.concatenate([kc,jnp.where(mask,kr,jnp.zeros_like(kr))],axis=1)
        for i in reversed(range(LEN//BLOCK)):
            a,b=i*BLOCK,(i+1)*BLOCK
            q=jnp.concatenate([q_ref[a:b,h*DN:(h+1)*DN],q_ref[a:b,content:]],axis=1)
            do=do_ref[a:b,h*DV:(h+1)*DV]
            p=jnp.exp(causal_scores(q,k[:b],a)-lse_ref[a:b,h:h+1])
            dp=mm(do,v[:b],NT)
            along=jnp.sum(do.astype(F32)*mixed_ref[a:b,h*DV:(h+1)*DV].astype(F32),axis=-1,keepdims=True)
            ds=(p*(dp-along)).astype(BF)
            pv=mm(p.astype(BF),do,TN)
            pk=mm(ds,q,TN)
            if i==LEN//BLOCK-1:
                dv_acc[...]=pv; dk_acc[...]=pk
            else:
                dv_acc[:b]+=pv; dk_acc[:b]+=pk
            dq=mm(ds,k[:b],NN)*SCALE
            d=jnp.sum(dq*q.astype(F32),axis=-1,keepdims=True)
            if h==0: dot_ref[a:b]=d
            else: dot_ref[a:b]+=d
            dq_ref[a:b,h*DN:(h+1)*DN]=dq[:,:DN].astype(BF)
            turned=turn(dq[:,DN:],cos_ref[a:b],-sin_ref[a:b])
            turned=jnp.where(mask[:b-a],turned,0.0).astype(BF)
            if h==0: dq_ref[a:b,content:]=turned
            else: dq_ref[a:b,content:]+=turned
        dkv_ref[:,h*(DN+DV):h*(DN+DV)+DN]=(dk_acc[:,:DN]*SCALE).astype(BF)
        dkv_ref[:,h*(DN+DV)+DN:(h+1)*(DN+DV)]=dv_acc[...].astype(BF)
        part=jnp.where(mask,dk_acc[:,DN:]*SCALE,0.0)
        if h==0: dkr_ref[...]=part
        else: dkr_ref[...]+=part

def attend_back(q,kr,kv,mixed,lse,do,cosine,sine,heads):
    T=q.shape[0]
    def rows(n): return pl.BlockSpec((LEN,n),lambda i:(i,0))
    def whole(a): return pl.BlockSpec(a.shape,lambda i:(0,0))
    args=(q,kr,kv,mixed,lse,do)
    outs=[(q.shape[1],BF),(kv.shape[1],BF),(DN,F32),(1,F32)]
    return pl.pallas_call(functools.partial(attend_back_kernel,heads),grid=(T//LEN,),
        in_specs=[rows(a.shape[1]) for a in args]+[whole(cosine),whole(sine)],
        out_specs=[rows(n) for n,_ in outs],out_shape=[jax.ShapeDtypeStruct((T,n),d) for n,d in outs],
        scratch_shapes=[pltpu.VMEM((LEN,2*DN),F32),pltpu.VMEM((LEN,DV),F32)],
        compiler_params=params(1),
        cost_estimate=pl.CostEstimate(flops=T*LEN*heads*1400,bytes_accessed=T*6000,transcendentals=T*LEN*heads//2))(*args,cosine,sine)

def tables():
    position=np.arange(LEN,dtype=np.float32)
    spread=(10000.0**(-np.arange(DR//2,dtype=np.float32)/(DR//2))).astype(np.float32)
    phase=(position[:,None]*spread[None,:]).astype(np.float32)
    c,s=np.cos(phase),np.sin(phase)
    return np.concatenate([c]*4,1).astype(np.float32),np.concatenate([-s,-s,s,s],1).astype(np.float32)


class Line:
    def __init__(self):
        self.n = lax.axis_size("tensor")
        self.chips = self.n // 2
        index = lax.axis_index("tensor")
        self.index = index
        self.z = index // 2
        self.c = index % 2

    def swap(self, a):
        return lax.ppermute(a, "tensor", [(i, i ^ 1) for i in range(self.n)])

    def shift(self, a, step, sources):
        pairs = [
            (2 * s + c, 2 * (s + step) + c)
            for s in sources
            if 0 <= s + step < self.chips
            for c in (0, 1)
        ]
        return lax.ppermute(a, "tensor", pairs)

    def chip_gather(self, s, jobs=None):
        n = self.chips
        left, right = [s], [s]
        for k in range(1, n):
            pair = (
                self.shift(left[-1], 1, range(k - 1, n)),
                self.shift(right[-1], -1, range(0, n - k + 1)),
            )
            pair = beside(pair, jobs)
            left.append(pair[0])
            right.append(pair[1])
        return [s] + [jnp.where(self.z >= k, left[k], right[n - k]) for k in range(1, n)]

    def pieces(self, own, order):
        n = self.chips
        out, at = [], []
        for k, piece in enumerate(own):
            chip = (self.z - k + n) % n
            out += [piece, self.swap(piece)]
            at += [order(chip, self.c), order(chip, 1 - self.c)]
        return out, jnp.stack(at).astype(jnp.int32)

    def row_pieces(self, s, jobs=None):
        return self.pieces(self.chip_gather(s, jobs), lambda chip, core: core * self.chips + chip)

    def column_pieces(self, own):
        return self.pieces(own, lambda chip, core: chip * 2 + core)

    def chip_scatter(self, block, jobs=None):
        n = self.chips
        left = right = None
        for s in range(1, n):
            up = block(jnp.clip(n - s + self.z, 0, n - 1))
            down = block(jnp.clip(self.z - (n - s), 0, n - 1))
            if left is not None:
                up = (up.astype(F32) + left.astype(F32)).astype(BF)
                down = (down.astype(F32) + right.astype(F32)).astype(BF)
            left = self.shift(up, 1, range(0, s))
            right = self.shift(down, -1, range(n - s, n))
            left, right = beside((left, right), jobs)
        return block(self.z).astype(F32) + left.astype(F32) + right.astype(F32)

    def row_pair(self, p):
        half = p.shape[0] // 2
        mine = lax.dynamic_slice_in_dim(p, self.c * half, half, 0)
        theirs = lax.dynamic_slice_in_dim(p, (1 - self.c) * half, half, 0)
        return (mine.astype(F32) + self.swap(theirs).astype(F32)).astype(BF)

    def row_scatter(self, both, jobs=None):
        ch = both.shape[0] // self.chips
        return self.chip_scatter(lambda j: lax.dynamic_slice_in_dim(both, j * ch, ch, 0), jobs)

    def row_start(self, rows):
        ch = rows // self.n
        return (self.c * self.chips + self.z) * ch, ch

    def column_scatter(self, mine, arrived, jobs=None):
        both = (mine.astype(F32) + arrived.astype(F32)).astype(BF)
        return self.chip_scatter(lambda j: lax.dynamic_index_in_dim(both, j, 0, False), jobs)


class Jobs:
    def __init__(self, *steps):
        self.steps = list(steps)
        self.made = {}

    def rest(self):
        while self.steps:
            self.made.update(self.steps.pop(0)(self.made))
        return self.made


def beside(arrived, jobs):
    if jobs is None or not jobs.steps:
        return lax.optimization_barrier(arrived)
    step = jobs.steps.pop(0)(jobs.made)
    arrived, step = lax.optimization_barrier((arrived, step))
    jobs.made.update(step)
    return arrived


def gather_rows(packed):
    return lax.all_gather(packed, "dp", axis=1, tiled=True)


def scatter_rows(packed):
    return lax.psum_scatter(packed, "dp", scatter_dimension=1, tiled=True)


def split_rows(packed, counts):
    out, at = [], 0
    for count in counts:
        out.append(packed[at : at + count])
        at += count
    return out


def ranks(mask):
    number = mask.shape[0]
    block = 128
    pieces = mask.reshape(number // block, block, E).astype(BF)
    lower = jnp.tril(jnp.ones((block, block), BF), -1)
    inside = jnp.einsum("ij,bje->bie", lower, pieces, preferred_element_type=F32)
    totals = jnp.sum(pieces.astype(F32), axis=1).astype(BF)
    ahead = jnp.tril(jnp.ones((number // block, number // block), BF), -1)
    before = dot(ahead, totals, 1, 0)
    return (inside + before[:, None, :]).reshape(number, E)


def per_device(
    layer_input, cotangent, first_gain, query_weight, latent_down, latent_gain, latent_up,
    output_weight, second_gain, router_weight, expert_gate, expert_up, expert_down,
    shared_gate, shared_up, shared_down, routes,
):
    line = Line()
    n_dp = lax.axis_size("dp")
    wide = D // n_dp
    number = layer_input.shape[0]
    heads_here = output_weight.shape[0] // DV
    fe = expert_down.shape[1]
    my_columns = layer_input.shape[1]
    column_start = line.index * my_columns
    row_start, row_count = line.row_start(number)

    half = DR // 2
    spare_heads = 2 - heads_here
    up_rows = latent_up.size // wide
    by_head = query_weight.T.reshape(heads_here, DN + DR, wide)
    blank = jnp.zeros((spare_heads * half, wide), BF)
    gains = jnp.zeros((16, wide), BF)
    gains = gains.at[0].set(first_gain).at[1].set(second_gain)
    gains = gains.at[2, : latent_gain.shape[0]].set(latent_gain)
    down = latent_down.T
    queries_wide = heads_here * DN + DN
    latent_wide = R + DN
    attend_pack = [
        by_head[:, :DN].reshape(heads_here * DN, wide),
        by_head[:, DN : DN + half].reshape(heads_here * half, wide), blank,
        by_head[:, DN + half :].reshape(heads_here * half, wide), blank,
        down[: R + half], down[R : R + half], down[R + half :], down[R + half :],
        latent_up.reshape(up_rows, wide), gains, router_weight.T, output_weight,
    ]
    attend_packed = gather_rows(jnp.concatenate([m for m in attend_pack if m.shape[0]], axis=0))
    wproj, wup, gains, wr, wo = split_rows(
        attend_packed, [queries_wide + latent_wide, up_rows, 16, E, output_weight.shape[0]]
    )
    wup = wup.reshape(up_rows, n_dp, wide).transpose(1, 0, 2).reshape(R, -1)
    first_g = gains[0].astype(F32)
    second_g = gains[1].astype(F32)
    latent_g = gains[2].reshape(n_dp, wide)[:, : R // n_dp].reshape(R).astype(F32)
    cosine, sine = (jnp.asarray(table) for table in tables())

    shared = shared_down.shape[0]
    units_here = (E * fe + shared) // 2
    cut = units_here // fe
    assert cut * fe == units_here
    gate = expert_gate.transpose(0, 2, 1).reshape(E * fe, wide)
    up = expert_up.transpose(0, 2, 1).reshape(E * fe, wide)
    jobs = Jobs(
        lambda made: {"down": jnp.concatenate([expert_down.reshape(E * fe, wide), shared_down], axis=0)},
        lambda made: {"early": jnp.concatenate([gate[:units_here], up[:units_here]], axis=0)},
        lambda made: {"late": jnp.concatenate(
            [gate[units_here:], shared_gate.T, up[units_here:], shared_up.T], axis=0)},
    )
    input_own = line.chip_gather(layer_input, jobs)
    packs = jobs.rest()
    downs, early, late = gather_rows(packs["down"]), gather_rows(packs["early"]), gather_rows(packs["late"])

    tile = 256
    core = line.c.reshape(1).astype(jnp.int32)
    input_pieces, input_at = line.column_pieces(input_own)
    input_pieces, cotangent = lax.optimization_barrier((input_pieces, cotangent))

    def project(made):
        rows, first_round, r1 = place_columns(input_pieces, input_at, first_g)
        return {"rows": rows, "first": first_round, "r1": r1, "proj": dot(first_round, wproj, 1, 1)}

    def attention(made):
        kept = attend(made["proj"], wup, latent_g[None], cosine, sine, heads_here)
        return {"attend": kept, "terms": dot(kept[4], wo, 1, 0, BF)}

    jobs = Jobs(project, attention, lambda made: {"both": line.row_pair(made["terms"])})
    grad_own = line.chip_gather(cotangent, jobs)
    made = jobs.rest()
    rows, first_round, r1, proj = made["rows"], made["first"], made["r1"], made["proj"]
    q, kr, kv, latent, mixed, log_total = made["attend"]
    jobs = Jobs(
        lambda made: {"grad": place_columns(*line.column_pieces(grad_own))[0]},
        lambda made: {},
        lambda made: {"back0": lift_back(made["grad"], downs, 0, units_here, tile)},
        lambda made: {"back1": lift_back(made["grad"], downs, 1, units_here, tile)},
    )
    attend_rows = line.row_scatter(made["both"], jobs)
    hidden_rows = (
        lax.dynamic_slice_in_dim(rows, row_start, row_count, 0).astype(F32) + attend_rows
    ).astype(BF)
    hidden_pieces, hidden_at = line.row_pieces(hidden_rows, jobs)
    made = jobs.rest()
    grad, back0, back1 = made["grad"], made["back0"], made["back1"]
    named = jnp.any(routes[:, :, None] == jnp.arange(E, dtype=jnp.int32)[None, None, :], axis=1)
    kept = jnp.where(named & (ranks(named) < CAP), 1.0, 0.0)
    second_round, hidden_columns, gating, weight = norm_rows(
        hidden_pieces, hidden_at, line.index.reshape(1).astype(jnp.int32), my_columns, second_g, wr, kept
    )

    stack0, pair0 = units(second_round, early, back0, weight, fe, 0, cut, tile)
    deltas = outer(stack0, 0, 2, second_round, 3 * units_here, 0)
    deltas = outer(stack0, 2, 1, grad, 3 * units_here, 2, deltas)
    deltas, stack0 = lax.optimization_barrier((deltas, stack0))
    early_sums = scatter_rows(deltas)
    second_terms = back([(stack0, 0, early, units_here, 0), (stack0, 1, early, units_here, 1)], None, F32, tile)
    stack1, pair1 = units(second_round, late, back1, weight, fe, cut, E - cut, tile)
    second_terms = back(
        [(stack1, 0, late, units_here, 0), (stack1, 1, late, units_here, 1)],
        second_terms, BF, tile, (pair0, pair1),
    )

    branch_terms = [(stack0, 2, downs, units_here, 0), (stack1, 2, downs, units_here, 1)]
    jobs = Jobs(
        lambda made: {"deltas": outer(stack1, 0, 1, second_round, 3 * units_here, 0)},
        lambda made: {"deltas": outer(stack1, 1, 1, second_round, 3 * units_here, 1, made["deltas"])},
        lambda made: {"deltas": outer(stack1, 2, 1, grad, 3 * units_here, 2, made["deltas"])},
        lambda made: {"theirs": back(branch_terms, None, BF, tile, (), 1 - core, line.chips)},
        lambda made: {"mine": back(branch_terms, None, BF, tile, (), core, line.chips)},
    )
    summed = line.row_scatter(line.row_pair(second_terms), jobs)
    early_sums, summed, jobs.made = lax.optimization_barrier((early_sums, summed, jobs.made))
    late_sums = scatter_rows(jobs.made["deltas"])

    def own_rows(a):
        return lax.dynamic_slice_in_dim(a, row_start, row_count, 0)

    gating_rows, kept_rows, x2 = own_rows(gating), own_rows(kept), own_rows(second_round)
    u = summed[:, D : D + E] * kept_rows
    logits_delta = gating_rows * (u - jnp.sum(gating_rows * u, axis=-1, keepdims=True))
    router_delta = dot(x2, logits_delta.astype(BF), 0, 0)
    d2 = summed[:, :D] + dot(logits_delta.astype(BF), wr, 1, 0)
    v2 = hidden_rows.astype(F32)
    r2 = lax.rsqrt(jnp.mean(v2 * v2, axis=-1, keepdims=True) + EPSILON)
    vgd = jnp.mean(v2 * second_g * d2, axis=-1, keepdims=True)
    second_gain_delta = jnp.sum(d2 * v2 * r2, axis=0)
    hidden_delta = own_rows(grad).astype(F32) + r2 * second_g * d2 - v2 * (r2**3) * vgd
    delta_pieces, delta_at = line.row_pieces(hidden_delta.astype(BF), jobs)
    made = jobs.rest()
    delta_pieces, theirs, mine = lax.optimization_barrier((delta_pieces, made["theirs"], made["mine"]))

    def into_heads(made):
        placed = place_rows(delta_pieces, delta_at)
        return {"hidden": placed, "mixed": dot(placed, wo, 1, 1, BF)}

    def heads_back(made):
        return {"heads": attend_back(q, kr, kv, mixed, log_total, made["mixed"], cosine, sine, heads_here)}

    def small_terms(made):
        delta_queries, delta_pairs, delta_kr, query_dot = made["heads"]
        delta_wq = dot(delta_queries, first_round, 0, 0)
        query_gain = jnp.sum(wproj[:queries_wide].astype(F32) * delta_wq, axis=0)
        per_entry = jnp.concatenate([second_gain_delta[:, None], query_gain[:, None], router_delta], axis=1)
        if number > D:
            per_entry = jnp.concatenate([per_entry, jnp.zeros((number - D, E + 2), F32)], axis=0)
        small = jnp.concatenate(
            [dot(delta_pairs, wup, 1, 1),
             delta_kr[:, :half] + delta_kr[:, half:DR], delta_kr[:, DR : DR + half] + delta_kr[:, DR + half :],
             query_dot, per_entry, jnp.zeros((number, 63 - 2 - E), F32)], axis=1,
        ).astype(BF)
        return {"small": small, "wq": delta_wq.astype(BF)}

    jobs = Jobs(into_heads, heads_back, small_terms)
    branch = line.column_scatter(mine, line.swap(theirs), jobs)
    made = jobs.rest()
    layer_output = (hidden_columns.astype(F32) + branch).astype(BF)
    hidden_delta, (delta_queries, delta_pairs) = made["hidden"], made["heads"][:2]
    first_terms = [(delta_queries, 0, attend_packed, queries_wide, 0)]

    def attend_deltas(made):
        delta_wup = dot(latent, delta_pairs, 0, 0, BF)
        return {"deltas": jnp.concatenate(
            [made["wq"], delta_wup.reshape(n_dp, up_rows, wide).transpose(1, 0, 2).reshape(up_rows, D),
             dot(mixed, hidden_delta, 0, 0, BF)], axis=0)}

    jobs = Jobs(
        lambda made: {"theirs": back(first_terms, None, BF, tile, (), 1 - core, line.chips)},
        lambda made: {"mine": back(first_terms, None, BF, tile, (), core, line.chips)},
        attend_deltas,
    )
    jobs.made["wq"] = made["wq"]
    small = line.row_scatter(line.row_pair(made["small"]), jobs).astype(BF)
    made = jobs.rest()
    deltas, small = lax.optimization_barrier((made["deltas"], small))
    attend_sums = scatter_rows(deltas).astype(F32)
    small_pieces, small_at = line.row_pieces(small)
    small_pieces, arrived, late_sums = lax.optimization_barrier(
        (small_pieces, line.swap(made["theirs"]), late_sums)
    )
    wld = wproj[queries_wide:]

    def last(made):
        small = place_rows(small_pieces, small_at)
        delta_latent, dots, gain_delta = latent_back(small, proj, latent_g[None], cosine, sine)
        latent_row = jnp.pad(gain_delta.reshape(n_dp, R // n_dp), ((0, 0), (0, wide - R // n_dp))).reshape(1, D)
        return {"delta": delta_latent, "dots": dots,
                "pack": last_pack(delta_latent, first_round, wld, small, first_g[None], latent_row)}

    jobs = Jobs(last)
    first_share = line.column_scatter(made["mine"], arrived, jobs)
    made = jobs.rest()
    last_sums = scatter_rows(made["pack"]).astype(F32)
    dwld, vectors = last_sums[:latent_wide], last_sums[latent_wide:]
    dwq, dwup, dwo = split_rows(attend_sums, [queries_wide, up_rows, output_weight.shape[0]])
    content = heads_here * DN
    dwq = jnp.concatenate(
        [dwq[:content].reshape(heads_here, DN, wide),
         dwq[content : content + heads_here * half].reshape(heads_here, half, wide),
         dwq[content + DR : content + DR + heads_here * half].reshape(heads_here, half, wide)], axis=1
    ).reshape(heads_here * (DN + DR), wide)
    dwld = jnp.concatenate([dwld[: R + half], dwld[R + DR : R + DR + half]], axis=0)

    first_share = first_share + dot(
        made["delta"], lax.dynamic_slice_in_dim(wld, column_start, my_columns, 1), 1, 0
    )
    vc = layer_input.astype(F32)
    gc = lax.dynamic_slice_in_dim(first_g, column_start, my_columns, 0)
    input_delta = (
        lax.dynamic_slice_in_dim(hidden_delta, column_start, my_columns, 1).astype(F32)
        + r1 * gc * first_share
        - vc * (r1 * r1) * (made["dots"] / D)
    )

    def expert_delta(k):
        first = early_sums[k * units_here : (k + 1) * units_here]
        second = late_sums[k * units_here : k * units_here + E * fe - units_here]
        return jnp.concatenate([first, second], axis=0).astype(F32).reshape(E, fe, wide)

    def shared_delta(k):
        return late_sums[(k + 1) * units_here - shared : (k + 1) * units_here].astype(F32)

    return (
        layer_output, input_delta, vectors[E + 1], dwq.T, dwld.T, vectors[E + 2, : R // n_dp],
        dwup.reshape(latent_up.shape), dwo, vectors[E], vectors[:E].T,
        expert_delta(0).transpose(0, 2, 1), expert_delta(1).transpose(0, 2, 1), expert_delta(2),
        shared_delta(0).T, shared_delta(1).T, shared_delta(2),
    )


def solution(mesh):
    in_specs = (
        P("dp", "tensor"), P("dp", "tensor"), P("dp"), P("dp", "tensor"), P("dp", None), P("dp"),
        P("dp", "tensor"), P("tensor", "dp"), P("dp"), P("dp", None), P(None, "dp", "tensor"),
        P(None, "dp", "tensor"), P(None, "tensor", "dp"), P("dp", "tensor"), P("dp", "tensor"),
        P("tensor", "dp"), P("dp", None),
    )
    out_specs = (
        P("dp", "tensor"), P("dp", "tensor"), P("dp"), P("dp", "tensor"), P("dp", None), P("dp"),
        P("dp", "tensor"), P("tensor", "dp"), P("dp"), P("dp", None), P(None, "dp", "tensor"),
        P(None, "dp", "tensor"), P(None, "tensor", "dp"), P("dp", "tensor"), P("dp", "tensor"),
        P("tensor", "dp"),
    )
    return jax.shard_map(
        per_device, mesh=mesh, in_specs=in_specs, out_specs=out_specs, check_vma=False
    )
```

time: 2760 us -> 1160 us (0.42)
  local copies, waits for them, and re-layouts: 1080 us -> 72 us
  matrix products: 592 us -> 51.3 us
  Pallas kernels: 0 us -> 484 us
  waiting for transfers between devices: 680 us -> 296 us
  other arithmetic: 212 us -> 98.7 us
    dynamic_update_slice x33 -> x0, local copies, waits for them, and re-layouts: 731 us -> none  [the longest x20 372 us: gather(): lax.dynamic_update_slice(out, other[None], (order(chip, 1 - self.c),) + s...]
    pallas_call x0 -> x24, Pallas kernels: none -> 484 us  [the longest x6 142 us: back(): pl.pallas_call(body, grid=(T // bt,), in_specs=ins, out_specs=ospec, out_...]
    dot_general x43 -> x11, matrix products: 522 us -> 51.1 us  [dot(): lax.dot_general(a, b, (((ca,), (cb,)), ((), ())), preferred_element_type=...]
    ppermute x60, waiting for transfers between devices: 506 us -> 271 us  [shift(): return lax.ppermute(a, 'tensor', pairs)]
    psum x1 -> x0, waiting for transfers between devices: 108 us -> none  [per_device(): vectors = lax.psum(vectors, ('dp', 'tensor'))]
    broadcast_in_dim x29 -> x3, local copies, waits for them, and re-layouts: 91 us -> 3.12 us  [the longest x1 1.13 us: small_terms(): second_gain_delta[:, None]]
    unnamed x272 -> x163, local copies, waits for them, and re-layouts: 94.7 us -> 21.4 us
    dot_general x9 -> x0, matrix products: 69.5 us -> none  [the longest x1 12.7 us: per_device(): jnp.einsum('sihc,sjhc->shij', delta_mixed, value_seq, preferred_element_t...]
  transfers between devices with their start and end apart: 92 -> 93, of which waited for: 36 -> 36; matrix products, arithmetic and copies ran while one was open for 67% -> 17% of each run, Pallas kernels for 0% -> 42%
where the time goes in v2:
time: 1160 us; the launch traced here: 1150 us
  Pallas kernels  484 us (42%)
  waiting for transfers between devices  296 us (26%)
  starting transfers between devices  134 us (12%)
  other arithmetic  98.7 us (9%)
  local copies, waits for them, and re-layouts  72 us (6%)
  matrix products  51.3 us (4%)
  between operations  16.4 us (1%)
    ppermute x60, waiting for transfers between devices, shift(): return lax.ppermute(a, 'tensor', pairs)  271 us
    pallas_call x6, Pallas kernels, back(): pl.pallas_call(body, grid=(T // bt,), in_specs=ins, out_specs=ospec, out_...  142 us
    ppermute x60, starting transfers between devices, shift(): return lax.ppermute(a, 'tensor', pairs)  128 us
    pallas_call x5, Pallas kernels, outer(): pl.pallas_call(outer_kernel, grid=(count, D // bc), in_specs=ins, out_spe...  111 us
    pallas_call x2, Pallas kernels, units(): pl.pallas_call(functools.partial(units_kernel, fe, first, count), grid=(T...  89.9 us
    dot_general x11, matrix products, dot(): lax.dot_general(a, b, (((ca,), (cb,)), ((), ())), preferred_element_type=...  51.1 us
    pallas_call x2, Pallas kernels, lift_back(): pl.pallas_call(lift_kernel, grid=(T // bt,), in_specs=[pl.BlockSpec((bt,...  42.2 us
    ppermute x25, waiting for transfers between devices, swap(): return lax.ppermute(a, 'tensor', [(i, i ^ 1) for i in range(self.n)])  24.5 us
  transfers between devices with their start and end apart: 93, of which 36 were waited for; matrix products, arithmetic and copies ran while one was open for 17% of the time, Pallas kernels for 42%

profile of v2, /device:TPU:0, one launch (start us, length us, event | category | flops | bytes accessed | tf_op | source)
XLA Modules:
  0.0 1152.7 jit_solution(7101896938440468989)
XLA Ops:
  26.6 17.6 %collective-permute-done.1 = bf16[2048,256]{1,0:T(8,128)(2,1)} collective-permute-done((bf16[2048,256]{1,0:T(8,128)(2,1)}, bf16[2048,256]{1,0:T(8,128)(2,1)}, u32[]{:S(2)}, u32[]{:S(2)}) %collective-permute-start.1) | collective-permute-done | bytes 1048608 | tf_op jit(solution)/shard_map/ppermute | solution.py:423
  54.6 24.0 %collective-permute-done.4 = bf16[2048,256]{1,0:T(8,128)(2,1)} collective-permute-done((bf16[2048,256]{1,0:T(8,128)(2,1)}, bf16[2048,256]{1,0:T(8,128)(2,1)}, u32[]{:S(2)}, u32[]{:S(2)}) %collective-permute-start.4) | collective-permute-done | bytes 1048608 | tf_op jit(solution)/shard_map/ppermute | solution.py:423
  88.4 22.6 %collective-permute-done.6 = bf16[2048,256]{1,0:T(8,128)(2,1)} collective-permute-done((bf16[2048,256]{1,0:T(8,128)(2,1)}, bf16[2048,256]{1,0:T(8,128)(2,1)}, u32[]{:S(2)}, u32[]{:S(2)}) %collective-permute-start.6) | collective-permute-done | bytes 1048608 | tf_op jit(solution)/shard_map/ppermute | solution.py:423
  154.9 13.9 %shard_map.307 = (bf16[2048,384]{1,0:T(8,128)(2,1)}, bf16[2048,128]{1,0:T(8,128)(2,1)}, bf16[2048,512]{1,0:T(8,128)(2,1)}, bf16[2048,512]{1,0:T(8,128)(2,1)}, bf...) custom-call(f32[2048,1024]{1,0:T(8,128)} %fusion.proj_ref, bf16[512,512]{1,0:T(8,128)(2,1)} %bitcast.170, f32[1,512]{1,0:T(1,128)} %bitcast.188, ...), custom_call_target="tpu_custom_call" | custom-call | flops 2147483648 | bytes 16384000 | tf_op jit(solution)/shard_map/pallas_call | solution.py:340
  194.5 16.7 %collective-permute-done.15 = bf16[2048,256]{1,0:T(8,128)(2,1)S(1)} collective-permute-done((bf16[2048,256]{1,0:T(8,128)(2,1)}, bf16[2048,256]{1,0:T(8,128)(2,1)S(1)}, u32[]{:S(2)}, u32[]{:S(2)}) %collective-permute-start.15) | collective-permute-done | bytes 1048608 | tf_op jit(solution)/shard_map/ppermute | solution.py:423
  251.8 20.3 %collective-permute-done.23 = bf16[256,2048]{1,0:T(8,128)(2,1)S(1)} collective-permute-done((bf16[256,2048]{1,0:T(8,128)(2,1)}, bf16[256,2048]{1,0:T(8,128)(2,1)S(1)}, u32[]{:S(2)}, u32[]{:S(2)}) %collective-permute-start.23) | collective-permute-done | bytes 1048608 | tf_op jit(solution)/shard_map/ppermute | solution.py:423
  285.4 21.2 %shard_map.309.b_ref = bf16[2048,1584]{1,0:T(8,128)(2,1)} custom-call(bf16[2048,2048]{1,0:T(8,128)(2,1)} %shard_map.308.g_ref.x_ref, bf16[3168,2048]{1,0:T(8,128)(2,1)} %all-gather.7.cloned.1.call-done.w_ref.refs_1_.refs_3_), custom_call_target="tpu_custom_call" | custom-call | flops 13287555072 | bytes 21364736 | tf_op jit(solution)/shard_map/pallas_call | solution.py:82
  315.4 21.0 %shard_map.310.b_ref = bf16[2048,1584]{1,0:T(8,128)(2,1)} custom-call(bf16[2048,2048]{1,0:T(8,128)(2,1)} %shard_map.308.g_ref.x_ref, bf16[3168,2048]{1,0:T(8,128)(2,1)} %all-gather.7.cloned.1.call-done.w_ref.refs_1_.refs_3_), custom_call_target="tpu_custom_call" | custom-call | flops 13287555072 | bytes 21364736 | tf_op jit(solution)/shard_map/pallas_call | solution.py:82
  341.4 23.0 %collective-permute-done.31 = bf16[256,2048]{1,0:T(8,128)(2,1)} collective-permute-done((bf16[256,2048]{1,0:T(8,128)(2,1)S(1)}, bf16[256,2048]{1,0:T(8,128)(2,1)}, u32[]{:S(2)}, u32[]{:S(2)}) %collective-permute-start.31) | collective-permute-done | bytes 1048608 | tf_op jit(solution)/shard_map/ppermute | solution.py:423
  370.3 18.3 %collective-permute-done.33 = bf16[256,2048]{1,0:T(8,128)(2,1)} collective-permute-done((bf16[256,2048]{1,0:T(8,128)(2,1)}, bf16[256,2048]{1,0:T(8,128)(2,1)}, u32[]{:S(2)}, u32[]{:S(2)}) %collective-permute-start.33) | collective-permute-done | bytes 1048608 | tf_op jit(solution)/shard_map/ppermute | solution.py:423
  409.4 45.3 %shard_map.312 = (bf16[3,2048,1584]{2,1,0:T(8,128)(2,1)}, f32[2048,16]{1,0:T(8,128)}) custom-call(bf16[2048,2048]{1,0:T(8,128)(2,1)} %get-tuple-element.258.x_ref, bf16[3168,2048]{1,0:T(8,128)(2,1)} %all-gather.9.cloned.1.call-done.wg_ref.wu_ref.refs_1_.refs_3_, bf16[3168,2048]{1,0:T(8,128)(2,1)} %all-gather.9.cloned.1.call-done.wg_ref.wu_ref.refs_1_.refs_3_, ...), custom_call_target="tpu_custom_call" | custom-call | flops 26575110144 | bytes 47316992 | tf_op jit(solution)/shard_map/pallas_call | solution.py:72
  454.8 34.1 %shard_map.313.refs_0_ = bf16[4752,2048]{1,0:T(8,128)(2,1)} custom-call(bf16[3,2048,1584]{2,1,0:T(8,128)(2,1)} %get-tuple-element.264.s_ref.refs_0_.refs_2_, bf16[2048,2048]{1,0:T(8,128)(2,1)} %get-tuple-element.258.x_ref), custom_call_target="tpu_custom_call" | custom-call | flops 26575110144 | bytes 42729472 | tf_op jit(solution)/shard_map/pallas_call | solution.py:153
  488.8 19.2 %shard_map.314 = bf16[4752,2048]{1,0:T(8,128)(2,1)} custom-call(bf16[3,2048,1584]{2,1,0:T(8,128)(2,1)} %get-tuple-element.264.s_ref.refs_0_.refs_2_, bf16[2048,2048]{1,0:T(8,128)(2,1)} %shard_map.308.g_ref.x_ref, bf16[4752,2048]{1,0:T(8,128)(2,1)} %shard_map.313.refs_0_), custom_call_target="tpu_custom_call", output_to_operand_aliasing={{}: (2, {})} | custom-call | flops 13287555072 | bytes 21364736 | tf_op jit(solution)/shard_map/pallas_call | solution.py:153
  508.1 39.0 %shard_map.315.refs_0_ = f32[2048,2048]{1,0:T(8,128)} custom-call(bf16[3,2048,1584]{2,1,0:T(8,128)(2,1)} %get-tuple-element.264.s_ref.refs_0_.refs_2_, bf16[3168,2048]{1,0:T(8,128)(2,1)} %all-gather.9.cloned.1.call-done.wg_ref.wu_ref.refs_1_.refs_3_, bf16[3,2048,1584]{2,1,0:T(8,128)(2,1)} %get-tuple-element.264.s_ref.refs_0_.refs_2_, ...), custom_call_target="tpu_custom_call" | custom-call | flops 26575110144 | bytes 42729472 | tf_op jit(solution)/shard_map/pallas_call | solution.py:141
  547.0 44.6 %shard_map.316 = (bf16[3,2048,1584]{2,1,0:T(8,128)(2,1)}, f32[2048,16]{1,0:T(8,128)}) custom-call(bf16[2048,2048]{1,0:T(8,128)(2,1)} %get-tuple-element.258.x_ref, bf16[3168,2048]{1,0:T(8,128)(2,1)} %all-gather.11.cloned.1.call-done.wg_ref.wu_ref.refs_2_.refs_4_, bf16[3168,2048]{1,0:T(8,128)(2,1)} %all-gather.11.cloned.1.call-done.wg_ref.wu_ref.refs_2_.refs_4_, ...), custom_call_target="tpu_custom_call" | custom-call | flops 26575110144 | bytes 47316992 | tf_op jit(solution)/shard_map/pallas_call | solution.py:72
  591.6 39.6 %shard_map.317 = bf16[2048,2176]{1,0:T(8,128)(2,1)} custom-call(f32[2048,2048]{1,0:T(8,128)} %shard_map.315.refs_0_, bf16[3,2048,1584]{2,1,0:T(8,128)(2,1)} %get-tuple-element.267.refs_1_.refs_3_.s_ref.refs_2_, bf16[3168,2048]{1,0:T(8,128)(2,1)} %all-gather.11.cloned.1.call-done.wg_ref.wu_ref.refs_2_.refs_4_, ...), custom_call_target="tpu_custom_call" | custom-call | flops 26575110144 | bytes 42729472 | tf_op jit(solution)/shard_map/pallas_call | solution.py:141
  647.4 19.5 %shard_map.318.refs_0_ = bf16[4752,2048]{1,0:T(8,128)(2,1)} custom-call(bf16[3,2048,1584]{2,1,0:T(8,128)(2,1)} %get-tuple-element.267.refs_1_.refs_3_.s_ref.refs_2_, bf16[2048,2048]{1,0:T(8,128)(2,1)} %get-tuple-element.258.x_ref), custom_call_target="tpu_custom_call" | custom-call | flops 13287555072 | bytes 21364736 | tf_op jit(solution)/shard_map/pallas_call | solution.py:153
  679.5 19.3 %shard_map.319.refs_0_ = bf16[4752,2048]{1,0:T(8,128)(2,1)} custom-call(bf16[3,2048,1584]{2,1,0:T(8,128)(2,1)} %get-tuple-element.267.refs_1_.refs_3_.s_ref.refs_2_, bf16[2048,2048]{1,0:T(8,128)(2,1)} %get-tuple-element.258.x_ref, bf16[4752,2048]{1,0:T(8,128)(2,1)} %shard_map.318.refs_0_), custom_call_target="tpu_custom_call", output_to_operand_aliasing={{}: (2, {})} | custom-call | flops 13287555072 | bytes 21364736 | tf_op jit(solution)/shard_map/pallas_call | solution.py:153
  712.5 19.1 %shard_map.320 = bf16[4752,2048]{1,0:T(8,128)(2,1)} custom-call(bf16[3,2048,1584]{2,1,0:T(8,128)(2,1)} %get-tuple-element.267.refs_1_.refs_3_.s_ref.refs_2_, bf16[2048,2048]{1,0:T(8,128)(2,1)} %shard_map.308.g_ref.x_ref, bf16[4752,2048]{1,0:T(8,128)(2,1)} %shard_map.319.refs_0_), custom_call_target="tpu_custom_call", output_to_operand_aliasing={{}: (2, {})} | custom-call | flops 13287555072 | bytes 21364736 | tf_op jit(solution)/shard_map/pallas_call | solution.py:153
  750.5 23.9 %shard_map.321 = bf16[4,2048,256]{2,1,0:T(8,128)(2,1)} custom-call(s32[1]{0:T(128)S(6)} %sub.30.core_ref, bf16[3,2048,1584]{2,1,0:T(8,128)(2,1)} %get-tuple-element.264.s_ref.refs_0_.refs_2_, bf16[3168,2048]{1,0:T(8,128)(2,1)} %all-gather.7.cloned.1.call-done.w_ref.refs_1_.refs_3_, bf16[3,2048,1584]{2,1,0:T(8,128)(2,1)} %get-tuple-element.267.refs_1_.refs_3_.s_ref.refs_2_, ...), custom_call_target="tpu_custom_call" | custom-call | flops 13287555072 | bytes 42729472 | tf_op jit(solution)/shard_map/pallas_call | solution.py:141
  776.4 23.5 %shard_map.322 = bf16[4,2048,256]{2,1,0:T(8,128)(2,1)} custom-call(s32[1]{0:T(128)} %bitcast.42.core_ref, bf16[3,2048,1584]{2,1,0:T(8,128)(2,1)} %get-tuple-element.264.s_ref.refs_0_.refs_2_, bf16[3168,2048]{1,0:T(8,128)(2,1)} %all-gather.7.cloned.1.call-done.w_ref.refs_1_.refs_3_, bf16[3,2048,1584]{2,1,0:T(8,128)(2,1)} %get-tuple-element.267.refs_1_.refs_3_.s_ref.refs_2_, ...), custom_call_target="tpu_custom_call" | custom-call | flops 13287555072 | bytes 42729472 | tf_op jit(solution)/shard_map/pallas_call | solution.py:141
  805.1 21.9 %collective-permute-done.50 = bf16[256,2048]{1,0:T(8,128)(2,1)S(1)} collective-permute-done((bf16[256,2048]{1,0:T(8,128)(2,1)}, bf16[256,2048]{1,0:T(8,128)(2,1)S(1)}, u32[]{:S(2)}, u32[]{:S(2)}) %collective-permute-start.50) | collective-permute-done | bytes 1048608 | tf_op jit(solution)/shard_map/ppermute | solution.py:423
  879.1 18.1 %shard_map.324 = (bf16[2048,384]{1,0:T(8,128)(2,1)}, bf16[2048,512]{1,0:T(8,128)(2,1)}, f32[2048,128]{1,0:T(8,128)}, f32[2048,1]{1,0:T(8,128)}) custom-call(bf16[2048,384]{1,0:T(8,128)(2,1)} %get-tuple-element.301.q_ref, bf16[2048,128]{1,0:T(8,128)(2,1)} %get-tuple-element.302.kr_ref, bf16[2048,512]{1,0:T(8,128)(2,1)} %get-tuple-element.303.kv_ref, ...), custom_call_target="tpu_custom_call" | custom-call | flops 5872025600 | bytes 12288000 | tf_op jit(solution)/shard_map/pallas_call | solution.py:389
  1086.8 17.7 %collective-permute-done.81 = bf16[2048,256]{1,0:T(8,128)(2,1)S(1)} collective-permute-done((bf16[2048,256]{1,0:T(8,128)(2,1)S(1)}, bf16[2048,256]{1,0:T(8,128)(2,1)S(1)}, u32[]{:S(2)}, u32[]{:S(2)}) %collective-permute-start.81) | collective-permute-done | bytes 1048608 | tf_op jit(solution)/shard_map/ppermute | solution.py:423
  (479 shorter events, 553.2 us)
Async XLA Ops:
  7.2 113.5 %all-gather.5.cloned.1.call-start = ((), (), s32[]{:S(2)}) async-start(), calls=%async_computation.4 | async-start | bytes 7372800 | tf_op jit(solution)/shard_map/all_gather | solution.py:507
  16.5 268.9 %all-gather.7.cloned.1.call-start = ((), (), s32[]{:S(2)}) async-start(), calls=%async_computation.5 | async-start | bytes 16220160 | tf_op jit(solution)/shard_map/all_gather | solution.py:507
  49.3 360.1 %all-gather.9.cloned.1.call-start = ((), (), s32[]{:S(2)}) async-start(), calls=%async_computation.6 | async-start | bytes 16220160 | tf_op jit(solution)/shard_map/all_gather | solution.py:507
  78.7 468.4 %all-gather.11.cloned.1.call-start = ((), (), s32[]{:S(2)}) async-start(), calls=%async_computation.8 | async-start | bytes 16220160 | tf_op jit(solution)/shard_map/all_gather | solution.py:507
  78.7 36.2 %collective-permute-start = (bf16[2048,256]{1,0:T(8,128)(2,1)}, bf16[2048,256]{1,0:T(8,128)(2,1)}, u32[]{:S(2)}, u32[]{:S(2)}) collective-permute-start(bf16[2048,256]{1,0:T(8,128)(2,1)} %refs_0_), channel_id=1, source_target_pairs={{0,1},{1,0},{2,3},{3,2},{4,5},{5,4},{6,7},{7,6},{8,9},{9,8},{10,11... | collective-permute-start | bytes 3145736 | tf_op jit(solution)/shard_map/ppermute | solution.py:414
  117.0 31.8 %collective-permute-start.10 = (bf16[2048,256]{1,0:T(8,128)(2,1)}, bf16[2048,256]{1,0:T(8,128)(2,1)}, u32[]{:S(2)}, u32[]{:S(2)}) collective-permute-start(bf16[2048,256]{1,0:T(8,128)(2,1)} %refs_0_.1), channel_id=1, source_target_pairs={{0,2},{1,3},{2,4},{3,5},{4,6},{5,7},{8,10},{9,11},{10,12},{11,13},... | collective-permute-start | bytes 3145736 | tf_op jit(solution)/shard_map/ppermute | solution.py:423
  119.4 29.4 %collective-permute-start.11 = (bf16[2048,256]{1,0:T(8,128)(2,1)}, bf16[2048,256]{1,0:T(8,128)(2,1)}, u32[]{:S(2)}, u32[]{:S(2)}) collective-permute-start(bf16[2048,256]{1,0:T(8,128)(2,1)} %refs_0_.1), channel_id=1, source_target_pairs={{2,0},{3,1},{4,2},{5,3},{6,4},{7,5},{10,8},{11,9},{12,10},{13,11},... | collective-permute-start | bytes 3145736 | tf_op jit(solution)/shard_map/ppermute | solution.py:423
  150.4 28.6 %collective-permute-start.13 = (bf16[2048,256]{1,0:T(8,128)(2,1)}, bf16[2048,256]{1,0:T(8,128)(2,1)}, u32[]{:S(2)}, u32[]{:S(2)}) collective-permute-start(bf16[2048,256]{1,0:T(8,128)(2,1)} %collective-permute-done.11), channel_id=1, source_target_pairs={{2,0},{3,1},{4,2},{5,3},{10,8},{11,9},{12,10},{13,11},{18,16},{19,... | collective-permute-start | bytes 3145736 | tf_op jit(solution)/shard_map/ppermute | solution.py:423
  181.6 559.0 %reduce-scatter.5.cloned.1.call-start = ((), (), s32[]{:S(2)}) async-start(), calls=%async_computation.7 | async-start | bytes 24330240 | tf_op jit(solution)/shard_map/reduce_scatter | solution.py:511
  182.8 37.6 %collective-permute-start.19 = (bf16[2048,256]{1,0:T(8,128)(2,1)S(1)}, bf16[2048,256]{1,0:T(8,128)(2,1)S(1)}, u32[]{:S(2)}, u32[]{:S(2)}) collective-permute-start(bf16[2048,256]{1,0:T(8,128)(2,1)S(1)} %copy-done.43), channel_id=1, source_target_pairs={{0,1},{1,0},{2,3},{3,2},{4,5},{5,4},{6,7},{7,6},{8,9},{9,8},{10,11... | collective-permute-start | bytes 3145736 | tf_op jit(solution)/shard_map/ppermute | solution.py:414
  186.2 37.1 %collective-permute-start.21 = (bf16[2048,256]{1,0:T(8,128)(2,1)S(1)}, bf16[2048,256]{1,0:T(8,128)(2,1)}, u32[]{:S(2)}, u32[]{:S(2)}) collective-permute-start(bf16[2048,256]{1,0:T(8,128)(2,1)S(1)} %broadcast_select_fusion.8.refs_4_), channel_id=1, source_target_pairs={{0,1},{1,0},{2,3},{3,2},{4,5},{5,4},{6,7},{7,6},{8,9},{9,8},{10,11... | collective-permute-start | bytes 3145736 | tf_op jit(solution)/shard_map/ppermute | solution.py:414
  276.3 30.3 %collective-permute-start.25 = (bf16[256,2048]{1,0:T(8,128)(2,1)}, bf16[256,2048]{1,0:T(8,128)(2,1)S(1)}, u32[]{:S(2)}, u32[]{:S(2)}) collective-permute-start(bf16[256,2048]{1,0:T(8,128)(2,1)} %get-tuple-element.467), channel_id=1, source_target_pairs={{0,2},{1,3},{2,4},{3,5},{4,6},{5,7},{8,10},{9,11},{10,12},{11,13},... | collective-permute-start | bytes 3145736 | tf_op jit(solution)/shard_map/ppermute | solution.py:423
  367.4 30.0 %collective-permute-start.27 = (bf16[256,2048]{1,0:T(8,128)(2,1)S(1)}, bf16[256,2048]{1,0:T(8,128)(2,1)}, u32[]{:S(2)}, u32[]{:S(2)}) collective-permute-start(bf16[256,2048]{1,0:T(8,128)(2,1)S(1)} %get-tuple-element.435.refs_0_), channel_id=1, source_target_pairs={{0,1},{1,0},{2,3},{3,2},{4,5},{5,4},{6,7},{7,6},{8,9},{9,8},{10,11... | collective-permute-start | bytes 3145736 | tf_op jit(solution)/shard_map/ppermute | solution.py:414
  368.9 28.6 %collective-permute-start.35 = (bf16[256,2048]{1,0:T(8,128)(2,1)S(1)}, bf16[256,2048]{1,0:T(8,128)(2,1)}, u32[]{:S(2)}, u32[]{:S(2)}) collective-permute-start(bf16[256,2048]{1,0:T(8,128)(2,1)S(1)} %broadcast_select_fusion.3.refs_4_), channel_id=1, source_target_pairs={{0,1},{1,0},{2,3},{3,2},{4,5},{5,4},{6,7},{7,6},{8,9},{9,8},{10,11... | collective-permute-start | bytes 3145736 | tf_op jit(solution)/shard_map/ppermute | solution.py:414
  508.0 517.2 %reduce-scatter.7.cloned.1.call-start = ((), (), s32[]{:S(2)}) async-start(), calls=%async_computation.9 | async-start | bytes 24330240 | tf_op jit(solution)/shard_map/reduce_scatter | solution.py:511
  673.5 28.3 %collective-permute-start.40 = (bf16[256,2176]{1,0:T(8,128)(2,1)}, bf16[256,2176]{1,0:T(8,128)(2,1)S(1)}, u32[]{:S(2)}, u32[]{:S(2)}) collective-permute-start(bf16[256,2176]{1,0:T(8,128)(2,1)} %get-tuple-element.451), channel_id=1, source_target_pairs={{0,2},{1,3},{2,4},{3,5},{8,10},{9,11},{10,12},{11,13},{16,18},{17,... | collective-permute-start | bytes 3342344 | tf_op jit(solution)/shard_map/ppermute | solution.py:423
  705.9 28.4 %collective-permute-start.42 = (bf16[256,2176]{1,0:T(8,128)(2,1)}, bf16[256,2176]{1,0:T(8,128)(2,1)S(1)}, u32[]{:S(2)}, u32[]{:S(2)}) collective-permute-start(bf16[256,2176]{1,0:T(8,128)(2,1)} %get-tuple-element.449), channel_id=1, source_target_pairs={{0,2},{1,3},{2,4},{3,5},{4,6},{5,7},{8,10},{9,11},{10,12},{11,13},... | collective-permute-start | bytes 3342344 | tf_op jit(solution)/shard_map/ppermute | solution.py:423
  740.6 329.3 %reduce-scatter.11.cloned.1.call-start = ((), (), s32[]{:S(2)}) async-start(), calls=%async_computation.11 | async-start | bytes 3932160 | tf_op jit(solution)/shard_map/reduce_scatter | solution.py:511
  868.9 28.3 %collective-permute-start.57 = (bf16[2048,256]{1,0:T(8,128)(2,1)}, bf16[2048,256]{1,0:T(8,128)(2,1)S(1)}, u32[]{:S(2)}, u32[]{:S(2)}) collective-permute-start(bf16[2048,256]{1,0:T(8,128)(2,1)} %get-tuple-element.463), channel_id=1, source_target_pairs={{0,2},{1,3},{2,4},{3,5},{8,10},{9,11},{10,12},{11,13},{16,18},{17,... | collective-permute-start | bytes 3145736 | tf_op jit(solution)/shard_map/ppermute | solution.py:423
  900.5 30.9 %collective-permute-start.59 = (bf16[2048,256]{1,0:T(8,128)(2,1)}, bf16[2048,256]{1,0:T(8,128)(2,1)}, u32[]{:S(2)}, u32[]{:S(2)}) collective-permute-start(bf16[2048,256]{1,0:T(8,128)(2,1)} %get-tuple-element.461), channel_id=1, source_target_pairs={{0,2},{1,3},{2,4},{3,5},{4,6},{5,7},{8,10},{9,11},{10,12},{11,13},... | collective-permute-start | bytes 3145736 | tf_op jit(solution)/shard_map/ppermute | solution.py:423
  977.1 48.2 %collective-permute-start.78 = (bf16[4,2048,256]{2,1,0:T(8,128)(2,1)}, bf16[4,2048,256]{2,1,0:T(8,128)(2,1)}, u32[]{:S(2)}, u32[]{:S(2)}) collective-permute-start(bf16[4,2048,256]{2,1,0:T(8,128)(2,1)} %shard_map.325), channel_id=1, source_target_pairs={{0,1},{1,0},{2,3},{3,2},{4,5},{5,4},{6,7},{7,6},{8,9},{9,8},{10,11... | collective-permute-start | bytes 12582920 | tf_op jit(solution)/shard_map/ppermute | solution.py:414
  981.7 158.6 %reduce-scatter.9.cloned.1.call-start = ((), (), s32[]{:S(2)}) async-start(), calls=%async_computation.10 | async-start | bytes 3440640 | tf_op jit(solution)/shard_map/reduce_scatter | solution.py:511
  1033.6 32.7 %collective-permute-start.79 = (bf16[2048,256]{1,0:T(8,128)(2,1)}, bf16[2048,256]{1,0:T(8,128)(2,1)}, u32[]{:S(2)}, u32[]{:S(2)}) collective-permute-start(bf16[2048,256]{1,0:T(8,128)(2,1)} %get-tuple-element.459), channel_id=1, source_target_pairs={{0,2},{1,3},{8,10},{9,11},{16,18},{17,19},{24,26},{25,27}} | collective-permute-start | bytes 3145736 | tf_op jit(solution)/shard_map/ppermute | solution.py:423
  1036.0 30.3 %collective-permute-start.80 = (bf16[2048,256]{1,0:T(8,128)(2,1)}, bf16[2048,256]{1,0:T(8,128)(2,1)}, u32[]{:S(2)}, u32[]{:S(2)}) collective-permute-start(bf16[2048,256]{1,0:T(8,128)(2,1)} %get-tuple-element.458), channel_id=1, source_target_pairs={{6,4},{7,5},{14,12},{15,13},{22,20},{23,21},{30,28},{31,29}} | collective-permute-start | bytes 3145736 | tf_op jit(solution)/shard_map/ppermute | solution.py:423
  (143 other events, 2040.4 us)
Sparse Core Ops, SparseCore 0:
  16.6 69.4 all-gather.4
  88.5 125.6 all-gather.6
  216.6 125.6 all-gather.8
  344.0 125.6 all-gather.10
  508.2 174.3 reduce-scatter.4
  740.8 173.9 reduce-scatter.6
  981.8 43.3 reduce-scatter.10
  1066.5 38.2 reduce-scatter.8

commit v3 on v2

--- a/solution.py
+++ b/solution.py
@@ -43,18 +43,18 @@
 def once(shape, index):
     return pl.BlockSpec(shape, index, pipeline_mode=pl.Buffered(1))
 
-def place_matrix(fe, first, count, n):
-    col=lax.broadcasted_iota(jnp.int32,(E,n),1); row=(lax.broadcasted_iota(jnp.int32,(E,n),0)-first)*fe
-    return jnp.where((col>=row)&(col<row+fe)&(row<count*fe),1.0,0.0).astype(BF)
-
-def units_kernel(fe, first, count, x_ref, wg_ref, wu_ref, b_ref, w_ref, out_ref, pair_ref):
+def place_matrix(fe, first, n):
+    col=lax.broadcasted_iota(jnp.int32,(E,n),1)+first; row=lax.broadcasted_iota(jnp.int32,(E,n),0)*fe
+    return jnp.where((col>=row)&(col<row+fe),1.0,0.0).astype(BF)
+
+def units_kernel(fe, first, x_ref, wg_ref, wu_ref, b_ref, w_ref, out_ref, pair_ref):
     x=x_ref[...]; n=wg_ref.shape[0]
     pre=mm(x,wg_ref[...],NT); lift=mm(x,wu_ref[...],NT); back=b_ref[...].astype(F32)
     w=w_ref[...]; hi=w.astype(BF); lo=(w-hi.astype(F32)).astype(BF)
-    place=place_matrix(fe,first,count,n)
+    place=place_matrix(fe,first,n)
     spread=mm(jnp.concatenate([hi,lo],axis=1),jnp.concatenate([place,place],axis=0),NN)
-    if count*fe<n:
-        spread=jnp.where(lax.broadcasted_iota(jnp.int32,spread.shape,1)>=count*fe,1.0,spread)
+    if first+n>E*fe:
+        spread=jnp.where(lax.broadcasted_iota(jnp.int32,spread.shape,1)>=E*fe-first,1.0,spread)
     s=0.5+0.5*jnp.tanh(0.5*pre)
     silu=pre*s
     act=silu*lift
@@ -64,12 +64,12 @@
     out_ref[1]=(back*silu).astype(BF)
     out_ref[2]=(act*spread).astype(BF)
 
-def units(x,packed,back,weight,fe,first,count,bt):
+def units(x,packed,back,weight,fe,first,bt):
     T,D=x.shape; n=back.shape[1]; r=weight.shape[1]
     ins=[pl.BlockSpec((bt,D),lambda i:(i,0))]+[once((n,D),lambda i,k=k:(k,0)) for k in range(2)]
     ins+=[pl.BlockSpec((bt,n),lambda i:(i,0)),pl.BlockSpec((bt,r),lambda i:(i,0))]
     outs=[jax.ShapeDtypeStruct((3,T,n),BF),jax.ShapeDtypeStruct((T,r),F32)]
-    return pl.pallas_call(functools.partial(units_kernel,fe,first,count),grid=(T//bt,),in_specs=ins,
+    return pl.pallas_call(functools.partial(units_kernel,fe,first),grid=(T//bt,),in_specs=ins,
         out_specs=[pl.BlockSpec((3,bt,n),lambda i:(0,i,0)),pl.BlockSpec((bt,r),lambda i:(i,0))],out_shape=outs,
         compiler_params=params(1),
         cost_estimate=pl.CostEstimate(flops=4*T*D*n,bytes_accessed=2*(T*D+2*n*D+4*T*n),transcendentals=T*n))(x,packed,packed,back,weight)
@@ -422,19 +422,6 @@
         ]
         return lax.ppermute(a, "tensor", pairs)
 
-    def chip_gather(self, s, jobs=None):
-        n = self.chips
-        left, right = [s], [s]
-        for k in range(1, n):
-            pair = (
-                self.shift(left[-1], 1, range(k - 1, n)),
-                self.shift(right[-1], -1, range(0, n - k + 1)),
-            )
-            pair = beside(pair, jobs)
-            left.append(pair[0])
-            right.append(pair[1])
-        return [s] + [jnp.where(self.z >= k, left[k], right[n - k]) for k in range(1, n)]
-
     def pieces(self, own, order):
         n = self.chips
         out, at = [], []
@@ -444,63 +431,84 @@
             at += [order(chip, self.c), order(chip, 1 - self.c)]
         return out, jnp.stack(at).astype(jnp.int32)
 
-    def row_pieces(self, s, jobs=None):
-        return self.pieces(self.chip_gather(s, jobs), lambda chip, core: core * self.chips + chip)
+    def row_pieces(self, own):
+        return self.pieces(own, lambda chip, core: core * self.chips + chip)
 
     def column_pieces(self, own):
         return self.pieces(own, lambda chip, core: chip * 2 + core)
 
-    def chip_scatter(self, block, jobs=None):
-        n = self.chips
-        left = right = None
-        for s in range(1, n):
-            up = block(jnp.clip(n - s + self.z, 0, n - 1))
-            down = block(jnp.clip(self.z - (n - s), 0, n - 1))
-            if left is not None:
-                up = (up.astype(F32) + left.astype(F32)).astype(BF)
-                down = (down.astype(F32) + right.astype(F32)).astype(BF)
-            left = self.shift(up, 1, range(0, s))
-            right = self.shift(down, -1, range(n - s, n))
-            left, right = beside((left, right), jobs)
-        return block(self.z).astype(F32) + left.astype(F32) + right.astype(F32)
-
-    def row_pair(self, p):
+    def halves(self, p):
         half = p.shape[0] // 2
-        mine = lax.dynamic_slice_in_dim(p, self.c * half, half, 0)
-        theirs = lax.dynamic_slice_in_dim(p, (1 - self.c) * half, half, 0)
-        return (mine.astype(F32) + self.swap(theirs).astype(F32)).astype(BF)
-
-    def row_scatter(self, both, jobs=None):
+        return [lax.dynamic_slice_in_dim(p, c * half, half, 0) for c in (self.c, 1 - self.c)]
+
+    def row_scatter(self, both):
         ch = both.shape[0] // self.chips
-        return self.chip_scatter(lambda j: lax.dynamic_slice_in_dim(both, j * ch, ch, 0), jobs)
+        return Scatter(self, lambda j: lax.dynamic_slice_in_dim(both, j * ch, ch, 0))
+
+    def column_scatter(self, both):
+        return Scatter(self, lambda j: lax.dynamic_index_in_dim(both, j, 0, False))
 
     def row_start(self, rows):
         ch = rows // self.n
         return (self.c * self.chips + self.z) * ch, ch
 
-    def column_scatter(self, mine, arrived, jobs=None):
-        both = (mine.astype(F32) + arrived.astype(F32)).astype(BF)
-        return self.chip_scatter(lambda j: lax.dynamic_index_in_dim(both, j, 0, False), jobs)
-
-
-class Jobs:
-    def __init__(self, *steps):
-        self.steps = list(steps)
-        self.made = {}
-
-    def rest(self):
-        while self.steps:
-            self.made.update(self.steps.pop(0)(self.made))
-        return self.made
-
-
-def beside(arrived, jobs):
-    if jobs is None or not jobs.steps:
-        return lax.optimization_barrier(arrived)
-    step = jobs.steps.pop(0)(jobs.made)
-    arrived, step = lax.optimization_barrier((arrived, step))
-    jobs.made.update(step)
-    return arrived
+
+def total(mine, arrived):
+    return (mine.astype(F32) + arrived.astype(F32)).astype(BF)
+
+
+class Gather:
+    def __init__(self, line, block):
+        self.line, self.left, self.right = line, [block], [block]
+
+    def start(self):
+        n, k = self.line.chips, len(self.left)
+        return (
+            self.line.shift(self.left[-1], 1, range(k - 1, n)),
+            self.line.shift(self.right[-1], -1, range(0, n - k + 1)),
+        )
+
+    def take(self, arrived):
+        self.left.append(arrived[0])
+        self.right.append(arrived[1])
+
+    def result(self):
+        n, z = self.line.chips, self.line.z
+        return self.left[:1] + [jnp.where(z >= k, self.left[k], self.right[n - k]) for k in range(1, n)]
+
+
+class Scatter:
+    def __init__(self, line, block):
+        self.line, self.block, self.step, self.left, self.right = line, block, 0, None, None
+
+    def start(self):
+        self.step += 1
+        n, s, z = self.line.chips, self.step, self.line.z
+        up = self.block(jnp.clip(n - s + z, 0, n - 1))
+        down = self.block(jnp.clip(z - (n - s), 0, n - 1))
+        if self.left is not None:
+            up, down = total(up, self.left), total(down, self.right)
+        return self.line.shift(up, 1, range(0, s)), self.line.shift(down, -1, range(n - s, n))
+
+    def take(self, arrived):
+        self.left, self.right = arrived
+
+    def result(self):
+        return self.block(self.line.z).astype(F32) + self.left.astype(F32) + self.right.astype(F32)
+
+
+def beside(moves, job=None):
+    arrived, done = lax.optimization_barrier(([m.start() for m in moves], job() if job else None))
+    for move, a in zip(moves, arrived):
+        move.take(a)
+    return done
+
+
+def steps(move, count, jobs=()):
+    made = []
+    for k in range(count):
+        made.append(beside([move], jobs[k] if k < len(jobs) else None))
+    return made
 
 
 def gather_rows(packed):
@@ -574,82 +582,83 @@
     latent_g = gains[2].reshape(n_dp, wide)[:, : R // n_dp].reshape(R).astype(F32)
     cosine, sine = (jnp.asarray(table) for table in tables())
 
-    shared = shared_down.shape[0]
-    units_here = (E * fe + shared) // 2
-    cut = units_here // fe
-    assert cut * fe == units_here
+    n_units = E * fe + shared_down.shape[0]
+    n0 = n_units // 2 // 256 * 256
+    n1 = n_units - n0
+    last_step = line.chips - 1
     gate = expert_gate.transpose(0, 2, 1).reshape(E * fe, wide)
     up = expert_up.transpose(0, 2, 1).reshape(E * fe, wide)
-    jobs = Jobs(
-        lambda made: {"down": jnp.concatenate([expert_down.reshape(E * fe, wide), shared_down], axis=0)},
-        lambda made: {"early": jnp.concatenate([gate[:units_here], up[:units_here]], axis=0)},
-        lambda made: {"late": jnp.concatenate(
-            [gate[units_here:], shared_gate.T, up[units_here:], shared_up.T], axis=0)},
-    )
-    input_own = line.chip_gather(layer_input, jobs)
-    packs = jobs.rest()
-    downs, early, late = gather_rows(packs["down"]), gather_rows(packs["early"]), gather_rows(packs["late"])
+    move = Gather(line, layer_input)
+    downs, early, late = steps(move, 3, (
+        lambda: jnp.concatenate([expert_down.reshape(E * fe, wide), shared_down], axis=0),
+        lambda: jnp.concatenate([gate[:n0], up[:n0]], axis=0),
+        lambda: jnp.concatenate([gate[n0:], shared_gate.T, up[n0:], shared_up.T], axis=0),
+    ))
+    steps(move, last_step - 3)
+    downs, early, late = gather_rows(downs), gather_rows(early), gather_rows(late)
+    down0, down1 = downs[:n0], downs[n0:]
 
     tile = 256
     core = line.c.reshape(1).astype(jnp.int32)
-    input_pieces, input_at = line.column_pieces(input_own)
+    input_pieces, input_at = line.column_pieces(move.result())
     input_pieces, cotangent = lax.optimization_barrier((input_pieces, cotangent))
-
-    def project(made):
+    grad_move = Gather(line, cotangent)
+
+    def project():
         rows, first_round, r1 = place_columns(input_pieces, input_at, first_g)
-        return {"rows": rows, "first": first_round, "r1": r1, "proj": dot(first_round, wproj, 1, 1)}
-
-    def attention(made):
-        kept = attend(made["proj"], wup, latent_g[None], cosine, sine, heads_here)
-        return {"attend": kept, "terms": dot(kept[4], wo, 1, 0, BF)}
-
-    jobs = Jobs(project, attention, lambda made: {"both": line.row_pair(made["terms"])})
-    grad_own = line.chip_gather(cotangent, jobs)
-    made = jobs.rest()
-    rows, first_round, r1, proj = made["rows"], made["first"], made["r1"], made["proj"]
-    q, kr, kv, latent, mixed, log_total = made["attend"]
-    jobs = Jobs(
-        lambda made: {"grad": place_columns(*line.column_pieces(grad_own))[0]},
-        lambda made: {},
-        lambda made: {"back0": lift_back(made["grad"], downs, 0, units_here, tile)},
-        lambda made: {"back1": lift_back(made["grad"], downs, 1, units_here, tile)},
-    )
-    attend_rows = line.row_scatter(made["both"], jobs)
+        return rows, first_round, r1, dot(first_round, wproj, 1, 1)
+
+    rows, first_round, r1, proj = beside([grad_move], project)
+    q, kr, kv, latent, mixed, log_total = attend(proj, wup, latent_g[None], cosine, sine, heads_here)
+    mine, theirs = line.halves(mixed)
+    arrived = line.swap(dot(theirs, wo, 1, 0, BF))
+    move = line.row_scatter(total(dot(mine, wo, 1, 0, BF), arrived))
+    for _ in range(last_step - 1):
+        beside([move, grad_move])
+    (grad,) = beside([move], lambda: place_columns(*line.column_pieces(grad_move.result())))
     hidden_rows = (
-        lax.dynamic_slice_in_dim(rows, row_start, row_count, 0).astype(F32) + attend_rows
+        lax.dynamic_slice_in_dim(rows, row_start, row_count, 0).astype(F32) + move.result()
     ).astype(BF)
-    hidden_pieces, hidden_at = line.row_pieces(hidden_rows, jobs)
-    made = jobs.rest()
-    grad, back0, back1 = made["grad"], made["back0"], made["back1"]
+    move = Gather(line, hidden_rows)
+    back0, back1 = steps(move, 2, (
+        lambda: lift_back(grad, down0, 0, n0, tile),
+        lambda: lift_back(grad, down1, 0, n1, tile),
+    ))
+    steps(move, last_step - 2)
+    hidden_pieces, hidden_at = line.row_pieces(move.result())
     named = jnp.any(routes[:, :, None] == jnp.arange(E, dtype=jnp.int32)[None, None, :], axis=1)
     kept = jnp.where(named & (ranks(named) < CAP), 1.0, 0.0)
     second_round, hidden_columns, gating, weight = norm_rows(
         hidden_pieces, hidden_at, line.index.reshape(1).astype(jnp.int32), my_columns, second_g, wr, kept
     )
 
-    stack0, pair0 = units(second_round, early, back0, weight, fe, 0, cut, tile)
-    deltas = outer(stack0, 0, 2, second_round, 3 * units_here, 0)
-    deltas = outer(stack0, 2, 1, grad, 3 * units_here, 2, deltas)
+    stack0, pair0 = units(second_round, early, back0, weight, fe, 0, tile)
+    deltas = outer(stack0, 0, 2, second_round, 3 * n0, 0)
+    deltas = outer(stack0, 2, 1, grad, 3 * n0, 2, deltas)
     deltas, stack0 = lax.optimization_barrier((deltas, stack0))
     early_sums = scatter_rows(deltas)
-    second_terms = back([(stack0, 0, early, units_here, 0), (stack0, 1, early, units_here, 1)], None, F32, tile)
-    stack1, pair1 = units(second_round, late, back1, weight, fe, cut, E - cut, tile)
+    second_terms = back([(stack0, 0, early, n0, 0), (stack0, 1, early, n0, 1)], None, F32, tile)
+    stack1, pair1 = units(second_round, late, back1, weight, fe, n0, tile)
     second_terms = back(
-        [(stack1, 0, late, units_here, 0), (stack1, 1, late, units_here, 1)],
-        second_terms, BF, tile, (pair0, pair1),
-    )
-
-    branch_terms = [(stack0, 2, downs, units_here, 0), (stack1, 2, downs, units_here, 1)]
-    jobs = Jobs(
-        lambda made: {"deltas": outer(stack1, 0, 1, second_round, 3 * units_here, 0)},
-        lambda made: {"deltas": outer(stack1, 1, 1, second_round, 3 * units_here, 1, made["deltas"])},
-        lambda made: {"deltas": outer(stack1, 2, 1, grad, 3 * units_here, 2, made["deltas"])},
-        lambda made: {"theirs": back(branch_terms, None, BF, tile, (), 1 - core, line.chips)},
-        lambda made: {"mine": back(branch_terms, None, BF, tile, (), core, line.chips)},
-    )
-    summed = line.row_scatter(line.row_pair(second_terms), jobs)
-    early_sums, summed, jobs.made = lax.optimization_barrier((early_sums, summed, jobs.made))
-    late_sums = scatter_rows(jobs.made["deltas"])
+        [(stack1, 0, late, n1, 0), (stack1, 1, late, n1, 1)], second_terms, BF, tile, (pair0, pair1)
+    )
+
+    branch_terms = [(stack0, 2, down0, n0, 0), (stack1, 2, down1, n1, 0)]
+    mine, theirs = line.halves(second_terms)
+    arrived, branch_theirs = lax.optimization_barrier(
+        (line.swap(theirs), back(branch_terms, None, BF, tile, (), 1 - core, line.chips))
+    )
+    move = line.row_scatter(total(mine, arrived))
+    deltas = beside([move], lambda: outer(stack1, 0, 1, second_round, 3 * n1, 0))
+    deltas = beside([move], lambda: outer(stack1, 1, 1, second_round, 3 * n1, 1, deltas))
+    branch_arrived = line.swap(branch_theirs)
+    deltas, branch_arrived = beside(
+        [move], lambda: (outer(stack1, 2, 1, grad, 3 * n1, 2, deltas), branch_arrived)
+    )
+    steps(move, last_step - 3)
+    summed = move.result()
+    early_sums, summed, deltas = lax.optimization_barrier((early_sums, summed, deltas))
+    late_sums = scatter_rows(deltas)
 
     def own_rows(a):
         return lax.dynamic_slice_in_dim(a, row_start, row_count, 0)
@@ -657,78 +666,77 @@
     gating_rows, kept_rows, x2 = own_rows(gating), own_rows(kept), own_rows(second_round)
     u = summed[:, D : D + E] * kept_rows
     logits_delta = gating_rows * (u - jnp.sum(gating_rows * u, axis=-1, keepdims=True))
-    router_delta = dot(x2, logits_delta.astype(BF), 0, 0)
     d2 = summed[:, :D] + dot(logits_delta.astype(BF), wr, 1, 0)
     v2 = hidden_rows.astype(F32)
     r2 = lax.rsqrt(jnp.mean(v2 * v2, axis=-1, keepdims=True) + EPSILON)
     vgd = jnp.mean(v2 * second_g * d2, axis=-1, keepdims=True)
-    second_gain_delta = jnp.sum(d2 * v2 * r2, axis=0)
     hidden_delta = own_rows(grad).astype(F32) + r2 * second_g * d2 - v2 * (r2**3) * vgd
-    delta_pieces, delta_at = line.row_pieces(hidden_delta.astype(BF), jobs)
-    made = jobs.rest()
-    delta_pieces, theirs, mine = lax.optimization_barrier((delta_pieces, made["theirs"], made["mine"]))
-
-    def into_heads(made):
+    move = Gather(line, hidden_delta.astype(BF))
+    branch_mine = beside([move], lambda: back(branch_terms, None, BF, tile, (), core, line.chips))
+    branch_move = line.column_scatter(total(branch_mine, branch_arrived))
+    router_delta, second_gain_delta = beside([move, branch_move], lambda: (
+        dot(x2, logits_delta.astype(BF), 0, 0), jnp.sum(d2 * v2 * r2, axis=0)
+    ))
+    for _ in range(last_step - 2):
+        beside([move, branch_move])
+    delta_pieces, delta_at = line.row_pieces(move.result())
+
+    def heads_back():
         placed = place_rows(delta_pieces, delta_at)
-        return {"hidden": placed, "mixed": dot(placed, wo, 1, 1, BF)}
-
-    def heads_back(made):
-        return {"heads": attend_back(q, kr, kv, mixed, log_total, made["mixed"], cosine, sine, heads_here)}
-
-    def small_terms(made):
-        delta_queries, delta_pairs, delta_kr, query_dot = made["heads"]
-        delta_wq = dot(delta_queries, first_round, 0, 0)
-        query_gain = jnp.sum(wproj[:queries_wide].astype(F32) * delta_wq, axis=0)
-        per_entry = jnp.concatenate([second_gain_delta[:, None], query_gain[:, None], router_delta], axis=1)
-        if number > D:
-            per_entry = jnp.concatenate([per_entry, jnp.zeros((number - D, E + 2), F32)], axis=0)
-        small = jnp.concatenate(
-            [dot(delta_pairs, wup, 1, 1),
-             delta_kr[:, :half] + delta_kr[:, half:DR], delta_kr[:, DR : DR + half] + delta_kr[:, DR + half :],
-             query_dot, per_entry, jnp.zeros((number, 63 - 2 - E), F32)], axis=1,
-        ).astype(BF)
-        return {"small": small, "wq": delta_wq.astype(BF)}
-
-    jobs = Jobs(into_heads, heads_back, small_terms)
-    branch = line.column_scatter(mine, line.swap(theirs), jobs)
-    made = jobs.rest()
-    layer_output = (hidden_columns.astype(F32) + branch).astype(BF)
-    hidden_delta, (delta_queries, delta_pairs) = made["hidden"], made["heads"][:2]
+        delta_mixed = dot(placed, wo, 1, 1, BF)
+        return placed, attend_back(q, kr, kv, mixed, log_total, delta_mixed, cosine, sine, heads_here)
+
+    hidden_delta, heads = beside([branch_move], heads_back)
+    layer_output = (hidden_columns.astype(F32) + branch_move.result()).astype(BF)
+    delta_queries, delta_pairs, delta_kr, query_dot = heads
+    delta_wq = dot(delta_queries, first_round, 0, 0)
+    query_gain = jnp.sum(wproj[:queries_wide].astype(F32) * delta_wq, axis=0)
+    per_entry = jnp.concatenate([second_gain_delta[:, None], query_gain[:, None], router_delta], axis=1)
+    if number > D:
+        per_entry = jnp.concatenate([per_entry, jnp.zeros((number - D, E + 2), F32)], axis=0)
+    small = jnp.concatenate(
+        [dot(delta_pairs, wup, 1, 1),
+         delta_kr[:, :half] + delta_kr[:, half:DR], delta_kr[:, DR : DR + half] + delta_kr[:, DR + half :],
+         query_dot, per_entry, jnp.zeros((number, 63 - 2 - E), F32)], axis=1,
+    ).astype(BF)
     first_terms = [(delta_queries, 0, attend_packed, queries_wide, 0)]
-
-    def attend_deltas(made):
+    mine, theirs = line.halves(small)
+    move = line.row_scatter(total(mine, line.swap(theirs)))
+
+    def attend_deltas():
         delta_wup = dot(latent, delta_pairs, 0, 0, BF)
-        return {"deltas": jnp.concatenate(
-            [made["wq"], delta_wup.reshape(n_dp, up_rows, wide).transpose(1, 0, 2).reshape(up_rows, D),
-             dot(mixed, hidden_delta, 0, 0, BF)], axis=0)}
-
-    jobs = Jobs(
-        lambda made: {"theirs": back(first_terms, None, BF, tile, (), 1 - core, line.chips)},
-        lambda made: {"mine": back(first_terms, None, BF, tile, (), core, line.chips)},
+        return jnp.concatenate(
+            [delta_wq.astype(BF),
+             delta_wup.reshape(n_dp, up_rows, wide).transpose(1, 0, 2).reshape(up_rows, D),
+             dot(mixed, hidden_delta, 0, 0, BF)], axis=0)
+
+    theirs, mine, deltas = steps(move, 3, (
+        lambda: back(first_terms, None, BF, tile, (), 1 - core, line.chips),
+        lambda: back(first_terms, None, BF, tile, (), core, line.chips),
         attend_deltas,
-    )
-    jobs.made["wq"] = made["wq"]
-    small = line.row_scatter(line.row_pair(made["small"]), jobs).astype(BF)
-    made = jobs.rest()
-    deltas, small = lax.optimization_barrier((made["deltas"], small))
+    ))
+    steps(move, last_step - 3)
+    small = move.result().astype(BF)
+    deltas, small, layer_output = lax.optimization_barrier((deltas, small, layer_output))
     attend_sums = scatter_rows(deltas).astype(F32)
-    small_pieces, small_at = line.row_pieces(small)
-    small_pieces, arrived, late_sums = lax.optimization_barrier(
-        (small_pieces, line.swap(made["theirs"]), late_sums)
-    )
+    move = Gather(line, small)
+    first_move = line.column_scatter(total(mine, line.swap(theirs)))
+    steps(move, last_step - 1)
+    beside([move, first_move])
+    small_pieces, small_at = line.row_pieces(move.result())
+    small_pieces, late_sums = lax.optimization_barrier((small_pieces, late_sums))
     wld = wproj[queries_wide:]
 
-    def last(made):
+    def last():
         small = place_rows(small_pieces, small_at)
         delta_latent, dots, gain_delta = latent_back(small, proj, latent_g[None], cosine, sine)
         latent_row = jnp.pad(gain_delta.reshape(n_dp, R // n_dp), ((0, 0), (0, wide - R // n_dp))).reshape(1, D)
-        return {"delta": delta_latent, "dots": dots,
-                "pack": last_pack(delta_latent, first_round, wld, small, first_g[None], latent_row)}
-
-    jobs = Jobs(last)
-    first_share = line.column_scatter(made["mine"], arrived, jobs)
-    made = jobs.rest()
-    last_sums = scatter_rows(made["pack"]).astype(F32)
+        return delta_latent, dots, last_pack(delta_latent, first_round, wld, small, first_g[None], latent_row)
+
+    delta_latent, dots, pack = beside([first_move], last)
+    steps(first_move, last_step - 2)
+    first_share = first_move.result()
+    last_sums = scatter_rows(pack).astype(F32)
     dwld, vectors = last_sums[:latent_wide], last_sums[latent_wide:]
     dwq, dwup, dwo = split_rows(attend_sums, [queries_wide, up_rows, output_weight.shape[0]])
     content = heads_here * DN
@@ -740,23 +748,25 @@
     dwld = jnp.concatenate([dwld[: R + half], dwld[R + DR : R + DR + half]], axis=0)
 
     first_share = first_share + dot(
-        made["delta"], lax.dynamic_slice_in_dim(wld, column_start, my_columns, 1), 1, 0
+        delta_latent, lax.dynamic_slice_in_dim(wld, column_start, my_columns, 1), 1, 0
     )
     vc = layer_input.astype(F32)
     gc = lax.dynamic_slice_in_dim(first_g, column_start, my_columns, 0)
     input_delta = (
         lax.dynamic_slice_in_dim(hidden_delta, column_start, my_columns, 1).astype(F32)
         + r1 * gc * first_share
-        - vc * (r1 * r1) * (made["dots"] / D)
-    )
+        - vc * (r1 * r1) * (dots / D)
+    )
+
+    def units_delta(k):
+        return early_sums[k * n0 : (k + 1) * n0], late_sums[k * n1 : (k + 1) * n1]
 
     def expert_delta(k):
-        first = early_sums[k * units_here : (k + 1) * units_here]
-        second = late_sums[k * units_here : k * units_here + E * fe - units_here]
-        return jnp.concatenate([first, second], axis=0).astype(F32).reshape(E, fe, wide)
+        first, second = units_delta(k)
+        return jnp.concatenate([first, second[: E * fe - n0]], axis=0).astype(F32).reshape(E, fe, wide)
 
     def shared_delta(k):
-        return late_sums[(k + 1) * units_here - shared : (k + 1) * units_here].astype(F32)
+        return units_delta(k)[1][E * fe - n0 :].astype(F32)
 
     return (
         layer_output, input_delta, vectors[E + 1], dwq.T, dwld.T, vectors[E + 2, : R // n_dp],

time: 1160 us -> 1130 us (0.974)
  waiting for transfers between devices: 296 us -> 261 us
  Pallas kernels: 484 us -> 468 us
  local copies, waits for them, and re-layouts: 72 us -> 84.5 us
    ppermute x60, waiting for transfers between devices: 271 us -> 250 us  [shift(): return lax.ppermute(a, 'tensor', pairs)]
    ppermute x25, waiting for transfers between devices: 24.5 us -> 10.3 us  [swap(): return lax.ppermute(a, 'tensor', [(i, i ^ 1) for i in range(self.n)])]
    slice x6 -> x8, local copies, waits for them, and re-layouts: 9.27 us -> 22.8 us  [the longest x2 13.4 us: per_device(): down0, down1 = (downs[:n0], downs[n0:])]
    dot_general x11 -> x12, matrix products: 51.1 us -> 57.1 us  [dot(): lax.dot_general(a, b, (((ca,), (cb,)), ((), ())), preferred_element_type=...]
    convert_element_type x21 -> x20, other arithmetic: 51.1 us -> 57.1 us  [the longest x14 42.7 us: total(): return (mine.astype(F32) + arrived.astype(F32)).astype(BF)]
    unnamed x163 -> x159, local copies, waits for them, and re-layouts: 21.4 us -> 23.5 us
  transfers between devices with their start and end apart: 93 -> 93, of which waited for: 36 -> 29; matrix products, arithmetic and copies ran while one was open for 17% -> 20% of each run, Pallas kernels for 42% -> 42%
where the time goes in v3:
time: 1130 us; the launch traced here: 1120 us
  Pallas kernels  468 us (41%)
  waiting for transfers between devices  261 us (23%)
  starting transfers between devices  131 us (12%)
  other arithmetic  106 us (9%)
  local copies, waits for them, and re-layouts  84.5 us (7%)
  matrix products  57.3 us (5%)
  between operations  16.2 us (1%)
    ppermute x60, waiting for transfers between devices, shift(): return lax.ppermute(a, 'tensor', pairs)  250 us
    pallas_call x6, Pallas kernels, back(): pl.pallas_call(body, grid=(T // bt,), in_specs=ins, out_specs=ospec, out_...  136 us
    ppermute x60, starting transfers between devices, shift(): return lax.ppermute(a, 'tensor', pairs)  126 us
    pallas_call x5, Pallas kernels, outer(): pl.pallas_call(outer_kernel, grid=(count, D // bc), in_specs=ins, out_spe...  111 us
    pallas_call x2, Pallas kernels, units(): pl.pallas_call(functools.partial(units_kernel, fe, first), grid=(T // bt,...  84.7 us
    dot_general x12, matrix products, dot(): lax.dot_general(a, b, (((ca,), (cb,)), ((), ())), preferred_element_type=...  57.1 us
    convert_element_type x14, other arithmetic, total(): return (mine.astype(F32) + arrived.astype(F32)).astype(BF)  42.7 us
    pallas_call x2, Pallas kernels, lift_back(): pl.pallas_call(lift_kernel, grid=(T // bt,), in_specs=[pl.BlockSpec((bt,...  39.8 us
  transfers between devices with their start and end apart: 93, of which 29 were waited for; matrix products, arithmetic and copies ran while one was open for 20% of the time, Pallas kernels for 42%

profile of v3, /device:TPU:0, one launch (start us, length us, event | category | flops | bytes accessed | tf_op | source)
XLA Modules:
  0.0 1123.4 jit_solution(7805849208336577817)
XLA Ops:
  26.7 17.5 %collective-permute-done.1 = bf16[2048,256]{1,0:T(8,128)(2,1)} collective-permute-done((bf16[2048,256]{1,0:T(8,128)(2,1)}, bf16[2048,256]{1,0:T(8,128)(2,1)}, u32[]{:S(2)}, u32[]{:S(2)}) %collective-permute-start.1) | collective-permute-done | bytes 1048608 | tf_op jit(solution)/shard_map/ppermute | solution.py:423
  54.6 24.0 %collective-permute-done.4 = bf16[2048,256]{1,0:T(8,128)(2,1)} collective-permute-done((bf16[2048,256]{1,0:T(8,128)(2,1)}, bf16[2048,256]{1,0:T(8,128)(2,1)}, u32[]{:S(2)}, u32[]{:S(2)}) %collective-permute-start.4) | collective-permute-done | bytes 1048608 | tf_op jit(solution)/shard_map/ppermute | solution.py:423
  88.4 22.7 %collective-permute-done.6 = bf16[2048,256]{1,0:T(8,128)(2,1)} collective-permute-done((bf16[2048,256]{1,0:T(8,128)(2,1)}, bf16[2048,256]{1,0:T(8,128)(2,1)}, u32[]{:S(2)}, u32[]{:S(2)}) %collective-permute-start.6) | collective-permute-done | bytes 1048608 | tf_op jit(solution)/shard_map/ppermute | solution.py:423
  122.5 13.3 %shard_map.306 = (bf16[2048,2048]{1,0:T(8,128)(2,1)}, bf16[2048,2048]{1,0:T(8,128)(2,1)}, f32[2048,1]{1,0:T(8,128)}) custom-call(s32[8]{0:T(128)} %stack.44.at_ref, bf16[2048,256]{1,0:T(8,128)(2,1)} %refs_0_, bf16[2048,256]{1,0:T(8,128)(2,1)} %collective-permute-done.refs_1_, bf16[2048,256]{1,0:T(8,128)(2,1)} %copy-done.15, ...), custom_call_target="tpu_custom_call" | custom-call | flops 25165824 | bytes 25165824 | tf_op jit(solution)/shard_map/pallas_call | solution.py:184
  135.8 13.2 %fusion.proj_ref = f32[2048,1024]{1,0:T(8,128)} fusion(bf16[2048,2048]{1,0:T(8,128)(2,1)} %get-tuple-element.283.x_ref, bf16[1440,2048]{1,0:T(8,128)(2,1)S(1)} %copy-done), kind=kOutput, calls=%fused_computation.6 | convolution fusion | flops 8589934592 | bytes 20971520 | tf_op jit(solution)/shard_map/dot_general | solution.py:27
  152.8 13.9 %shard_map.307 = (bf16[2048,384]{1,0:T(8,128)(2,1)}, bf16[2048,128]{1,0:T(8,128)(2,1)}, bf16[2048,512]{1,0:T(8,128)(2,1)}, bf16[2048,512]{1,0:T(8,128)(2,1)}, bf...) custom-call(f32[2048,1024]{1,0:T(8,128)} %fusion.proj_ref, bf16[512,512]{1,0:T(8,128)(2,1)} %bitcast.165, f32[1,512]{1,0:T(1,128)} %bitcast.183, ...), custom_call_target="tpu_custom_call" | custom-call | flops 2147483648 | bytes 16384000 | tf_op jit(solution)/shard_map/pallas_call | solution.py:340
  227.4 15.9 %collective-permute-done.17 = bf16[256,2048]{1,0:T(8,128)(2,1)} collective-permute-done((bf16[256,2048]{1,0:T(8,128)(2,1)}, bf16[256,2048]{1,0:T(8,128)(2,1)}, u32[]{:S(2)}, u32[]{:S(2)}) %collective-permute-start.17) | collective-permute-done | bytes 1048608 | tf_op jit(solution)/shard_map/ppermute | solution.py:423
  301.3 18.7 %shard_map.309.b_ref = bf16[2048,1536]{1,0:T(8,128)(2,1)} custom-call(bf16[2048,2048]{1,0:T(8,128)(2,1)} %shard_map.308.g_ref.x_ref, bf16[1536,2048]{1,0:T(8,128)(2,1)} %slice.290.w_ref.refs_1_), custom_call_target="tpu_custom_call" | custom-call | flops 12884901888 | bytes 20971520 | tf_op jit(solution)/shard_map/pallas_call | solution.py:82
  329.8 21.1 %shard_map.310.b_ref = bf16[2048,1632]{1,0:T(8,128)(2,1)} custom-call(bf16[2048,2048]{1,0:T(8,128)(2,1)} %shard_map.308.g_ref.x_ref, bf16[1632,2048]{1,0:T(8,128)(2,1)} %slice.291.w_ref.refs_3_), custom_call_target="tpu_custom_call" | custom-call | flops 13690208256 | bytes 21757952 | tf_op jit(solution)/shard_map/pallas_call | solution.py:82
  357.2 23.8 %collective-permute-done.33 = bf16[256,2048]{1,0:T(8,128)(2,1)} collective-permute-done((bf16[256,2048]{1,0:T(8,128)(2,1)}, bf16[256,2048]{1,0:T(8,128)(2,1)}, u32[]{:S(2)}, u32[]{:S(2)}) %collective-permute-start.33) | collective-permute-done | bytes 1048608 | tf_op jit(solution)/shard_map/ppermute | solution.py:423
  401.5 40.2 %shard_map.312 = (bf16[3,2048,1536]{2,1,0:T(8,128)(2,1)}, f32[2048,16]{1,0:T(8,128)}) custom-call(bf16[2048,2048]{1,0:T(8,128)(2,1)} %get-tuple-element.233.x_ref, bf16[3072,2048]{1,0:T(8,128)(2,1)} %all-gather.9.cloned.1.call-done.wg_ref.wu_ref.refs_1_.refs_3_, bf16[3072,2048]{1,0:T(8,128)(2,1)} %all-gather.9.cloned.1.call-done.wg_ref.wu_ref.refs_1_.refs_3_, ...), custom_call_target="tpu_custom_call" | custom-call | flops 25769803776 | bytes 46137344 | tf_op jit(solution)/shard_map/pallas_call | solution.py:72
  441.6 33.0 %shard_map.313.refs_0_ = bf16[4608,2048]{1,0:T(8,128)(2,1)} custom-call(bf16[3,2048,1536]{2,1,0:T(8,128)(2,1)} %get-tuple-element.239.s_ref.refs_0_.refs_2_, bf16[2048,2048]{1,0:T(8,128)(2,1)} %get-tuple-element.233.x_ref), custom_call_target="tpu_custom_call" | custom-call | flops 25769803776 | bytes 41943040 | tf_op jit(solution)/shard_map/pallas_call | solution.py:153
  474.7 18.6 %shard_map.314 = bf16[4608,2048]{1,0:T(8,128)(2,1)} custom-call(bf16[3,2048,1536]{2,1,0:T(8,128)(2,1)} %get-tuple-element.239.s_ref.refs_0_.refs_2_, bf16[2048,2048]{1,0:T(8,128)(2,1)} %shard_map.308.g_ref.x_ref, bf16[4608,2048]{1,0:T(8,128)(2,1)} %shard_map.313.refs_0_), custom_call_target="tpu_custom_call", output_to_operand_aliasing={{}: (2, {})} | custom-call | flops 12884901888 | bytes 20971520 | tf_op jit(solution)/shard_map/pallas_call | solution.py:153
  493.3 34.0 %shard_map.315.refs_0_ = f32[2048,2048]{1,0:T(8,128)} custom-call(bf16[3,2048,1536]{2,1,0:T(8,128)(2,1)} %get-tuple-element.239.s_ref.refs_0_.refs_2_, bf16[3072,2048]{1,0:T(8,128)(2,1)} %all-gather.9.cloned.1.call-done.wg_ref.wu_ref.refs_1_.refs_3_, bf16[3,2048,1536]{2,1,0:T(8,128)(2,1)} %get-tuple-element.239.s_ref.refs_0_.refs_2_, ...), custom_call_target="tpu_custom_call" | custom-call | flops 25769803776 | bytes 41943040 | tf_op jit(solution)/shard_map/pallas_call | solution.py:141
  527.4 44.5 %shard_map.316 = (bf16[3,2048,1632]{2,1,0:T(8,128)(2,1)}, f32[2048,16]{1,0:T(8,128)}) custom-call(bf16[2048,2048]{1,0:T(8,128)(2,1)} %get-tuple-element.233.x_ref, bf16[3264,2048]{1,0:T(8,128)(2,1)} %all-gather.11.cloned.1.call-done.wg_ref.wu_ref.refs_2_.refs_4_, bf16[3264,2048]{1,0:T(8,128)(2,1)} %all-gather.11.cloned.1.call-done.wg_ref.wu_ref.refs_2_.refs_4_, ...), custom_call_target="tpu_custom_call" | custom-call | flops 27380416512 | bytes 48496640 | tf_op jit(solution)/shard_map/pallas_call | solution.py:72
  571.9 39.9 %shard_map.317 = bf16[2048,2176]{1,0:T(8,128)(2,1)} custom-call(f32[2048,2048]{1,0:T(8,128)} %shard_map.315.refs_0_, bf16[3,2048,1632]{2,1,0:T(8,128)(2,1)} %get-tuple-element.242.refs_1_.refs_3_.refs_2_.s_ref, bf16[3264,2048]{1,0:T(8,128)(2,1)} %all-gather.11.cloned.1.call-done.wg_ref.wu_ref.refs_2_.refs_4_, ...), custom_call_target="tpu_custom_call" | custom-call | flops 27380416512 | bytes 43515904 | tf_op jit(solution)/shard_map/pallas_call | solution.py:141
  614.8 23.2 %shard_map.318 = bf16[4,2048,256]{2,1,0:T(8,128)(2,1)} custom-call(s32[1]{0:T(128)S(6)} %sub.27.core_ref, bf16[3,2048,1536]{2,1,0:T(8,128)(2,1)} %get-tuple-element.239.s_ref.refs_0_.refs_2_, bf16[1536,2048]{1,0:T(8,128)(2,1)} %slice.290.w_ref.refs_1_, bf16[3,2048,1632]{2,1,0:T(8,128)(2,1)} %get-tuple-element.242.refs_1_.refs_3_.refs_2_.s_ref, ...), custom_call_target="tpu_custom_call" | custom-call | flops 13287555072 | bytes 42729472 | tf_op jit(solution)/shard_map/pallas_call | solution.py:141
  648.1 19.9 %shard_map.319.refs_0_ = bf16[4896,2048]{1,0:T(8,128)(2,1)} custom-call(bf16[3,2048,1632]{2,1,0:T(8,128)(2,1)} %get-tuple-element.242.refs_1_.refs_3_.refs_2_.s_ref, bf16[2048,2048]{1,0:T(8,128)(2,1)} %get-tuple-element.233.x_ref), custom_call_target="tpu_custom_call" | custom-call | flops 13690208256 | bytes 21757952 | tf_op jit(solution)/shard_map/pallas_call | solution.py:153
  679.4 19.6 %shard_map.320.refs_0_ = bf16[4896,2048]{1,0:T(8,128)(2,1)} custom-call(bf16[3,2048,1632]{2,1,0:T(8,128)(2,1)} %get-tuple-element.242.refs_1_.refs_3_.refs_2_.s_ref, bf16[2048,2048]{1,0:T(8,128)(2,1)} %get-tuple-element.233.x_ref, bf16[4896,2048]{1,0:T(8,128)(2,1)} %shard_map.319.refs_0_), custom_call_target="tpu_custom_call", output_to_operand_aliasing={{}: (2, {})} | custom-call | flops 13690208256 | bytes 21757952 | tf_op jit(solution)/shard_map/pallas_call | solution.py:153
  714.8 19.7 %shard_map.321 = bf16[4896,2048]{1,0:T(8,128)(2,1)} custom-call(bf16[3,2048,1632]{2,1,0:T(8,128)(2,1)} %get-tuple-element.242.refs_1_.refs_3_.refs_2_.s_ref, bf16[2048,2048]{1,0:T(8,128)(2,1)} %shard_map.308.g_ref.x_ref, bf16[4896,2048]{1,0:T(8,128)(2,1)} %shard_map.320.refs_0_), custom_call_target="tpu_custom_call", output_to_operand_aliasing={{}: (2, {})} | custom-call | flops 13690208256 | bytes 21757952 | tf_op jit(solution)/shard_map/pallas_call | solution.py:153
  752.4 22.5 %shard_map.322 = bf16[4,2048,256]{2,1,0:T(8,128)(2,1)} custom-call(s32[1]{0:T(128)} %bitcast.42.core_ref, bf16[3,2048,1536]{2,1,0:T(8,128)(2,1)} %get-tuple-element.239.s_ref.refs_0_.refs_2_, bf16[1536,2048]{1,0:T(8,128)(2,1)} %slice.290.w_ref.refs_1_, bf16[3,2048,1632]{2,1,0:T(8,128)(2,1)} %get-tuple-element.242.refs_1_.refs_3_.refs_2_.s_ref, ...), custom_call_target="tpu_custom_call" | custom-call | flops 13287555072 | bytes 42729472 | tf_op jit(solution)/shard_map/pallas_call | solution.py:141
  815.7 14.4 %collective-permute-done.52 = bf16[256,2048]{1,0:T(8,128)(2,1)S(1)} collective-permute-done((bf16[256,2048]{1,0:T(8,128)(2,1)S(1)}, bf16[256,2048]{1,0:T(8,128)(2,1)S(1)}, u32[]{:S(2)}, u32[]{:S(2)}) %collective-permute-start.52) | collective-permute-done | bytes 1048608 | tf_op jit(solution)/shard_map/ppermute | solution.py:423
  863.4 17.6 %shard_map.324 = (bf16[2048,384]{1,0:T(8,128)(2,1)}, bf16[2048,512]{1,0:T(8,128)(2,1)}, f32[2048,128]{1,0:T(8,128)}, f32[2048,1]{1,0:T(8,128)}) custom-call(bf16[2048,384]{1,0:T(8,128)(2,1)} %get-tuple-element.270.q_ref, bf16[2048,128]{1,0:T(8,128)(2,1)} %get-tuple-element.271.kr_ref, bf16[2048,512]{1,0:T(8,128)(2,1)} %get-tuple-element.272.kv_ref, ...), custom_call_target="tpu_custom_call" | custom-call | flops 5872025600 | bytes 12288000 | tf_op jit(solution)/shard_map/pallas_call | solution.py:389
  976.9 24.9 %collective-permute-done.69 = bf16[256,640]{1,0:T(8,128)(2,1)S(1)} collective-permute-done((bf16[256,640]{1,0:T(8,128)(2,1)S(1)}, bf16[256,640]{1,0:T(8,128)(2,1)S(1)}, u32[]{:S(2)}, u32[]{:S(2)}) %collective-permute-start.69) | collective-permute-done | bytes 327712 | tf_op jit(solution)/shard_map/ppermute | solution.py:423
  (476 shorter events, 551.0 us)
Async XLA Ops:
  7.2 113.8 %all-gather.5.cloned.1.call-start = ((), (), s32[]{:S(2)}) async-start(), calls=%async_computation.4 | async-start | bytes 7372800 | tf_op jit(solution)/shard_map/all_gather | solution.py:515
  16.5 278.2 %all-gather.7.cloned.1.call-start = ((), (), s32[]{:S(2)}) async-start(), calls=%async_computation.5 | async-start | bytes 16220160 | tf_op jit(solution)/shard_map/all_gather | solution.py:515
  49.4 352.1 %all-gather.9.cloned.1.call-start = ((), (), s32[]{:S(2)}) async-start(), calls=%async_computation.6 | async-start | bytes 15728640 | tf_op jit(solution)/shard_map/all_gather | solution.py:515
  78.7 448.7 %all-gather.11.cloned.1.call-start = ((), (), s32[]{:S(2)}) async-start(), calls=%async_computation.8 | async-start | bytes 16711680 | tf_op jit(solution)/shard_map/all_gather | solution.py:515
  78.7 36.3 %collective-permute-start = (bf16[2048,256]{1,0:T(8,128)(2,1)}, bf16[2048,256]{1,0:T(8,128)(2,1)}, u32[]{:S(2)}, u32[]{:S(2)}) collective-permute-start(bf16[2048,256]{1,0:T(8,128)(2,1)} %refs_0_), channel_id=1, source_target_pairs={{0,1},{1,0},{2,3},{3,2},{4,5},{5,4},{6,7},{7,6},{8,9},{9,8},{10,11... | collective-permute-start | bytes 3145736 | tf_op jit(solution)/shard_map/ppermute | solution.py:414
  117.0 32.1 %collective-permute-start.10 = (bf16[2048,256]{1,0:T(8,128)(2,1)}, bf16[2048,256]{1,0:T(8,128)(2,1)}, u32[]{:S(2)}, u32[]{:S(2)}) collective-permute-start(bf16[2048,256]{1,0:T(8,128)(2,1)} %refs_0_.1), channel_id=1, source_target_pairs={{0,2},{1,3},{2,4},{3,5},{4,6},{5,7},{8,10},{9,11},{10,12},{11,13},... | collective-permute-start | bytes 3145736 | tf_op jit(solution)/shard_map/ppermute | solution.py:423
  171.5 570.1 %reduce-scatter.5.cloned.1.call-start = ((), (), s32[]{:S(2)}) async-start(), calls=%async_computation.7 | async-start | bytes 23592960 | tf_op jit(solution)/shard_map/reduce_scatter | solution.py:519
  225.7 34.7 %collective-permute-start.23 = (bf16[2048,256]{1,0:T(8,128)(2,1)}, bf16[2048,256]{1,0:T(8,128)(2,1)}, u32[]{:S(2)}, u32[]{:S(2)}) collective-permute-start(bf16[2048,256]{1,0:T(8,128)(2,1)} %refs_0_.1), channel_id=1, source_target_pairs={{0,1},{1,0},{2,3},{3,2},{4,5},{5,4},{6,7},{7,6},{8,9},{9,8},{10,11... | collective-permute-start | bytes 3145736 | tf_op jit(solution)/shard_map/ppermute | solution.py:414
  320.0 30.9 %collective-permute-start.30 = (bf16[256,2048]{1,0:T(8,128)(2,1)S(1)}, bf16[256,2048]{1,0:T(8,128)(2,1)}, u32[]{:S(2)}, u32[]{:S(2)}) collective-permute-start(bf16[256,2048]{1,0:T(8,128)(2,1)S(1)} %collective-permute-done.28), channel_id=1, source_target_pairs={{2,4},{3,5},{4,6},{5,7},{10,12},{11,13},{12,14},{13,15},{18,20},{1... | collective-permute-start | bytes 3145736 | tf_op jit(solution)/shard_map/ppermute | solution.py:423
  354.2 35.6 %collective-permute-start.27 = (bf16[256,2048]{1,0:T(8,128)(2,1)S(1)}, bf16[256,2048]{1,0:T(8,128)(2,1)}, u32[]{:S(2)}, u32[]{:S(2)}) collective-permute-start(bf16[256,2048]{1,0:T(8,128)(2,1)S(1)} %get-tuple-element.385.refs_0_), channel_id=1, source_target_pairs={{0,1},{1,0},{2,3},{3,2},{4,5},{5,4},{6,7},{7,6},{8,9},{9,8},{10,11... | collective-permute-start | bytes 3145736 | tf_op jit(solution)/shard_map/ppermute | solution.py:414
  355.8 34.0 %collective-permute-start.35 = (bf16[256,2048]{1,0:T(8,128)(2,1)S(1)}, bf16[256,2048]{1,0:T(8,128)(2,1)}, u32[]{:S(2)}, u32[]{:S(2)}) collective-permute-start(bf16[256,2048]{1,0:T(8,128)(2,1)S(1)} %broadcast_select_fusion.3.refs_4_), channel_id=1, source_target_pairs={{0,1},{1,0},{2,3},{3,2},{4,5},{5,4},{6,7},{7,6},{8,9},{9,8},{10,11... | collective-permute-start | bytes 3145736 | tf_op jit(solution)/shard_map/ppermute | solution.py:414
  493.3 540.8 %reduce-scatter.7.cloned.1.call-start = ((), (), s32[]{:S(2)}) async-start(), calls=%async_computation.9 | async-start | bytes 25067520 | tf_op jit(solution)/shard_map/reduce_scatter | solution.py:519
  668.0 71.2 %collective-permute-start.44 = (bf16[4,2048,256]{2,1,0:T(8,128)(2,1)}, bf16[4,2048,256]{2,1,0:T(8,128)(2,1)}, u32[]{:S(2)}, u32[]{:S(2)}) collective-permute-start(bf16[4,2048,256]{2,1,0:T(8,128)(2,1)} %shard_map.318), channel_id=1, source_target_pairs={{0,1},{1,0},{2,3},{3,2},{4,5},{5,4},{6,7},{7,6},{8,9},{9,8},{10,11... | collective-permute-start | bytes 12582920 | tf_op jit(solution)/shard_map/ppermute | solution.py:414
  741.6 324.7 %reduce-scatter.11.cloned.1.call-start = ((), (), s32[]{:S(2)}) async-start(), calls=%async_computation.11 | async-start | bytes 3932160 | tf_op jit(solution)/shard_map/reduce_scatter | solution.py:519
  814.9 33.0 %collective-permute-start.57 = (bf16[256,2048]{1,0:T(8,128)(2,1)}, bf16[256,2048]{1,0:T(8,128)(2,1)}, u32[]{:S(2)}, u32[]{:S(2)}) collective-permute-start(bf16[256,2048]{1,0:T(8,128)(2,1)} %fusion.5.refs_0_), channel_id=1, source_target_pairs={{0,1},{1,0},{2,3},{3,2},{4,5},{5,4},{6,7},{7,6},{8,9},{9,8},{10,11... | collective-permute-start | bytes 3145736 | tf_op jit(solution)/shard_map/ppermute | solution.py:414
  815.1 34.1 %collective-permute-start.59 = (bf16[256,2048]{1,0:T(8,128)(2,1)S(1)}, bf16[256,2048]{1,0:T(8,128)(2,1)}, u32[]{:S(2)}, u32[]{:S(2)}) collective-permute-start(bf16[256,2048]{1,0:T(8,128)(2,1)S(1)} %broadcast_select_fusion.2.refs_4_), channel_id=1, source_target_pairs={{0,1},{1,0},{2,3},{3,2},{4,5},{5,4},{6,7},{7,6},{8,9},{9,8},{10,11... | collective-permute-start | bytes 3145736 | tf_op jit(solution)/shard_map/ppermute | solution.py:414
  839.6 41.4 %collective-permute-start.55 = (bf16[2048,256]{1,0:T(8,128)(2,1)}, bf16[2048,256]{1,0:T(8,128)(2,1)S(1)}, u32[]{:S(2)}, u32[]{:S(2)}) collective-permute-start(bf16[2048,256]{1,0:T(8,128)(2,1)} %get-tuple-element.411), channel_id=1, source_target_pairs={{0,2},{1,3},{2,4},{3,5},{4,6},{5,7},{8,10},{9,11},{10,12},{11,13},... | collective-permute-start | bytes 3145736 | tf_op jit(solution)/shard_map/ppermute | solution.py:423
  848.0 33.1 %collective-permute-start.56 = (bf16[2048,256]{1,0:T(8,128)(2,1)}, bf16[2048,256]{1,0:T(8,128)(2,1)S(1)}, u32[]{:S(2)}, u32[]{:S(2)}) collective-permute-start(bf16[2048,256]{1,0:T(8,128)(2,1)} %get-tuple-element.410), channel_id=1, source_target_pairs={{2,0},{3,1},{4,2},{5,3},{6,4},{7,5},{10,8},{11,9},{12,10},{13,11},... | collective-permute-start | bytes 3145736 | tf_op jit(solution)/shard_map/ppermute | solution.py:423
  932.0 33.3 %collective-permute-start.68 = (bf16[4,2048,256]{2,1,0:T(8,128)(2,1)}, bf16[4,2048,256]{2,1,0:T(8,128)(2,1)}, u32[]{:S(2)}, u32[]{:S(2)}) collective-permute-start(bf16[4,2048,256]{2,1,0:T(8,128)(2,1)} %shard_map.325), channel_id=1, source_target_pairs={{0,1},{1,0},{2,3},{3,2},{4,5},{5,4},{6,7},{7,6},{8,9},{9,8},{10,11... | collective-permute-start | bytes 12582920 | tf_op jit(solution)/shard_map/ppermute | solution.py:414
  965.3 146.0 %reduce-scatter.9.cloned.1.call-start = ((), (), s32[]{:S(2)}) async-start(), calls=%async_computation.10 | async-start | bytes 3440640 | tf_op jit(solution)/shard_map/reduce_scatter | solution.py:519
  969.9 55.0 %collective-permute-start.75 = (bf16[2048,256]{1,0:T(8,128)(2,1)S(1)}, bf16[2048,256]{1,0:T(8,128)(2,1)S(1)}, u32[]{:S(2)}, u32[]{:S(2)}) collective-permute-start(bf16[2048,256]{1,0:T(8,128)(2,1)S(1)} %get-tuple-element.409), channel_id=1, source_target_pairs={{0,2},{1,3},{8,10},{9,11},{16,18},{17,19},{24,26},{25,27}} | collective-permute-start | bytes 3145736 | tf_op jit(solution)/shard_map/ppermute | solution.py:423
  973.6 51.4 %collective-permute-start.76 = (bf16[2048,256]{1,0:T(8,128)(2,1)S(1)}, bf16[2048,256]{1,0:T(8,128)(2,1)S(1)}, u32[]{:S(2)}, u32[]{:S(2)}) collective-permute-start(bf16[2048,256]{1,0:T(8,128)(2,1)S(1)} %get-tuple-element.408), channel_id=1, source_target_pairs={{6,4},{7,5},{14,12},{15,13},{22,20},{23,21},{30,28},{31,29}} | collective-permute-start | bytes 3145736 | tf_op jit(solution)/shard_map/ppermute | solution.py:423
  1026.8 33.0 %collective-permute-start.77 = (bf16[2048,256]{1,0:T(8,128)(2,1)}, bf16[2048,256]{1,0:T(8,128)(2,1)S(1)}, u32[]{:S(2)}, u32[]{:S(2)}) collective-permute-start(bf16[2048,256]{1,0:T(8,128)(2,1)} %get-tuple-element.407), channel_id=1, source_target_pairs={{0,2},{1,3},{2,4},{3,5},{8,10},{9,11},{10,12},{11,13},{16,18},{17,... | collective-permute-start | bytes 3145736 | tf_op jit(solution)/shard_map/ppermute | solution.py:423
  1028.3 31.5 %collective-permute-start.78 = (bf16[2048,256]{1,0:T(8,128)(2,1)}, bf16[2048,256]{1,0:T(8,128)(2,1)S(1)}, u32[]{:S(2)}, u32[]{:S(2)}) collective-permute-start(bf16[2048,256]{1,0:T(8,128)(2,1)} %get-tuple-element.406), channel_id=1, source_target_pairs={{4,2},{5,3},{6,4},{7,5},{12,10},{13,11},{14,12},{15,13},{20,18},{2... | collective-permute-start | bytes 3145736 | tf_op jit(solution)/shard_map/ppermute | solution.py:423
  (141 other events, 2100.7 us)
Sparse Core Ops, SparseCore 0:
  16.6 69.4 all-gather.4
  88.5 125.6 all-gather.6
  216.0 122.3 all-gather.8
  340.7 128.9 all-gather.10
  493.4 171.8 reduce-scatter.4
  741.7 178.1 reduce-scatter.6
  965.4 42.9 reduce-scatter.10
  1060.0 40.7 reduce-scatter.8

commit v4 on v3

--- a/solution.py
+++ b/solution.py
@@ -42,6 +42,9 @@
 
 def once(shape, index):
     return pl.BlockSpec(shape, index, pipeline_mode=pl.Buffered(1))
+
+def rows_once(n, wide, first):
+    return pl.BlockSpec((pl.Element(n), pl.Element(wide)), lambda i: (first, 0), pipeline_mode=pl.Buffered(1))
 
 def place_matrix(fe, first, n):
     col=lax.broadcasted_iota(jnp.int32,(E,n),1)+first; row=lax.broadcasted_iota(jnp.int32,(E,n),0)*fe
@@ -80,7 +83,7 @@
 def lift_back(g,packed,at,n,bt):
     T,D=g.shape
     return pl.pallas_call(lift_kernel,grid=(T//bt,),
-        in_specs=[pl.BlockSpec((bt,D),lambda i:(i,0)),once((n,D),lambda i:(at,0))],
+        in_specs=[pl.BlockSpec((bt,D),lambda i:(i,0)),rows_once(n,D,at)],
         out_specs=pl.BlockSpec((bt,n),lambda i:(i,0)),out_shape=jax.ShapeDtypeStruct((T,n),BF),compiler_params=params(1),
         cost_estimate=pl.CostEstimate(flops=2*T*D*n,bytes_accessed=2*(T*D+n*D+T*n),transcendentals=0))(g,packed)
 
@@ -125,7 +128,7 @@
     for st,k,packed,n,at in terms:
         if st.ndim==3: ins.append(pl.BlockSpec((1,bt,n),lambda i,k=k:(k,i,0)))
         else: ins.append(pl.BlockSpec((bt,n),lambda i:(i,0)))
-        ins.append(once((n,D),lambda i,at=at:(at,0)))
+        ins.append(rows_once(n,D,at))
         args+= [st,packed]; fl+=2*T*D*n; by+=2*(T*n+n*D)
     for more in beside:
         ins.append(pl.BlockSpec((bt,more.shape[1]),lambda i:(i,0))); args.append(more)
@@ -160,7 +163,7 @@
     pieces=refs[:2*chips]
     refs=refs[2*chips:]
     if norm:
-        gain_ref, out_ref, round_ref, r_ref = refs
+        gain_ref, w_ref, out_ref, round_ref, r_ref, proj_ref = refs
     else:
         (out_ref,) = refs
     w=pieces[0].shape[1]
@@ -171,34 +174,44 @@
         r=lax.rsqrt(jnp.mean(v*v,axis=-1,keepdims=True)+EPSILON)
         round_ref[...]=(v*r*gain_ref[...]).astype(BF)
         r_ref[...]=r
-
-def place_columns(pieces, at, gain=None, bt=256):
+        proj_ref[...]=mm(round_ref[...],w_ref[...],NT)
+
+def place_columns(pieces, at, gain=None, packed=None, count=0, bt=256):
     T,w=pieces[0].shape; n=len(pieces)
     ins=[pl.BlockSpec(memory_space=pltpu.SMEM)]+[pl.BlockSpec((bt,w),lambda i:(i,0))]*n
     args=[at]+list(pieces)
     outs=[jax.ShapeDtypeStruct((T,n*w),BF)]; specs=[pl.BlockSpec((bt,n*w),lambda i:(i,0))]
     if gain is not None:
-        ins.append(pl.BlockSpec((1,n*w),lambda i:(0,0))); args.append(gain[None])
-        outs+=[jax.ShapeDtypeStruct((T,n*w),BF),jax.ShapeDtypeStruct((T,1),F32)]
-        specs+=[pl.BlockSpec((bt,n*w),lambda i:(i,0)),pl.BlockSpec((bt,1),lambda i:(i,0))]
+        ins+=[pl.BlockSpec((1,n*w),lambda i:(0,0)),rows_once(count,n*w,0)]; args+=[gain[None],packed]
+        outs+=[jax.ShapeDtypeStruct((T,n*w),BF),jax.ShapeDtypeStruct((T,1),F32),jax.ShapeDtypeStruct((T,count),F32)]
+        specs+=[pl.BlockSpec((bt,n*w),lambda i:(i,0)),pl.BlockSpec((bt,1),lambda i:(i,0)),pl.BlockSpec((bt,count),lambda i:(i,0))]
     return pl.pallas_call(functools.partial(place_columns_kernel,n//2,gain is not None),grid=(T//bt,),
         in_specs=ins,out_specs=specs,out_shape=outs,compiler_params=params(1),
-        cost_estimate=pl.CostEstimate(flops=6*T*n*w,bytes_accessed=6*T*n*w,transcendentals=T))(*args)
-
-def place_rows_kernel(n, at_ref, *refs):
-    pieces=refs[:n]; out_ref=refs[n]; sem=refs[n+1]
+        cost_estimate=pl.CostEstimate(flops=(6+2*count)*T*n*w,bytes_accessed=6*T*n*w,transcendentals=T))(*args)
+
+def place_rows_kernel(n, times, at_ref, *refs):
+    pieces=refs[:n]; refs=refs[n:]
+    if times: w_ref,out_ref,made_ref,sem=refs
+    else: out_ref,sem=refs
     rows=pieces[0].shape[0]
-    copies=[pltpu.make_async_copy(pieces[k],out_ref.at[pl.ds(pl.multiple_of(at_ref[k]*rows,rows),rows)],sem.at[k]) for k in range(n)]
+    to=[pl.ds(pl.multiple_of(at_ref[k]*rows,rows),rows) for k in range(n)]
+    copies=[pltpu.make_async_copy(pieces[k],out_ref.at[to[k]],sem.at[k]) for k in range(n)]
     for c in copies: c.start()
+    if times:
+        for k in range(n): made_ref[to[k]]=mm(pieces[k][...],w_ref[...],NT).astype(BF)
     for c in copies: c.wait()
 
-def place_rows(pieces, at):
+def place_rows(pieces, at, weight=None):
     rows,w=pieces[0].shape; n=len(pieces)
-    return pl.pallas_call(functools.partial(place_rows_kernel,n),
-        in_specs=[pl.BlockSpec(memory_space=pltpu.SMEM)]+[pl.BlockSpec(memory_space=pltpu.VMEM)]*n,
-        out_specs=pl.BlockSpec(memory_space=pl.ANY),out_shape=jax.ShapeDtypeStruct((n*rows,w),BF),
+    vmem=pl.BlockSpec(memory_space=pltpu.VMEM)
+    outs=[jax.ShapeDtypeStruct((n*rows,w),BF)]; specs=[pl.BlockSpec(memory_space=pl.ANY)]; more=[]
+    if weight is not None:
+        outs.append(jax.ShapeDtypeStruct((n*rows,weight.shape[0]),BF)); specs.append(vmem); more=[weight]
+    return pl.pallas_call(functools.partial(place_rows_kernel,n,bool(more)),
+        in_specs=[pl.BlockSpec(memory_space=pltpu.SMEM)]+[vmem]*(n+len(more)),
+        out_specs=specs,out_shape=outs,
         scratch_shapes=[pltpu.SemaphoreType.DMA((n,))],compiler_params=pltpu.CompilerParams(vmem_limit_bytes=VMEM_LIMIT),
-        cost_estimate=pl.CostEstimate(flops=0,bytes_accessed=4*n*rows*w,transcendentals=0))(at,*pieces)
+        cost_estimate=pl.CostEstimate(flops=2*n*rows*w*(weight.shape[0] if more else 0),bytes_accessed=4*n*rows*w,transcendentals=0))(at,*pieces,*more)
 
 def norm_rows_kernel(n, at_ref, col_ref, gain_ref, wr_ref, kept_ref, *refs):
     pieces=refs[:n]; round_ref,cols_ref,gating_ref,weight_ref,made,cut,sem,sem2=refs[n:]
@@ -230,6 +243,24 @@
         scratch_shapes=[pltpu.VMEM((n,rows,wide),BF),pltpu.VMEM((n,rows,w),BF),pltpu.SemaphoreType.DMA((n,)),pltpu.SemaphoreType.DMA((n,))],
         compiler_params=pltpu.CompilerParams(vmem_limit_bytes=VMEM_LIMIT),
         cost_estimate=pl.CostEstimate(flops=6*n*rows*wide,bytes_accessed=4*n*rows*wide,transcendentals=n*rows))(at,column,gain[None],router,kept,*pieces)
+
+def small_kernel(pairs_ref, up_ref, kr_ref, dot_ref, entry_ref, out_ref):
+    bt=out_ref.shape[0]
+    out_ref[:,:R]=mm(pairs_ref[...],up_ref[...],NT).astype(BF)
+    h=DR//2
+    kr=kr_ref[...]
+    gap=jnp.zeros((bt,DR-1-entry_ref.shape[1]),F32)
+    out_ref[:,R:]=jnp.concatenate(
+        [kr[:,:h]+kr[:,h:DR],kr[:,DR:DR+h]+kr[:,DR+h:],dot_ref[...],entry_ref[...],gap],axis=1).astype(BF)
+
+def small_terms(pairs, up, kr, dots, entries, bt=512):
+    T=pairs.shape[0]
+    def rows(a): return pl.BlockSpec((bt,a.shape[1]),lambda i:(i,0))
+    return pl.pallas_call(small_kernel,grid=(T//bt,),
+        in_specs=[rows(pairs),pl.BlockSpec(up.shape,lambda i:(0,0)),rows(kr),rows(dots),rows(entries)],
+        out_specs=pl.BlockSpec((bt,R+DN),lambda i:(i,0)),out_shape=jax.ShapeDtypeStruct((T,R+DN),BF),
+        compiler_params=params(1),
+        cost_estimate=pl.CostEstimate(flops=2*T*R*pairs.shape[1],bytes_accessed=8*T*R,transcendentals=0))(pairs,up,kr,dots,entries)
 
 def latent_back_kernel(small_ref, proj_ref, gain_ref, cos_ref, sin_ref, delta_ref, dots_ref, gain_delta_ref):
     i=pl.program_id(0)
@@ -596,7 +627,6 @@
     ))
     steps(move, last_step - 3)
     downs, early, late = gather_rows(downs), gather_rows(early), gather_rows(late)
-    down0, down1 = downs[:n0], downs[n0:]
 
     tile = 256
     core = line.c.reshape(1).astype(jnp.int32)
@@ -605,8 +635,7 @@
     grad_move = Gather(line, cotangent)
 
     def project():
-        rows, first_round, r1 = place_columns(input_pieces, input_at, first_g)
-        return rows, first_round, r1, dot(first_round, wproj, 1, 1)
+        return place_columns(input_pieces, input_at, first_g, attend_packed, queries_wide + latent_wide)
 
     rows, first_round, r1, proj = beside([grad_move], project)
     q, kr, kv, latent, mixed, log_total = attend(proj, wup, latent_g[None], cosine, sine, heads_here)
@@ -621,8 +650,8 @@
     ).astype(BF)
     move = Gather(line, hidden_rows)
     back0, back1 = steps(move, 2, (
-        lambda: lift_back(grad, down0, 0, n0, tile),
-        lambda: lift_back(grad, down1, 0, n1, tile),
+        lambda: lift_back(grad, downs, 0, n0, tile),
+        lambda: lift_back(grad, downs, n0, n1, tile),
     ))
     steps(move, last_step - 2)
     hidden_pieces, hidden_at = line.row_pieces(move.result())
@@ -637,13 +666,13 @@
     deltas = outer(stack0, 2, 1, grad, 3 * n0, 2, deltas)
     deltas, stack0 = lax.optimization_barrier((deltas, stack0))
     early_sums = scatter_rows(deltas)
-    second_terms = back([(stack0, 0, early, n0, 0), (stack0, 1, early, n0, 1)], None, F32, tile)
+    second_terms = back([(stack0, 0, early, n0, 0), (stack0, 1, early, n0, n0)], None, F32, tile)
     stack1, pair1 = units(second_round, late, back1, weight, fe, n0, tile)
     second_terms = back(
-        [(stack1, 0, late, n1, 0), (stack1, 1, late, n1, 1)], second_terms, BF, tile, (pair0, pair1)
-    )
-
-    branch_terms = [(stack0, 2, down0, n0, 0), (stack1, 2, down1, n1, 0)]
+        [(stack1, 0, late, n1, 0), (stack1, 1, late, n1, n1)], second_terms, BF, tile, (pair0, pair1)
+    )
+
+    branch_terms = [(stack0, 2, downs, n0, 0), (stack1, 2, downs, n1, n0)]
     mine, theirs = line.halves(second_terms)
     arrived, branch_theirs = lax.optimization_barrier(
         (line.swap(theirs), back(branch_terms, None, BF, tile, (), 1 - core, line.chips))
@@ -682,8 +711,7 @@
     delta_pieces, delta_at = line.row_pieces(move.result())
 
     def heads_back():
-        placed = place_rows(delta_pieces, delta_at)
-        delta_mixed = dot(placed, wo, 1, 1, BF)
+        placed, delta_mixed = place_rows(delta_pieces, delta_at, wo)
         return placed, attend_back(q, kr, kv, mixed, log_total, delta_mixed, cosine, sine, heads_here)
 
     hidden_delta, heads = beside([branch_move], heads_back)
@@ -694,11 +722,7 @@
     per_entry = jnp.concatenate([second_gain_delta[:, None], query_gain[:, None], router_delta], axis=1)
     if number > D:
         per_entry = jnp.concatenate([per_entry, jnp.zeros((number - D, E + 2), F32)], axis=0)
-    small = jnp.concatenate(
-        [dot(delta_pairs, wup, 1, 1),
-         delta_kr[:, :half] + delta_kr[:, half:DR], delta_kr[:, DR : DR + half] + delta_kr[:, DR + half :],
-         query_dot, per_entry, jnp.zeros((number, 63 - 2 - E), F32)], axis=1,
-    ).astype(BF)
+    small = small_terms(delta_pairs, wup, delta_kr, query_dot, per_entry)
     first_terms = [(delta_queries, 0, attend_packed, queries_wide, 0)]
     mine, theirs = line.halves(small)
     move = line.row_scatter(total(mine, line.swap(theirs)))
@@ -710,25 +734,28 @@
              delta_wup.reshape(n_dp, up_rows, wide).transpose(1, 0, 2).reshape(up_rows, D),
              dot(mixed, hidden_delta, 0, 0, BF)], axis=0)
 
-    theirs, mine, deltas = steps(move, 3, (
+    theirs, mine = steps(move, 2, (
         lambda: back(first_terms, None, BF, tile, (), 1 - core, line.chips),
         lambda: back(first_terms, None, BF, tile, (), core, line.chips),
-        attend_deltas,
     ))
-    steps(move, last_step - 3)
-    small = move.result().astype(BF)
-    deltas, small, layer_output = lax.optimization_barrier((deltas, small, layer_output))
+    steps(move, last_step - 2)
+    small, theirs, mine, layer_output = lax.optimization_barrier(
+        (move.result().astype(BF), theirs, mine, layer_output)
+    )
+    move = Gather(line, small)
+    deltas, arrived = beside([move], lambda: (attend_deltas(), line.swap(theirs)))
     attend_sums = scatter_rows(deltas).astype(F32)
-    move = Gather(line, small)
-    first_move = line.column_scatter(total(mine, line.swap(theirs)))
-    steps(move, last_step - 1)
+    steps(move, last_step - 2)
+    both, ahead = lax.optimization_barrier((total(mine, arrived), (move.left[-1], move.right[-1])))
+    move.left[-1], move.right[-1] = ahead
+    first_move = line.column_scatter(both)
     beside([move, first_move])
     small_pieces, small_at = line.row_pieces(move.result())
     small_pieces, late_sums = lax.optimization_barrier((small_pieces, late_sums))
     wld = wproj[queries_wide:]
 
     def last():
-        small = place_rows(small_pieces, small_at)
+        (small,) = place_rows(small_pieces, small_at)
         delta_latent, dots, gain_delta = latent_back(small, proj, latent_g[None], cosine, sine)
         latent_row = jnp.pad(gain_delta.reshape(n_dp, R // n_dp), ((0, 0), (0, wide - R // n_dp))).reshape(1, D)
         return delta_latent, dots, last_pack(delta_latent, first_round, wld, small, first_g[None], latent_row)

time: 1130 us -> 1090 us (0.965)
  matrix products: 57.3 us -> 32.3 us
  local copies, waits for them, and re-layouts: 84.5 us -> 61.9 us
  other arithmetic: 106 us -> 91.3 us
  Pallas kernels: 468 us -> 480 us
    dot_general x12 -> x9, matrix products: 57.1 us -> 32.1 us  [dot(): lax.dot_general(a, b, (((ca,), (cb,)), ((), ())), preferred_element_type=...]
    slice x2 -> x0, local copies, waits for them, and re-layouts: 13.4 us -> none  [per_device(): down0, down1 = (downs[:n0], downs[n0:])]
    unnamed x159 -> x171, local copies, waits for them, and re-layouts: 23.5 us -> 24.9 us
  transfers between devices with their start and end apart: 93 -> 93, of which waited for: 29 -> 37; matrix products, arithmetic and copies ran while one was open for 20% -> 15% of each run, Pallas kernels for 42% -> 45%
where the time goes in v4:
time: 1090 us; the launch traced here: 1080 us
  Pallas kernels  480 us (44%)
  waiting for transfers between devices  258 us (24%)
  starting transfers between devices  138 us (13%)
  other arithmetic  91.3 us (8%)
  local copies, waits for them, and re-layouts  61.9 us (6%)
  matrix products  32.3 us (3%)
  between operations  16.4 us (2%)
    ppermute x60, waiting for transfers between devices, shift(): return lax.ppermute(a, 'tensor', pairs)  248 us
    pallas_call x6, Pallas kernels, back(): pl.pallas_call(body, grid=(T // bt,), in_specs=ins, out_specs=ospec, out_...  136 us
    ppermute x60, starting transfers between devices, shift(): return lax.ppermute(a, 'tensor', pairs)  132 us
    pallas_call x5, Pallas kernels, outer(): pl.pallas_call(outer_kernel, grid=(count, D // bc), in_specs=ins, out_spe...  111 us
    pallas_call x2, Pallas kernels, units(): pl.pallas_call(functools.partial(units_kernel, fe, first), grid=(T // bt,...  84.3 us
    pallas_call x2, Pallas kernels, lift_back(): pl.pallas_call(lift_kernel, grid=(T // bt,), in_specs=[pl.BlockSpec((bt,...  39.8 us
    convert_element_type x14, other arithmetic, total(): return (mine.astype(F32) + arrived.astype(F32)).astype(BF)  36.7 us
    dot_general x9, matrix products, dot(): lax.dot_general(a, b, (((ca,), (cb,)), ((), ())), preferred_element_type=...  32.1 us
  transfers between devices with their start and end apart: 93, of which 37 were waited for; matrix products, arithmetic and copies ran while one was open for 15% of the time, Pallas kernels for 45%

profile of v4, /device:TPU:0, one launch (start us, length us, event | category | flops | bytes accessed | tf_op | source)
XLA Modules:
  0.0 1077.8 jit_solution(2645013944208687454)
XLA Ops:
  26.6 17.6 %collective-permute-done.1 = bf16[2048,256]{1,0:T(8,128)(2,1)} collective-permute-done((bf16[2048,256]{1,0:T(8,128)(2,1)}, bf16[2048,256]{1,0:T(8,128)(2,1)}, u32[]{:S(2)}, u32[]{:S(2)}) %collective-permute-start.1) | collective-permute-done | bytes 1048608 | tf_op jit(solution)/shard_map/ppermute | solution.py:454
  54.6 24.0 %collective-permute-done.4 = bf16[2048,256]{1,0:T(8,128)(2,1)} collective-permute-done((bf16[2048,256]{1,0:T(8,128)(2,1)}, bf16[2048,256]{1,0:T(8,128)(2,1)}, u32[]{:S(2)}, u32[]{:S(2)}) %collective-permute-start.4) | collective-permute-done | bytes 1048608 | tf_op jit(solution)/shard_map/ppermute | solution.py:454
  88.4 22.7 %collective-permute-done.6 = bf16[2048,256]{1,0:T(8,128)(2,1)} collective-permute-done((bf16[2048,256]{1,0:T(8,128)(2,1)}, bf16[2048,256]{1,0:T(8,128)(2,1)}, u32[]{:S(2)}, u32[]{:S(2)}) %collective-permute-start.6) | collective-permute-done | bytes 1048608 | tf_op jit(solution)/shard_map/ppermute | solution.py:454
  122.9 17.3 %shard_map.306 = (bf16[2048,2048]{1,0:T(8,128)(2,1)}, bf16[2048,2048]{1,0:T(8,128)(2,1)}, f32[2048,1]{1,0:T(8,128)}, f32[2048,1024]{1,0:T(8,128)}) custom-call(s32[8]{0:T(128)} %stack.44.at_ref, bf16[2048,256]{1,0:T(8,128)(2,1)} %refs_0_, bf16[2048,256]{1,0:T(8,128)(2,1)} %collective-permute-done.refs_1_, bf16[2048,256]{1,0:T(8,128)(2,1)} %copy-done.40, ...), custom_call_target="tpu_custom_call" | custom-call | flops 8615100416 | bytes 25165824 | tf_op jit(solution)/shard_map/pallas_call | solution.py:188
  149.4 14.0 %shard_map.307 = (bf16[2048,384]{1,0:T(8,128)(2,1)}, bf16[2048,128]{1,0:T(8,128)(2,1)}, bf16[2048,512]{1,0:T(8,128)(2,1)}, bf16[2048,512]{1,0:T(8,128)(2,1)}, bf...) custom-call(f32[2048,1024]{1,0:T(8,128)} %get-tuple-element.219.proj_ref, bf16[512,512]{1,0:T(8,128)(2,1)} %bitcast.154, ...), custom_call_target="tpu_custom_call" | custom-call | flops 2147483648 | bytes 16384000 | tf_op jit(solution)/shard_map/pallas_call | solution.py:371
  185.4 11.8 %collective-permute-done.16 = bf16[2048,256]{1,0:T(8,128)(2,1)} collective-permute-done((bf16[2048,256]{1,0:T(8,128)(2,1)S(1)}, bf16[2048,256]{1,0:T(8,128)(2,1)}, u32[]{:S(2)}, u32[]{:S(2)}) %collective-permute-start.16) | collective-permute-done | bytes 1048608 | tf_op jit(solution)/shard_map/ppermute | solution.py:454
  220.4 16.1 %collective-permute-done.17 = bf16[256,2048]{1,0:T(8,128)(2,1)} collective-permute-done((bf16[256,2048]{1,0:T(8,128)(2,1)}, bf16[256,2048]{1,0:T(8,128)(2,1)}, u32[]{:S(2)}, u32[]{:S(2)}) %collective-permute-start.17) | collective-permute-done | bytes 1048608 | tf_op jit(solution)/shard_map/ppermute | solution.py:454
  289.2 18.7 %shard_map.309.b_ref = bf16[2048,1536]{1,0:T(8,128)(2,1)} custom-call(bf16[2048,2048]{1,0:T(8,128)(2,1)} %shard_map.308.g_ref.x_ref, bf16[3168,2048]{1,0:T(8,128)(2,1)} %all-gather.7.cloned.1.call-done.w_ref.refs_1_.refs_3_), custom_call_target="tpu_custom_call" | custom-call | flops 12884901888 | bytes 20971520 | tf_op jit(solution)/shard_map/pallas_call | solution.py:85
  316.9 21.1 %shard_map.310.b_ref = bf16[2048,1632]{1,0:T(8,128)(2,1)} custom-call(bf16[2048,2048]{1,0:T(8,128)(2,1)} %shard_map.308.g_ref.x_ref, bf16[3168,2048]{1,0:T(8,128)(2,1)} %all-gather.7.cloned.1.call-done.w_ref.refs_1_.refs_3_), custom_call_target="tpu_custom_call" | custom-call | flops 13690208256 | bytes 21757952 | tf_op jit(solution)/shard_map/pallas_call | solution.py:85
  347.9 19.2 %collective-permute-done.33 = bf16[256,2048]{1,0:T(8,128)(2,1)} collective-permute-done((bf16[256,2048]{1,0:T(8,128)(2,1)}, bf16[256,2048]{1,0:T(8,128)(2,1)}, u32[]{:S(2)}, u32[]{:S(2)}) %collective-permute-start.33) | collective-permute-done | bytes 1048608 | tf_op jit(solution)/shard_map/ppermute | solution.py:454
  375.9 11.6 %shard_map.311 = (bf16[2048,2048]{1,0:T(8,128)(2,1)}, bf16[2048,256]{1,0:T(8,128)(2,1)}, f32[2048,16]{1,0:T(8,128)}, f32[2048,16]{1,0:T(8,128)}) custom-call(s32[8]{0:T(128)} %stack.98.at_ref, s32[1]{0:T(128)} %bitcast.38.col_ref, f32[1,2048]{1,0:T(1,128)} %get-tuple-element.418.gain_ref, bf16[16,2048]{1,0:T(8,128)(2,1)} %slice.261.wr_ref, ...), custom_call_target="tpu_custom_call" | custom-call | flops 25165824 | bytes 16777216 | tf_op jit(solution)/shard_map/pallas_call | solution.py:239
  387.6 39.6 %shard_map.312 = (bf16[3,2048,1536]{2,1,0:T(8,128)(2,1)}, f32[2048,16]{1,0:T(8,128)}) custom-call(bf16[2048,2048]{1,0:T(8,128)(2,1)} %get-tuple-element.242.x_ref, bf16[3072,2048]{1,0:T(8,128)(2,1)} %all-gather.9.cloned.1.call-done.wg_ref.wu_ref.refs_1_.refs_3_, bf16[3072,2048]{1,0:T(8,128)(2,1)} %all-gather.9.cloned.1.call-done.wg_ref.wu_ref.refs_1_.refs_3_, ...), custom_call_target="tpu_custom_call" | custom-call | flops 25769803776 | bytes 46137344 | tf_op jit(solution)/shard_map/pallas_call | solution.py:75
  427.1 33.0 %shard_map.313.refs_0_ = bf16[4608,2048]{1,0:T(8,128)(2,1)} custom-call(bf16[3,2048,1536]{2,1,0:T(8,128)(2,1)} %get-tuple-element.248.s_ref.refs_0_.refs_2_, bf16[2048,2048]{1,0:T(8,128)(2,1)} %get-tuple-element.242.x_ref), custom_call_target="tpu_custom_call" | custom-call | flops 25769803776 | bytes 41943040 | tf_op jit(solution)/shard_map/pallas_call | solution.py:156
  460.1 18.6 %shard_map.314 = bf16[4608,2048]{1,0:T(8,128)(2,1)} custom-call(bf16[3,2048,1536]{2,1,0:T(8,128)(2,1)} %get-tuple-element.248.s_ref.refs_0_.refs_2_, bf16[2048,2048]{1,0:T(8,128)(2,1)} %shard_map.308.g_ref.x_ref, bf16[4608,2048]{1,0:T(8,128)(2,1)} %shard_map.313.refs_0_), custom_call_target="tpu_custom_call", output_to_operand_aliasing={{}: (2, {})} | custom-call | flops 12884901888 | bytes 20971520 | tf_op jit(solution)/shard_map/pallas_call | solution.py:156
  478.8 34.0 %shard_map.315.refs_0_ = f32[2048,2048]{1,0:T(8,128)} custom-call(bf16[3,2048,1536]{2,1,0:T(8,128)(2,1)} %get-tuple-element.248.s_ref.refs_0_.refs_2_, bf16[3072,2048]{1,0:T(8,128)(2,1)} %all-gather.9.cloned.1.call-done.wg_ref.wu_ref.refs_1_.refs_3_, bf16[3,2048,1536]{2,1,0:T(8,128)(2,1)} %get-tuple-element.248.s_ref.refs_0_.refs_2_, ...), custom_call_target="tpu_custom_call" | custom-call | flops 25769803776 | bytes 41943040 | tf_op jit(solution)/shard_map/pallas_call | solution.py:144
  512.8 44.8 %shard_map.316 = (bf16[3,2048,1632]{2,1,0:T(8,128)(2,1)}, f32[2048,16]{1,0:T(8,128)}) custom-call(bf16[2048,2048]{1,0:T(8,128)(2,1)} %get-tuple-element.242.x_ref, bf16[3264,2048]{1,0:T(8,128)(2,1)} %all-gather.11.cloned.1.call-done.wg_ref.wu_ref.refs_2_.refs_4_, bf16[3264,2048]{1,0:T(8,128)(2,1)} %all-gather.11.cloned.1.call-done.wg_ref.wu_ref.refs_2_.refs_4_, ...), custom_call_target="tpu_custom_call" | custom-call | flops 27380416512 | bytes 48496640 | tf_op jit(solution)/shard_map/pallas_call | solution.py:75
  557.6 39.7 %shard_map.317 = bf16[2048,2176]{1,0:T(8,128)(2,1)} custom-call(f32[2048,2048]{1,0:T(8,128)} %shard_map.315.refs_0_, bf16[3,2048,1632]{2,1,0:T(8,128)(2,1)} %get-tuple-element.251.refs_1_.refs_3_.refs_2_.s_ref, bf16[3264,2048]{1,0:T(8,128)(2,1)} %all-gather.11.cloned.1.call-done.wg_ref.wu_ref.refs_2_.refs_4_, ...), custom_call_target="tpu_custom_call" | custom-call | flops 27380416512 | bytes 43515904 | tf_op jit(solution)/shard_map/pallas_call | solution.py:144
  599.9 23.5 %shard_map.318 = bf16[4,2048,256]{2,1,0:T(8,128)(2,1)} custom-call(s32[1]{0:T(128)S(6)} %sub.27.core_ref, bf16[3,2048,1536]{2,1,0:T(8,128)(2,1)} %get-tuple-element.248.s_ref.refs_0_.refs_2_, bf16[3168,2048]{1,0:T(8,128)(2,1)} %all-gather.7.cloned.1.call-done.w_ref.refs_1_.refs_3_, bf16[3,2048,1632]{2,1,0:T(8,128)(2,1)} %get-tuple-element.251.refs_1_.refs_3_.refs_2_.s_ref, ...), custom_call_target="tpu_custom_call" | custom-call | flops 13287555072 | bytes 42729472 | tf_op jit(solution)/shard_map/pallas_call | solution.py:144
  633.1 19.7 %shard_map.319.refs_0_ = bf16[4896,2048]{1,0:T(8,128)(2,1)} custom-call(bf16[3,2048,1632]{2,1,0:T(8,128)(2,1)} %get-tuple-element.251.refs_1_.refs_3_.refs_2_.s_ref, bf16[2048,2048]{1,0:T(8,128)(2,1)} %get-tuple-element.242.x_ref), custom_call_target="tpu_custom_call" | custom-call | flops 13690208256 | bytes 21757952 | tf_op jit(solution)/shard_map/pallas_call | solution.py:156
  664.7 19.6 %shard_map.320.refs_0_ = bf16[4896,2048]{1,0:T(8,128)(2,1)} custom-call(bf16[3,2048,1632]{2,1,0:T(8,128)(2,1)} %get-tuple-element.251.refs_1_.refs_3_.refs_2_.s_ref, bf16[2048,2048]{1,0:T(8,128)(2,1)} %get-tuple-element.242.x_ref, bf16[4896,2048]{1,0:T(8,128)(2,1)} %shard_map.319.refs_0_), custom_call_target="tpu_custom_call", output_to_operand_aliasing={{}: (2, {})} | custom-call | flops 13690208256 | bytes 21757952 | tf_op jit(solution)/shard_map/pallas_call | solution.py:156
  698.1 19.8 %shard_map.321 = bf16[4896,2048]{1,0:T(8,128)(2,1)} custom-call(bf16[3,2048,1632]{2,1,0:T(8,128)(2,1)} %get-tuple-element.251.refs_1_.refs_3_.refs_2_.s_ref, bf16[2048,2048]{1,0:T(8,128)(2,1)} %shard_map.308.g_ref.x_ref, bf16[4896,2048]{1,0:T(8,128)(2,1)} %shard_map.320.refs_0_), custom_call_target="tpu_custom_call", output_to_operand_aliasing={{}: (2, {})} | custom-call | flops 13690208256 | bytes 21757952 | tf_op jit(solution)/shard_map/pallas_call | solution.py:156
  734.8 22.3 %shard_map.322 = bf16[4,2048,256]{2,1,0:T(8,128)(2,1)} custom-call(s32[1]{0:T(128)} %bitcast.42.core_ref, bf16[3,2048,1536]{2,1,0:T(8,128)(2,1)} %get-tuple-element.248.s_ref.refs_0_.refs_2_, bf16[3168,2048]{1,0:T(8,128)(2,1)} %all-gather.7.cloned.1.call-done.w_ref.refs_1_.refs_3_, bf16[3,2048,1632]{2,1,0:T(8,128)(2,1)} %get-tuple-element.251.refs_1_.refs_3_.refs_2_.s_ref, ...), custom_call_target="tpu_custom_call" | custom-call | flops 13287555072 | bytes 42729472 | tf_op jit(solution)/shard_map/pallas_call | solution.py:144
  798.3 14.3 %collective-permute-done.52 = bf16[256,2048]{1,0:T(8,128)(2,1)S(1)} collective-permute-done((bf16[256,2048]{1,0:T(8,128)(2,1)S(1)}, bf16[256,2048]{1,0:T(8,128)(2,1)S(1)}, u32[]{:S(2)}, u32[]{:S(2)}) %collective-permute-start.52) | collective-permute-done | bytes 1048608 | tf_op jit(solution)/shard_map/ppermute | solution.py:454
  841.3 18.0 %shard_map.324 = (bf16[2048,384]{1,0:T(8,128)(2,1)}, bf16[2048,512]{1,0:T(8,128)(2,1)}, f32[2048,128]{1,0:T(8,128)}, f32[2048,1]{1,0:T(8,128)}) custom-call(bf16[2048,384]{1,0:T(8,128)(2,1)} %get-tuple-element.280.q_ref, bf16[2048,128]{1,0:T(8,128)(2,1)} %get-tuple-element.281.kr_ref, bf16[2048,512]{1,0:T(8,128)(2,1)} %get-tuple-element.282.kv_ref, ...), custom_call_target="tpu_custom_call" | custom-call | flops 5872025600 | bytes 12288000 | tf_op jit(solution)/shard_map/pallas_call | solution.py:420
  (482 shorter events, 520.6 us)
Async XLA Ops:
  7.2 114.2 %all-gather.5.cloned.1.call-start = ((), (), s32[]{:S(2)}) async-start(), calls=%async_computation.4 | async-start | bytes 7372800 | tf_op jit(solution)/shard_map/all_gather | solution.py:546
  16.5 272.7 %all-gather.7.cloned.1.call-start = ((), (), s32[]{:S(2)}) async-start(), calls=%async_computation.5 | async-start | bytes 16220160 | tf_op jit(solution)/shard_map/all_gather | solution.py:546
  16.5 27.7 %collective-permute-start.1 = (bf16[2048,256]{1,0:T(8,128)(2,1)}, bf16[2048,256]{1,0:T(8,128)(2,1)}, u32[]{:S(2)}, u32[]{:S(2)}) collective-permute-start(bf16[2048,256]{1,0:T(8,128)(2,1)} %refs_0_), channel_id=1, source_target_pairs={{0,2},{1,3},{2,4},{3,5},{4,6},{5,7},{8,10},{9,11},{10,12},{11,13},... | collective-permute-start | bytes 3145736 | tf_op jit(solution)/shard_map/ppermute | solution.py:454
  49.3 338.2 %all-gather.9.cloned.1.call-start = ((), (), s32[]{:S(2)}) async-start(), calls=%async_computation.6 | async-start | bytes 15728640 | tf_op jit(solution)/shard_map/all_gather | solution.py:546
  78.7 434.2 %all-gather.11.cloned.1.call-start = ((), (), s32[]{:S(2)}) async-start(), calls=%async_computation.8 | async-start | bytes 16711680 | tf_op jit(solution)/shard_map/all_gather | solution.py:546
  78.7 35.8 %collective-permute-start = (bf16[2048,256]{1,0:T(8,128)(2,1)}, bf16[2048,256]{1,0:T(8,128)(2,1)}, u32[]{:S(2)}, u32[]{:S(2)}) collective-permute-start(bf16[2048,256]{1,0:T(8,128)(2,1)} %refs_0_), channel_id=1, source_target_pairs={{0,1},{1,0},{2,3},{3,2},{4,5},{5,4},{6,7},{7,6},{8,9},{9,8},{10,11... | collective-permute-start | bytes 3145736 | tf_op jit(solution)/shard_map/ppermute | solution.py:445
  83.4 27.7 %collective-permute-start.6 = (bf16[2048,256]{1,0:T(8,128)(2,1)}, bf16[2048,256]{1,0:T(8,128)(2,1)}, u32[]{:S(2)}, u32[]{:S(2)}) collective-permute-start(bf16[2048,256]{1,0:T(8,128)(2,1)} %collective-permute-done.4), channel_id=1, source_target_pairs={{2,0},{3,1},{10,8},{11,9},{18,16},{19,17},{26,24},{27,25}} | collective-permute-start | bytes 3145736 | tf_op jit(solution)/shard_map/ppermute | solution.py:454
  167.9 557.0 %reduce-scatter.5.cloned.1.call-start = ((), (), s32[]{:S(2)}) async-start(), calls=%async_computation.7 | async-start | bytes 23592960 | tf_op jit(solution)/shard_map/reduce_scatter | solution.py:550
  218.9 33.7 %collective-permute-start.23 = (bf16[2048,256]{1,0:T(8,128)(2,1)}, bf16[2048,256]{1,0:T(8,128)(2,1)}, u32[]{:S(2)}, u32[]{:S(2)}) collective-permute-start(bf16[2048,256]{1,0:T(8,128)(2,1)} %refs_0_.1), channel_id=1, source_target_pairs={{0,1},{1,0},{2,3},{3,2},{4,5},{5,4},{6,7},{7,6},{8,9},{9,8},{10,11... | collective-permute-start | bytes 3145736 | tf_op jit(solution)/shard_map/ppermute | solution.py:445
  345.0 30.9 %collective-permute-start.27 = (bf16[256,2048]{1,0:T(8,128)(2,1)S(1)}, bf16[256,2048]{1,0:T(8,128)(2,1)}, u32[]{:S(2)}, u32[]{:S(2)}) collective-permute-start(bf16[256,2048]{1,0:T(8,128)(2,1)S(1)} %get-tuple-element.417.refs_0_), channel_id=1, source_target_pairs={{0,1},{1,0},{2,3},{3,2},{4,5},{5,4},{6,7},{7,6},{8,9},{9,8},{10,11... | collective-permute-start | bytes 3145736 | tf_op jit(solution)/shard_map/ppermute | solution.py:445
  346.5 29.4 %collective-permute-start.35 = (bf16[256,2048]{1,0:T(8,128)(2,1)S(1)}, bf16[256,2048]{1,0:T(8,128)(2,1)}, u32[]{:S(2)}, u32[]{:S(2)}) collective-permute-start(bf16[256,2048]{1,0:T(8,128)(2,1)S(1)} %broadcast_select_fusion.3.refs_4_), channel_id=1, source_target_pairs={{0,1},{1,0},{2,3},{3,2},{4,5},{5,4},{6,7},{7,6},{8,9},{9,8},{10,11... | collective-permute-start | bytes 3145736 | tf_op jit(solution)/shard_map/ppermute | solution.py:445
  478.7 511.4 %reduce-scatter.7.cloned.1.call-start = ((), (), s32[]{:S(2)}) async-start(), calls=%async_computation.9 | async-start | bytes 25067520 | tf_op jit(solution)/shard_map/reduce_scatter | solution.py:550
  652.8 69.7 %collective-permute-start.44 = (bf16[4,2048,256]{2,1,0:T(8,128)(2,1)}, bf16[4,2048,256]{2,1,0:T(8,128)(2,1)}, u32[]{:S(2)}, u32[]{:S(2)}) collective-permute-start(bf16[4,2048,256]{2,1,0:T(8,128)(2,1)} %shard_map.318), channel_id=1, source_target_pairs={{0,1},{1,0},{2,3},{3,2},{4,5},{5,4},{6,7},{7,6},{8,9},{9,8},{10,11... | collective-permute-start | bytes 12582920 | tf_op jit(solution)/shard_map/ppermute | solution.py:445
  658.7 27.7 %collective-permute-start.40 = (bf16[256,2176]{1,0:T(8,128)(2,1)}, bf16[256,2176]{1,0:T(8,128)(2,1)S(1)}, u32[]{:S(2)}, u32[]{:S(2)}) collective-permute-start(bf16[256,2176]{1,0:T(8,128)(2,1)} %get-tuple-element.433), channel_id=1, source_target_pairs={{0,2},{1,3},{2,4},{3,5},{8,10},{9,11},{10,12},{11,13},{16,18},{17,... | collective-permute-start | bytes 3342344 | tf_op jit(solution)/shard_map/ppermute | solution.py:454
  690.4 28.1 %collective-permute-start.42 = (bf16[256,2176]{1,0:T(8,128)(2,1)}, bf16[256,2176]{1,0:T(8,128)(2,1)S(1)}, u32[]{:S(2)}, u32[]{:S(2)}) collective-permute-start(bf16[256,2176]{1,0:T(8,128)(2,1)} %get-tuple-element.431), channel_id=1, source_target_pairs={{0,2},{1,3},{2,4},{3,5},{4,6},{5,7},{8,10},{9,11},{10,12},{11,13},... | collective-permute-start | bytes 3342344 | tf_op jit(solution)/shard_map/ppermute | solution.py:454
  724.9 297.0 %reduce-scatter.11.cloned.1.call-start = ((), (), s32[]{:S(2)}) async-start(), calls=%async_computation.11 | async-start | bytes 3932160 | tf_op jit(solution)/shard_map/reduce_scatter | solution.py:550
  797.5 29.2 %collective-permute-start.57 = (bf16[256,2048]{1,0:T(8,128)(2,1)}, bf16[256,2048]{1,0:T(8,128)(2,1)S(1)}, u32[]{:S(2)}, u32[]{:S(2)}) collective-permute-start(bf16[256,2048]{1,0:T(8,128)(2,1)} %fusion.3.refs_0_), channel_id=1, source_target_pairs={{0,1},{1,0},{2,3},{3,2},{4,5},{5,4},{6,7},{7,6},{8,9},{9,8},{10,11... | collective-permute-start | bytes 3145736 | tf_op jit(solution)/shard_map/ppermute | solution.py:445
  797.8 31.4 %collective-permute-start.59 = (bf16[256,2048]{1,0:T(8,128)(2,1)S(1)}, bf16[256,2048]{1,0:T(8,128)(2,1)S(1)}, u32[]{:S(2)}, u32[]{:S(2)}) collective-permute-start(bf16[256,2048]{1,0:T(8,128)(2,1)S(1)} %broadcast_select_fusion.2.refs_4_), channel_id=1, source_target_pairs={{0,1},{1,0},{2,3},{3,2},{4,5},{5,4},{6,7},{7,6},{8,9},{9,8},{10,11... | collective-permute-start | bytes 3145736 | tf_op jit(solution)/shard_map/ppermute | solution.py:445
  817.4 42.0 %collective-permute-start.55 = (bf16[2048,256]{1,0:T(8,128)(2,1)}, bf16[2048,256]{1,0:T(8,128)(2,1)}, u32[]{:S(2)}, u32[]{:S(2)}) collective-permute-start(bf16[2048,256]{1,0:T(8,128)(2,1)} %get-tuple-element.443), channel_id=1, source_target_pairs={{0,2},{1,3},{2,4},{3,5},{4,6},{5,7},{8,10},{9,11},{10,12},{11,13},... | collective-permute-start | bytes 3145736 | tf_op jit(solution)/shard_map/ppermute | solution.py:454
  826.7 32.6 %collective-permute-start.56 = (bf16[2048,256]{1,0:T(8,128)(2,1)}, bf16[2048,256]{1,0:T(8,128)(2,1)}, u32[]{:S(2)}, u32[]{:S(2)}) collective-permute-start(bf16[2048,256]{1,0:T(8,128)(2,1)} %get-tuple-element.442), channel_id=1, source_target_pairs={{2,0},{3,1},{4,2},{5,3},{6,4},{7,5},{10,8},{11,9},{12,10},{13,11},... | collective-permute-start | bytes 3145736 | tf_op jit(solution)/shard_map/ppermute | solution.py:454
  941.4 125.1 %reduce-scatter.9.cloned.1.call-start = ((), (), s32[]{:S(2)}) async-start(), calls=%async_computation.10 | async-start | bytes 3440640 | tf_op jit(solution)/shard_map/reduce_scatter | solution.py:550
  959.7 30.4 %collective-permute-start.81 = (bf16[256,640]{1,0:T(8,128)(2,1)S(1)}, bf16[256,640]{1,0:T(8,128)(2,1)S(1)}, u32[]{:S(2)}, u32[]{:S(2)}) collective-permute-start(bf16[256,640]{1,0:T(8,128)(2,1)S(1)} %broadcast_select_fusion.13.refs_4_), channel_id=1, source_target_pairs={{0,1},{1,0},{2,3},{3,2},{4,5},{5,4},{6,7},{7,6},{8,9},{9,8},{10,11... | collective-permute-start | bytes 983048 | tf_op jit(solution)/shard_map/ppermute | solution.py:445
  979.6 36.1 %collective-permute-start.77 = (bf16[2048,256]{1,0:T(8,128)(2,1)}, bf16[2048,256]{1,0:T(8,128)(2,1)S(1)}, u32[]{:S(2)}, u32[]{:S(2)}) collective-permute-start(bf16[2048,256]{1,0:T(8,128)(2,1)} %get-tuple-element.439), channel_id=1, source_target_pairs={{0,2},{1,3},{2,4},{3,5},{8,10},{9,11},{10,12},{11,13},{16,18},{17,... | collective-permute-start | bytes 3145736 | tf_op jit(solution)/shard_map/ppermute | solution.py:454
  984.1 31.6 %collective-permute-start.78 = (bf16[2048,256]{1,0:T(8,128)(2,1)}, bf16[2048,256]{1,0:T(8,128)(2,1)}, u32[]{:S(2)}, u32[]{:S(2)}) collective-permute-start(bf16[2048,256]{1,0:T(8,128)(2,1)} %get-tuple-element.438), channel_id=1, source_target_pairs={{4,2},{5,3},{6,4},{7,5},{12,10},{13,11},{14,12},{15,13},{20,18},{2... | collective-permute-start | bytes 3145736 | tf_op jit(solution)/shard_map/ppermute | solution.py:454
  (148 other events, 2111.6 us)
Sparse Core Ops, SparseCore 0:
  16.6 69.4 all-gather.4
  88.5 125.6 all-gather.6
  216.0 122.3 all-gather.8
  340.7 128.9 all-gather.10
  478.9 169.8 reduce-scatter.4
  725.0 178.3 reduce-scatter.6
  941.5 41.4 reduce-scatter.10
  1015.9 39.3 reduce-scatter.8

commit v5 on v4

--- a/solution.py
+++ b/solution.py
@@ -163,7 +163,8 @@
     pieces=refs[:2*chips]
     refs=refs[2*chips:]
     if norm:
-        gain_ref, w_ref, out_ref, round_ref, r_ref, proj_ref = refs
+        gain_ref, w_ref = refs[:2]
+        out_ref, round_ref, r_ref, proj_ref = refs[-4:]
     else:
         (out_ref,) = refs
     w=pieces[0].shape[1]
@@ -176,17 +177,22 @@
         r_ref[...]=r
         proj_ref[...]=mm(round_ref[...],w_ref[...],NT)
 
-def place_columns(pieces, at, gain=None, packed=None, count=0, bt=256):
+def place_columns(pieces, at, gain=None, packed=None, count=0, rows=None, first=0, into=(), bt=256):
     T,w=pieces[0].shape; n=len(pieces)
+    total_rows=rows or T
+    start=first//bt
     ins=[pl.BlockSpec(memory_space=pltpu.SMEM)]+[pl.BlockSpec((bt,w),lambda i:(i,0))]*n
     args=[at]+list(pieces)
-    outs=[jax.ShapeDtypeStruct((T,n*w),BF)]; specs=[pl.BlockSpec((bt,n*w),lambda i:(i,0))]
+    wides=[(n*w,BF)]
     if gain is not None:
         ins+=[pl.BlockSpec((1,n*w),lambda i:(0,0)),rows_once(count,n*w,0)]; args+=[gain[None],packed]
-        outs+=[jax.ShapeDtypeStruct((T,n*w),BF),jax.ShapeDtypeStruct((T,1),F32),jax.ShapeDtypeStruct((T,count),F32)]
-        specs+=[pl.BlockSpec((bt,n*w),lambda i:(i,0)),pl.BlockSpec((bt,1),lambda i:(i,0)),pl.BlockSpec((bt,count),lambda i:(i,0))]
+        wides+=[(n*w,BF),(1,F32),(count,F32)]
+    aliases={len(args)+k:k for k in range(len(into))}
+    ins+=[pl.BlockSpec(memory_space=pl.ANY)]*len(into); args+=list(into)
     return pl.pallas_call(functools.partial(place_columns_kernel,n//2,gain is not None),grid=(T//bt,),
-        in_specs=ins,out_specs=specs,out_shape=outs,compiler_params=params(1),
+        in_specs=ins,out_specs=[pl.BlockSpec((bt,m),lambda i:(i+start,0)) for m,_ in wides],
+        out_shape=[jax.ShapeDtypeStruct((total_rows,m),d) for m,d in wides],
+        input_output_aliases=aliases,compiler_params=params(1),
         cost_estimate=pl.CostEstimate(flops=(6+2*count)*T*n*w,bytes_accessed=6*T*n*w,transcendentals=T))(*args)
 
 def place_rows_kernel(n, times, at_ref, *refs):
@@ -336,7 +342,8 @@
     col=lax.broadcasted_iota(jnp.int32,s.shape,1)
     return jnp.where(col<=row,s,-1e30)
 
-def attend_kernel(heads, proj_ref, up_ref, gain_ref, cos_ref, sin_ref, q_ref, kr_ref, kv_ref, latent_ref, mixed_ref, lse_ref):
+def attend_kernel(heads, proj_ref, up_ref, gain_ref, cos_ref, sin_ref, *refs):
+    q_ref, kr_ref, kv_ref, latent_ref, mixed_ref, lse_ref = refs[-6:]
     content=heads*DN
     at=content+DN
     q_ref[:,:content]=proj_ref[:,:content].astype(BF)
@@ -362,17 +369,18 @@
             mixed_ref[a:b,h*DV:(h+1)*DV]=mm(p,v[:b],NN).astype(BF)
             lse_ref[a:b,h:h+1]=m+jnp.log(t)
 
-def attend(proj, up, gain, cosine, sine, heads):
+def attend(proj, up, gain, cosine, sine, heads, sequence, into=()):
     T=proj.shape[0]; wide=proj.shape[1]
-    def rows(n): return pl.BlockSpec((LEN,n),lambda i:(i,0))
+    def rows(n): return pl.BlockSpec((LEN,n),lambda i:(sequence,0))
     def whole(a): return pl.BlockSpec(a.shape,lambda i:(0,0))
     qn=heads*DN+DN
     outs=[(qn,BF),(DN,BF),(heads*(DN+DV),BF),(R,BF),(heads*DV,BF),(heads,F32)]
-    return pl.pallas_call(functools.partial(attend_kernel,heads),grid=(T//LEN,),
-        in_specs=[rows(wide),whole(up),whole(gain),whole(cosine),whole(sine)],
+    args=[proj,up,gain,cosine,sine]
+    return pl.pallas_call(functools.partial(attend_kernel,heads),grid=(1,),
+        in_specs=[rows(wide)]+[whole(a) for a in args[1:]]+[pl.BlockSpec(memory_space=pl.ANY)]*len(into),
         out_specs=[rows(n) for n,_ in outs],out_shape=[jax.ShapeDtypeStruct((T,n),d) for n,d in outs],
-        compiler_params=params(1),
-        cost_estimate=pl.CostEstimate(flops=T*LEN*heads*512,bytes_accessed=T*8000,transcendentals=T*LEN*heads//2))(proj,up,gain,cosine,sine)
+        input_output_aliases={len(args)+k:k for k in range(len(into))},compiler_params=params(1),
+        cost_estimate=pl.CostEstimate(flops=LEN*LEN*heads*512,bytes_accessed=LEN*8000,transcendentals=LEN*LEN*heads//2))(*args,*into)
 
 def attend_back_kernel(heads, q_ref, kr_ref, kv_ref, mixed_ref, lse_ref, do_ref, cos_ref, sin_ref, dq_ref, dkv_ref, dkr_ref, dot_ref, dk_acc, dv_acc):
     content=heads*DN
@@ -619,7 +627,7 @@
     last_step = line.chips - 1
     gate = expert_gate.transpose(0, 2, 1).reshape(E * fe, wide)
     up = expert_up.transpose(0, 2, 1).reshape(E * fe, wide)
-    move = Gather(line, layer_input)
+    move = Gather(line, layer_input[:LEN])
     downs, early, late = steps(move, 3, (
         lambda: jnp.concatenate([expert_down.reshape(E * fe, wide), shared_down], axis=0),
         lambda: jnp.concatenate([gate[:n0], up[:n0]], axis=0),
@@ -630,15 +638,31 @@
 
     tile = 256
     core = line.c.reshape(1).astype(jnp.int32)
-    input_pieces, input_at = line.column_pieces(move.result())
-    input_pieces, cotangent = lax.optimization_barrier((input_pieces, cotangent))
+    placed, attended = (), ()
+
+    def place(move, sequence):
+        pieces, at = line.column_pieces(move.result())
+        return place_columns(
+            pieces, at, first_g, attend_packed, queries_wide + latent_wide, number, sequence * LEN, placed
+        )
+
+    def attention(sequence):
+        return attend(placed[3], wup, latent_g[None], cosine, sine, heads_here, sequence, attended)
+
+    for sequence in range(1, number // LEN):
+        ahead, after = move, layer_input[sequence * LEN : (sequence + 1) * LEN]
+        ahead.left[-1], ahead.right[-1], after = lax.optimization_barrier((ahead.left[-1], ahead.right[-1], after))
+        move = Gather(line, after)
+        beside([move])
+        placed = beside([move], lambda: place(ahead, sequence - 1))
+        steps(move, last_step - 3)
+        attended = beside([move], lambda: attention(sequence - 1))
+    move.left[-1], move.right[-1], cotangent = lax.optimization_barrier((move.left[-1], move.right[-1], cotangent))
     grad_move = Gather(line, cotangent)
-
-    def project():
-        return place_columns(input_pieces, input_at, first_g, attend_packed, queries_wide + latent_wide)
-
-    rows, first_round, r1, proj = beside([grad_move], project)
-    q, kr, kv, latent, mixed, log_total = attend(proj, wup, latent_g[None], cosine, sine, heads_here)
+    placed = place(move, number // LEN - 1)
+    attended = beside([grad_move], lambda: attention(number // LEN - 1))
+    rows, first_round, r1, proj = placed
+    q, kr, kv, latent, mixed, log_total = attended
     mine, theirs = line.halves(mixed)
     arrived = line.swap(dot(theirs, wo, 1, 0, BF))
     move = line.row_scatter(total(dot(mine, wo, 1, 0, BF), arrived))
@@ -666,28 +690,20 @@
     deltas = outer(stack0, 2, 1, grad, 3 * n0, 2, deltas)
     deltas, stack0 = lax.optimization_barrier((deltas, stack0))
     early_sums = scatter_rows(deltas)
-    second_terms = back([(stack0, 0, early, n0, 0), (stack0, 1, early, n0, n0)], None, F32, tile)
     stack1, pair1 = units(second_round, late, back1, weight, fe, n0, tile)
     second_terms = back(
-        [(stack1, 0, late, n1, 0), (stack1, 1, late, n1, n1)], second_terms, BF, tile, (pair0, pair1)
+        [(stack0, 0, early, n0, 0), (stack0, 1, early, n0, n0), (stack1, 0, late, n1, 0), (stack1, 1, late, n1, n1)],
+        None, BF, tile, (pair0, pair1),
     )
 
     branch_terms = [(stack0, 2, downs, n0, 0), (stack1, 2, downs, n1, n0)]
     mine, theirs = line.halves(second_terms)
-    arrived, branch_theirs = lax.optimization_barrier(
-        (line.swap(theirs), back(branch_terms, None, BF, tile, (), 1 - core, line.chips))
-    )
-    move = line.row_scatter(total(mine, arrived))
+    move = line.row_scatter(total(mine, line.swap(theirs)))
     deltas = beside([move], lambda: outer(stack1, 0, 1, second_round, 3 * n1, 0))
     deltas = beside([move], lambda: outer(stack1, 1, 1, second_round, 3 * n1, 1, deltas))
-    branch_arrived = line.swap(branch_theirs)
-    deltas, branch_arrived = beside(
-        [move], lambda: (outer(stack1, 2, 1, grad, 3 * n1, 2, deltas), branch_arrived)
-    )
+    branch_theirs = beside([move], lambda: back(branch_terms, None, BF, tile, (), 1 - core, line.chips))
     steps(move, last_step - 3)
     summed = move.result()
-    early_sums, summed, deltas = lax.optimization_barrier((early_sums, summed, deltas))
-    late_sums = scatter_rows(deltas)
 
     def own_rows(a):
         return lax.dynamic_slice_in_dim(a, row_start, row_count, 0)
@@ -701,11 +717,15 @@
     vgd = jnp.mean(v2 * second_g * d2, axis=-1, keepdims=True)
     hidden_delta = own_rows(grad).astype(F32) + r2 * second_g * d2 - v2 * (r2**3) * vgd
     move = Gather(line, hidden_delta.astype(BF))
-    branch_mine = beside([move], lambda: back(branch_terms, None, BF, tile, (), core, line.chips))
+    branch_mine, branch_arrived = beside([move], lambda: (
+        back(branch_terms, None, BF, tile, (), core, line.chips), line.swap(branch_theirs)
+    ))
     branch_move = line.column_scatter(total(branch_mine, branch_arrived))
-    router_delta, second_gain_delta = beside([move, branch_move], lambda: (
-        dot(x2, logits_delta.astype(BF), 0, 0), jnp.sum(d2 * v2 * r2, axis=0)
-    ))
+    deltas = beside([move, branch_move], lambda: outer(stack1, 2, 1, grad, 3 * n1, 2, deltas))
+    router_delta = dot(x2, logits_delta.astype(BF), 0, 0)
+    second_gain_delta = jnp.sum(d2 * v2 * r2, axis=0)
+    early_sums, deltas, move.left[-1] = lax.optimization_barrier((early_sums, deltas, move.left[-1]))
+    late_sums = scatter_rows(deltas)
     for _ in range(last_step - 2):
         beside([move, branch_move])
     delta_pieces, delta_at = line.row_pieces(move.result())
@@ -738,18 +758,16 @@
         lambda: back(first_terms, None, BF, tile, (), 1 - core, line.chips),
         lambda: back(first_terms, None, BF, tile, (), core, line.chips),
     ))
-    steps(move, last_step - 2)
-    small, theirs, mine, layer_output = lax.optimization_barrier(
-        (move.result().astype(BF), theirs, mine, layer_output)
+    arrived = beside([move], lambda: line.swap(theirs))
+    steps(move, last_step - 3)
+    small, both, layer_output = lax.optimization_barrier(
+        (move.result().astype(BF), total(mine, arrived), layer_output)
     )
     move = Gather(line, small)
-    deltas, arrived = beside([move], lambda: (attend_deltas(), line.swap(theirs)))
+    first_move = line.column_scatter(both)
+    deltas = beside([move, first_move], attend_deltas)
     attend_sums = scatter_rows(deltas).astype(F32)
-    steps(move, last_step - 2)
-    both, ahead = lax.optimization_barrier((total(mine, arrived), (move.left[-1], move.right[-1])))
-    move.left[-1], move.right[-1] = ahead
-    first_move = line.column_scatter(both)
-    beside([move, first_move])
+    steps(move, last_step - 1)
     small_pieces, small_at = line.row_pieces(move.result())
     small_pieces, late_sums = lax.optimization_barrier((small_pieces, late_sums))
     wld = wproj[queries_wide:]

time: 1090 us -> 1090 us (level)
  waiting for transfers between devices: 258 us -> 235 us
  starting transfers between devices: 138 us -> 151 us
    ppermute x60 -> x66, waiting for transfers between devices: 248 us -> 217 us  [shift(): return lax.ppermute(a, 'tensor', pairs)]
    ppermute x60 -> x66, starting transfers between devices: 132 us -> 146 us  [shift(): return lax.ppermute(a, 'tensor', pairs)]
    pallas_call x6 -> x5, Pallas kernels: 136 us -> 131 us  [back(): pl.pallas_call(body, grid=(T // bt,), in_specs=ins, out_specs=ospec, out_...]
    pallas_call x2 -> x3, Pallas kernels: 26.4 us -> 30.8 us  [place_columns(): pl.pallas_call(functools.partial(place_columns_kernel, n // 2, gain is no...]
    unnamed x171 -> x185, local copies, waits for them, and re-layouts: 24.9 us -> 27.9 us
  transfers between devices with their start and end apart: 93 -> 103, of which waited for: 37 -> 36; matrix products, arithmetic and copies ran while one was open for 15% -> 15% of each run, Pallas kernels for 45% -> 45%
where the time goes in v5:
time: 1090 us; the launch traced here: 1080 us
  Pallas kernels  483 us (44%)
  waiting for transfers between devices  235 us (22%)
  starting transfers between devices  151 us (14%)
  other arithmetic  96.9 us (9%)
  local copies, waits for them, and re-layouts  65.6 us (6%)
  matrix products  28.7 us (3%)
  between operations  16.6 us (2%)
    ppermute x66, waiting for transfers between devices, shift(): return lax.ppermute(a, 'tensor', pairs)  217 us
    ppermute x66, starting transfers between devices, shift(): return lax.ppermute(a, 'tensor', pairs)  146 us
    pallas_call x5, Pallas kernels, back(): pl.pallas_call(body, grid=(T // bt,), in_specs=ins, out_specs=ospec, out_...  131 us
    pallas_call x5, Pallas kernels, outer(): pl.pallas_call(outer_kernel, grid=(count, D // bc), in_specs=ins, out_spe...  111 us
    pallas_call x2, Pallas kernels, units(): pl.pallas_call(functools.partial(units_kernel, fe, first), grid=(T // bt,...  84.3 us
    pallas_call x2, Pallas kernels, lift_back(): pl.pallas_call(lift_kernel, grid=(T // bt,), in_specs=[pl.BlockSpec((bt,...  39.8 us
    convert_element_type x14, other arithmetic, total(): return (mine.astype(F32) + arrived.astype(F32)).astype(BF)  36.9 us
    pallas_call x3, Pallas kernels, place_columns(): pl.pallas_call(functools.partial(place_columns_kernel, n // 2, gain is no...  30.8 us
  transfers between devices with their start and end apart: 103, of which 36 were waited for; matrix products, arithmetic and copies ran while one was open for 15% of the time, Pallas kernels for 45%

profile of v5, /device:TPU:0, one launch (start us, length us, event | category | flops | bytes accessed | tf_op | source)
XLA Modules:
  0.0 1076.9 jit_solution(6211725716874109036)
XLA Ops:
  44.2 12.9 %collective-permute-done.3 = bf16[1024,256]{1,0:T(8,128)(2,1)} collective-permute-done((bf16[1024,256]{1,0:T(8,128)(2,1)S(1)}, bf16[1024,256]{1,0:T(8,128)(2,1)}, u32[]{:S(2)}, u32[]{:S(2)}) %collective-permute-start.3) | collective-permute-done | bytes 524320 | tf_op jit(solution)/shard_map/ppermute | solution.py:462
  64.4 11.5 %collective-permute-done.5 = bf16[1024,256]{1,0:T(8,128)(2,1)S(1)} collective-permute-done((bf16[1024,256]{1,0:T(8,128)(2,1)}, bf16[1024,256]{1,0:T(8,128)(2,1)S(1)}, u32[]{:S(2)}, u32[]{:S(2)}) %collective-permute-start.5) | collective-permute-done | bytes 524320 | tf_op jit(solution)/shard_map/ppermute | solution.py:462
  181.3 11.1 %collective-permute-done.26 = bf16[2048,256]{1,0:T(8,128)(2,1)} collective-permute-done((bf16[2048,256]{1,0:T(8,128)(2,1)}, bf16[2048,256]{1,0:T(8,128)(2,1)}, u32[]{:S(2)}, u32[]{:S(2)}) %collective-permute-start.26) | collective-permute-done | bytes 1048608 | tf_op jit(solution)/shard_map/ppermute | solution.py:462
  216.5 15.8 %collective-permute-done.27 = bf16[256,2048]{1,0:T(8,128)(2,1)} collective-permute-done((bf16[256,2048]{1,0:T(8,128)(2,1)}, bf16[256,2048]{1,0:T(8,128)(2,1)}, u32[]{:S(2)}, u32[]{:S(2)}) %collective-permute-start.27) | collective-permute-done | bytes 1048608 | tf_op jit(solution)/shard_map/ppermute | solution.py:462
  262.2 11.6 %collective-permute-done.31 = bf16[256,2048]{1,0:T(8,128)(2,1)} collective-permute-done((bf16[256,2048]{1,0:T(8,128)(2,1)}, bf16[256,2048]{1,0:T(8,128)(2,1)}, u32[]{:S(2)}, u32[]{:S(2)}) %collective-permute-start.31) | collective-permute-done | bytes 1048608 | tf_op jit(solution)/shard_map/ppermute | solution.py:462
  287.1 18.7 %shard_map.311.b_ref = bf16[2048,1536]{1,0:T(8,128)(2,1)} custom-call(bf16[2048,2048]{1,0:T(8,128)(2,1)} %shard_map.310.g_ref.x_ref, bf16[3168,2048]{1,0:T(8,128)(2,1)} %all-gather.7.cloned.1.call-done.w_ref.refs_1_.refs_3_), custom_call_target="tpu_custom_call" | custom-call | flops 12884901888 | bytes 20971520 | tf_op jit(solution)/shard_map/pallas_call | solution.py:85
  314.8 21.1 %shard_map.312.b_ref = bf16[2048,1632]{1,0:T(8,128)(2,1)} custom-call(bf16[2048,2048]{1,0:T(8,128)(2,1)} %shard_map.310.g_ref.x_ref, bf16[3168,2048]{1,0:T(8,128)(2,1)} %all-gather.7.cloned.1.call-done.w_ref.refs_1_.refs_3_), custom_call_target="tpu_custom_call" | custom-call | flops 13690208256 | bytes 21757952 | tf_op jit(solution)/shard_map/pallas_call | solution.py:85
  345.7 19.3 %collective-permute-done.43 = bf16[256,2048]{1,0:T(8,128)(2,1)} collective-permute-done((bf16[256,2048]{1,0:T(8,128)(2,1)}, bf16[256,2048]{1,0:T(8,128)(2,1)}, u32[]{:S(2)}, u32[]{:S(2)}) %collective-permute-start.43) | collective-permute-done | bytes 1048608 | tf_op jit(solution)/shard_map/ppermute | solution.py:462
  373.8 11.7 %shard_map.313 = (bf16[2048,2048]{1,0:T(8,128)(2,1)}, bf16[2048,256]{1,0:T(8,128)(2,1)}, f32[2048,16]{1,0:T(8,128)}, f32[2048,16]{1,0:T(8,128)}) custom-call(s32[8]{0:T(128)} %stack.53.at_ref, s32[1]{0:T(128)} %bitcast.38.col_ref, f32[1,2048]{1,0:T(1,128)} %get-tuple-element.455.gain_ref, bf16[16,2048]{1,0:T(8,128)(2,1)} %slice.269.wr_ref, ...), custom_call_target="tpu_custom_call" | custom-call | flops 25165824 | bytes 16777216 | tf_op jit(solution)/shard_map/pallas_call | solution.py:245
  385.5 39.9 %shard_map.314 = (bf16[3,2048,1536]{2,1,0:T(8,128)(2,1)}, f32[2048,16]{1,0:T(8,128)}) custom-call(bf16[2048,2048]{1,0:T(8,128)(2,1)} %get-tuple-element.285.x_ref, bf16[3072,2048]{1,0:T(8,128)(2,1)} %all-gather.9.cloned.1.call-done.wg_ref.wu_ref.refs_1_.refs_3_, bf16[3072,2048]{1,0:T(8,128)(2,1)} %all-gather.9.cloned.1.call-done.wg_ref.wu_ref.refs_1_.refs_3_, ...), custom_call_target="tpu_custom_call" | custom-call | flops 25769803776 | bytes 46137344 | tf_op jit(solution)/shard_map/pallas_call | solution.py:75
  425.4 33.0 %shard_map.315.refs_0_ = bf16[4608,2048]{1,0:T(8,128)(2,1)} custom-call(bf16[3,2048,1536]{2,1,0:T(8,128)(2,1)} %get-tuple-element.290.s_ref.refs_0_.refs_2_, bf16[2048,2048]{1,0:T(8,128)(2,1)} %get-tuple-element.285.x_ref), custom_call_target="tpu_custom_call" | custom-call | flops 25769803776 | bytes 41943040 | tf_op jit(solution)/shard_map/pallas_call | solution.py:156
  458.4 18.6 %shard_map.316 = bf16[4608,2048]{1,0:T(8,128)(2,1)} custom-call(bf16[3,2048,1536]{2,1,0:T(8,128)(2,1)} %get-tuple-element.290.s_ref.refs_0_.refs_2_, bf16[2048,2048]{1,0:T(8,128)(2,1)} %shard_map.310.g_ref.x_ref, bf16[4608,2048]{1,0:T(8,128)(2,1)} %shard_map.315.refs_0_), custom_call_target="tpu_custom_call", output_to_operand_aliasing={{}: (2, {})} | custom-call | flops 12884901888 | bytes 20971520 | tf_op jit(solution)/shard_map/pallas_call | solution.py:156
  477.1 44.4 %shard_map.317 = (bf16[3,2048,1632]{2,1,0:T(8,128)(2,1)}, f32[2048,16]{1,0:T(8,128)}) custom-call(bf16[2048,2048]{1,0:T(8,128)(2,1)} %get-tuple-element.285.x_ref, bf16[3264,2048]{1,0:T(8,128)(2,1)} %all-gather.11.cloned.1.call-done.wg_ref.wu_ref.refs_5_.refs_7_, bf16[3264,2048]{1,0:T(8,128)(2,1)} %all-gather.11.cloned.1.call-done.wg_ref.wu_ref.refs_5_.refs_7_, ...), custom_call_target="tpu_custom_call" | custom-call | flops 27380416512 | bytes 48496640 | tf_op jit(solution)/shard_map/pallas_call | solution.py:75
  521.5 69.7 %shard_map.318 = bf16[2048,2176]{1,0:T(8,128)(2,1)} custom-call(bf16[3,2048,1536]{2,1,0:T(8,128)(2,1)} %get-tuple-element.290.s_ref.refs_0_.refs_2_, bf16[3072,2048]{1,0:T(8,128)(2,1)} %all-gather.9.cloned.1.call-done.wg_ref.wu_ref.refs_1_.refs_3_, bf16[3,2048,1536]{2,1,0:T(8,128)(2,1)} %get-tuple-element.290.s_ref.refs_0_.refs_2_, ...), custom_call_target="tpu_custom_call" | custom-call | flops 53150220288 | bytes 68681728 | tf_op jit(solution)/shard_map/pallas_call | solution.py:144
  608.2 20.0 %shard_map.319.refs_0_ = bf16[4896,2048]{1,0:T(8,128)(2,1)} custom-call(bf16[3,2048,1632]{2,1,0:T(8,128)(2,1)} %get-tuple-element.293.refs_4_.refs_6_.s_ref.refs_2_, bf16[2048,2048]{1,0:T(8,128)(2,1)} %get-tuple-element.285.x_ref), custom_call_target="tpu_custom_call" | custom-call | flops 13690208256 | bytes 21757952 | tf_op jit(solution)/shard_map/pallas_call | solution.py:156
  640.3 19.6 %shard_map.320.refs_0_ = bf16[4896,2048]{1,0:T(8,128)(2,1)} custom-call(bf16[3,2048,1632]{2,1,0:T(8,128)(2,1)} %get-tuple-element.293.refs_4_.refs_6_.s_ref.refs_2_, bf16[2048,2048]{1,0:T(8,128)(2,1)} %get-tuple-element.285.x_ref, bf16[4896,2048]{1,0:T(8,128)(2,1)} %shard_map.319.refs_0_), custom_call_target="tpu_custom_call", output_to_operand_aliasing={{}: (2, {})} | custom-call | flops 13690208256 | bytes 21757952 | tf_op jit(solution)/shard_map/pallas_call | solution.py:156
  675.7 22.5 %shard_map.321 = bf16[4,2048,256]{2,1,0:T(8,128)(2,1)} custom-call(s32[1]{0:T(128)S(6)} %sub.27.core_ref, bf16[3,2048,1536]{2,1,0:T(8,128)(2,1)} %get-tuple-element.290.s_ref.refs_0_.refs_2_, bf16[3168,2048]{1,0:T(8,128)(2,1)} %all-gather.7.cloned.1.call-done.w_ref.refs_1_.refs_3_, bf16[3,2048,1632]{2,1,0:T(8,128)(2,1)} %get-tuple-element.293.refs_4_.refs_6_.s_ref.refs_2_, ...), custom_call_target="tpu_custom_call" | custom-call | flops 13287555072 | bytes 42729472 | tf_op jit(solution)/shard_map/pallas_call | solution.py:144
  713.9 22.3 %shard_map.322 = bf16[4,2048,256]{2,1,0:T(8,128)(2,1)} custom-call(s32[1]{0:T(128)} %bitcast.42.core_ref, bf16[3,2048,1536]{2,1,0:T(8,128)(2,1)} %get-tuple-element.290.s_ref.refs_0_.refs_2_, bf16[3168,2048]{1,0:T(8,128)(2,1)} %all-gather.7.cloned.1.call-done.w_ref.refs_1_.refs_3_, bf16[3,2048,1632]{2,1,0:T(8,128)(2,1)} %get-tuple-element.293.refs_4_.refs_6_.s_ref.refs_2_, ...), custom_call_target="tpu_custom_call" | custom-call | flops 13287555072 | bytes 42729472 | tf_op jit(solution)/shard_map/pallas_call | solution.py:144
  756.5 19.6 %shard_map.323 = bf16[4896,2048]{1,0:T(8,128)(2,1)} custom-call(bf16[3,2048,1632]{2,1,0:T(8,128)(2,1)} %get-tuple-element.293.refs_4_.refs_6_.s_ref.refs_2_, bf16[2048,2048]{1,0:T(8,128)(2,1)} %shard_map.310.g_ref.x_ref, bf16[4896,2048]{1,0:T(8,128)(2,1)} %shard_map.320.refs_0_), custom_call_target="tpu_custom_call", output_to_operand_aliasing={{}: (2, {})} | custom-call | flops 13690208256 | bytes 21757952 | tf_op jit(solution)/shard_map/pallas_call | solution.py:156
  788.0 14.2 %collective-permute-done.62 = bf16[256,2048]{1,0:T(8,128)(2,1)S(1)} collective-permute-done((bf16[256,2048]{1,0:T(8,128)(2,1)}, bf16[256,2048]{1,0:T(8,128)(2,1)S(1)}, u32[]{:S(2)}, u32[]{:S(2)}) %collective-permute-start.62) | collective-permute-done | bytes 1048608 | tf_op jit(solution)/shard_map/ppermute | solution.py:462
  836.7 17.8 %shard_map.325 = (bf16[2048,384]{1,0:T(8,128)(2,1)}, bf16[2048,512]{1,0:T(8,128)(2,1)}, f32[2048,128]{1,0:T(8,128)}, f32[2048,1]{1,0:T(8,128)}) custom-call(bf16[2048,384]{1,0:T(8,128)(2,1)} %get-tuple-element.322.q_ref, bf16[2048,128]{1,0:T(8,128)(2,1)} %get-tuple-element.323.kr_ref, bf16[2048,512]{1,0:T(8,128)(2,1)} %get-tuple-element.324.kv_ref, ...), custom_call_target="tpu_custom_call" | custom-call | flops 5872025600 | bytes 12288000 | tf_op jit(solution)/shard_map/pallas_call | solution.py:428
  940.4 16.4 %collective-permute-done.79 = bf16[256,640]{1,0:T(8,128)(2,1)S(1)} collective-permute-done((bf16[256,640]{1,0:T(8,128)(2,1)S(1)}, bf16[256,640]{1,0:T(8,128)(2,1)S(1)}, u32[]{:S(2)}, u32[]{:S(2)}) %collective-permute-start.79) | collective-permute-done | bytes 327712 | tf_op jit(solution)/shard_map/ppermute | solution.py:462
  959.0 12.4 %collective-permute-done.87 = bf16[256,640]{1,0:T(8,128)(2,1)S(1)} collective-permute-done((bf16[256,640]{1,0:T(8,128)(2,1)S(1)}, bf16[256,640]{1,0:T(8,128)(2,1)S(1)}, u32[]{:S(2)}, u32[]{:S(2)}) %collective-permute-start.87) | collective-permute-done | bytes 327712 | tf_op jit(solution)/shard_map/ppermute | solution.py:462
  1003.7 11.5 %shard_map.331 = bf16[672,2048]{1,0:T(8,128)(2,1)} custom-call(bf16[2048,640]{1,0:T(8,128)(2,1)} %get-tuple-element.378.delta_ref, bf16[2048,2048]{1,0:T(8,128)(2,1)} %get-tuple-element.335.x_ref, bf16[640,2048]{1,0:T(8,128)(2,1)} %slice.273.w_ref, bf16[2048,640]{1,0:T(8,128)(2,1)} %shard_map.329.small_ref, f32[1,2048]{1,0:T(1,128)} %get-tuple-element.456.refs_8_.g_ref, ...), custom_call_target="tpu_custom_call" | custom-call | flops 5368709120 | bytes 16252928 | tf_op jit(solution)/shard_map/pallas_call | solution.py:323
  (523 shorter events, 544.7 us)
Async XLA Ops:
  7.3 88.6 %all-gather.5.cloned.1.call-start = ((), (), s32[]{:S(2)}) async-start(), calls=%async_computation.4 | async-start | bytes 7372800 | tf_op jit(solution)/shard_map/all_gather | solution.py:554
  15.6 271.5 %all-gather.7.cloned.1.call-start = ((), (), s32[]{:S(2)}) async-start(), calls=%async_computation.5 | async-start | bytes 16220160 | tf_op jit(solution)/shard_map/all_gather | solution.py:554
  39.1 346.4 %all-gather.9.cloned.1.call-start = ((), (), s32[]{:S(2)}) async-start(), calls=%async_computation.6 | async-start | bytes 15728640 | tf_op jit(solution)/shard_map/all_gather | solution.py:554
  57.1 419.9 %all-gather.11.cloned.1.call-start = ((), (), s32[]{:S(2)}) async-start(), calls=%async_computation.7 | async-start | bytes 16711680 | tf_op jit(solution)/shard_map/all_gather | solution.py:554
  57.2 37.3 %collective-permute-start.10 = (bf16[1024,256]{1,0:T(8,128)(2,1)}, bf16[1024,256]{1,0:T(8,128)(2,1)}, u32[]{:S(2)}, u32[]{:S(2)}) collective-permute-start(bf16[1024,256]{1,0:T(8,128)(2,1)} %get-tuple-element.499.refs_0_), channel_id=1, source_target_pairs={{0,1},{1,0},{2,3},{3,2},{4,5},{5,4},{6,7},{7,6},{8,9},{9,8},{10,11... | collective-permute-start | bytes 1572872 | tf_op jit(solution)/shard_map/ppermute | solution.py:453
  63.9 33.5 %collective-permute-start.12 = (bf16[1024,256]{1,0:T(8,128)(2,1)S(1)}, bf16[1024,256]{1,0:T(8,128)(2,1)}, u32[]{:S(2)}, u32[]{:S(2)}) collective-permute-start(bf16[1024,256]{1,0:T(8,128)(2,1)S(1)} %broadcast_select_fusion.12.refs_4_), channel_id=1, source_target_pairs={{0,1},{1,0},{2,3},{3,2},{4,5},{5,4},{6,7},{7,6},{8,9},{9,8},{10,11... | collective-permute-start | bytes 1572872 | tf_op jit(solution)/shard_map/ppermute | solution.py:453
  97.3 36.0 %collective-permute-start.18 = (bf16[1024,256]{1,0:T(8,128)(2,1)}, bf16[1024,256]{1,0:T(8,128)(2,1)}, u32[]{:S(2)}, u32[]{:S(2)}) collective-permute-start(bf16[1024,256]{1,0:T(8,128)(2,1)} %get-tuple-element.224.refs_0_), channel_id=1, source_target_pairs={{0,1},{1,0},{2,3},{3,2},{4,5},{5,4},{6,7},{7,6},{8,9},{9,8},{10,11... | collective-permute-start | bytes 1572872 | tf_op jit(solution)/shard_map/ppermute | solution.py:453
  161.7 614.4 %reduce-scatter.5.cloned.1.call-start = ((), (), s32[]{:S(2)}) async-start(), calls=%async_computation.8 | async-start | bytes 23592960 | tf_op jit(solution)/shard_map/reduce_scatter | solution.py:558
  162.6 29.7 %collective-permute-start.26 = (bf16[2048,256]{1,0:T(8,128)(2,1)}, bf16[2048,256]{1,0:T(8,128)(2,1)}, u32[]{:S(2)}, u32[]{:S(2)}) collective-permute-start(bf16[2048,256]{1,0:T(8,128)(2,1)} %collective-permute-done.17), channel_id=1, source_target_pairs={{2,0},{3,1},{4,2},{5,3},{10,8},{11,9},{12,10},{13,11},{18,16},{19,... | collective-permute-start | bytes 3145736 | tf_op jit(solution)/shard_map/ppermute | solution.py:462
  215.1 36.6 %collective-permute-start.33 = (bf16[2048,256]{1,0:T(8,128)(2,1)}, bf16[2048,256]{1,0:T(8,128)(2,1)}, u32[]{:S(2)}, u32[]{:S(2)}) collective-permute-start(bf16[2048,256]{1,0:T(8,128)(2,1)} %refs_0_), channel_id=1, source_target_pairs={{0,1},{1,0},{2,3},{3,2},{4,5},{5,4},{6,7},{7,6},{8,9},{9,8},{10,11... | collective-permute-start | bytes 3145736 | tf_op jit(solution)/shard_map/ppermute | solution.py:453
  342.7 31.1 %collective-permute-start.37 = (bf16[256,2048]{1,0:T(8,128)(2,1)S(1)}, bf16[256,2048]{1,0:T(8,128)(2,1)}, u32[]{:S(2)}, u32[]{:S(2)}) collective-permute-start(bf16[256,2048]{1,0:T(8,128)(2,1)S(1)} %get-tuple-element.453.refs_0_), channel_id=1, source_target_pairs={{0,1},{1,0},{2,3},{3,2},{4,5},{5,4},{6,7},{7,6},{8,9},{9,8},{10,11... | collective-permute-start | bytes 3145736 | tf_op jit(solution)/shard_map/ppermute | solution.py:453
  477.0 512.0 %reduce-scatter.7.cloned.1.call-start = ((), (), s32[]{:S(2)}) async-start(), calls=%async_computation.9 | async-start | bytes 25067520 | tf_op jit(solution)/shard_map/reduce_scatter | solution.py:558
  666.5 31.7 %collective-permute-start.52 = (bf16[256,2176]{1,0:T(8,128)(2,1)}, bf16[256,2176]{1,0:T(8,128)(2,1)}, u32[]{:S(2)}, u32[]{:S(2)}) collective-permute-start(bf16[256,2176]{1,0:T(8,128)(2,1)} %get-tuple-element.467), channel_id=1, source_target_pairs={{0,2},{1,3},{2,4},{3,5},{4,6},{5,7},{8,10},{9,11},{10,12},{11,13},... | collective-permute-start | bytes 3342344 | tf_op jit(solution)/shard_map/ppermute | solution.py:462
  701.3 38.7 %collective-permute-start.56 = (bf16[4,2048,256]{2,1,0:T(8,128)(2,1)}, bf16[4,2048,256]{2,1,0:T(8,128)(2,1)}, u32[]{:S(2)}, u32[]{:S(2)}) collective-permute-start(bf16[4,2048,256]{2,1,0:T(8,128)(2,1)} %shard_map.321), channel_id=1, source_target_pairs={{0,1},{1,0},{2,3},{3,2},{4,5},{5,4},{6,7},{7,6},{8,9},{9,8},{10,11... | collective-permute-start | bytes 12582920 | tf_op jit(solution)/shard_map/ppermute | solution.py:453
  740.0 36.1 %collective-permute-start.57 = (bf16[256,2048]{1,0:T(8,128)(2,1)}, bf16[256,2048]{1,0:T(8,128)(2,1)}, u32[]{:S(2)}, u32[]{:S(2)}) collective-permute-start(bf16[256,2048]{1,0:T(8,128)(2,1)} %collective-permute-done.54), channel_id=1, source_target_pairs={{2,4},{3,5},{4,6},{5,7},{10,12},{11,13},{12,14},{13,15},{18,20},{1... | collective-permute-start | bytes 3145736 | tf_op jit(solution)/shard_map/ppermute | solution.py:462
  741.6 34.5 %collective-permute-start.58 = (bf16[256,2048]{1,0:T(8,128)(2,1)S(1)}, bf16[256,2048]{1,0:T(8,128)(2,1)}, u32[]{:S(2)}, u32[]{:S(2)}) collective-permute-start(bf16[256,2048]{1,0:T(8,128)(2,1)S(1)} %collective-permute-done.55), channel_id=1, source_target_pairs={{2,0},{3,1},{4,2},{5,3},{10,8},{11,9},{12,10},{13,11},{18,16},{19,... | collective-permute-start | bytes 3145736 | tf_op jit(solution)/shard_map/ppermute | solution.py:462
  776.1 245.2 %reduce-scatter.11.cloned.1.call-start = ((), (), s32[]{:S(2)}) async-start(), calls=%async_computation.11 | async-start | bytes 3932160 | tf_op jit(solution)/shard_map/reduce_scatter | solution.py:558
  786.4 33.9 %collective-permute-start.67 = (bf16[256,2048]{1,0:T(8,128)(2,1)}, bf16[256,2048]{1,0:T(8,128)(2,1)S(1)}, u32[]{:S(2)}, u32[]{:S(2)}) collective-permute-start(bf16[256,2048]{1,0:T(8,128)(2,1)} %fusion.3.refs_0_), channel_id=1, source_target_pairs={{0,1},{1,0},{2,3},{3,2},{4,5},{5,4},{6,7},{7,6},{8,9},{9,8},{10,11... | collective-permute-start | bytes 3145736 | tf_op jit(solution)/shard_map/ppermute | solution.py:453
  810.8 43.7 %collective-permute-start.65 = (bf16[2048,256]{1,0:T(8,128)(2,1)}, bf16[2048,256]{1,0:T(8,128)(2,1)}, u32[]{:S(2)}, u32[]{:S(2)}) collective-permute-start(bf16[2048,256]{1,0:T(8,128)(2,1)} %get-tuple-element.479), channel_id=1, source_target_pairs={{0,2},{1,3},{2,4},{3,5},{4,6},{5,7},{8,10},{9,11},{10,12},{11,13},... | collective-permute-start | bytes 3145736 | tf_op jit(solution)/shard_map/ppermute | solution.py:462
  820.3 34.2 %collective-permute-start.66 = (bf16[2048,256]{1,0:T(8,128)(2,1)}, bf16[2048,256]{1,0:T(8,128)(2,1)}, u32[]{:S(2)}, u32[]{:S(2)}) collective-permute-start(bf16[2048,256]{1,0:T(8,128)(2,1)} %get-tuple-element.478), channel_id=1, source_target_pairs={{2,0},{3,1},{4,2},{5,3},{6,4},{7,5},{10,8},{11,9},{12,10},{13,11},... | collective-permute-start | bytes 3145736 | tf_op jit(solution)/shard_map/ppermute | solution.py:462
  924.7 32.1 %collective-permute-start.81 = (bf16[2048,256]{1,0:T(8,128)(2,1)S(1)}, bf16[2048,256]{1,0:T(8,128)(2,1)}, u32[]{:S(2)}, u32[]{:S(2)}) collective-permute-start(bf16[2048,256]{1,0:T(8,128)(2,1)S(1)} %get-tuple-element.477), channel_id=1, source_target_pairs={{0,2},{1,3},{8,10},{9,11},{16,18},{17,19},{24,26},{25,27}} | collective-permute-start | bytes 3145736 | tf_op jit(solution)/shard_map/ppermute | solution.py:462
  956.8 108.4 %reduce-scatter.9.cloned.1.call-start = ((), (), s32[]{:S(2)}) async-start(), calls=%async_computation.10 | async-start | bytes 3440640 | tf_op jit(solution)/shard_map/reduce_scatter | solution.py:558
  977.6 37.6 %collective-permute-start.83 = (bf16[2048,256]{1,0:T(8,128)(2,1)}, bf16[2048,256]{1,0:T(8,128)(2,1)S(1)}, u32[]{:S(2)}, u32[]{:S(2)}) collective-permute-start(bf16[2048,256]{1,0:T(8,128)(2,1)} %get-tuple-element.475), channel_id=1, source_target_pairs={{0,2},{1,3},{2,4},{3,5},{8,10},{9,11},{10,12},{11,13},{16,18},{17,... | collective-permute-start | bytes 3145736 | tf_op jit(solution)/shard_map/ppermute | solution.py:462
  982.1 33.2 %collective-permute-start.84 = (bf16[2048,256]{1,0:T(8,128)(2,1)}, bf16[2048,256]{1,0:T(8,128)(2,1)}, u32[]{:S(2)}, u32[]{:S(2)}) collective-permute-start(bf16[2048,256]{1,0:T(8,128)(2,1)} %get-tuple-element.474), channel_id=1, source_target_pairs={{4,2},{5,3},{6,4},{7,5},{12,10},{13,11},{14,12},{15,13},{20,18},{2... | collective-permute-start | bytes 3145736 | tf_op jit(solution)/shard_map/ppermute | solution.py:462
  (165 other events, 2396.3 us)
Sparse Core Ops, SparseCore 0:
  15.7 69.4 all-gather.4
  87.6 125.6 all-gather.6
  215.1 122.3 all-gather.8
  339.8 128.9 all-gather.10
  477.1 169.8 reduce-scatter.4
  776.3 182.6 reduce-scatter.6
  962.5 43.9 reduce-scatter.10
  1015.4 38.7 reduce-scatter.8

commit v6 on v5

--- a/solution.py
+++ b/solution.py
@@ -317,14 +317,15 @@
     v=jnp.where(line==E+1,(v+sums)/g_ref[...],v)
     out_ref[n:]=jnp.where(line==E+2,latent_ref[...],v).astype(BF)
 
-def last_pack(delta, x, w, small, gain, latent_row, bc=512):
+def last_pack(delta, x, packed, first, small, gain, latent_row, bc=512):
     T,D=x.shape; n=delta.shape[1]
     def cols(a): return pl.BlockSpec((a.shape[0],bc),lambda j:(0,j))
     return pl.pallas_call(last_pack_kernel,grid=(D//bc,),
-        in_specs=[pl.BlockSpec((T,n),lambda j:(0,0)),cols(x),cols(w),pl.BlockSpec((bc,DN),lambda j:(j,R//DN)),cols(gain),cols(latent_row)],
+        in_specs=[pl.BlockSpec((T,n),lambda j:(0,0)),cols(x),
+                  pl.BlockSpec((pl.Element(n),pl.Element(bc)),lambda j:(first,j*bc)),pl.BlockSpec((bc,DN),lambda j:(j,R//DN)),cols(gain),cols(latent_row)],
         out_specs=pl.BlockSpec((n+32,bc),lambda j:(0,j)),out_shape=jax.ShapeDtypeStruct((n+32,D),BF),
         compiler_params=params(1),
-        cost_estimate=pl.CostEstimate(flops=2*T*D*n,bytes_accessed=2*(T*D+2*n*D+T*n),transcendentals=0))(delta,x,w,small,gain,latent_row)
+        cost_estimate=pl.CostEstimate(flops=2*T*D*n,bytes_accessed=2*(T*D+2*n*D+T*n),transcendentals=0))(delta,x,packed,small,gain,latent_row)
 
 
 def turn(x, cosine, sine):
@@ -622,7 +623,7 @@
     cosine, sine = (jnp.asarray(table) for table in tables())
 
     n_units = E * fe + shared_down.shape[0]
-    n0 = n_units // 2 // 256 * 256
+    n0 = (n_units // 512 + 1) * 256
     n1 = n_units - n0
     last_step = line.chips - 1
     gate = expert_gate.transpose(0, 2, 1).reshape(E * fe, wide)
@@ -758,16 +759,17 @@
         lambda: back(first_terms, None, BF, tile, (), 1 - core, line.chips),
         lambda: back(first_terms, None, BF, tile, (), core, line.chips),
     ))
-    arrived = beside([move], lambda: line.swap(theirs))
+    deltas, arrived = beside([move], lambda: (attend_deltas(), line.swap(theirs)))
+    attend_sums = scatter_rows(deltas).astype(F32)
     steps(move, last_step - 3)
     small, both, layer_output = lax.optimization_barrier(
         (move.result().astype(BF), total(mine, arrived), layer_output)
     )
     move = Gather(line, small)
+    steps(move, last_step - 1)
+    move.left[-1], move.right[-1], both = lax.optimization_barrier((move.left[-1], move.right[-1], both))
     first_move = line.column_scatter(both)
-    deltas = beside([move, first_move], attend_deltas)
-    attend_sums = scatter_rows(deltas).astype(F32)
-    steps(move, last_step - 1)
+    beside([move, first_move])
     small_pieces, small_at = line.row_pieces(move.result())
     small_pieces, late_sums = lax.optimization_barrier((small_pieces, late_sums))
     wld = wproj[queries_wide:]
@@ -776,7 +778,8 @@
         (small,) = place_rows(small_pieces, small_at)
         delta_latent, dots, gain_delta = latent_back(small, proj, latent_g[None], cosine, sine)
         latent_row = jnp.pad(gain_delta.reshape(n_dp, R // n_dp), ((0, 0), (0, wide - R // n_dp))).reshape(1, D)
-        return delta_latent, dots, last_pack(delta_latent, first_round, wld, small, first_g[None], latent_row)
+        return delta_latent, dots, last_pack(
+            delta_latent, first_round, attend_packed, queries_wide, small, first_g[None], latent_row)
 
     delta_latent, dots, pack = beside([first_move], last)
     steps(first_move, last_step - 2)

time: 1090 us -> 1100 us (level)
  waiting for transfers between devices: 235 us -> 247 us
  transfers between devices with their start and end apart: 103 -> 103, of which waited for: 36 -> 39; matrix products, arithmetic and copies ran while one was open for 15% -> 15% of each run, Pallas kernels for 45% -> 44%
where the time goes in v6:
time: 1100 us; the launch traced here: 1090 us
  Pallas kernels  482 us (44%)
  waiting for transfers between devices  247 us (22%)
  starting transfers between devices  149 us (14%)
  other arithmetic  98.8 us (9%)
  local copies, waits for them, and re-layouts  64.2 us (6%)
  matrix products  33.3 us (3%)
  between operations  16.5 us (2%)
    ppermute x66, waiting for transfers between devices, shift(): return lax.ppermute(a, 'tensor', pairs)  228 us
    ppermute x66, starting transfers between devices, shift(): return lax.ppermute(a, 'tensor', pairs)  144 us
    pallas_call x5, Pallas kernels, back(): pl.pallas_call(body, grid=(T // bt,), in_specs=ins, out_specs=ospec, out_...  131 us
    pallas_call x5, Pallas kernels, outer(): pl.pallas_call(outer_kernel, grid=(count, D // bc), in_specs=ins, out_spe...  110 us
    pallas_call x2, Pallas kernels, units(): pl.pallas_call(functools.partial(units_kernel, fe, first), grid=(T // bt,...  84.4 us
    pallas_call x2, Pallas kernels, lift_back(): pl.pallas_call(lift_kernel, grid=(T // bt,), in_specs=[pl.BlockSpec((bt,...  40.1 us
    convert_element_type x14, other arithmetic, total(): return (mine.astype(F32) + arrived.astype(F32)).astype(BF)  37.4 us
    dot_general x9, matrix products, dot(): lax.dot_general(a, b, (((ca,), (cb,)), ((), ())), preferred_element_type=...  33.1 us
  transfers between devices with their start and end apart: 103, of which 39 were waited for; matrix products, arithmetic and copies ran while one was open for 15% of the time, Pallas kernels for 44%

profile of v6, /device:TPU:0, one launch (start us, length us, event | category | flops | bytes accessed | tf_op | source)
XLA Modules:
  0.0 1090.4 jit_solution(7954075511597488349)
XLA Ops:
  45.3 12.7 %collective-permute-done.3 = bf16[1024,256]{1,0:T(8,128)(2,1)S(1)} collective-permute-done((bf16[1024,256]{1,0:T(8,128)(2,1)S(1)}, bf16[1024,256]{1,0:T(8,128)(2,1)S(1)}, u32[]{:S(2)}, u32[]{:S(2)}) %collective-permute-start.3) | collective-permute-done | bytes 524320 | tf_op jit(solution)/shard_map/ppermute | solution.py:463
  67.0 11.6 %collective-permute-done.5 = bf16[1024,256]{1,0:T(8,128)(2,1)} collective-permute-done((bf16[1024,256]{1,0:T(8,128)(2,1)S(1)}, bf16[1024,256]{1,0:T(8,128)(2,1)}, u32[]{:S(2)}, u32[]{:S(2)}) %collective-permute-start.5) | collective-permute-done | bytes 524320 | tf_op jit(solution)/shard_map/ppermute | solution.py:463
  100.0 11.0 %shard_map.306 = (bf16[2048,2048]{1,0:T(8,128)(2,1)}, bf16[2048,2048]{1,0:T(8,128)(2,1)}, f32[2048,1]{1,0:T(8,128)}, f32[2048,1024]{1,0:T(8,128)}) custom-call(s32[8]{0:T(128)} %stack.44.at_ref, bf16[1024,256]{1,0:T(8,128)(2,1)} %get-tuple-element.505.refs_0_, bf16[1024,256]{1,0:T(8,128)(2,1)} %collective-permute-done.10.refs_1_, ...), custom_call_target="tpu_custom_call" | custom-call | flops 4307550208 | bytes 12582912 | tf_op jit(solution)/shard_map/pallas_call | solution.py:192
  137.0 10.6 shard_map.308
  182.4 10.6 collective-permute-done.26
  217.6 15.9 %collective-permute-done.27 = bf16[256,2048]{1,0:T(8,128)(2,1)} collective-permute-done((bf16[256,2048]{1,0:T(8,128)(2,1)}, bf16[256,2048]{1,0:T(8,128)(2,1)}, u32[]{:S(2)}, u32[]{:S(2)}) %collective-permute-start.27) | collective-permute-done | bytes 1048608 | tf_op jit(solution)/shard_map/ppermute | solution.py:463
  263.4 11.6 %collective-permute-done.31 = bf16[256,2048]{1,0:T(8,128)(2,1)} collective-permute-done((bf16[256,2048]{1,0:T(8,128)(2,1)}, bf16[256,2048]{1,0:T(8,128)(2,1)}, u32[]{:S(2)}, u32[]{:S(2)}) %collective-permute-start.31) | collective-permute-done | bytes 1048608 | tf_op jit(solution)/shard_map/ppermute | solution.py:463
  288.4 21.6 %shard_map.311.b_ref = bf16[2048,1792]{1,0:T(8,128)(2,1)} custom-call(bf16[2048,2048]{1,0:T(8,128)(2,1)} %shard_map.310.g_ref.x_ref, bf16[3168,2048]{1,0:T(8,128)(2,1)} %all-gather.7.cloned.1.call-done.w_ref.refs_1_.refs_3_), custom_call_target="tpu_custom_call" | custom-call | flops 15032385536 | bytes 23068672 | tf_op jit(solution)/shard_map/pallas_call | solution.py:85
  316.1 18.5 %shard_map.312.b_ref = bf16[2048,1376]{1,0:T(8,128)(2,1)} custom-call(bf16[2048,2048]{1,0:T(8,128)(2,1)} %shard_map.310.g_ref.x_ref, bf16[3168,2048]{1,0:T(8,128)(2,1)} %all-gather.7.cloned.1.call-done.w_ref.refs_1_.refs_3_), custom_call_target="tpu_custom_call" | custom-call | flops 11542724608 | bytes 19660800 | tf_op jit(solution)/shard_map/pallas_call | solution.py:85
  346.7 19.6 %collective-permute-done.43 = bf16[256,2048]{1,0:T(8,128)(2,1)} collective-permute-done((bf16[256,2048]{1,0:T(8,128)(2,1)}, bf16[256,2048]{1,0:T(8,128)(2,1)}, u32[]{:S(2)}, u32[]{:S(2)}) %collective-permute-start.43) | collective-permute-done | bytes 1048608 | tf_op jit(solution)/shard_map/ppermute | solution.py:463
  375.2 11.6 %shard_map.313 = (bf16[2048,2048]{1,0:T(8,128)(2,1)}, bf16[2048,256]{1,0:T(8,128)(2,1)}, f32[2048,16]{1,0:T(8,128)}, f32[2048,16]{1,0:T(8,128)}) custom-call(s32[8]{0:T(128)} %stack.53.at_ref, s32[1]{0:T(128)} %bitcast.38.col_ref, f32[1,2048]{1,0:T(1,128)} %get-tuple-element.461.gain_ref, bf16[16,2048]{1,0:T(8,128)(2,1)} %slice.269.wr_ref, ...), custom_call_target="tpu_custom_call" | custom-call | flops 25165824 | bytes 16777216 | tf_op jit(solution)/shard_map/pallas_call | solution.py:245
  386.9 45.7 %shard_map.314 = (bf16[3,2048,1792]{2,1,0:T(8,128)(2,1)}, f32[2048,16]{1,0:T(8,128)}) custom-call(bf16[2048,2048]{1,0:T(8,128)(2,1)} %get-tuple-element.288.x_ref, bf16[3584,2048]{1,0:T(8,128)(2,1)} %all-gather.9.cloned.1.call-done.wg_ref.wu_ref.refs_1_.refs_3_, bf16[3584,2048]{1,0:T(8,128)(2,1)} %all-gather.9.cloned.1.call-done.wg_ref.wu_ref.refs_1_.refs_3_, ...), custom_call_target="tpu_custom_call" | custom-call | flops 30064771072 | bytes 52428800 | tf_op jit(solution)/shard_map/pallas_call | solution.py:75
  432.6 37.7 %shard_map.315.refs_0_ = bf16[5376,2048]{1,0:T(8,128)(2,1)} custom-call(bf16[3,2048,1792]{2,1,0:T(8,128)(2,1)} %get-tuple-element.293.s_ref.refs_0_.refs_2_, bf16[2048,2048]{1,0:T(8,128)(2,1)} %get-tuple-element.288.x_ref), custom_call_target="tpu_custom_call" | custom-call | flops 30064771072 | bytes 46137344 | tf_op jit(solution)/shard_map/pallas_call | solution.py:156
  470.2 21.1 %shard_map.316 = bf16[5376,2048]{1,0:T(8,128)(2,1)} custom-call(bf16[3,2048,1792]{2,1,0:T(8,128)(2,1)} %get-tuple-element.293.s_ref.refs_0_.refs_2_, bf16[2048,2048]{1,0:T(8,128)(2,1)} %shard_map.310.g_ref.x_ref, bf16[5376,2048]{1,0:T(8,128)(2,1)} %shard_map.315.refs_0_), custom_call_target="tpu_custom_call", output_to_operand_aliasing={{}: (2, {})} | custom-call | flops 15032385536 | bytes 23068672 | tf_op jit(solution)/shard_map/pallas_call | solution.py:156
  491.5 38.7 %shard_map.317 = (bf16[3,2048,1376]{2,1,0:T(8,128)(2,1)}, f32[2048,16]{1,0:T(8,128)}) custom-call(bf16[2048,2048]{1,0:T(8,128)(2,1)} %get-tuple-element.288.x_ref, bf16[2752,2048]{1,0:T(8,128)(2,1)} %all-gather.11.cloned.1.call-done.wg_ref.wu_ref.refs_5_.refs_7_, bf16[2752,2048]{1,0:T(8,128)(2,1)} %all-gather.11.cloned.1.call-done.wg_ref.wu_ref.refs_5_.refs_7_, ...), custom_call_target="tpu_custom_call" | custom-call | flops 23085449216 | bytes 42205184 | tf_op jit(solution)/shard_map/pallas_call | solution.py:75
  530.2 69.5 %shard_map.318 = bf16[2048,2176]{1,0:T(8,128)(2,1)} custom-call(bf16[3,2048,1792]{2,1,0:T(8,128)(2,1)} %get-tuple-element.293.s_ref.refs_0_.refs_2_, bf16[3584,2048]{1,0:T(8,128)(2,1)} %all-gather.9.cloned.1.call-done.wg_ref.wu_ref.refs_1_.refs_3_, bf16[3,2048,1792]{2,1,0:T(8,128)(2,1)} %get-tuple-element.293.s_ref.refs_0_.refs_2_, ...), custom_call_target="tpu_custom_call" | custom-call | flops 53150220288 | bytes 68681728 | tf_op jit(solution)/shard_map/pallas_call | solution.py:144
  616.4 17.3 %shard_map.319.refs_0_ = bf16[4128,2048]{1,0:T(8,128)(2,1)} custom-call(bf16[3,2048,1376]{2,1,0:T(8,128)(2,1)} %get-tuple-element.296.refs_4_.refs_6_.s_ref.refs_2_, bf16[2048,2048]{1,0:T(8,128)(2,1)} %get-tuple-element.288.x_ref), custom_call_target="tpu_custom_call" | custom-call | flops 11542724608 | bytes 19660800 | tf_op jit(solution)/shard_map/pallas_call | solution.py:156
  648.5 17.3 %shard_map.320.refs_0_ = bf16[4128,2048]{1,0:T(8,128)(2,1)} custom-call(bf16[3,2048,1376]{2,1,0:T(8,128)(2,1)} %get-tuple-element.296.refs_4_.refs_6_.s_ref.refs_2_, bf16[2048,2048]{1,0:T(8,128)(2,1)} %get-tuple-element.288.x_ref, bf16[4128,2048]{1,0:T(8,128)(2,1)} %shard_map.319.refs_0_), custom_call_target="tpu_custom_call", output_to_operand_aliasing={{}: (2, {})} | custom-call | flops 11542724608 | bytes 19660800 | tf_op jit(solution)/shard_map/pallas_call | solution.py:156
  683.5 22.4 %shard_map.321 = bf16[4,2048,256]{2,1,0:T(8,128)(2,1)} custom-call(s32[1]{0:T(128)S(6)} %sub.27.core_ref, bf16[3,2048,1792]{2,1,0:T(8,128)(2,1)} %get-tuple-element.293.s_ref.refs_0_.refs_2_, bf16[3168,2048]{1,0:T(8,128)(2,1)} %all-gather.7.cloned.1.call-done.w_ref.refs_1_.refs_3_, bf16[3,2048,1376]{2,1,0:T(8,128)(2,1)} %get-tuple-element.296.refs_4_.refs_6_.s_ref.refs_2_, ...), custom_call_target="tpu_custom_call" | custom-call | flops 13287555072 | bytes 42729472 | tf_op jit(solution)/shard_map/pallas_call | solution.py:144
  721.7 22.1 %shard_map.322 = bf16[4,2048,256]{2,1,0:T(8,128)(2,1)} custom-call(s32[1]{0:T(128)} %bitcast.42.core_ref, bf16[3,2048,1792]{2,1,0:T(8,128)(2,1)} %get-tuple-element.293.s_ref.refs_0_.refs_2_, bf16[3168,2048]{1,0:T(8,128)(2,1)} %all-gather.7.cloned.1.call-done.w_ref.refs_1_.refs_3_, bf16[3,2048,1376]{2,1,0:T(8,128)(2,1)} %get-tuple-element.296.refs_4_.refs_6_.s_ref.refs_2_, ...), custom_call_target="tpu_custom_call" | custom-call | flops 13287555072 | bytes 42729472 | tf_op jit(solution)/shard_map/pallas_call | solution.py:144
  765.0 17.0 %shard_map.323 = bf16[4128,2048]{1,0:T(8,128)(2,1)} custom-call(bf16[3,2048,1376]{2,1,0:T(8,128)(2,1)} %get-tuple-element.296.refs_4_.refs_6_.s_ref.refs_2_, bf16[2048,2048]{1,0:T(8,128)(2,1)} %shard_map.310.g_ref.x_ref, bf16[4128,2048]{1,0:T(8,128)(2,1)} %shard_map.320.refs_0_), custom_call_target="tpu_custom_call", output_to_operand_aliasing={{}: (2, {})} | custom-call | flops 11542724608 | bytes 19660800 | tf_op jit(solution)/shard_map/pallas_call | solution.py:156
  796.1 14.0 %collective-permute-done.62 = bf16[256,2048]{1,0:T(8,128)(2,1)S(1)} collective-permute-done((bf16[256,2048]{1,0:T(8,128)(2,1)}, bf16[256,2048]{1,0:T(8,128)(2,1)S(1)}, u32[]{:S(2)}, u32[]{:S(2)}) %collective-permute-start.62) | collective-permute-done | bytes 1048608 | tf_op jit(solution)/shard_map/ppermute | solution.py:463
  844.9 17.9 %shard_map.325 = (bf16[2048,384]{1,0:T(8,128)(2,1)}, bf16[2048,512]{1,0:T(8,128)(2,1)}, f32[2048,128]{1,0:T(8,128)}, f32[2048,1]{1,0:T(8,128)}) custom-call(bf16[2048,384]{1,0:T(8,128)(2,1)} %get-tuple-element.325.q_ref, bf16[2048,128]{1,0:T(8,128)(2,1)} %get-tuple-element.326.kr_ref, bf16[2048,512]{1,0:T(8,128)(2,1)} %get-tuple-element.327.kv_ref, ...), custom_call_target="tpu_custom_call" | custom-call | flops 5872025600 | bytes 12288000 | tf_op jit(solution)/shard_map/pallas_call | solution.py:429
  1018.6 10.7 shard_map.331
  (523 shorter events, 567.3 us)
Async XLA Ops:
  7.3 90.4 %all-gather.5.cloned.1.call-start = ((), (), s32[]{:S(2)}) async-start(), calls=%async_computation.4 | async-start | bytes 7372800 | tf_op jit(solution)/shard_map/all_gather | solution.py:555
  15.6 272.8 %all-gather.7.cloned.1.call-start = ((), (), s32[]{:S(2)}) async-start(), calls=%async_computation.5 | async-start | bytes 16220160 | tf_op jit(solution)/shard_map/all_gather | solution.py:555
  39.1 347.8 %all-gather.9.cloned.1.call-start = ((), (), s32[]{:S(2)}) async-start(), calls=%async_computation.6 | async-start | bytes 18350080 | tf_op jit(solution)/shard_map/all_gather | solution.py:555
  58.0 433.4 %all-gather.11.cloned.1.call-start = ((), (), s32[]{:S(2)}) async-start(), calls=%async_computation.7 | async-start | bytes 14090240 | tf_op jit(solution)/shard_map/all_gather | solution.py:555
  58.1 38.3 %collective-permute-start.10 = (bf16[1024,256]{1,0:T(8,128)(2,1)}, bf16[1024,256]{1,0:T(8,128)(2,1)}, u32[]{:S(2)}, u32[]{:S(2)}) collective-permute-start(bf16[1024,256]{1,0:T(8,128)(2,1)} %get-tuple-element.505.refs_0_), channel_id=1, source_target_pairs={{0,1},{1,0},{2,3},{3,2},{4,5},{5,4},{6,7},{7,6},{8,9},{9,8},{10,11... | collective-permute-start | bytes 1572872 | tf_op jit(solution)/shard_map/ppermute | solution.py:454
  66.9 32.3 %collective-permute-start.12 = (bf16[1024,256]{1,0:T(8,128)(2,1)S(1)}, bf16[1024,256]{1,0:T(8,128)(2,1)}, u32[]{:S(2)}, u32[]{:S(2)}) collective-permute-start(bf16[1024,256]{1,0:T(8,128)(2,1)S(1)} %broadcast_select_fusion.12.refs_4_), channel_id=1, source_target_pairs={{0,1},{1,0},{2,3},{3,2},{4,5},{5,4},{6,7},{7,6},{8,9},{9,8},{10,11... | collective-permute-start | bytes 1572872 | tf_op jit(solution)/shard_map/ppermute | solution.py:454
  99.2 35.5 %collective-permute-start.18 = (bf16[1024,256]{1,0:T(8,128)(2,1)}, bf16[1024,256]{1,0:T(8,128)(2,1)}, u32[]{:S(2)}, u32[]{:S(2)}) collective-permute-start(bf16[1024,256]{1,0:T(8,128)(2,1)} %get-tuple-element.227.refs_0_), channel_id=1, source_target_pairs={{0,1},{1,0},{2,3},{3,2},{4,5},{5,4},{6,7},{7,6},{8,9},{9,8},{10,11... | collective-permute-start | bytes 1572872 | tf_op jit(solution)/shard_map/ppermute | solution.py:454
  163.5 29.4 %collective-permute-start.26 = (bf16[2048,256]{1,0:T(8,128)(2,1)}, bf16[2048,256]{1,0:T(8,128)(2,1)}, u32[]{:S(2)}, u32[]{:S(2)}) collective-permute-start(bf16[2048,256]{1,0:T(8,128)(2,1)} %collective-permute-done.17), channel_id=1, source_target_pairs={{2,0},{3,1},{4,2},{5,3},{10,8},{11,9},{12,10},{13,11},{18,16},{19,... | collective-permute-start | bytes 3145736 | tf_op jit(solution)/shard_map/ppermute | solution.py:463
  182.3 601.9 %reduce-scatter.5.cloned.1.call-start = ((), (), s32[]{:S(2)}) async-start(), calls=%async_computation.8 | async-start | bytes 27525120 | tf_op jit(solution)/shard_map/reduce_scatter | solution.py:559
  216.2 36.7 %collective-permute-start.33 = (bf16[2048,256]{1,0:T(8,128)(2,1)}, bf16[2048,256]{1,0:T(8,128)(2,1)}, u32[]{:S(2)}, u32[]{:S(2)}) collective-permute-start(bf16[2048,256]{1,0:T(8,128)(2,1)} %refs_0_), channel_id=1, source_target_pairs={{0,1},{1,0},{2,3},{3,2},{4,5},{5,4},{6,7},{7,6},{8,9},{9,8},{10,11... | collective-permute-start | bytes 3145736 | tf_op jit(solution)/shard_map/ppermute | solution.py:454
  343.7 31.5 %collective-permute-start.37 = (bf16[256,2048]{1,0:T(8,128)(2,1)S(1)}, bf16[256,2048]{1,0:T(8,128)(2,1)}, u32[]{:S(2)}, u32[]{:S(2)}) collective-permute-start(bf16[256,2048]{1,0:T(8,128)(2,1)S(1)} %get-tuple-element.459.refs_0_), channel_id=1, source_target_pairs={{0,1},{1,0},{2,3},{3,2},{4,5},{5,4},{6,7},{7,6},{8,9},{9,8},{10,11... | collective-permute-start | bytes 3145736 | tf_op jit(solution)/shard_map/ppermute | solution.py:454
  345.2 30.0 %collective-permute-start.45 = (bf16[256,2048]{1,0:T(8,128)(2,1)S(1)}, bf16[256,2048]{1,0:T(8,128)(2,1)}, u32[]{:S(2)}, u32[]{:S(2)}) collective-permute-start(bf16[256,2048]{1,0:T(8,128)(2,1)S(1)} %broadcast_select_fusion.3.refs_4_), channel_id=1, source_target_pairs={{0,1},{1,0},{2,3},{3,2},{4,5},{5,4},{6,7},{7,6},{8,9},{9,8},{10,11... | collective-permute-start | bytes 3145736 | tf_op jit(solution)/shard_map/ppermute | solution.py:454
  491.4 513.1 %reduce-scatter.7.cloned.1.call-start = ((), (), s32[]{:S(2)}) async-start(), calls=%async_computation.9 | async-start | bytes 21135360 | tf_op jit(solution)/shard_map/reduce_scatter | solution.py:559
  674.9 31.0 %collective-permute-start.52 = (bf16[256,2176]{1,0:T(8,128)(2,1)}, bf16[256,2176]{1,0:T(8,128)(2,1)}, u32[]{:S(2)}, u32[]{:S(2)}) collective-permute-start(bf16[256,2176]{1,0:T(8,128)(2,1)} %get-tuple-element.467), channel_id=1, source_target_pairs={{0,2},{1,3},{2,4},{3,5},{4,6},{5,7},{8,10},{9,11},{10,12},{11,13},... | collective-permute-start | bytes 3342344 | tf_op jit(solution)/shard_map/ppermute | solution.py:463
  709.2 38.6 %collective-permute-start.56 = (bf16[4,2048,256]{2,1,0:T(8,128)(2,1)}, bf16[4,2048,256]{2,1,0:T(8,128)(2,1)}, u32[]{:S(2)}, u32[]{:S(2)}) collective-permute-start(bf16[4,2048,256]{2,1,0:T(8,128)(2,1)} %shard_map.321), channel_id=1, source_target_pairs={{0,1},{1,0},{2,3},{3,2},{4,5},{5,4},{6,7},{7,6},{8,9},{9,8},{10,11... | collective-permute-start | bytes 12582920 | tf_op jit(solution)/shard_map/ppermute | solution.py:454
  747.9 34.1 %collective-permute-start.57 = (bf16[256,2048]{1,0:T(8,128)(2,1)}, bf16[256,2048]{1,0:T(8,128)(2,1)}, u32[]{:S(2)}, u32[]{:S(2)}) collective-permute-start(bf16[256,2048]{1,0:T(8,128)(2,1)} %collective-permute-done.54), channel_id=1, source_target_pairs={{2,4},{3,5},{4,6},{5,7},{10,12},{11,13},{12,14},{13,15},{18,20},{1... | collective-permute-start | bytes 3145736 | tf_op jit(solution)/shard_map/ppermute | solution.py:463
  749.5 32.5 %collective-permute-start.58 = (bf16[256,2048]{1,0:T(8,128)(2,1)S(1)}, bf16[256,2048]{1,0:T(8,128)(2,1)}, u32[]{:S(2)}, u32[]{:S(2)}) collective-permute-start(bf16[256,2048]{1,0:T(8,128)(2,1)S(1)} %collective-permute-done.55), channel_id=1, source_target_pairs={{2,0},{3,1},{4,2},{5,3},{10,8},{11,9},{12,10},{13,11},{18,16},{19,... | collective-permute-start | bytes 3145736 | tf_op jit(solution)/shard_map/ppermute | solution.py:463
  784.2 252.1 %reduce-scatter.11.cloned.1.call-start = ((), (), s32[]{:S(2)}) async-start(), calls=%async_computation.11 | async-start | bytes 3932160 | tf_op jit(solution)/shard_map/reduce_scatter | solution.py:559
  794.4 33.9 %collective-permute-start.67 = (bf16[256,2048]{1,0:T(8,128)(2,1)}, bf16[256,2048]{1,0:T(8,128)(2,1)S(1)}, u32[]{:S(2)}, u32[]{:S(2)}) collective-permute-start(bf16[256,2048]{1,0:T(8,128)(2,1)} %fusion.3.refs_0_), channel_id=1, source_target_pairs={{0,1},{1,0},{2,3},{3,2},{4,5},{5,4},{6,7},{7,6},{8,9},{9,8},{10,11... | collective-permute-start | bytes 3145736 | tf_op jit(solution)/shard_map/ppermute | solution.py:454
  818.7 44.1 %collective-permute-start.65 = (bf16[2048,256]{1,0:T(8,128)(2,1)}, bf16[2048,256]{1,0:T(8,128)(2,1)}, u32[]{:S(2)}, u32[]{:S(2)}) collective-permute-start(bf16[2048,256]{1,0:T(8,128)(2,1)} %get-tuple-element.485), channel_id=1, source_target_pairs={{0,2},{1,3},{2,4},{3,5},{4,6},{5,7},{8,10},{9,11},{10,12},{11,13},... | collective-permute-start | bytes 3145736 | tf_op jit(solution)/shard_map/ppermute | solution.py:463
  828.3 34.4 %collective-permute-start.66 = (bf16[2048,256]{1,0:T(8,128)(2,1)}, bf16[2048,256]{1,0:T(8,128)(2,1)}, u32[]{:S(2)}, u32[]{:S(2)}) collective-permute-start(bf16[2048,256]{1,0:T(8,128)(2,1)} %get-tuple-element.484), channel_id=1, source_target_pairs={{2,0},{3,1},{4,2},{5,3},{6,4},{7,5},{10,8},{11,9},{12,10},{13,11},... | collective-permute-start | bytes 3145736 | tf_op jit(solution)/shard_map/ppermute | solution.py:463
  897.2 38.8 %collective-permute-start.78 = (bf16[4,2048,256]{2,1,0:T(8,128)(2,1)}, bf16[4,2048,256]{2,1,0:T(8,128)(2,1)}, u32[]{:S(2)}, u32[]{:S(2)}) collective-permute-start(bf16[4,2048,256]{2,1,0:T(8,128)(2,1)} %shard_map.327), channel_id=1, source_target_pairs={{0,1},{1,0},{2,3},{3,2},{4,5},{5,4},{6,7},{7,6},{8,9},{9,8},{10,11... | collective-permute-start | bytes 12582920 | tf_op jit(solution)/shard_map/ppermute | solution.py:454
  936.1 142.0 %reduce-scatter.9.cloned.1.call-start = ((), (), s32[]{:S(2)}) async-start(), calls=%async_computation.10 | async-start | bytes 3440640 | tf_op jit(solution)/shard_map/reduce_scatter | solution.py:559
  995.5 33.8 %collective-permute-start.87 = (bf16[2048,256]{1,0:T(8,128)(2,1)}, bf16[2048,256]{1,0:T(8,128)(2,1)S(1)}, u32[]{:S(2)}, u32[]{:S(2)}) collective-permute-start(bf16[2048,256]{1,0:T(8,128)(2,1)} %get-tuple-element.481), channel_id=1, source_target_pairs={{0,2},{1,3},{2,4},{3,5},{8,10},{9,11},{10,12},{11,13},{16,18},{17,... | collective-permute-start | bytes 3145736 | tf_op jit(solution)/shard_map/ppermute | solution.py:463
  (166 other events, 2385.8 us)
Sparse Core Ops, SparseCore 0:
  15.7 69.4 all-gather.4
  87.6 125.6 all-gather.6
  215.7 139.8 all-gather.8
  357.2 111.4 all-gather.10
  491.5 194.5 reduce-scatter.4
  784.3 157.4 reduce-scatter.6
  944.8 43.9 reduce-scatter.10
  1029.5 38.9 reduce-scatter.8

commit v7 on v6

--- a/solution.py
+++ b/solution.py
@@ -477,16 +477,20 @@
     def column_pieces(self, own):
         return self.pieces(own, lambda chip, core: chip * 2 + core)
 
-    def halves(self, p):
-        half = p.shape[0] // 2
-        return [lax.dynamic_slice_in_dim(p, c * half, half, 0) for c in (self.c, 1 - self.c)]
-
-    def row_scatter(self, both):
-        ch = both.shape[0] // self.chips
-        return Scatter(self, lambda j: lax.dynamic_slice_in_dim(both, j * ch, ch, 0))
-
-    def column_scatter(self, both):
-        return Scatter(self, lambda j: lax.dynamic_index_in_dim(both, j, 0, False))
+    def half(self, p, core):
+        count = p.shape[0] // 2
+        return lax.dynamic_slice_in_dim(p, core * count, count, 0)
+
+    def row_scatter(self, p, first, arrived):
+        ch = arrived.shape[0] // self.chips
+        return Scatter(self, lambda j: total(
+            lax.dynamic_slice_in_dim(p, first + j * ch, ch, 0), lax.dynamic_slice_in_dim(arrived, j * ch, ch, 0)
+        ))
+
+    def column_scatter(self, mine, arrived):
+        return Scatter(self, lambda j: total(
+            lax.dynamic_index_in_dim(mine, j, 0, False), lax.dynamic_index_in_dim(arrived, j, 0, False)
+        ))
 
     def row_start(self, rows):
         ch = rows // self.n
@@ -623,7 +627,7 @@
     cosine, sine = (jnp.asarray(table) for table in tables())
 
     n_units = E * fe + shared_down.shape[0]
-    n0 = (n_units // 512 + 1) * 256
+    n0 = n_units // 2 // 256 * 256
     n1 = n_units - n0
     last_step = line.chips - 1
     gate = expert_gate.transpose(0, 2, 1).reshape(E * fe, wide)
@@ -664,9 +668,8 @@
     attended = beside([grad_move], lambda: attention(number // LEN - 1))
     rows, first_round, r1, proj = placed
     q, kr, kv, latent, mixed, log_total = attended
-    mine, theirs = line.halves(mixed)
-    arrived = line.swap(dot(theirs, wo, 1, 0, BF))
-    move = line.row_scatter(total(dot(mine, wo, 1, 0, BF), arrived))
+    arrived = line.swap(dot(line.half(mixed, 1 - line.c), wo, 1, 0, BF))
+    move = line.row_scatter(dot(line.half(mixed, line.c), wo, 1, 0, BF), 0, arrived)
     for _ in range(last_step - 1):
         beside([move, grad_move])
     (grad,) = beside([move], lambda: place_columns(*line.column_pieces(grad_move.result())))
@@ -698,8 +701,9 @@
     )
 
     branch_terms = [(stack0, 2, downs, n0, 0), (stack1, 2, downs, n1, n0)]
-    mine, theirs = line.halves(second_terms)
-    move = line.row_scatter(total(mine, line.swap(theirs)))
+    move = line.row_scatter(
+        second_terms, line.c * (number // 2), line.swap(line.half(second_terms, 1 - line.c))
+    )
     deltas = beside([move], lambda: outer(stack1, 0, 1, second_round, 3 * n1, 0))
     deltas = beside([move], lambda: outer(stack1, 1, 1, second_round, 3 * n1, 1, deltas))
     branch_theirs = beside([move], lambda: back(branch_terms, None, BF, tile, (), 1 - core, line.chips))
@@ -721,7 +725,7 @@
     branch_mine, branch_arrived = beside([move], lambda: (
         back(branch_terms, None, BF, tile, (), core, line.chips), line.swap(branch_theirs)
     ))
-    branch_move = line.column_scatter(total(branch_mine, branch_arrived))
+    branch_move = line.column_scatter(branch_mine, branch_arrived)
     deltas = beside([move, branch_move], lambda: outer(stack1, 2, 1, grad, 3 * n1, 2, deltas))
     router_delta = dot(x2, logits_delta.astype(BF), 0, 0)
     second_gain_delta = jnp.sum(d2 * v2 * r2, axis=0)
@@ -745,30 +749,28 @@
         per_entry = jnp.concatenate([per_entry, jnp.zeros((number - D, E + 2), F32)], axis=0)
     small = small_terms(delta_pairs, wup, delta_kr, query_dot, per_entry)
     first_terms = [(delta_queries, 0, attend_packed, queries_wide, 0)]
-    mine, theirs = line.halves(small)
-    move = line.row_scatter(total(mine, line.swap(theirs)))
+    move = line.row_scatter(small, line.c * (number // 2), line.swap(line.half(small, 1 - line.c)))
+
+    beside([move])
+    delta_wo = beside([move], lambda: dot(mixed, hidden_delta, 0, 0, BF))
 
     def attend_deltas():
         delta_wup = dot(latent, delta_pairs, 0, 0, BF)
         return jnp.concatenate(
             [delta_wq.astype(BF),
-             delta_wup.reshape(n_dp, up_rows, wide).transpose(1, 0, 2).reshape(up_rows, D),
-             dot(mixed, hidden_delta, 0, 0, BF)], axis=0)
-
-    theirs, mine = steps(move, 2, (
-        lambda: back(first_terms, None, BF, tile, (), 1 - core, line.chips),
-        lambda: back(first_terms, None, BF, tile, (), core, line.chips),
-    ))
-    deltas, arrived = beside([move], lambda: (attend_deltas(), line.swap(theirs)))
+             delta_wup.reshape(n_dp, up_rows, wide).transpose(1, 0, 2).reshape(up_rows, D), delta_wo], axis=0)
+
+    deltas = beside([move], attend_deltas)
     attend_sums = scatter_rows(deltas).astype(F32)
     steps(move, last_step - 3)
-    small, both, layer_output = lax.optimization_barrier(
-        (move.result().astype(BF), total(mine, arrived), layer_output)
-    )
+    small, layer_output = lax.optimization_barrier((move.result().astype(BF), layer_output))
     move = Gather(line, small)
-    steps(move, last_step - 1)
-    move.left[-1], move.right[-1], both = lax.optimization_barrier((move.left[-1], move.right[-1], both))
-    first_move = line.column_scatter(both)
+    theirs = beside([move], lambda: back(first_terms, None, BF, tile, (), 1 - core, line.chips))
+    mine, arrived = beside([move], lambda: (
+        back(first_terms, None, BF, tile, (), core, line.chips), line.swap(theirs)
+    ))
+    steps(move, last_step - 3)
+    first_move = line.column_scatter(mine, arrived)
     beside([move, first_move])
     small_pieces, small_at = line.row_pieces(move.result())
     small_pieces, late_sums = lax.optimization_barrier((small_pieces, late_sums))

time: 1100 us -> 1090 us (level)
  waiting for transfers between devices: 247 us -> 234 us
  other arithmetic: 98.8 us -> 111 us
    convert_element_type x14 -> x15, other arithmetic: 37.4 us -> 47.5 us  [total(): return (mine.astype(F32) + arrived.astype(F32)).astype(BF)]
    unnamed x185 -> x177, local copies, waits for them, and re-layouts: 28.4 us -> 23.5 us
  transfers between devices with their start and end apart: 103 -> 103, of which waited for: 39 -> 41; matrix products, arithmetic and copies ran while one was open for 15% -> 16% of each run, Pallas kernels for 44% -> 45%
where the time goes in v7:
time: 1090 us; the launch traced here: 1080 us
  Pallas kernels  482 us (44%)
  waiting for transfers between devices  234 us (21%)
  starting transfers between devices  148 us (14%)
  other arithmetic  111 us (10%)
  local copies, waits for them, and re-layouts  58.2 us (5%)
  matrix products  31 us (3%)
  between operations  16.5 us (2%)
    ppermute x66, waiting for transfers between devices, shift(): return lax.ppermute(a, 'tensor', pairs)  217 us
    ppermute x66, starting transfers between devices, shift(): return lax.ppermute(a, 'tensor', pairs)  143 us
    pallas_call x5, Pallas kernels, back(): pl.pallas_call(body, grid=(T // bt,), in_specs=ins, out_specs=ospec, out_...  131 us
    pallas_call x5, Pallas kernels, outer(): pl.pallas_call(outer_kernel, grid=(count, D // bc), in_specs=ins, out_spe...  111 us
    pallas_call x2, Pallas kernels, units(): pl.pallas_call(functools.partial(units_kernel, fe, first), grid=(T // bt,...  84.2 us
    convert_element_type x15, other arithmetic, total(): return (mine.astype(F32) + arrived.astype(F32)).astype(BF)  47.5 us
    pallas_call x2, Pallas kernels, lift_back(): pl.pallas_call(lift_kernel, grid=(T // bt,), in_specs=[pl.BlockSpec((bt,...  39.8 us
    dot_general x9, matrix products, dot(): lax.dot_general(a, b, (((ca,), (cb,)), ((), ())), preferred_element_type=...  30.7 us
  transfers between devices with their start and end apart: 103, of which 41 were waited for; matrix products, arithmetic and copies ran while one was open for 16% of the time, Pallas kernels for 45%

profile of v7, /device:TPU:0, one launch (start us, length us, event | category | flops | bytes accessed | tf_op | source)
XLA Modules:
  0.0 1080.3 jit_solution(18044420509661472218)
XLA Ops:
  44.2 12.9 %collective-permute-done.3 = bf16[1024,256]{1,0:T(8,128)(2,1)} collective-permute-done((bf16[1024,256]{1,0:T(8,128)(2,1)S(1)}, bf16[1024,256]{1,0:T(8,128)(2,1)}, u32[]{:S(2)}, u32[]{:S(2)}) %collective-permute-start.3) | collective-permute-done | bytes 524320 | tf_op jit(solution)/shard_map/ppermute | solution.py:463
  64.4 11.5 %collective-permute-done.5 = bf16[1024,256]{1,0:T(8,128)(2,1)S(1)} collective-permute-done((bf16[1024,256]{1,0:T(8,128)(2,1)}, bf16[1024,256]{1,0:T(8,128)(2,1)S(1)}, u32[]{:S(2)}, u32[]{:S(2)}) %collective-permute-start.5) | collective-permute-done | bytes 524320 | tf_op jit(solution)/shard_map/ppermute | solution.py:463
  98.2 10.9 %shard_map.306 = (bf16[2048,2048]{1,0:T(8,128)(2,1)}, bf16[2048,2048]{1,0:T(8,128)(2,1)}, f32[2048,1]{1,0:T(8,128)}, f32[2048,1024]{1,0:T(8,128)}) custom-call(s32[8]{0:T(128)} %stack.44.at_ref, bf16[1024,256]{1,0:T(8,128)(2,1)} %get-tuple-element.499.refs_0_, bf16[1024,256]{1,0:T(8,128)(2,1)} %collective-permute-done.10.refs_1_, ...), custom_call_target="tpu_custom_call" | custom-call | flops 4307550208 | bytes 12582912 | tf_op jit(solution)/shard_map/pallas_call | solution.py:192
  135.8 10.6 shard_map.308
  179.1 13.3 %collective-permute-done.26 = bf16[2048,256]{1,0:T(8,128)(2,1)} collective-permute-done((bf16[2048,256]{1,0:T(8,128)(2,1)}, bf16[2048,256]{1,0:T(8,128)(2,1)}, u32[]{:S(2)}, u32[]{:S(2)}) %collective-permute-start.26) | collective-permute-done | bytes 1048608 | tf_op jit(solution)/shard_map/ppermute | solution.py:463
  215.7 16.7 %collective-permute-done.27 = bf16[256,2048]{1,0:T(8,128)(2,1)S(1)} collective-permute-done((bf16[256,2048]{1,0:T(8,128)(2,1)}, bf16[256,2048]{1,0:T(8,128)(2,1)S(1)}, u32[]{:S(2)}, u32[]{:S(2)}) %collective-permute-start.27) | collective-permute-done | bytes 1048608 | tf_op jit(solution)/shard_map/ppermute | solution.py:463
  262.3 11.5 %collective-permute-done.31 = bf16[256,2048]{1,0:T(8,128)(2,1)} collective-permute-done((bf16[256,2048]{1,0:T(8,128)(2,1)}, bf16[256,2048]{1,0:T(8,128)(2,1)}, u32[]{:S(2)}, u32[]{:S(2)}) %collective-permute-start.31) | collective-permute-done | bytes 1048608 | tf_op jit(solution)/shard_map/ppermute | solution.py:463
  286.8 18.7 %shard_map.311.b_ref = bf16[2048,1536]{1,0:T(8,128)(2,1)} custom-call(bf16[2048,2048]{1,0:T(8,128)(2,1)} %shard_map.310.g_ref.x_ref, bf16[3168,2048]{1,0:T(8,128)(2,1)} %all-gather.7.cloned.1.call-done.w_ref.refs_1_.refs_3_), custom_call_target="tpu_custom_call" | custom-call | flops 12884901888 | bytes 20971520 | tf_op jit(solution)/shard_map/pallas_call | solution.py:85
  314.3 21.1 %shard_map.312.b_ref = bf16[2048,1632]{1,0:T(8,128)(2,1)} custom-call(bf16[2048,2048]{1,0:T(8,128)(2,1)} %shard_map.310.g_ref.x_ref, bf16[3168,2048]{1,0:T(8,128)(2,1)} %all-gather.7.cloned.1.call-done.w_ref.refs_1_.refs_3_), custom_call_target="tpu_custom_call" | custom-call | flops 13690208256 | bytes 21757952 | tf_op jit(solution)/shard_map/pallas_call | solution.py:85
  345.0 19.1 %collective-permute-done.43 = bf16[256,2048]{1,0:T(8,128)(2,1)} collective-permute-done((bf16[256,2048]{1,0:T(8,128)(2,1)}, bf16[256,2048]{1,0:T(8,128)(2,1)}, u32[]{:S(2)}, u32[]{:S(2)}) %collective-permute-start.43) | collective-permute-done | bytes 1048608 | tf_op jit(solution)/shard_map/ppermute | solution.py:463
  373.0 11.6 %shard_map.313 = (bf16[2048,2048]{1,0:T(8,128)(2,1)}, bf16[2048,256]{1,0:T(8,128)(2,1)}, f32[2048,16]{1,0:T(8,128)}, f32[2048,16]{1,0:T(8,128)}) custom-call(s32[8]{0:T(128)} %stack.53.at_ref, s32[1]{0:T(128)} %bitcast.38.col_ref, f32[1,2048]{1,0:T(1,128)} %get-tuple-element.479.gain_ref, bf16[16,2048]{1,0:T(8,128)(2,1)} %slice.269.wr_ref, ...), custom_call_target="tpu_custom_call" | custom-call | flops 25165824 | bytes 16777216 | tf_op jit(solution)/shard_map/pallas_call | solution.py:245
  384.6 39.9 %shard_map.314 = (bf16[3,2048,1536]{2,1,0:T(8,128)(2,1)}, f32[2048,16]{1,0:T(8,128)}) custom-call(bf16[2048,2048]{1,0:T(8,128)(2,1)} %get-tuple-element.285.x_ref, bf16[3072,2048]{1,0:T(8,128)(2,1)} %all-gather.9.cloned.1.call-done.wg_ref.wu_ref.refs_1_.refs_3_, bf16[3072,2048]{1,0:T(8,128)(2,1)} %all-gather.9.cloned.1.call-done.wg_ref.wu_ref.refs_1_.refs_3_, ...), custom_call_target="tpu_custom_call" | custom-call | flops 25769803776 | bytes 46137344 | tf_op jit(solution)/shard_map/pallas_call | solution.py:75
  424.5 33.0 %shard_map.315.refs_0_ = bf16[4608,2048]{1,0:T(8,128)(2,1)} custom-call(bf16[3,2048,1536]{2,1,0:T(8,128)(2,1)} %get-tuple-element.290.s_ref.refs_0_.refs_2_, bf16[2048,2048]{1,0:T(8,128)(2,1)} %get-tuple-element.285.x_ref), custom_call_target="tpu_custom_call" | custom-call | flops 25769803776 | bytes 41943040 | tf_op jit(solution)/shard_map/pallas_call | solution.py:156
  457.5 18.6 %shard_map.316 = bf16[4608,2048]{1,0:T(8,128)(2,1)} custom-call(bf16[3,2048,1536]{2,1,0:T(8,128)(2,1)} %get-tuple-element.290.s_ref.refs_0_.refs_2_, bf16[2048,2048]{1,0:T(8,128)(2,1)} %shard_map.310.g_ref.x_ref, bf16[4608,2048]{1,0:T(8,128)(2,1)} %shard_map.315.refs_0_), custom_call_target="tpu_custom_call", output_to_operand_aliasing={{}: (2, {})} | custom-call | flops 12884901888 | bytes 20971520 | tf_op jit(solution)/shard_map/pallas_call | solution.py:156
  476.2 44.4 %shard_map.317 = (bf16[3,2048,1632]{2,1,0:T(8,128)(2,1)}, f32[2048,16]{1,0:T(8,128)}) custom-call(bf16[2048,2048]{1,0:T(8,128)(2,1)} %get-tuple-element.285.x_ref, bf16[3264,2048]{1,0:T(8,128)(2,1)} %all-gather.11.cloned.1.call-done.wg_ref.wu_ref.refs_5_.refs_7_, bf16[3264,2048]{1,0:T(8,128)(2,1)} %all-gather.11.cloned.1.call-done.wg_ref.wu_ref.refs_5_.refs_7_, ...), custom_call_target="tpu_custom_call" | custom-call | flops 27380416512 | bytes 48496640 | tf_op jit(solution)/shard_map/pallas_call | solution.py:75
  520.5 69.7 %shard_map.318 = bf16[2048,2176]{1,0:T(8,128)(2,1)} custom-call(bf16[3,2048,1536]{2,1,0:T(8,128)(2,1)} %get-tuple-element.290.s_ref.refs_0_.refs_2_, bf16[3072,2048]{1,0:T(8,128)(2,1)} %all-gather.9.cloned.1.call-done.wg_ref.wu_ref.refs_1_.refs_3_, bf16[3,2048,1536]{2,1,0:T(8,128)(2,1)} %get-tuple-element.290.s_ref.refs_0_.refs_2_, ...), custom_call_target="tpu_custom_call" | custom-call | flops 53150220288 | bytes 68681728 | tf_op jit(solution)/shard_map/pallas_call | solution.py:144
  608.4 20.0 %shard_map.319.refs_0_ = bf16[4896,2048]{1,0:T(8,128)(2,1)} custom-call(bf16[3,2048,1632]{2,1,0:T(8,128)(2,1)} %get-tuple-element.293.refs_4_.refs_6_.s_ref.refs_2_, bf16[2048,2048]{1,0:T(8,128)(2,1)} %get-tuple-element.285.x_ref), custom_call_target="tpu_custom_call" | custom-call | flops 13690208256 | bytes 21757952 | tf_op jit(solution)/shard_map/pallas_call | solution.py:156
  640.6 19.7 %shard_map.320.refs_0_ = bf16[4896,2048]{1,0:T(8,128)(2,1)} custom-call(bf16[3,2048,1632]{2,1,0:T(8,128)(2,1)} %get-tuple-element.293.refs_4_.refs_6_.s_ref.refs_2_, bf16[2048,2048]{1,0:T(8,128)(2,1)} %get-tuple-element.285.x_ref, bf16[4896,2048]{1,0:T(8,128)(2,1)} %shard_map.319.refs_0_), custom_call_target="tpu_custom_call", output_to_operand_aliasing={{}: (2, {})} | custom-call | flops 13690208256 | bytes 21757952 | tf_op jit(solution)/shard_map/pallas_call | solution.py:156
  675.1 22.9 %shard_map.321 = bf16[4,2048,256]{2,1,0:T(8,128)(2,1)} custom-call(s32[1]{0:T(128)S(6)} %sub.27.core_ref, bf16[3,2048,1536]{2,1,0:T(8,128)(2,1)} %get-tuple-element.290.s_ref.refs_0_.refs_2_, bf16[3168,2048]{1,0:T(8,128)(2,1)} %all-gather.7.cloned.1.call-done.w_ref.refs_1_.refs_3_, bf16[3,2048,1632]{2,1,0:T(8,128)(2,1)} %get-tuple-element.293.refs_4_.refs_6_.s_ref.refs_2_, ...), custom_call_target="tpu_custom_call" | custom-call | flops 13287555072 | bytes 42729472 | tf_op jit(solution)/shard_map/pallas_call | solution.py:144
  713.5 21.9 %shard_map.322 = bf16[4,2048,256]{2,1,0:T(8,128)(2,1)} custom-call(s32[1]{0:T(128)} %bitcast.42.core_ref, bf16[3,2048,1536]{2,1,0:T(8,128)(2,1)} %get-tuple-element.290.s_ref.refs_0_.refs_2_, bf16[3168,2048]{1,0:T(8,128)(2,1)} %all-gather.7.cloned.1.call-done.w_ref.refs_1_.refs_3_, bf16[3,2048,1632]{2,1,0:T(8,128)(2,1)} %get-tuple-element.293.refs_4_.refs_6_.s_ref.refs_2_, ...), custom_call_target="tpu_custom_call" | custom-call | flops 13287555072 | bytes 42729472 | tf_op jit(solution)/shard_map/pallas_call | solution.py:144
  751.9 19.6 %shard_map.323 = bf16[4896,2048]{1,0:T(8,128)(2,1)} custom-call(bf16[3,2048,1632]{2,1,0:T(8,128)(2,1)} %get-tuple-element.293.refs_4_.refs_6_.s_ref.refs_2_, bf16[2048,2048]{1,0:T(8,128)(2,1)} %shard_map.310.g_ref.x_ref, bf16[4896,2048]{1,0:T(8,128)(2,1)} %shard_map.320.refs_0_), custom_call_target="tpu_custom_call", output_to_operand_aliasing={{}: (2, {})} | custom-call | flops 13690208256 | bytes 21757952 | tf_op jit(solution)/shard_map/pallas_call | solution.py:156
  785.2 13.3 %collective-permute-done.62 = bf16[256,2048]{1,0:T(8,128)(2,1)S(1)} collective-permute-done((bf16[256,2048]{1,0:T(8,128)(2,1)}, bf16[256,2048]{1,0:T(8,128)(2,1)S(1)}, u32[]{:S(2)}, u32[]{:S(2)}) %collective-permute-start.62) | collective-permute-done | bytes 1048608 | tf_op jit(solution)/shard_map/ppermute | solution.py:463
  835.8 17.6 %shard_map.325 = (bf16[2048,384]{1,0:T(8,128)(2,1)}, bf16[2048,512]{1,0:T(8,128)(2,1)}, f32[2048,128]{1,0:T(8,128)}, f32[2048,1]{1,0:T(8,128)}) custom-call(bf16[2048,384]{1,0:T(8,128)(2,1)} %get-tuple-element.322.q_ref, bf16[2048,128]{1,0:T(8,128)(2,1)} %get-tuple-element.323.kr_ref, bf16[2048,512]{1,0:T(8,128)(2,1)} %get-tuple-element.324.kv_ref, ...), custom_call_target="tpu_custom_call" | custom-call | flops 5872025600 | bytes 12288000 | tf_op jit(solution)/shard_map/pallas_call | solution.py:429
  1004.8 10.7 shard_map.331
  (510 shorter events, 554.4 us)
Async XLA Ops:
  7.3 88.6 %all-gather.5.cloned.1.call-start = ((), (), s32[]{:S(2)}) async-start(), calls=%async_computation.4 | async-start | bytes 7372800 | tf_op jit(solution)/shard_map/all_gather | solution.py:559
  15.6 271.2 %all-gather.7.cloned.1.call-start = ((), (), s32[]{:S(2)}) async-start(), calls=%async_computation.5 | async-start | bytes 16220160 | tf_op jit(solution)/shard_map/all_gather | solution.py:559
  39.1 345.5 %all-gather.9.cloned.1.call-start = ((), (), s32[]{:S(2)}) async-start(), calls=%async_computation.6 | async-start | bytes 15728640 | tf_op jit(solution)/shard_map/all_gather | solution.py:559
  57.1 419.0 %all-gather.11.cloned.1.call-start = ((), (), s32[]{:S(2)}) async-start(), calls=%async_computation.7 | async-start | bytes 16711680 | tf_op jit(solution)/shard_map/all_gather | solution.py:559
  57.2 37.3 %collective-permute-start.10 = (bf16[1024,256]{1,0:T(8,128)(2,1)}, bf16[1024,256]{1,0:T(8,128)(2,1)}, u32[]{:S(2)}, u32[]{:S(2)}) collective-permute-start(bf16[1024,256]{1,0:T(8,128)(2,1)} %get-tuple-element.499.refs_0_), channel_id=1, source_target_pairs={{0,1},{1,0},{2,3},{3,2},{4,5},{5,4},{6,7},{7,6},{8,9},{9,8},{10,11... | collective-permute-start | bytes 1572872 | tf_op jit(solution)/shard_map/ppermute | solution.py:454
  63.9 33.5 %collective-permute-start.12 = (bf16[1024,256]{1,0:T(8,128)(2,1)S(1)}, bf16[1024,256]{1,0:T(8,128)(2,1)}, u32[]{:S(2)}, u32[]{:S(2)}) collective-permute-start(bf16[1024,256]{1,0:T(8,128)(2,1)S(1)} %broadcast_select_fusion.12.refs_4_), channel_id=1, source_target_pairs={{0,1},{1,0},{2,3},{3,2},{4,5},{5,4},{6,7},{7,6},{8,9},{9,8},{10,11... | collective-permute-start | bytes 1572872 | tf_op jit(solution)/shard_map/ppermute | solution.py:454
  97.4 36.1 %collective-permute-start.18 = (bf16[1024,256]{1,0:T(8,128)(2,1)}, bf16[1024,256]{1,0:T(8,128)(2,1)}, u32[]{:S(2)}, u32[]{:S(2)}) collective-permute-start(bf16[1024,256]{1,0:T(8,128)(2,1)} %get-tuple-element.224.refs_0_), channel_id=1, source_target_pairs={{0,1},{1,0},{2,3},{3,2},{4,5},{5,4},{6,7},{7,6},{8,9},{9,8},{10,11... | collective-permute-start | bytes 1572872 | tf_op jit(solution)/shard_map/ppermute | solution.py:454
  161.7 611.5 %reduce-scatter.5.cloned.1.call-start = ((), (), s32[]{:S(2)}) async-start(), calls=%async_computation.8 | async-start | bytes 23592960 | tf_op jit(solution)/shard_map/reduce_scatter | solution.py:563
  162.6 29.7 %collective-permute-start.26 = (bf16[2048,256]{1,0:T(8,128)(2,1)}, bf16[2048,256]{1,0:T(8,128)(2,1)}, u32[]{:S(2)}, u32[]{:S(2)}) collective-permute-start(bf16[2048,256]{1,0:T(8,128)(2,1)} %collective-permute-done.17), channel_id=1, source_target_pairs={{2,0},{3,1},{4,2},{5,3},{10,8},{11,9},{12,10},{13,11},{18,16},{19,... | collective-permute-start | bytes 3145736 | tf_op jit(solution)/shard_map/ppermute | solution.py:463
  214.3 37.6 %collective-permute-start.33 = (bf16[2048,256]{1,0:T(8,128)(2,1)}, bf16[2048,256]{1,0:T(8,128)(2,1)}, u32[]{:S(2)}, u32[]{:S(2)}) collective-permute-start(bf16[2048,256]{1,0:T(8,128)(2,1)} %refs_0_), channel_id=1, source_target_pairs={{0,1},{1,0},{2,3},{3,2},{4,5},{5,4},{6,7},{7,6},{8,9},{9,8},{10,11... | collective-permute-start | bytes 3145736 | tf_op jit(solution)/shard_map/ppermute | solution.py:454
  342.0 31.0 %collective-permute-start.37 = (bf16[256,2048]{1,0:T(8,128)(2,1)S(1)}, bf16[256,2048]{1,0:T(8,128)(2,1)}, u32[]{:S(2)}, u32[]{:S(2)}) collective-permute-start(bf16[256,2048]{1,0:T(8,128)(2,1)S(1)} %get-tuple-element.453.refs_0_), channel_id=1, source_target_pairs={{0,1},{1,0},{2,3},{3,2},{4,5},{5,4},{6,7},{7,6},{8,9},{9,8},{10,11... | collective-permute-start | bytes 3145736 | tf_op jit(solution)/shard_map/ppermute | solution.py:454
  476.1 514.4 %reduce-scatter.7.cloned.1.call-start = ((), (), s32[]{:S(2)}) async-start(), calls=%async_computation.9 | async-start | bytes 25067520 | tf_op jit(solution)/shard_map/reduce_scatter | solution.py:563
  666.6 31.4 %collective-permute-start.52 = (bf16[256,2176]{1,0:T(8,128)(2,1)S(1)}, bf16[256,2176]{1,0:T(8,128)(2,1)S(1)}, u32[]{:S(2)}, u32[]{:S(2)}) collective-permute-start(bf16[256,2176]{1,0:T(8,128)(2,1)S(1)} %get-tuple-element.455), channel_id=1, source_target_pairs={{0,2},{1,3},{2,4},{3,5},{4,6},{5,7},{8,10},{9,11},{10,12},{11,13},... | collective-permute-start | bytes 3342344 | tf_op jit(solution)/shard_map/ppermute | solution.py:463
  700.4 39.1 %collective-permute-start.56 = (bf16[4,2048,256]{2,1,0:T(8,128)(2,1)}, bf16[4,2048,256]{2,1,0:T(8,128)(2,1)}, u32[]{:S(2)}, u32[]{:S(2)}) collective-permute-start(bf16[4,2048,256]{2,1,0:T(8,128)(2,1)} %shard_map.321), channel_id=1, source_target_pairs={{0,1},{1,0},{2,3},{3,2},{4,5},{5,4},{6,7},{7,6},{8,9},{9,8},{10,11... | collective-permute-start | bytes 12582920 | tf_op jit(solution)/shard_map/ppermute | solution.py:454
  739.6 32.0 %collective-permute-start.57 = (bf16[256,2048]{1,0:T(8,128)(2,1)}, bf16[256,2048]{1,0:T(8,128)(2,1)}, u32[]{:S(2)}, u32[]{:S(2)}) collective-permute-start(bf16[256,2048]{1,0:T(8,128)(2,1)} %collective-permute-done.54), channel_id=1, source_target_pairs={{2,4},{3,5},{4,6},{5,7},{10,12},{11,13},{12,14},{13,15},{18,20},{1... | collective-permute-start | bytes 3145736 | tf_op jit(solution)/shard_map/ppermute | solution.py:463
  741.3 30.3 %collective-permute-start.58 = (bf16[256,2048]{1,0:T(8,128)(2,1)S(1)}, bf16[256,2048]{1,0:T(8,128)(2,1)}, u32[]{:S(2)}, u32[]{:S(2)}) collective-permute-start(bf16[256,2048]{1,0:T(8,128)(2,1)S(1)} %collective-permute-done.55), channel_id=1, source_target_pairs={{2,0},{3,1},{4,2},{5,3},{10,8},{11,9},{12,10},{13,11},{18,16},{19,... | collective-permute-start | bytes 3145736 | tf_op jit(solution)/shard_map/ppermute | solution.py:463
  773.1 248.8 %reduce-scatter.11.cloned.1.call-start = ((), (), s32[]{:S(2)}) async-start(), calls=%async_computation.11 | async-start | bytes 3932160 | tf_op jit(solution)/shard_map/reduce_scatter | solution.py:563
  783.8 35.7 %collective-permute-start.67 = (bf16[256,2048]{1,0:T(8,128)(2,1)}, bf16[256,2048]{1,0:T(8,128)(2,1)S(1)}, u32[]{:S(2)}, u32[]{:S(2)}) collective-permute-start(bf16[256,2048]{1,0:T(8,128)(2,1)} %fusion.3.refs_0_), channel_id=1, source_target_pairs={{0,1},{1,0},{2,3},{3,2},{4,5},{5,4},{6,7},{7,6},{8,9},{9,8},{10,11... | collective-permute-start | bytes 3145736 | tf_op jit(solution)/shard_map/ppermute | solution.py:454
  810.3 43.2 %collective-permute-start.65 = (bf16[2048,256]{1,0:T(8,128)(2,1)}, bf16[2048,256]{1,0:T(8,128)(2,1)}, u32[]{:S(2)}, u32[]{:S(2)}) collective-permute-start(bf16[2048,256]{1,0:T(8,128)(2,1)} %get-tuple-element.467), channel_id=1, source_target_pairs={{0,2},{1,3},{2,4},{3,5},{4,6},{5,7},{8,10},{9,11},{10,12},{11,13},... | collective-permute-start | bytes 3145736 | tf_op jit(solution)/shard_map/ppermute | solution.py:463
  819.5 34.0 %collective-permute-start.66 = (bf16[2048,256]{1,0:T(8,128)(2,1)}, bf16[2048,256]{1,0:T(8,128)(2,1)}, u32[]{:S(2)}, u32[]{:S(2)}) collective-permute-start(bf16[2048,256]{1,0:T(8,128)(2,1)} %get-tuple-element.466), channel_id=1, source_target_pairs={{2,0},{3,1},{4,2},{5,3},{6,4},{7,5},{10,8},{11,9},{12,10},{13,11},... | collective-permute-start | bytes 3145736 | tf_op jit(solution)/shard_map/ppermute | solution.py:463
  934.2 134.5 %reduce-scatter.9.cloned.1.call-start = ((), (), s32[]{:S(2)}) async-start(), calls=%async_computation.10 | async-start | bytes 3440640 | tf_op jit(solution)/shard_map/reduce_scatter | solution.py:563
  958.1 29.9 %collective-permute-start.89 = (bf16[256,640]{1,0:T(8,128)(2,1)S(1)}, bf16[256,640]{1,0:T(8,128)(2,1)S(1)}, u32[]{:S(2)}, u32[]{:S(2)}) collective-permute-start(bf16[256,640]{1,0:T(8,128)(2,1)S(1)} %add_convert_fusion.37.refs_0_), channel_id=1, source_target_pairs={{0,1},{1,0},{2,3},{3,2},{4,5},{5,4},{6,7},{7,6},{8,9},{9,8},{10,11... | collective-permute-start | bytes 983048 | tf_op jit(solution)/shard_map/ppermute | solution.py:454
  958.2 31.0 %collective-permute-start.91 = (bf16[256,640]{1,0:T(8,128)(2,1)S(1)}, bf16[256,640]{1,0:T(8,128)(2,1)}, u32[]{:S(2)}, u32[]{:S(2)}) collective-permute-start(bf16[256,640]{1,0:T(8,128)(2,1)S(1)} %broadcast_select_fusion.16.refs_4_), channel_id=1, source_target_pairs={{0,1},{1,0},{2,3},{3,2},{4,5},{5,4},{6,7},{7,6},{8,9},{9,8},{10,11... | collective-permute-start | bytes 983048 | tf_op jit(solution)/shard_map/ppermute | solution.py:454
  981.5 34.0 %collective-permute-start.87 = (bf16[2048,256]{1,0:T(8,128)(2,1)}, bf16[2048,256]{1,0:T(8,128)(2,1)S(1)}, u32[]{:S(2)}, u32[]{:S(2)}) collective-permute-start(bf16[2048,256]{1,0:T(8,128)(2,1)} %get-tuple-element.463), channel_id=1, source_target_pairs={{0,2},{1,3},{2,4},{3,5},{8,10},{9,11},{10,12},{11,13},{16,18},{17,... | collective-permute-start | bytes 3145736 | tf_op jit(solution)/shard_map/ppermute | solution.py:463
  (162 other events, 2341.2 us)
Sparse Core Ops, SparseCore 0:
  15.7 69.4 all-gather.4
  87.0 125.6 all-gather.6
  214.5 122.3 all-gather.8
  339.2 128.9 all-gather.10
  476.2 170.0 reduce-scatter.4
  773.3 181.3 reduce-scatter.6
  958.2 43.9 reduce-scatter.10
  1015.6 40.7 reduce-scatter.8

commit v8 on v7

--- a/solution.py
+++ b/solution.py
@@ -304,7 +304,7 @@
         compiler_params=params(1),
         cost_estimate=pl.CostEstimate(flops=30*T*wide,bytes_accessed=8*T*wide,transcendentals=T))(small,proj,gain,cosine,sine)
 
-def last_pack_kernel(delta_ref, x_ref, w_ref, small_ref, g_ref, latent_ref, out_ref):
+def last_pack_kernel(delta_ref, x_ref, w_ref, small_ref, g_ref, latent_ref, more_ref, out_ref):
     n=delta_ref.shape[1]
     d=mm(delta_ref[...],x_ref[...],TN)
     out_ref[:n]=d.astype(BF)
@@ -315,17 +315,18 @@
     v=mm(jnp.where(pick,1.0,0.0).astype(BF),small_ref[...],NT)
     line=lax.broadcasted_iota(jnp.int32,v.shape,0)
     v=jnp.where(line==E+1,(v+sums)/g_ref[...],v)
-    out_ref[n:]=jnp.where(line==E+2,latent_ref[...],v).astype(BF)
-
-def last_pack(delta, x, packed, first, small, gain, latent_row, bc=512):
+    out_ref[n:n+32]=jnp.where(line==E+2,latent_ref[...],v).astype(BF)
+    out_ref[n+32:]=more_ref[...]
+
+def last_pack(delta, x, packed, first, small, gain, latent_row, more, bc=512):
     T,D=x.shape; n=delta.shape[1]
     def cols(a): return pl.BlockSpec((a.shape[0],bc),lambda j:(0,j))
     return pl.pallas_call(last_pack_kernel,grid=(D//bc,),
         in_specs=[pl.BlockSpec((T,n),lambda j:(0,0)),cols(x),
-                  pl.BlockSpec((pl.Element(n),pl.Element(bc)),lambda j:(first,j*bc)),pl.BlockSpec((bc,DN),lambda j:(j,R//DN)),cols(gain),cols(latent_row)],
-        out_specs=pl.BlockSpec((n+32,bc),lambda j:(0,j)),out_shape=jax.ShapeDtypeStruct((n+32,D),BF),
+                  pl.BlockSpec((pl.Element(n),pl.Element(bc)),lambda j:(first,j*bc)),pl.BlockSpec((bc,DN),lambda j:(j,R//DN)),cols(gain),cols(latent_row),cols(more)],
+        out_specs=pl.BlockSpec((n+32+more.shape[0],bc),lambda j:(0,j)),out_shape=jax.ShapeDtypeStruct((n+32+more.shape[0],D),BF),
         compiler_params=params(1),
-        cost_estimate=pl.CostEstimate(flops=2*T*D*n,bytes_accessed=2*(T*D+2*n*D+T*n),transcendentals=0))(delta,x,packed,small,gain,latent_row)
+        cost_estimate=pl.CostEstimate(flops=2*T*D*n,bytes_accessed=2*(T*D+2*n*D+T*n),transcendentals=0))(delta,x,packed,small,gain,latent_row,more)
 
 
 def turn(x, cosine, sine):
@@ -462,6 +463,11 @@
         ]
         return lax.ppermute(a, "tensor", pairs)
 
+    def across(self, a, step):
+        n = self.chips
+        pairs = [(2 * k + c, 2 * ((k + step) % n) + c) for k in range(n) for c in (0, 1)]
+        return lax.ppermute(a, "tensor", pairs)
+
     def pieces(self, own, order):
         n = self.chips
         out, at = [], []
@@ -539,6 +545,35 @@
 
     def result(self):
         return self.block(self.line.z).astype(F32) + self.left.astype(F32) + self.right.astype(F32)
+
+
+class GatherAtOnce:
+    def __init__(self, line, block):
+        self.line, self.block = line, block
+
+    def start(self):
+        return [self.line.across(self.block, k) for k in range(1, self.line.chips)]
+
+    def take(self, arrived):
+        self.arrived = list(arrived)
+
+    def result(self):
+        return [self.block] + self.arrived
+
+
+class ScatterAtOnce:
+    def __init__(self, line, block):
+        self.line, self.block = line, block
+
+    def start(self):
+        n, z = self.line.chips, self.line.z
+        return [self.line.across(self.block((z + k) % n), k) for k in range(1, n)]
+
+    def take(self, arrived):
+        self.arrived = list(arrived)
+
+    def result(self):
+        return sum((a.astype(F32) for a in self.arrived), self.block(self.line.z).astype(F32))
 
 
 def beside(moves, job=None):
@@ -748,32 +783,32 @@
     if number > D:
         per_entry = jnp.concatenate([per_entry, jnp.zeros((number - D, E + 2), F32)], axis=0)
     small = small_terms(delta_pairs, wup, delta_kr, query_dot, per_entry)
-    first_terms = [(delta_queries, 0, attend_packed, queries_wide, 0)]
     move = line.row_scatter(small, line.c * (number // 2), line.swap(line.half(small, 1 - line.c)))
 
-    beside([move])
-    delta_wo = beside([move], lambda: dot(mixed, hidden_delta, 0, 0, BF))
+    move = ScatterAtOnce(line, move.block)
 
     def attend_deltas():
         delta_wup = dot(latent, delta_pairs, 0, 0, BF)
         return jnp.concatenate(
             [delta_wq.astype(BF),
-             delta_wup.reshape(n_dp, up_rows, wide).transpose(1, 0, 2).reshape(up_rows, D), delta_wo], axis=0)
+             delta_wup.reshape(n_dp, up_rows, wide).transpose(1, 0, 2).reshape(up_rows, D),
+             dot(mixed, hidden_delta, 0, 0, BF)], axis=0)
 
     deltas = beside([move], attend_deltas)
-    attend_sums = scatter_rows(deltas).astype(F32)
-    steps(move, last_step - 3)
-    small, layer_output = lax.optimization_barrier((move.result().astype(BF), layer_output))
-    move = Gather(line, small)
-    theirs = beside([move], lambda: back(first_terms, None, BF, tile, (), 1 - core, line.chips))
-    mine, arrived = beside([move], lambda: (
-        back(first_terms, None, BF, tile, (), core, line.chips), line.swap(theirs)
-    ))
-    steps(move, last_step - 3)
+    small, layer_output, late_queries = lax.optimization_barrier(
+        (move.result().astype(BF), layer_output, delta_queries)
+    )
+    first_terms = [(late_queries, 0, attend_packed, queries_wide, 0)]
+    move = GatherAtOnce(line, small)
+
+    def first_products():
+        theirs = back(first_terms, None, BF, tile, (), 1 - core, line.chips)
+        return back(first_terms, None, BF, tile, (), core, line.chips), line.swap(theirs)
+
+    mine, arrived = beside([move], first_products)
+    small_pieces, small_at = line.row_pieces(move.result())
+    small_pieces, late_sums, mine = lax.optimization_barrier((small_pieces, late_sums, mine))
     first_move = line.column_scatter(mine, arrived)
-    beside([move, first_move])
-    small_pieces, small_at = line.row_pieces(move.result())
-    small_pieces, late_sums = lax.optimization_barrier((small_pieces, late_sums))
     wld = wproj[queries_wide:]
 
     def last():
@@ -781,14 +816,14 @@
         delta_latent, dots, gain_delta = latent_back(small, proj, latent_g[None], cosine, sine)
         latent_row = jnp.pad(gain_delta.reshape(n_dp, R // n_dp), ((0, 0), (0, wide - R // n_dp))).reshape(1, D)
         return delta_latent, dots, last_pack(
-            delta_latent, first_round, attend_packed, queries_wide, small, first_g[None], latent_row)
+            delta_latent, first_round, attend_packed, queries_wide, small, first_g[None], latent_row, deltas)
 
     delta_latent, dots, pack = beside([first_move], last)
-    steps(first_move, last_step - 2)
+    steps(first_move, last_step - 1)
     first_share = first_move.result()
-    last_sums = scatter_rows(pack).astype(F32)
-    dwld, vectors = last_sums[:latent_wide], last_sums[latent_wide:]
-    dwq, dwup, dwo = split_rows(attend_sums, [queries_wide, up_rows, output_weight.shape[0]])
+    dwld, vectors, dwq, dwup, dwo = split_rows(
+        scatter_rows(pack).astype(F32), [latent_wide, 32, queries_wide, up_rows, output_weight.shape[0]]
+    )
     content = heads_here * DN
     dwq = jnp.concatenate(
         [dwq[:content].reshape(heads_here, DN, wide),

time: 1090 us -> 1090 us (level)
  waiting for transfers between devices: 234 us -> 256 us
  starting transfers between devices: 148 us -> 136 us
    ppermute x0 -> x6, waiting for transfers between devices: none -> 28.8 us  [across(): return lax.ppermute(a, 'tensor', pairs)]
    ppermute x66 -> x54, starting transfers between devices: 143 us -> 117 us  [shift(): return lax.ppermute(a, 'tensor', pairs)]
    ppermute x0 -> x6, starting transfers between devices: none -> 15.3 us  [across(): return lax.ppermute(a, 'tensor', pairs)]
    ppermute x66 -> x54, waiting for transfers between devices: 217 us -> 210 us  [shift(): return lax.ppermute(a, 'tensor', pairs)]
    convert_element_type x15 -> x13, other arithmetic: 47.5 us -> 42.3 us  [total(): return (mine.astype(F32) + arrived.astype(F32)).astype(BF)]
    unnamed x177 -> x171, local copies, waits for them, and re-layouts: 23.5 us -> 21 us
  transfers between devices with their start and end apart: 103 -> 96, of which waited for: 41 -> 39; matrix products, arithmetic and copies ran while one was open for 16% -> 14% of each run, Pallas kernels for 45% -> 45%
where the time goes in v8:
time: 1090 us; the launch traced here: 1080 us
  Pallas kernels  485 us (44%)
  waiting for transfers between devices  256 us (23%)
  starting transfers between devices  136 us (12%)
  other arithmetic  103 us (9%)
  local copies, waits for them, and re-layouts  48.6 us (4%)
  matrix products  31.2 us (3%)
  between operations  16.2 us (1%)
    ppermute x54, waiting for transfers between devices, shift(): return lax.ppermute(a, 'tensor', pairs)  210 us
    pallas_call x5, Pallas kernels, back(): pl.pallas_call(body, grid=(T // bt,), in_specs=ins, out_specs=ospec, out_...  131 us
    ppermute x54, starting transfers between devices, shift(): return lax.ppermute(a, 'tensor', pairs)  117 us
    pallas_call x5, Pallas kernels, outer(): pl.pallas_call(outer_kernel, grid=(count, D // bc), in_specs=ins, out_spe...  111 us
    pallas_call x2, Pallas kernels, units(): pl.pallas_call(functools.partial(units_kernel, fe, first), grid=(T // bt,...  84.1 us
    convert_element_type x13, other arithmetic, total(): return (mine.astype(F32) + arrived.astype(F32)).astype(BF)  42.3 us
    pallas_call x2, Pallas kernels, lift_back(): pl.pallas_call(lift_kernel, grid=(T // bt,), in_specs=[pl.BlockSpec((bt,...  39.8 us
    dot_general x9, matrix products, dot(): lax.dot_general(a, b, (((ca,), (cb,)), ((), ())), preferred_element_type=...  31 us
  transfers between devices with their start and end apart: 96, of which 39 were waited for; matrix products, arithmetic and copies ran while one was open for 14% of the time, Pallas kernels for 45%

profile of v8, /device:TPU:0, one launch (start us, length us, event | category | flops | bytes accessed | tf_op | source)
XLA Modules:
  0.0 1076.0 jit_solution(12228714437556210911)
XLA Ops:
  44.2 12.9 %collective-permute-done.3 = bf16[1024,256]{1,0:T(8,128)(2,1)} collective-permute-done((bf16[1024,256]{1,0:T(8,128)(2,1)S(1)}, bf16[1024,256]{1,0:T(8,128)(2,1)}, u32[]{:S(2)}, u32[]{:S(2)}) %collective-permute-start.3) | collective-permute-done | bytes 524320 | tf_op jit(solution)/shard_map/ppermute | solution.py:464
  64.4 11.5 %collective-permute-done.5 = bf16[1024,256]{1,0:T(8,128)(2,1)S(1)} collective-permute-done((bf16[1024,256]{1,0:T(8,128)(2,1)}, bf16[1024,256]{1,0:T(8,128)(2,1)S(1)}, u32[]{:S(2)}, u32[]{:S(2)}) %collective-permute-start.5) | collective-permute-done | bytes 524320 | tf_op jit(solution)/shard_map/ppermute | solution.py:464
  179.1 13.3 %collective-permute-done.26 = bf16[2048,256]{1,0:T(8,128)(2,1)} collective-permute-done((bf16[2048,256]{1,0:T(8,128)(2,1)}, bf16[2048,256]{1,0:T(8,128)(2,1)}, u32[]{:S(2)}, u32[]{:S(2)}) %collective-permute-start.26) | collective-permute-done | bytes 1048608 | tf_op jit(solution)/shard_map/ppermute | solution.py:464
  215.9 16.6 %collective-permute-done.27 = bf16[256,2048]{1,0:T(8,128)(2,1)S(1)} collective-permute-done((bf16[256,2048]{1,0:T(8,128)(2,1)}, bf16[256,2048]{1,0:T(8,128)(2,1)S(1)}, u32[]{:S(2)}, u32[]{:S(2)}) %collective-permute-start.27) | collective-permute-done | bytes 1048608 | tf_op jit(solution)/shard_map/ppermute | solution.py:464
  286.9 18.7 %shard_map.311.b_ref = bf16[2048,1536]{1,0:T(8,128)(2,1)} custom-call(bf16[2048,2048]{1,0:T(8,128)(2,1)} %shard_map.310.g_ref.x_ref, bf16[3168,2048]{1,0:T(8,128)(2,1)} %all-gather.7.cloned.1.call-done.w_ref.refs_1_.refs_3_), custom_call_target="tpu_custom_call" | custom-call | flops 12884901888 | bytes 20971520 | tf_op jit(solution)/shard_map/pallas_call | solution.py:85
  314.4 21.1 %shard_map.312.b_ref = bf16[2048,1632]{1,0:T(8,128)(2,1)} custom-call(bf16[2048,2048]{1,0:T(8,128)(2,1)} %shard_map.310.g_ref.x_ref, bf16[3168,2048]{1,0:T(8,128)(2,1)} %all-gather.7.cloned.1.call-done.w_ref.refs_1_.refs_3_), custom_call_target="tpu_custom_call" | custom-call | flops 13690208256 | bytes 21757952 | tf_op jit(solution)/shard_map/pallas_call | solution.py:85
  345.0 19.2 %collective-permute-done.43 = bf16[256,2048]{1,0:T(8,128)(2,1)} collective-permute-done((bf16[256,2048]{1,0:T(8,128)(2,1)}, bf16[256,2048]{1,0:T(8,128)(2,1)}, u32[]{:S(2)}, u32[]{:S(2)}) %collective-permute-start.43) | collective-permute-done | bytes 1048608 | tf_op jit(solution)/shard_map/ppermute | solution.py:464
  373.0 11.6 %shard_map.313 = (bf16[2048,2048]{1,0:T(8,128)(2,1)}, bf16[2048,256]{1,0:T(8,128)(2,1)}, f32[2048,16]{1,0:T(8,128)}, f32[2048,16]{1,0:T(8,128)}) custom-call(s32[8]{0:T(128)} %stack.53.at_ref, s32[1]{0:T(128)} %bitcast.38.col_ref, f32[1,2048]{1,0:T(1,128)} %get-tuple-element.467.gain_ref, bf16[16,2048]{1,0:T(8,128)(2,1)} %slice.269.wr_ref, ...), custom_call_target="tpu_custom_call" | custom-call | flops 25165824 | bytes 16777216 | tf_op jit(solution)/shard_map/pallas_call | solution.py:245
  384.7 39.6 %shard_map.314 = (bf16[3,2048,1536]{2,1,0:T(8,128)(2,1)}, f32[2048,16]{1,0:T(8,128)}) custom-call(bf16[2048,2048]{1,0:T(8,128)(2,1)} %get-tuple-element.279.x_ref, bf16[3072,2048]{1,0:T(8,128)(2,1)} %all-gather.9.cloned.1.call-done.wg_ref.wu_ref.refs_1_.refs_3_, bf16[3072,2048]{1,0:T(8,128)(2,1)} %all-gather.9.cloned.1.call-done.wg_ref.wu_ref.refs_1_.refs_3_, ...), custom_call_target="tpu_custom_call" | custom-call | flops 25769803776 | bytes 46137344 | tf_op jit(solution)/shard_map/pallas_call | solution.py:75
  424.3 33.0 %shard_map.315.refs_0_ = bf16[4608,2048]{1,0:T(8,128)(2,1)} custom-call(bf16[3,2048,1536]{2,1,0:T(8,128)(2,1)} %get-tuple-element.284.s_ref.refs_0_.refs_2_, bf16[2048,2048]{1,0:T(8,128)(2,1)} %get-tuple-element.279.x_ref), custom_call_target="tpu_custom_call" | custom-call | flops 25769803776 | bytes 41943040 | tf_op jit(solution)/shard_map/pallas_call | solution.py:156
  457.3 18.6 %shard_map.316 = bf16[4608,2048]{1,0:T(8,128)(2,1)} custom-call(bf16[3,2048,1536]{2,1,0:T(8,128)(2,1)} %get-tuple-element.284.s_ref.refs_0_.refs_2_, bf16[2048,2048]{1,0:T(8,128)(2,1)} %shard_map.310.g_ref.x_ref, bf16[4608,2048]{1,0:T(8,128)(2,1)} %shard_map.315.refs_0_), custom_call_target="tpu_custom_call", output_to_operand_aliasing={{}: (2, {})} | custom-call | flops 12884901888 | bytes 20971520 | tf_op jit(solution)/shard_map/pallas_call | solution.py:156
  476.0 44.5 %shard_map.317 = (bf16[3,2048,1632]{2,1,0:T(8,128)(2,1)}, f32[2048,16]{1,0:T(8,128)}) custom-call(bf16[2048,2048]{1,0:T(8,128)(2,1)} %get-tuple-element.279.x_ref, bf16[3264,2048]{1,0:T(8,128)(2,1)} %all-gather.11.cloned.1.call-done.wg_ref.wu_ref.refs_5_.refs_7_, bf16[3264,2048]{1,0:T(8,128)(2,1)} %all-gather.11.cloned.1.call-done.wg_ref.wu_ref.refs_5_.refs_7_, ...), custom_call_target="tpu_custom_call" | custom-call | flops 27380416512 | bytes 48496640 | tf_op jit(solution)/shard_map/pallas_call | solution.py:75
  520.5 69.7 %shard_map.318 = bf16[2048,2176]{1,0:T(8,128)(2,1)} custom-call(bf16[3,2048,1536]{2,1,0:T(8,128)(2,1)} %get-tuple-element.284.s_ref.refs_0_.refs_2_, bf16[3072,2048]{1,0:T(8,128)(2,1)} %all-gather.9.cloned.1.call-done.wg_ref.wu_ref.refs_1_.refs_3_, bf16[3,2048,1536]{2,1,0:T(8,128)(2,1)} %get-tuple-element.284.s_ref.refs_0_.refs_2_, ...), custom_call_target="tpu_custom_call" | custom-call | flops 53150220288 | bytes 68681728 | tf_op jit(solution)/shard_map/pallas_call | solution.py:144
  608.5 20.3 %shard_map.319.refs_0_ = bf16[4896,2048]{1,0:T(8,128)(2,1)} custom-call(bf16[3,2048,1632]{2,1,0:T(8,128)(2,1)} %get-tuple-element.287.refs_4_.refs_6_.s_ref.refs_2_, bf16[2048,2048]{1,0:T(8,128)(2,1)} %get-tuple-element.279.x_ref), custom_call_target="tpu_custom_call" | custom-call | flops 13690208256 | bytes 21757952 | tf_op jit(solution)/shard_map/pallas_call | solution.py:156
  640.6 19.7 %shard_map.320.refs_0_ = bf16[4896,2048]{1,0:T(8,128)(2,1)} custom-call(bf16[3,2048,1632]{2,1,0:T(8,128)(2,1)} %get-tuple-element.287.refs_4_.refs_6_.s_ref.refs_2_, bf16[2048,2048]{1,0:T(8,128)(2,1)} %get-tuple-element.279.x_ref, bf16[4896,2048]{1,0:T(8,128)(2,1)} %shard_map.319.refs_0_), custom_call_target="tpu_custom_call", output_to_operand_aliasing={{}: (2, {})} | custom-call | flops 13690208256 | bytes 21757952 | tf_op jit(solution)/shard_map/pallas_call | solution.py:156
  675.0 22.7 %shard_map.321 = bf16[4,2048,256]{2,1,0:T(8,128)(2,1)} custom-call(s32[1]{0:T(128)S(6)} %sub.27.core_ref, bf16[3,2048,1536]{2,1,0:T(8,128)(2,1)} %get-tuple-element.284.s_ref.refs_0_.refs_2_, bf16[3168,2048]{1,0:T(8,128)(2,1)} %all-gather.7.cloned.1.call-done.w_ref.refs_1_.refs_3_, bf16[3,2048,1632]{2,1,0:T(8,128)(2,1)} %get-tuple-element.287.refs_4_.refs_6_.s_ref.refs_2_, ...), custom_call_target="tpu_custom_call" | custom-call | flops 13287555072 | bytes 42729472 | tf_op jit(solution)/shard_map/pallas_call | solution.py:144
  713.3 21.9 %shard_map.322 = bf16[4,2048,256]{2,1,0:T(8,128)(2,1)} custom-call(s32[1]{0:T(128)} %bitcast.42.core_ref, bf16[3,2048,1536]{2,1,0:T(8,128)(2,1)} %get-tuple-element.284.s_ref.refs_0_.refs_2_, bf16[3168,2048]{1,0:T(8,128)(2,1)} %all-gather.7.cloned.1.call-done.w_ref.refs_1_.refs_3_, bf16[3,2048,1632]{2,1,0:T(8,128)(2,1)} %get-tuple-element.287.refs_4_.refs_6_.s_ref.refs_2_, ...), custom_call_target="tpu_custom_call" | custom-call | flops 13287555072 | bytes 42729472 | tf_op jit(solution)/shard_map/pallas_call | solution.py:144
  751.7 19.6 %shard_map.323 = bf16[4896,2048]{1,0:T(8,128)(2,1)} custom-call(bf16[3,2048,1632]{2,1,0:T(8,128)(2,1)} %get-tuple-element.287.refs_4_.refs_6_.s_ref.refs_2_, bf16[2048,2048]{1,0:T(8,128)(2,1)} %shard_map.310.g_ref.x_ref, bf16[4896,2048]{1,0:T(8,128)(2,1)} %shard_map.320.refs_0_), custom_call_target="tpu_custom_call", output_to_operand_aliasing={{}: (2, {})} | custom-call | flops 13690208256 | bytes 21757952 | tf_op jit(solution)/shard_map/pallas_call | solution.py:156
  785.3 13.1 %collective-permute-done.62 = bf16[256,2048]{1,0:T(8,128)(2,1)S(1)} collective-permute-done((bf16[256,2048]{1,0:T(8,128)(2,1)}, bf16[256,2048]{1,0:T(8,128)(2,1)S(1)}, u32[]{:S(2)}, u32[]{:S(2)}) %collective-permute-start.62) | collective-permute-done | bytes 1048608 | tf_op jit(solution)/shard_map/ppermute | solution.py:464
  835.9 17.8 %shard_map.325 = (bf16[2048,384]{1,0:T(8,128)(2,1)}, bf16[2048,512]{1,0:T(8,128)(2,1)}, f32[2048,128]{1,0:T(8,128)}, f32[2048,1]{1,0:T(8,128)}) custom-call(bf16[2048,384]{1,0:T(8,128)(2,1)} %get-tuple-element.316.q_ref, bf16[2048,128]{1,0:T(8,128)(2,1)} %get-tuple-element.317.kr_ref, bf16[2048,512]{1,0:T(8,128)(2,1)} %get-tuple-element.318.kv_ref, ...), custom_call_target="tpu_custom_call" | custom-call | flops 5872025600 | bytes 12288000 | tf_op jit(solution)/shard_map/pallas_call | solution.py:430
  895.9 13.7 %collective-permute-done.73 = bf16[256,640]{1,0:T(8,128)(2,1)S(1)} collective-permute-done((bf16[256,640]{1,0:T(8,128)(2,1)S(1)}, bf16[256,640]{1,0:T(8,128)(2,1)S(1)}, u32[]{:S(2)}, u32[]{:S(2)}) %collective-permute-start.73) | collective-permute-done | bytes 327712 | tf_op jit(solution)/shard_map/ppermute | solution.py:469
  936.6 11.6 %collective-permute-done.77.refs_4_ = bf16[256,640]{1,0:T(8,128)(2,1)S(1)} collective-permute-done((bf16[256,640]{1,0:T(8,128)(2,1)S(1)}, bf16[256,640]{1,0:T(8,128)(2,1)S(1)}, u32[]{:S(2)}, u32[]{:S(2)}) %collective-permute-start.77) | collective-permute-done | bytes 327712 | tf_op jit(solution)/shard_map/ppermute | solution.py:469
  978.4 12.6 %shard_map.331 = bf16[1440,2048]{1,0:T(8,128)(2,1)} custom-call(bf16[2048,640]{1,0:T(8,128)(2,1)} %get-tuple-element.367.delta_ref, bf16[2048,2048]{1,0:T(8,128)(2,1)} %get-tuple-element.329.x_ref, bf16[1440,2048]{1,0:T(8,128)(2,1)} %all-gather.5.cloned.1.call-done.refs_9_.refs_1_.w_ref, bf16[2048,640]{1,0:T(8,128)(2,1)} %shard_map.329.small_ref, ...), custom_call_target="tpu_custom_call" | custom-call | flops 5368709120 | bytes 16252928 | tf_op jit(solution)/shard_map/pallas_call | solution.py:324
  1002.9 20.3 %collective-permute-done.85 = bf16[2048,256]{1,0:T(8,128)(2,1)S(1)} collective-permute-done((bf16[2048,256]{1,0:T(8,128)(2,1)S(1)}, bf16[2048,256]{1,0:T(8,128)(2,1)S(1)}, u32[]{:S(2)}, u32[]{:S(2)}) %collective-permute-start.85) | collective-permute-done | bytes 1048608 | tf_op jit(solution)/shard_map/ppermute | solution.py:464
  (485 shorter events, 536.3 us)
Async XLA Ops:
  7.3 88.6 %all-gather.5.cloned.1.call-start = ((), (), s32[]{:S(2)}) async-start(), calls=%async_computation.3 | async-start | bytes 7372800 | tf_op jit(solution)/shard_map/all_gather | solution.py:594
  15.6 271.3 %all-gather.7.cloned.1.call-start = ((), (), s32[]{:S(2)}) async-start(), calls=%async_computation.4 | async-start | bytes 16220160 | tf_op jit(solution)/shard_map/all_gather | solution.py:594
  39.1 345.6 %all-gather.9.cloned.1.call-start = ((), (), s32[]{:S(2)}) async-start(), calls=%async_computation.5 | async-start | bytes 15728640 | tf_op jit(solution)/shard_map/all_gather | solution.py:594
  57.1 418.8 %all-gather.11.cloned.1.call-start = ((), (), s32[]{:S(2)}) async-start(), calls=%async_computation.6 | async-start | bytes 16711680 | tf_op jit(solution)/shard_map/all_gather | solution.py:594
  57.2 37.3 %collective-permute-start.10 = (bf16[1024,256]{1,0:T(8,128)(2,1)}, bf16[1024,256]{1,0:T(8,128)(2,1)}, u32[]{:S(2)}, u32[]{:S(2)}) collective-permute-start(bf16[1024,256]{1,0:T(8,128)(2,1)} %get-tuple-element.490.refs_0_), channel_id=1, source_target_pairs={{0,1},{1,0},{2,3},{3,2},{4,5},{5,4},{6,7},{7,6},{8,9},{9,8},{10,11... | collective-permute-start | bytes 1572872 | tf_op jit(solution)/shard_map/ppermute | solution.py:455
  63.9 33.4 %collective-permute-start.12 = (bf16[1024,256]{1,0:T(8,128)(2,1)S(1)}, bf16[1024,256]{1,0:T(8,128)(2,1)}, u32[]{:S(2)}, u32[]{:S(2)}) collective-permute-start(bf16[1024,256]{1,0:T(8,128)(2,1)S(1)} %broadcast_select_fusion.12.refs_4_), channel_id=1, source_target_pairs={{0,1},{1,0},{2,3},{3,2},{4,5},{5,4},{6,7},{7,6},{8,9},{9,8},{10,11... | collective-permute-start | bytes 1572872 | tf_op jit(solution)/shard_map/ppermute | solution.py:455
  97.3 36.2 %collective-permute-start.18 = (bf16[1024,256]{1,0:T(8,128)(2,1)}, bf16[1024,256]{1,0:T(8,128)(2,1)}, u32[]{:S(2)}, u32[]{:S(2)}) collective-permute-start(bf16[1024,256]{1,0:T(8,128)(2,1)} %get-tuple-element.218.refs_0_), channel_id=1, source_target_pairs={{0,1},{1,0},{2,3},{3,2},{4,5},{5,4},{6,7},{7,6},{8,9},{9,8},{10,11... | collective-permute-start | bytes 1572872 | tf_op jit(solution)/shard_map/ppermute | solution.py:455
  161.7 611.2 %reduce-scatter.4.cloned.1.call-start = ((), (), s32[]{:S(2)}) async-start(), calls=%async_computation.7 | async-start | bytes 23592960 | tf_op jit(solution)/shard_map/reduce_scatter | solution.py:598
  162.6 29.7 %collective-permute-start.26 = (bf16[2048,256]{1,0:T(8,128)(2,1)}, bf16[2048,256]{1,0:T(8,128)(2,1)}, u32[]{:S(2)}, u32[]{:S(2)}) collective-permute-start(bf16[2048,256]{1,0:T(8,128)(2,1)} %collective-permute-done.17), channel_id=1, source_target_pairs={{2,0},{3,1},{4,2},{5,3},{10,8},{11,9},{12,10},{13,11},{18,16},{19,... | collective-permute-start | bytes 3145736 | tf_op jit(solution)/shard_map/ppermute | solution.py:464
  212.7 28.4 %collective-permute-start.30 = (bf16[2048,256]{1,0:T(8,128)(2,1)}, bf16[2048,256]{1,0:T(8,128)(2,1)}, u32[]{:S(2)}, u32[]{:S(2)}) collective-permute-start(bf16[2048,256]{1,0:T(8,128)(2,1)} %collective-permute-done.26), channel_id=1, source_target_pairs={{2,0},{3,1},{10,8},{11,9},{18,16},{19,17},{26,24},{27,25}} | collective-permute-start | bytes 3145736 | tf_op jit(solution)/shard_map/ppermute | solution.py:464
  214.4 37.5 %collective-permute-start.33 = (bf16[2048,256]{1,0:T(8,128)(2,1)}, bf16[2048,256]{1,0:T(8,128)(2,1)}, u32[]{:S(2)}, u32[]{:S(2)}) collective-permute-start(bf16[2048,256]{1,0:T(8,128)(2,1)} %refs_0_), channel_id=1, source_target_pairs={{0,1},{1,0},{2,3},{3,2},{4,5},{5,4},{6,7},{7,6},{8,9},{9,8},{10,11... | collective-permute-start | bytes 3145736 | tf_op jit(solution)/shard_map/ppermute | solution.py:455
  342.0 31.0 %collective-permute-start.37 = (bf16[256,2048]{1,0:T(8,128)(2,1)S(1)}, bf16[256,2048]{1,0:T(8,128)(2,1)}, u32[]{:S(2)}, u32[]{:S(2)}) collective-permute-start(bf16[256,2048]{1,0:T(8,128)(2,1)S(1)} %get-tuple-element.441.refs_0_), channel_id=1, source_target_pairs={{0,1},{1,0},{2,3},{3,2},{4,5},{5,4},{6,7},{7,6},{8,9},{9,8},{10,11... | collective-permute-start | bytes 3145736 | tf_op jit(solution)/shard_map/ppermute | solution.py:455
  343.5 29.5 %collective-permute-start.45 = (bf16[256,2048]{1,0:T(8,128)(2,1)S(1)}, bf16[256,2048]{1,0:T(8,128)(2,1)}, u32[]{:S(2)}, u32[]{:S(2)}) collective-permute-start(bf16[256,2048]{1,0:T(8,128)(2,1)S(1)} %broadcast_select_fusion.3.refs_4_), channel_id=1, source_target_pairs={{0,1},{1,0},{2,3},{3,2},{4,5},{5,4},{6,7},{7,6},{8,9},{9,8},{10,11... | collective-permute-start | bytes 3145736 | tf_op jit(solution)/shard_map/ppermute | solution.py:455
  475.9 478.4 %reduce-scatter.6.cloned.1.call-start = ((), (), s32[]{:S(2)}) async-start(), calls=%async_computation.8 | async-start | bytes 25067520 | tf_op jit(solution)/shard_map/reduce_scatter | solution.py:598
  666.5 31.2 %collective-permute-start.52 = (bf16[256,2176]{1,0:T(8,128)(2,1)S(1)}, bf16[256,2176]{1,0:T(8,128)(2,1)S(1)}, u32[]{:S(2)}, u32[]{:S(2)}) collective-permute-start(bf16[256,2176]{1,0:T(8,128)(2,1)S(1)} %get-tuple-element.443), channel_id=1, source_target_pairs={{0,2},{1,3},{2,4},{3,5},{4,6},{5,7},{8,10},{9,11},{10,12},{11,13},... | collective-permute-start | bytes 3342344 | tf_op jit(solution)/shard_map/ppermute | solution.py:464
  700.3 39.0 %collective-permute-start.56 = (bf16[4,2048,256]{2,1,0:T(8,128)(2,1)}, bf16[4,2048,256]{2,1,0:T(8,128)(2,1)}, u32[]{:S(2)}, u32[]{:S(2)}) collective-permute-start(bf16[4,2048,256]{2,1,0:T(8,128)(2,1)} %shard_map.321), channel_id=1, source_target_pairs={{0,1},{1,0},{2,3},{3,2},{4,5},{5,4},{6,7},{7,6},{8,9},{9,8},{10,11... | collective-permute-start | bytes 12582920 | tf_op jit(solution)/shard_map/ppermute | solution.py:455
  739.3 31.9 %collective-permute-start.57 = (bf16[256,2048]{1,0:T(8,128)(2,1)}, bf16[256,2048]{1,0:T(8,128)(2,1)}, u32[]{:S(2)}, u32[]{:S(2)}) collective-permute-start(bf16[256,2048]{1,0:T(8,128)(2,1)} %collective-permute-done.54), channel_id=1, source_target_pairs={{2,4},{3,5},{4,6},{5,7},{10,12},{11,13},{12,14},{13,15},{18,20},{1... | collective-permute-start | bytes 3145736 | tf_op jit(solution)/shard_map/ppermute | solution.py:464
  741.1 30.2 %collective-permute-start.58 = (bf16[256,2048]{1,0:T(8,128)(2,1)S(1)}, bf16[256,2048]{1,0:T(8,128)(2,1)}, u32[]{:S(2)}, u32[]{:S(2)}) collective-permute-start(bf16[256,2048]{1,0:T(8,128)(2,1)S(1)} %collective-permute-done.55), channel_id=1, source_target_pairs={{2,0},{3,1},{4,2},{5,3},{10,8},{11,9},{12,10},{13,11},{18,16},{19,... | collective-permute-start | bytes 3145736 | tf_op jit(solution)/shard_map/ppermute | solution.py:464
  772.9 288.2 %reduce-scatter.8.cloned.1.call-start = ((), (), s32[]{:S(2)}) async-start(), calls=%async_computation.9 | async-start | bytes 7372800 | tf_op jit(solution)/shard_map/reduce_scatter | solution.py:598
  783.8 35.6 %collective-permute-start.67 = (bf16[256,2048]{1,0:T(8,128)(2,1)}, bf16[256,2048]{1,0:T(8,128)(2,1)S(1)}, u32[]{:S(2)}, u32[]{:S(2)}) collective-permute-start(bf16[256,2048]{1,0:T(8,128)(2,1)} %fusion.3.refs_0_), channel_id=1, source_target_pairs={{0,1},{1,0},{2,3},{3,2},{4,5},{5,4},{6,7},{7,6},{8,9},{9,8},{10,11... | collective-permute-start | bytes 3145736 | tf_op jit(solution)/shard_map/ppermute | solution.py:455
  810.2 43.5 %collective-permute-start.65 = (bf16[2048,256]{1,0:T(8,128)(2,1)}, bf16[2048,256]{1,0:T(8,128)(2,1)}, u32[]{:S(2)}, u32[]{:S(2)}) collective-permute-start(bf16[2048,256]{1,0:T(8,128)(2,1)} %get-tuple-element.455), channel_id=1, source_target_pairs={{0,2},{1,3},{2,4},{3,5},{4,6},{5,7},{8,10},{9,11},{10,12},{11,13},... | collective-permute-start | bytes 3145736 | tf_op jit(solution)/shard_map/ppermute | solution.py:464
  819.5 34.3 %collective-permute-start.66 = (bf16[2048,256]{1,0:T(8,128)(2,1)}, bf16[2048,256]{1,0:T(8,128)(2,1)}, u32[]{:S(2)}, u32[]{:S(2)}) collective-permute-start(bf16[2048,256]{1,0:T(8,128)(2,1)} %get-tuple-element.454), channel_id=1, source_target_pairs={{2,0},{3,1},{4,2},{5,3},{6,4},{7,5},{10,8},{11,9},{12,10},{13,11},... | collective-permute-start | bytes 3145736 | tf_op jit(solution)/shard_map/ppermute | solution.py:464
  918.4 29.8 %collective-permute-start.79 = (bf16[4,2048,256]{2,1,0:T(8,128)(2,1)}, bf16[4,2048,256]{2,1,0:T(8,128)(2,1)}, u32[]{:S(2)}, u32[]{:S(2)}) collective-permute-start(bf16[4,2048,256]{2,1,0:T(8,128)(2,1)} %shard_map.328), channel_id=1, source_target_pairs={{0,1},{1,0},{2,3},{3,2},{4,5},{5,4},{6,7},{7,6},{8,9},{9,8},{10,11... | collective-permute-start | bytes 12582920 | tf_op jit(solution)/shard_map/ppermute | solution.py:455
  958.0 33.0 %collective-permute-start.83 = (bf16[2048,256]{1,0:T(8,128)(2,1)}, bf16[2048,256]{1,0:T(8,128)(2,1)S(1)}, u32[]{:S(2)}, u32[]{:S(2)}) collective-permute-start(bf16[2048,256]{1,0:T(8,128)(2,1)} %get-tuple-element.453), channel_id=1, source_target_pairs={{0,2},{1,3},{8,10},{9,11},{16,18},{17,19},{24,26},{25,27}} | collective-permute-start | bytes 3145736 | tf_op jit(solution)/shard_map/ppermute | solution.py:464
  (152 other events, 2218.8 us)
Sparse Core Ops, SparseCore 0:
  15.7 69.4 all-gather.4
  87.0 125.6 all-gather.6
  214.5 122.3 all-gather.8
  339.2 128.9 all-gather.10
  476.0 170.0 reduce-scatter.3
  773.1 181.2 reduce-scatter.5
  991.1 64.8 reduce-scatter.7

commit v9 on v8

--- a/solution.py
+++ b/solution.py
@@ -782,7 +782,9 @@
     per_entry = jnp.concatenate([second_gain_delta[:, None], query_gain[:, None], router_delta], axis=1)
     if number > D:
         per_entry = jnp.concatenate([per_entry, jnp.zeros((number - D, E + 2), F32)], axis=0)
-    small = small_terms(delta_pairs, wup, delta_kr, query_dot, per_entry)
+    small, late_queries = lax.optimization_barrier(
+        (small_terms(delta_pairs, wup, delta_kr, query_dot, per_entry), delta_queries)
+    )
     move = line.row_scatter(small, line.c * (number // 2), line.swap(line.half(small, 1 - line.c)))
 
     move = ScatterAtOnce(line, move.block)
@@ -794,18 +796,16 @@
              delta_wup.reshape(n_dp, up_rows, wide).transpose(1, 0, 2).reshape(up_rows, D),
              dot(mixed, hidden_delta, 0, 0, BF)], axis=0)
 
-    deltas = beside([move], attend_deltas)
+    def first_products(which, queries):
+        return back([(queries, 0, attend_packed, queries_wide, 0)], None, BF, tile, (), which, line.chips)
+
+    deltas, theirs = beside([move], lambda: (attend_deltas(), first_products(1 - core, late_queries)))
     small, layer_output, late_queries = lax.optimization_barrier(
-        (move.result().astype(BF), layer_output, delta_queries)
-    )
-    first_terms = [(late_queries, 0, attend_packed, queries_wide, 0)]
+        (move.result().astype(BF), layer_output, late_queries)
+    )
     move = GatherAtOnce(line, small)
 
-    def first_products():
-        theirs = back(first_terms, None, BF, tile, (), 1 - core, line.chips)
-        return back(first_terms, None, BF, tile, (), core, line.chips), line.swap(theirs)
-
-    mine, arrived = beside([move], first_products)
+    mine, arrived = beside([move], lambda: (first_products(core, late_queries), line.swap(theirs)))
     small_pieces, small_at = line.row_pieces(move.result())
     small_pieces, late_sums, mine = lax.optimization_barrier((small_pieces, late_sums, mine))
     first_move = line.column_scatter(mine, arrived)

time: 1090 us -> 1090 us (level)
  transfers between devices with their start and end apart: 96 -> 96, of which waited for: 39 -> 38; matrix products, arithmetic and copies ran while one was open for 14% -> 15% of each run, Pallas kernels for 45% -> 45%
where the time goes in v9:
time: 1090 us; the launch traced here: 1080 us
  Pallas kernels  484 us (44%)
  waiting for transfers between devices  251 us (23%)
  starting transfers between devices  135 us (12%)
  other arithmetic  106 us (10%)
  local copies, waits for them, and re-layouts  50.9 us (5%)
  matrix products  32.9 us (3%)
  between operations  16.2 us (1%)
    ppermute x54, waiting for transfers between devices, shift(): return lax.ppermute(a, 'tensor', pairs)  211 us
    pallas_call x5, Pallas kernels, back(): pl.pallas_call(body, grid=(T // bt,), in_specs=ins, out_specs=ospec, out_...  131 us
    ppermute x54, starting transfers between devices, shift(): return lax.ppermute(a, 'tensor', pairs)  116 us
    pallas_call x5, Pallas kernels, outer(): pl.pallas_call(outer_kernel, grid=(count, D // bc), in_specs=ins, out_spe...  111 us
    pallas_call x2, Pallas kernels, units(): pl.pallas_call(functools.partial(units_kernel, fe, first), grid=(T // bt,...  84.1 us
    convert_element_type x13, other arithmetic, total(): return (mine.astype(F32) + arrived.astype(F32)).astype(BF)  44.3 us
    pallas_call x2, Pallas kernels, lift_back(): pl.pallas_call(lift_kernel, grid=(T // bt,), in_specs=[pl.BlockSpec((bt,...  39.8 us
    dot_general x9, matrix products, dot(): lax.dot_general(a, b, (((ca,), (cb,)), ((), ())), preferred_element_type=...  32.7 us
  transfers between devices with their start and end apart: 96, of which 38 were waited for; matrix products, arithmetic and copies ran while one was open for 15% of the time, Pallas kernels for 45%

profile of v9, /device:TPU:0, one launch (start us, length us, event | category | flops | bytes accessed | tf_op | source)
XLA Modules:
  0.0 1075.7 jit_solution(12695706074605070548)
XLA Ops:
  44.2 12.9 %collective-permute-done.3 = bf16[1024,256]{1,0:T(8,128)(2,1)} collective-permute-done((bf16[1024,256]{1,0:T(8,128)(2,1)S(1)}, bf16[1024,256]{1,0:T(8,128)(2,1)}, u32[]{:S(2)}, u32[]{:S(2)}) %collective-permute-start.3) | collective-permute-done | bytes 524320 | tf_op jit(solution)/shard_map/ppermute | solution.py:464
  64.4 11.5 %collective-permute-done.5 = bf16[1024,256]{1,0:T(8,128)(2,1)S(1)} collective-permute-done((bf16[1024,256]{1,0:T(8,128)(2,1)}, bf16[1024,256]{1,0:T(8,128)(2,1)S(1)}, u32[]{:S(2)}, u32[]{:S(2)}) %collective-permute-start.5) | collective-permute-done | bytes 524320 | tf_op jit(solution)/shard_map/ppermute | solution.py:464
  179.1 13.3 %collective-permute-done.26 = bf16[2048,256]{1,0:T(8,128)(2,1)} collective-permute-done((bf16[2048,256]{1,0:T(8,128)(2,1)}, bf16[2048,256]{1,0:T(8,128)(2,1)}, u32[]{:S(2)}, u32[]{:S(2)}) %collective-permute-start.26) | collective-permute-done | bytes 1048608 | tf_op jit(solution)/shard_map/ppermute | solution.py:464
  215.9 16.6 %collective-permute-done.27 = bf16[256,2048]{1,0:T(8,128)(2,1)S(1)} collective-permute-done((bf16[256,2048]{1,0:T(8,128)(2,1)}, bf16[256,2048]{1,0:T(8,128)(2,1)S(1)}, u32[]{:S(2)}, u32[]{:S(2)}) %collective-permute-start.27) | collective-permute-done | bytes 1048608 | tf_op jit(solution)/shard_map/ppermute | solution.py:464
  262.4 11.5 %collective-permute-done.31 = bf16[256,2048]{1,0:T(8,128)(2,1)} collective-permute-done((bf16[256,2048]{1,0:T(8,128)(2,1)}, bf16[256,2048]{1,0:T(8,128)(2,1)}, u32[]{:S(2)}, u32[]{:S(2)}) %collective-permute-start.31) | collective-permute-done | bytes 1048608 | tf_op jit(solution)/shard_map/ppermute | solution.py:464
  286.9 18.7 %shard_map.311.b_ref = bf16[2048,1536]{1,0:T(8,128)(2,1)} custom-call(bf16[2048,2048]{1,0:T(8,128)(2,1)} %shard_map.310.g_ref.x_ref, bf16[3168,2048]{1,0:T(8,128)(2,1)} %all-gather.7.cloned.1.call-done.w_ref.refs_1_.refs_3_), custom_call_target="tpu_custom_call" | custom-call | flops 12884901888 | bytes 20971520 | tf_op jit(solution)/shard_map/pallas_call | solution.py:85
  314.4 21.1 %shard_map.312.b_ref = bf16[2048,1632]{1,0:T(8,128)(2,1)} custom-call(bf16[2048,2048]{1,0:T(8,128)(2,1)} %shard_map.310.g_ref.x_ref, bf16[3168,2048]{1,0:T(8,128)(2,1)} %all-gather.7.cloned.1.call-done.w_ref.refs_1_.refs_3_), custom_call_target="tpu_custom_call" | custom-call | flops 13690208256 | bytes 21757952 | tf_op jit(solution)/shard_map/pallas_call | solution.py:85
  345.0 19.2 %collective-permute-done.43 = bf16[256,2048]{1,0:T(8,128)(2,1)} collective-permute-done((bf16[256,2048]{1,0:T(8,128)(2,1)}, bf16[256,2048]{1,0:T(8,128)(2,1)}, u32[]{:S(2)}, u32[]{:S(2)}) %collective-permute-start.43) | collective-permute-done | bytes 1048608 | tf_op jit(solution)/shard_map/ppermute | solution.py:464
  373.0 11.6 %shard_map.313 = (bf16[2048,2048]{1,0:T(8,128)(2,1)}, bf16[2048,256]{1,0:T(8,128)(2,1)}, f32[2048,16]{1,0:T(8,128)}, f32[2048,16]{1,0:T(8,128)}) custom-call(s32[8]{0:T(128)} %stack.53.at_ref, s32[1]{0:T(128)} %bitcast.38.col_ref, f32[1,2048]{1,0:T(1,128)} %get-tuple-element.473.gain_ref, bf16[16,2048]{1,0:T(8,128)(2,1)} %slice.269.wr_ref, ...), custom_call_target="tpu_custom_call" | custom-call | flops 25165824 | bytes 16777216 | tf_op jit(solution)/shard_map/pallas_call | solution.py:245
  384.7 39.6 %shard_map.314 = (bf16[3,2048,1536]{2,1,0:T(8,128)(2,1)}, f32[2048,16]{1,0:T(8,128)}) custom-call(bf16[2048,2048]{1,0:T(8,128)(2,1)} %get-tuple-element.282.x_ref, bf16[3072,2048]{1,0:T(8,128)(2,1)} %all-gather.9.cloned.1.call-done.wg_ref.wu_ref.refs_1_.refs_3_, bf16[3072,2048]{1,0:T(8,128)(2,1)} %all-gather.9.cloned.1.call-done.wg_ref.wu_ref.refs_1_.refs_3_, ...), custom_call_target="tpu_custom_call" | custom-call | flops 25769803776 | bytes 46137344 | tf_op jit(solution)/shard_map/pallas_call | solution.py:75
  424.3 33.0 %shard_map.315.refs_0_ = bf16[4608,2048]{1,0:T(8,128)(2,1)} custom-call(bf16[3,2048,1536]{2,1,0:T(8,128)(2,1)} %get-tuple-element.287.s_ref.refs_0_.refs_2_, bf16[2048,2048]{1,0:T(8,128)(2,1)} %get-tuple-element.282.x_ref), custom_call_target="tpu_custom_call" | custom-call | flops 25769803776 | bytes 41943040 | tf_op jit(solution)/shard_map/pallas_call | solution.py:156
  457.3 18.6 %shard_map.316 = bf16[4608,2048]{1,0:T(8,128)(2,1)} custom-call(bf16[3,2048,1536]{2,1,0:T(8,128)(2,1)} %get-tuple-element.287.s_ref.refs_0_.refs_2_, bf16[2048,2048]{1,0:T(8,128)(2,1)} %shard_map.310.g_ref.x_ref, bf16[4608,2048]{1,0:T(8,128)(2,1)} %shard_map.315.refs_0_), custom_call_target="tpu_custom_call", output_to_operand_aliasing={{}: (2, {})} | custom-call | flops 12884901888 | bytes 20971520 | tf_op jit(solution)/shard_map/pallas_call | solution.py:156
  476.0 44.5 %shard_map.317 = (bf16[3,2048,1632]{2,1,0:T(8,128)(2,1)}, f32[2048,16]{1,0:T(8,128)}) custom-call(bf16[2048,2048]{1,0:T(8,128)(2,1)} %get-tuple-element.282.x_ref, bf16[3264,2048]{1,0:T(8,128)(2,1)} %all-gather.11.cloned.1.call-done.wg_ref.wu_ref.refs_5_.refs_7_, bf16[3264,2048]{1,0:T(8,128)(2,1)} %all-gather.11.cloned.1.call-done.wg_ref.wu_ref.refs_5_.refs_7_, ...), custom_call_target="tpu_custom_call" | custom-call | flops 27380416512 | bytes 48496640 | tf_op jit(solution)/shard_map/pallas_call | solution.py:75
  520.5 69.7 %shard_map.318 = bf16[2048,2176]{1,0:T(8,128)(2,1)} custom-call(bf16[3,2048,1536]{2,1,0:T(8,128)(2,1)} %get-tuple-element.287.s_ref.refs_0_.refs_2_, bf16[3072,2048]{1,0:T(8,128)(2,1)} %all-gather.9.cloned.1.call-done.wg_ref.wu_ref.refs_1_.refs_3_, bf16[3,2048,1536]{2,1,0:T(8,128)(2,1)} %get-tuple-element.287.s_ref.refs_0_.refs_2_, ...), custom_call_target="tpu_custom_call" | custom-call | flops 53150220288 | bytes 68681728 | tf_op jit(solution)/shard_map/pallas_call | solution.py:144
  608.5 20.3 %shard_map.319.refs_0_ = bf16[4896,2048]{1,0:T(8,128)(2,1)} custom-call(bf16[3,2048,1632]{2,1,0:T(8,128)(2,1)} %get-tuple-element.290.refs_4_.refs_6_.s_ref.refs_2_, bf16[2048,2048]{1,0:T(8,128)(2,1)} %get-tuple-element.282.x_ref), custom_call_target="tpu_custom_call" | custom-call | flops 13690208256 | bytes 21757952 | tf_op jit(solution)/shard_map/pallas_call | solution.py:156
  640.6 19.7 %shard_map.320.refs_0_ = bf16[4896,2048]{1,0:T(8,128)(2,1)} custom-call(bf16[3,2048,1632]{2,1,0:T(8,128)(2,1)} %get-tuple-element.290.refs_4_.refs_6_.s_ref.refs_2_, bf16[2048,2048]{1,0:T(8,128)(2,1)} %get-tuple-element.282.x_ref, bf16[4896,2048]{1,0:T(8,128)(2,1)} %shard_map.319.refs_0_), custom_call_target="tpu_custom_call", output_to_operand_aliasing={{}: (2, {})} | custom-call | flops 13690208256 | bytes 21757952 | tf_op jit(solution)/shard_map/pallas_call | solution.py:156
  675.0 22.7 %shard_map.321 = bf16[4,2048,256]{2,1,0:T(8,128)(2,1)} custom-call(s32[1]{0:T(128)S(6)} %sub.27.core_ref, bf16[3,2048,1536]{2,1,0:T(8,128)(2,1)} %get-tuple-element.287.s_ref.refs_0_.refs_2_, bf16[3168,2048]{1,0:T(8,128)(2,1)} %all-gather.7.cloned.1.call-done.w_ref.refs_1_.refs_3_, bf16[3,2048,1632]{2,1,0:T(8,128)(2,1)} %get-tuple-element.290.refs_4_.refs_6_.s_ref.refs_2_, ...), custom_call_target="tpu_custom_call" | custom-call | flops 13287555072 | bytes 42729472 | tf_op jit(solution)/shard_map/pallas_call | solution.py:144
  713.2 21.9 %shard_map.322 = bf16[4,2048,256]{2,1,0:T(8,128)(2,1)} custom-call(s32[1]{0:T(128)} %bitcast.42.core_ref, bf16[3,2048,1536]{2,1,0:T(8,128)(2,1)} %get-tuple-element.287.s_ref.refs_0_.refs_2_, bf16[3168,2048]{1,0:T(8,128)(2,1)} %all-gather.7.cloned.1.call-done.w_ref.refs_1_.refs_3_, bf16[3,2048,1632]{2,1,0:T(8,128)(2,1)} %get-tuple-element.290.refs_4_.refs_6_.s_ref.refs_2_, ...), custom_call_target="tpu_custom_call" | custom-call | flops 13287555072 | bytes 42729472 | tf_op jit(solution)/shard_map/pallas_call | solution.py:144
  751.6 19.6 %shard_map.323 = bf16[4896,2048]{1,0:T(8,128)(2,1)} custom-call(bf16[3,2048,1632]{2,1,0:T(8,128)(2,1)} %get-tuple-element.290.refs_4_.refs_6_.s_ref.refs_2_, bf16[2048,2048]{1,0:T(8,128)(2,1)} %shard_map.310.g_ref.x_ref, bf16[4896,2048]{1,0:T(8,128)(2,1)} %shard_map.320.refs_0_), custom_call_target="tpu_custom_call", output_to_operand_aliasing={{}: (2, {})} | custom-call | flops 13690208256 | bytes 21757952 | tf_op jit(solution)/shard_map/pallas_call | solution.py:156
  785.2 13.1 %collective-permute-done.62 = bf16[256,2048]{1,0:T(8,128)(2,1)S(1)} collective-permute-done((bf16[256,2048]{1,0:T(8,128)(2,1)}, bf16[256,2048]{1,0:T(8,128)(2,1)S(1)}, u32[]{:S(2)}, u32[]{:S(2)}) %collective-permute-start.62) | collective-permute-done | bytes 1048608 | tf_op jit(solution)/shard_map/ppermute | solution.py:464
  835.8 17.8 %shard_map.325 = (bf16[2048,384]{1,0:T(8,128)(2,1)}, bf16[2048,512]{1,0:T(8,128)(2,1)}, f32[2048,128]{1,0:T(8,128)}, f32[2048,1]{1,0:T(8,128)}) custom-call(bf16[2048,384]{1,0:T(8,128)(2,1)} %get-tuple-element.319.q_ref, bf16[2048,128]{1,0:T(8,128)(2,1)} %get-tuple-element.320.kr_ref, bf16[2048,512]{1,0:T(8,128)(2,1)} %get-tuple-element.321.kv_ref, ...), custom_call_target="tpu_custom_call" | custom-call | flops 5872025600 | bytes 12288000 | tf_op jit(solution)/shard_map/pallas_call | solution.py:430
  935.4 11.8 %collective-permute-done.77.refs_4_ = bf16[256,640]{1,0:T(8,128)(2,1)S(1)} collective-permute-done((bf16[256,640]{1,0:T(8,128)(2,1)S(1)}, bf16[256,640]{1,0:T(8,128)(2,1)S(1)}, u32[]{:S(2)}, u32[]{:S(2)}) %collective-permute-start.77) | collective-permute-done | bytes 327712 | tf_op jit(solution)/shard_map/ppermute | solution.py:469
  977.6 12.6 %shard_map.331 = bf16[1440,2048]{1,0:T(8,128)(2,1)} custom-call(bf16[2048,640]{1,0:T(8,128)(2,1)} %get-tuple-element.373.delta_ref, bf16[2048,2048]{1,0:T(8,128)(2,1)} %get-tuple-element.332.x_ref, bf16[1440,2048]{1,0:T(8,128)(2,1)} %all-gather.5.cloned.1.call-done.refs_9_.refs_1_.w_ref, bf16[2048,640]{1,0:T(8,128)(2,1)} %shard_map.329.small_ref, ...), custom_call_target="tpu_custom_call" | custom-call | flops 5368709120 | bytes 16252928 | tf_op jit(solution)/shard_map/pallas_call | solution.py:324
  1002.3 20.4 %collective-permute-done.85 = bf16[2048,256]{1,0:T(8,128)(2,1)S(1)} collective-permute-done((bf16[2048,256]{1,0:T(8,128)(2,1)S(1)}, bf16[2048,256]{1,0:T(8,128)(2,1)S(1)}, u32[]{:S(2)}, u32[]{:S(2)}) %collective-permute-start.85) | collective-permute-done | bytes 1048608 | tf_op jit(solution)/shard_map/ppermute | solution.py:464
  (485 shorter events, 537.9 us)
Async XLA Ops:
  7.3 88.6 %all-gather.5.cloned.1.call-start = ((), (), s32[]{:S(2)}) async-start(), calls=%async_computation.3 | async-start | bytes 7372800 | tf_op jit(solution)/shard_map/all_gather | solution.py:594
  15.6 271.3 %all-gather.7.cloned.1.call-start = ((), (), s32[]{:S(2)}) async-start(), calls=%async_computation.4 | async-start | bytes 16220160 | tf_op jit(solution)/shard_map/all_gather | solution.py:594
  39.1 345.6 %all-gather.9.cloned.1.call-start = ((), (), s32[]{:S(2)}) async-start(), calls=%async_computation.5 | async-start | bytes 15728640 | tf_op jit(solution)/shard_map/all_gather | solution.py:594
  57.1 418.8 %all-gather.11.cloned.1.call-start = ((), (), s32[]{:S(2)}) async-start(), calls=%async_computation.6 | async-start | bytes 16711680 | tf_op jit(solution)/shard_map/all_gather | solution.py:594
  57.2 37.3 %collective-permute-start.10 = (bf16[1024,256]{1,0:T(8,128)(2,1)}, bf16[1024,256]{1,0:T(8,128)(2,1)}, u32[]{:S(2)}, u32[]{:S(2)}) collective-permute-start(bf16[1024,256]{1,0:T(8,128)(2,1)} %get-tuple-element.496.refs_0_), channel_id=1, source_target_pairs={{0,1},{1,0},{2,3},{3,2},{4,5},{5,4},{6,7},{7,6},{8,9},{9,8},{10,11... | collective-permute-start | bytes 1572872 | tf_op jit(solution)/shard_map/ppermute | solution.py:455
  63.9 33.4 %collective-permute-start.12 = (bf16[1024,256]{1,0:T(8,128)(2,1)S(1)}, bf16[1024,256]{1,0:T(8,128)(2,1)}, u32[]{:S(2)}, u32[]{:S(2)}) collective-permute-start(bf16[1024,256]{1,0:T(8,128)(2,1)S(1)} %broadcast_select_fusion.12.refs_4_), channel_id=1, source_target_pairs={{0,1},{1,0},{2,3},{3,2},{4,5},{5,4},{6,7},{7,6},{8,9},{9,8},{10,11... | collective-permute-start | bytes 1572872 | tf_op jit(solution)/shard_map/ppermute | solution.py:455
  97.3 36.2 %collective-permute-start.18 = (bf16[1024,256]{1,0:T(8,128)(2,1)}, bf16[1024,256]{1,0:T(8,128)(2,1)}, u32[]{:S(2)}, u32[]{:S(2)}) collective-permute-start(bf16[1024,256]{1,0:T(8,128)(2,1)} %get-tuple-element.221.refs_0_), channel_id=1, source_target_pairs={{0,1},{1,0},{2,3},{3,2},{4,5},{5,4},{6,7},{7,6},{8,9},{9,8},{10,11... | collective-permute-start | bytes 1572872 | tf_op jit(solution)/shard_map/ppermute | solution.py:455
  161.7 611.2 %reduce-scatter.4.cloned.1.call-start = ((), (), s32[]{:S(2)}) async-start(), calls=%async_computation.7 | async-start | bytes 23592960 | tf_op jit(solution)/shard_map/reduce_scatter | solution.py:598
  162.6 29.7 %collective-permute-start.26 = (bf16[2048,256]{1,0:T(8,128)(2,1)}, bf16[2048,256]{1,0:T(8,128)(2,1)}, u32[]{:S(2)}, u32[]{:S(2)}) collective-permute-start(bf16[2048,256]{1,0:T(8,128)(2,1)} %collective-permute-done.17), channel_id=1, source_target_pairs={{2,0},{3,1},{4,2},{5,3},{10,8},{11,9},{12,10},{13,11},{18,16},{19,... | collective-permute-start | bytes 3145736 | tf_op jit(solution)/shard_map/ppermute | solution.py:464
  212.7 28.4 %collective-permute-start.30 = (bf16[2048,256]{1,0:T(8,128)(2,1)}, bf16[2048,256]{1,0:T(8,128)(2,1)}, u32[]{:S(2)}, u32[]{:S(2)}) collective-permute-start(bf16[2048,256]{1,0:T(8,128)(2,1)} %collective-permute-done.26), channel_id=1, source_target_pairs={{2,0},{3,1},{10,8},{11,9},{18,16},{19,17},{26,24},{27,25}} | collective-permute-start | bytes 3145736 | tf_op jit(solution)/shard_map/ppermute | solution.py:464
  214.4 37.5 %collective-permute-start.33 = (bf16[2048,256]{1,0:T(8,128)(2,1)}, bf16[2048,256]{1,0:T(8,128)(2,1)}, u32[]{:S(2)}, u32[]{:S(2)}) collective-permute-start(bf16[2048,256]{1,0:T(8,128)(2,1)} %refs_0_), channel_id=1, source_target_pairs={{0,1},{1,0},{2,3},{3,2},{4,5},{5,4},{6,7},{7,6},{8,9},{9,8},{10,11... | collective-permute-start | bytes 3145736 | tf_op jit(solution)/shard_map/ppermute | solution.py:455
  342.0 31.0 %collective-permute-start.37 = (bf16[256,2048]{1,0:T(8,128)(2,1)S(1)}, bf16[256,2048]{1,0:T(8,128)(2,1)}, u32[]{:S(2)}, u32[]{:S(2)}) collective-permute-start(bf16[256,2048]{1,0:T(8,128)(2,1)S(1)} %get-tuple-element.447.refs_0_), channel_id=1, source_target_pairs={{0,1},{1,0},{2,3},{3,2},{4,5},{5,4},{6,7},{7,6},{8,9},{9,8},{10,11... | collective-permute-start | bytes 3145736 | tf_op jit(solution)/shard_map/ppermute | solution.py:455
  343.5 29.5 %collective-permute-start.45 = (bf16[256,2048]{1,0:T(8,128)(2,1)S(1)}, bf16[256,2048]{1,0:T(8,128)(2,1)}, u32[]{:S(2)}, u32[]{:S(2)}) collective-permute-start(bf16[256,2048]{1,0:T(8,128)(2,1)S(1)} %broadcast_select_fusion.3.refs_4_), channel_id=1, source_target_pairs={{0,1},{1,0},{2,3},{3,2},{4,5},{5,4},{6,7},{7,6},{8,9},{9,8},{10,11... | collective-permute-start | bytes 3145736 | tf_op jit(solution)/shard_map/ppermute | solution.py:455
  475.9 478.5 %reduce-scatter.6.cloned.1.call-start = ((), (), s32[]{:S(2)}) async-start(), calls=%async_computation.8 | async-start | bytes 25067520 | tf_op jit(solution)/shard_map/reduce_scatter | solution.py:598
  666.5 31.2 %collective-permute-start.52 = (bf16[256,2176]{1,0:T(8,128)(2,1)S(1)}, bf16[256,2176]{1,0:T(8,128)(2,1)S(1)}, u32[]{:S(2)}, u32[]{:S(2)}) collective-permute-start(bf16[256,2176]{1,0:T(8,128)(2,1)S(1)} %get-tuple-element.449), channel_id=1, source_target_pairs={{0,2},{1,3},{2,4},{3,5},{4,6},{5,7},{8,10},{9,11},{10,12},{11,13},... | collective-permute-start | bytes 3342344 | tf_op jit(solution)/shard_map/ppermute | solution.py:464
  700.3 39.0 %collective-permute-start.56 = (bf16[4,2048,256]{2,1,0:T(8,128)(2,1)}, bf16[4,2048,256]{2,1,0:T(8,128)(2,1)}, u32[]{:S(2)}, u32[]{:S(2)}) collective-permute-start(bf16[4,2048,256]{2,1,0:T(8,128)(2,1)} %shard_map.321), channel_id=1, source_target_pairs={{0,1},{1,0},{2,3},{3,2},{4,5},{5,4},{6,7},{7,6},{8,9},{9,8},{10,11... | collective-permute-start | bytes 12582920 | tf_op jit(solution)/shard_map/ppermute | solution.py:455
  739.3 31.9 %collective-permute-start.57 = (bf16[256,2048]{1,0:T(8,128)(2,1)}, bf16[256,2048]{1,0:T(8,128)(2,1)}, u32[]{:S(2)}, u32[]{:S(2)}) collective-permute-start(bf16[256,2048]{1,0:T(8,128)(2,1)} %collective-permute-done.54), channel_id=1, source_target_pairs={{2,4},{3,5},{4,6},{5,7},{10,12},{11,13},{12,14},{13,15},{18,20},{1... | collective-permute-start | bytes 3145736 | tf_op jit(solution)/shard_map/ppermute | solution.py:464
  741.0 30.2 %collective-permute-start.58 = (bf16[256,2048]{1,0:T(8,128)(2,1)S(1)}, bf16[256,2048]{1,0:T(8,128)(2,1)}, u32[]{:S(2)}, u32[]{:S(2)}) collective-permute-start(bf16[256,2048]{1,0:T(8,128)(2,1)S(1)} %collective-permute-done.55), channel_id=1, source_target_pairs={{2,0},{3,1},{4,2},{5,3},{10,8},{11,9},{12,10},{13,11},{18,16},{19,... | collective-permute-start | bytes 3145736 | tf_op jit(solution)/shard_map/ppermute | solution.py:464
  772.9 288.0 %reduce-scatter.8.cloned.1.call-start = ((), (), s32[]{:S(2)}) async-start(), calls=%async_computation.9 | async-start | bytes 7372800 | tf_op jit(solution)/shard_map/reduce_scatter | solution.py:598
  783.8 35.6 %collective-permute-start.67 = (bf16[256,2048]{1,0:T(8,128)(2,1)}, bf16[256,2048]{1,0:T(8,128)(2,1)S(1)}, u32[]{:S(2)}, u32[]{:S(2)}) collective-permute-start(bf16[256,2048]{1,0:T(8,128)(2,1)} %fusion.3.refs_0_), channel_id=1, source_target_pairs={{0,1},{1,0},{2,3},{3,2},{4,5},{5,4},{6,7},{7,6},{8,9},{9,8},{10,11... | collective-permute-start | bytes 3145736 | tf_op jit(solution)/shard_map/ppermute | solution.py:455
  810.1 43.6 %collective-permute-start.65 = (bf16[2048,256]{1,0:T(8,128)(2,1)}, bf16[2048,256]{1,0:T(8,128)(2,1)}, u32[]{:S(2)}, u32[]{:S(2)}) collective-permute-start(bf16[2048,256]{1,0:T(8,128)(2,1)} %get-tuple-element.461), channel_id=1, source_target_pairs={{0,2},{1,3},{2,4},{3,5},{4,6},{5,7},{8,10},{9,11},{10,12},{11,13},... | collective-permute-start | bytes 3145736 | tf_op jit(solution)/shard_map/ppermute | solution.py:464
  819.4 34.2 %collective-permute-start.66 = (bf16[2048,256]{1,0:T(8,128)(2,1)}, bf16[2048,256]{1,0:T(8,128)(2,1)}, u32[]{:S(2)}, u32[]{:S(2)}) collective-permute-start(bf16[2048,256]{1,0:T(8,128)(2,1)} %get-tuple-element.460), channel_id=1, source_target_pairs={{2,0},{3,1},{4,2},{5,3},{6,4},{7,5},{10,8},{11,9},{12,10},{13,11},... | collective-permute-start | bytes 3145736 | tf_op jit(solution)/shard_map/ppermute | solution.py:464
  911.4 35.9 %collective-permute-start.79 = (bf16[4,2048,256]{2,1,0:T(8,128)(2,1)}, bf16[4,2048,256]{2,1,0:T(8,128)(2,1)}, u32[]{:S(2)}, u32[]{:S(2)}) collective-permute-start(bf16[4,2048,256]{2,1,0:T(8,128)(2,1)} %shard_map.327), channel_id=1, source_target_pairs={{0,1},{1,0},{2,3},{3,2},{4,5},{5,4},{6,7},{7,6},{8,9},{9,8},{10,11... | collective-permute-start | bytes 12582920 | tf_op jit(solution)/shard_map/ppermute | solution.py:455
  958.1 32.2 %collective-permute-start.83 = (bf16[2048,256]{1,0:T(8,128)(2,1)}, bf16[2048,256]{1,0:T(8,128)(2,1)S(1)}, u32[]{:S(2)}, u32[]{:S(2)}) collective-permute-start(bf16[2048,256]{1,0:T(8,128)(2,1)} %get-tuple-element.459), channel_id=1, source_target_pairs={{0,2},{1,3},{8,10},{9,11},{16,18},{17,19},{24,26},{25,27}} | collective-permute-start | bytes 3145736 | tf_op jit(solution)/shard_map/ppermute | solution.py:464
  (152 other events, 2197.6 us)
Sparse Core Ops, SparseCore 0:
  15.7 69.4 all-gather.4
  87.0 125.6 all-gather.6
  214.5 122.3 all-gather.8
  339.2 128.9 all-gather.10
  476.0 170.0 reduce-scatter.3
  773.0 181.3 reduce-scatter.5
  990.4 64.6 reduce-scatter.7
